TPU v7x, 32 devices: a whole 2x2x4 slice. The times are simulated.
32 devices in a mesh: grp: 2 (over x), tm: 16 (over z, y, core).
Axes of the slice: x: 2, y: 2, z: 4, core: 2. Of those that a mesh axis runs over, the one named last changes fastest.
Arguments:
- inputs: bfloat16 [2, 2048, 1536], P('grp', 'tm'), may hold values from -16 to 16
- norm_gain: float32 [1536], replicated, may hold values from 0.1 to 1.9
- query_weight: bfloat16 [1536, 768], P('tm', 'grp'), may hold values from -0.15625 to 0.15625
- key_weight: bfloat16 [1536, 768], P('tm', 'grp'), may hold values from -0.15625 to 0.15625
- value_weight: bfloat16 [1536, 768], P('tm', 'grp'), may hold values from -0.15625 to 0.15625
- output_weight: bfloat16 [1536, 768], P('tm', 'grp'), may hold values from -0.5 to 0.5
- content_bias: float32 [768], replicated, may hold values from -4 to 4
- position_bias: float32 [768], replicated, may hold values from -4 to 4
- position_keys: bfloat16 [256, 768], replicated, may hold values from -6 to 6
- start_flags: int32 [2, 16], P('grp', 'tm'), may hold values from 0 to 1, as said below
- cotangent: bfloat16 [2, 2048, 1536], P('grp', 'tm'), may hold values from -6 to 6
Outputs:
- layer_out: bfloat16 [2, 2048, 1536], P('grp', 'tm')
- input_grad: bfloat16 [2, 2048, 1536], P('grp', 'tm')
Inputs may be any that keep to these rules, and one draw needn't show every extreme that they name: start_flags[r, 0] is 1 for every recording r.
All inputs are finite; a program needn't handle non-finite values.
Results may differ from a plain program's by a relative error of at most 0.013.
Values may be sent and summed in bfloat16 or wider, within the bound.
No kernel may reach another device: no remote copies, remote signals or barrier semaphores. Data moves between devices by JAX's collectives and lax.ppermute only.
A program may use at most 64 MiB of HBM per device.

v0:
```python
import jax
import jax.numpy as jnp
from jax import lax
from jax.sharding import PartitionSpec as P

H = 6
DH = 128


epsilon = 1e-05


def from_behind(block, axis, distance):
    devices = range(lax.axis_size(axis))
    route = [(i - distance, i) for i in devices if i - distance in devices]
    return lax.ppermute(block, axis, route)


def normalize_project(
    inputs, norm_gain, query_weight, key_weight, value_weight, content_bias, position_bias
):
    widened = inputs.astype(jnp.float32)
    center = jnp.mean(widened, axis=-1, keepdims=True)
    spread = jnp.mean(jnp.square(widened - center), axis=-1, keepdims=True)
    normed = ((widened - center) * lax.rsqrt(spread + epsilon) * norm_gain).astype(jnp.bfloat16)
    projected = jnp.dot(normed, query_weight, preferred_element_type=jnp.float32)
    content_query = (projected + content_bias).astype(jnp.bfloat16)
    position_query = (projected + position_bias).astype(jnp.bfloat16)
    key_rows = jnp.dot(normed, key_weight, preferred_element_type=jnp.float32).astype(jnp.bfloat16)
    value_rows = jnp.dot(normed, value_weight, preferred_element_type=jnp.float32).astype(
        jnp.bfloat16
    )
    return (content_query, position_query, key_rows, value_rows)


def attend(
    content_query,
    position_query,
    key_rows,
    value_rows,
    memory_keys,
    memory_values,
    position_keys,
    keep_memory,
):
    length = content_query.shape[0]
    all_keys = jnp.concatenate([memory_keys, key_rows], axis=0).reshape(2 * length, H, DH)
    all_values = jnp.concatenate([memory_values, value_rows], axis=0).reshape(2 * length, H, DH)
    content = content_query.reshape(length, H, DH)
    located = position_query.reshape(length, H, DH)
    distance_keys = position_keys[::-1].reshape(2 * length, H, DH)
    direct = jnp.einsum("ihd,jhd->hij", content, all_keys, preferred_element_type=jnp.float32)
    relative = jnp.einsum(
        "ihd,jhd->hij", located, distance_keys, preferred_element_type=jnp.float32
    )
    padded = jnp.pad(relative, ((0, 0), (0, 0), (0, 1)))
    skewed = padded.reshape(H, length * (2 * length + 1))[
        :, length - 1 : length - 1 + 2 * length * length
    ]
    skewed = skewed.reshape(H, length, 2 * length)
    scores = (direct + skewed) * DH ** (-0.5)
    key_index = lax.broadcasted_iota(jnp.int32, (length, 2 * length), 1)
    query_index = lax.broadcasted_iota(jnp.int32, (length, 2 * length), 0)
    allowed = (key_index <= query_index + length) & (keep_memory | (key_index >= length))
    scores = jnp.where(allowed[None], scores, -jnp.inf)
    row_peak = lax.stop_gradient(jnp.max(scores, axis=-1, keepdims=True))
    raised = jnp.exp(scores - row_peak)
    attention = (raised / jnp.sum(raised, axis=-1, keepdims=True)).astype(jnp.bfloat16)
    gathered = jnp.einsum("hij,jhd->ihd", attention, all_values, preferred_element_type=jnp.float32)
    return gathered.reshape(length, H * DH).astype(jnp.bfloat16)


def finish(inputs, context, output_weight):
    update = lax.dot_general(
        context,
        output_weight,
        (((context.ndim - 1,), (1,)), ((), ())),
        preferred_element_type=jnp.float32,
    )
    return (inputs.astype(jnp.float32) + update).astype(jnp.bfloat16)


def shards(
    inputs,
    norm_gain,
    query_weight,
    key_weight,
    value_weight,
    output_weight,
    content_bias,
    position_bias,
    position_keys,
    start_flags,
    cotangent,
):
    partial_weights = (
        lax.all_gather(query_weight, "grp", axis=1, tiled=True),
        lax.all_gather(key_weight, "grp", axis=1, tiled=True),
        lax.all_gather(value_weight, "grp", axis=1, tiled=True),
        lax.all_gather(output_weight, "grp", axis=1, tiled=True),
    )
    full_weights = (
        lax.all_gather(partial_weights[0], "tm", axis=0, tiled=True),
        lax.all_gather(partial_weights[1], "tm", axis=0, tiled=True),
        lax.all_gather(partial_weights[2], "tm", axis=0, tiled=True),
        lax.all_gather(partial_weights[3], "tm", axis=0, tiled=True),
    )
    query_full, key_full, value_full, output_full = full_weights
    own_inputs = inputs[0]
    own_cotangent = cotangent[0]
    keep_memory = start_flags[0, 0] == 0

    def project(local_inputs):
        return normalize_project(
            local_inputs, norm_gain, query_full, key_full, value_full, content_bias, position_bias
        )

    projections, project_back = jax.vjp(project, own_inputs)
    content_query, position_query, key_rows, value_rows = projections
    memory_keys, memory_values = from_behind((key_rows, value_rows), "tm", 1)

    def attend_local(
        local_content, local_position, local_keys, local_values, prior_keys, prior_values
    ):
        return attend(
            local_content,
            local_position,
            local_keys,
            local_values,
            prior_keys,
            prior_values,
            position_keys,
            keep_memory,
        )

    context, attend_back = jax.vjp(
        attend_local,
        content_query,
        position_query,
        key_rows,
        value_rows,
        memory_keys,
        memory_values,
    )

    def combine(local_inputs, local_context):
        return finish(local_inputs, local_context, output_full)

    layer_out, finish_back = jax.vjp(combine, own_inputs, context)
    residual_grad, context_grad = finish_back(own_cotangent)
    attend_grads = attend_back(context_grad)
    returned_keys, returned_values = from_behind((attend_grads[4], attend_grads[5]), "tm", -1)
    key_grad = attend_grads[2] + returned_keys
    value_grad = attend_grads[3] + returned_values
    (norm_grad,) = project_back((attend_grads[0], attend_grads[1], key_grad, value_grad))
    input_grad = residual_grad + norm_grad
    return (layer_out[None], input_grad[None])


def solution(mesh):
    in_specs = (
        P("grp", "tm", None),
        P(),
        P("tm", "grp"),
        P("tm", "grp"),
        P("tm", "grp"),
        P("tm", "grp"),
        P(),
        P(),
        P(),
        P("grp", "tm"),
        P("grp", "tm", None),
    )
    out_specs = (P("grp", "tm", None), P("grp", "tm", None))
    return jax.shard_map(shards, mesh=mesh, in_specs=in_specs, out_specs=out_specs, check_vma=False)
```

profile of v0, /device:TPU:21, one launch (start us, length us, event | category | flops | bytes accessed | tf_op | source)
XLA Modules:
  0.0 231.2 jit_solution(11514636673767849575)
XLA Ops:
  7.2 5.6 %all_gather.24 = bf16[96,768]{1,0:T(8,128)(2,1)} all-gather(bf16[96,384]{1,0:T(8,128)(2,1)} %param.15), channel_id=1, replica_groups=mesh['grp'=2,'tm'=16] {'grp'}, dimensions={1}, use_global_device_ids=true | all-gather | bytes 221184 | tf_op jit(solution)/shard_map/all_gather | solution.py:99
  12.9 4.5 %all_gather.28 = bf16[96,768]{1,0:T(8,128)(2,1)} all-gather(bf16[96,384]{1,0:T(8,128)(2,1)} %param.14), channel_id=1, replica_groups=mesh['grp'=2,'tm'=16] {'grp'}, dimensions={1}, use_global_device_ids=true | all-gather | bytes 221184 | tf_op jit(solution)/shard_map/all_gather | solution.py:98
  17.4 5.4 %all_gather.26 = bf16[96,768]{1,0:T(8,128)(2,1)} all-gather(bf16[96,384]{1,0:T(8,128)(2,1)} %param.13), channel_id=1, replica_groups=mesh['grp'=2,'tm'=16] {'grp'}, dimensions={1}, use_global_device_ids=true | all-gather | bytes 221184 | tf_op jit(solution)/shard_map/all_gather | solution.py:97
  22.9 4.8 %all_gather.30 = bf16[96,768]{1,0:T(8,128)(2,1)} all-gather(bf16[96,384]{1,0:T(8,128)(2,1)} %param.16), channel_id=1, replica_groups=mesh['grp'=2,'tm'=16] {'grp'}, dimensions={1}, use_global_device_ids=true | all-gather | bytes 221184 | tf_op jit(solution)/shard_map/all_gather | solution.py:100
  28.9 1.2 rev.3
  31.4 23.1 %all-gather.5.cloned.1.call-done = bf16[1536,768]{1,0:T(8,128)(2,1)} async-done(((bf16[96,768]{1,0:T(8,128)(2,1)}), bf16[1536,768]{1,0:T(8,128)(2,1)}) %all-gather.5.cloned.1.call-update) | async-done | bytes 2359312 | tf_op jit(solution)/shard_map/all_gather | solution.py:105
  54.5 2.9 %convolution_convert_fusion.11 = bf16[128,768]{1,0:T(8,128)(2,1)} fusion(bf16[1536,768]{1,0:T(8,128)(2,1)} %all-gather.5.cloned.1.call-done, bf16[1,128,1536]{2,1,0:T(8,128)(2,1)S(1)} %copy-done, f32[1536]{0:T(1024)S(1)} %copy-done.10, f32[128]{0:T(128)S(1)} %fusion.35, f32[128]{0:T(128)S(1)} %broadcast_multiply_fusion), kind=kOutput, calls=%fused_computation.27 | convolution fusion | flops 303071232 | bytes 2956288 | tf_op jit(solution)/shard_map/jvp()/dot_general | solution.py:30
  57.3 4.2 %collective-permute-start = (bf16[128,768]{1,0:T(8,128)(2,1)}, bf16[128,768]{1,0:T(8,128)(2,1)}, u32[]{:S(2)}, u32[]{:S(2)}) collective-permute-start(bf16[128,768]{1,0:T(8,128)(2,1)} %convolution_convert_fusion.11), channel_id=1, source_target_pairs={{0,1},{1,2},{2,3},{3,4},{4,5},{5,6},{6,7},{7,8},{8,9},{9,10},{10,1... | collective-permute-start | bytes 589832 | tf_op jit(solution)/shard_map/ppermute | solution.py:16
  61.6 36.2 %all-gather.9.cloned.1.call-done = bf16[1536,768]{1,0:T(8,128)(2,1)} async-done(((bf16[96,768]{1,0:T(8,128)(2,1)}), bf16[1536,768]{1,0:T(8,128)(2,1)}) %all-gather.9.cloned.1.call-update) | async-done | bytes 2359312 | tf_op jit(solution)/shard_map/all_gather | solution.py:104
  97.8 2.9 %convolution_convert_fusion.10 = bf16[128,768]{1,0:T(8,128)(2,1)} fusion(bf16[1536,768]{1,0:T(8,128)(2,1)} %all-gather.9.cloned.1.call-done, bf16[1,128,1536]{2,1,0:T(8,128)(2,1)S(1)} %copy-done, f32[1536]{0:T(1024)S(1)} %copy-done.10, f32[128]{0:T(128)S(1)} %fusion.35, f32[128]{0:T(128)S(1)} %broadcast_multiply_fusion), kind=kOutput, calls=%fused_computation.26 | convolution fusion | flops 303071232 | bytes 2956288 | tf_op jit(solution)/shard_map/jvp()/dot_general | solution.py:29
  100.6 4.4 %collective-permute-start.1 = (bf16[128,768]{1,0:T(8,128)(2,1)}, bf16[128,768]{1,0:T(8,128)(2,1)}, u32[]{:S(2)}, u32[]{:S(2)}) collective-permute-start(bf16[128,768]{1,0:T(8,128)(2,1)} %convolution_convert_fusion.10), channel_id=1, source_target_pairs={{0,1},{1,2},{2,3},{3,4},{4,5},{5,6},{6,7},{7,8},{8,9},{9,10},{10,1... | collective-permute-start | bytes 589832 | tf_op jit(solution)/shard_map/ppermute | solution.py:16
  105.0 36.1 %all-gather.7.cloned.1.call-done = bf16[1536,768]{1,0:T(8,128)(2,1)} async-done(((bf16[96,768]{1,0:T(8,128)(2,1)}), bf16[1536,768]{1,0:T(8,128)(2,1)}) %all-gather.7.cloned.1.call-update) | async-done | bytes 2359312 | tf_op jit(solution)/shard_map/all_gather | solution.py:103
  141.1 2.2 add_convert_fusion
  143.5 40.8 %all-gather.11.cloned.1.call-done = bf16[1536,768]{1,0:T(8,128)(2,1)} async-done(((bf16[96,768]{1,0:T(8,128)(2,1)}), bf16[1536,768]{1,0:T(8,128)(2,1)}) %all-gather.11.cloned.1.call-update) | async-done | bytes 2359312 | tf_op jit(solution)/shard_map/all_gather | solution.py:106
  184.3 2.8 %convolution_convert_fusion.8 = bf16[128,768]{1,0:T(8,128)(2,1)} fusion(bf16[1536,768]{1,0:T(8,128)(2,1)} %all-gather.11.cloned.1.call-done, bf16[1,128,1536]{2,1,0:T(8,128)(2,1)S(1)} %copy-done.7), kind=kOutput, calls=%fused_computation.24 | convolution fusion | flops 302088192 | bytes 2949120 | tf_op jit(solution)/shard_map/transpose(jvp())/dot_general | solution.py:74
  188.8 1.7 copy.33
  195.5 3.2 %convolution_convert_fusion.9 = bf16[6,128,128]{2,1,0:T(8,128)(2,1)} fusion(bf16[256,6,128]{0,2,1:T(8,128)(2,1)} %bitcast.114, f32[6,128]{1,0:T(8,128)S(1)} %get-tuple-element.10, f32[6,128,256]{2,1,0:T(8,128)S(1)} %fusion.10), kind=kOutput, calls=%fused_computation.25 | convolution fusion | flops 51020800 | bytes 1379328 | tf_op jit(solution)/shard_map/jvp(hij,jhd->ihd)/dot_general | solution.py:69
  198.7 1.3 multiply_reduce_fusion
  202.3 3.2 %fusion.12 = bf16[256,6,128]{0,2,1:T(8,128)(2,1)} fusion(bf16[6,128,128]{2,1,0:T(8,128)(2,1)} %bitcast.117, f32[6,128]{1,0:T(8,128)S(1)} %get-tuple-element.10, f32[6,128,256]{2,1,0:T(8,128)S(1)} %fusion.10), kind=kOutput, calls=%fused_computation.20 | convolution fusion | flops 51119104 | bytes 1379328 | tf_op jit(solution)/shard_map/transpose(jvp(hij,jhd->ihd))/dot_general | solution.py:69
  206.7 2.9 %reshape.131 = bf16[6,128,257]{2,1,0:T(8,128)(2,1)} reshape(bf16[6,32896]{1,0:T(8,128)(2,1)} %pad.13) | data formatting | bytes 789504 | tf_op jit(solution)/shard_map/transpose(jvp())/reshape | solution.py:57
  209.7 2.2 collective-permute-start.3
  213.0 3.5 %collective-permute-start.2 = (bf16[128,768]{0,1:T(8,128)(2,1)S(1)}, bf16[128,768]{0,1:T(8,128)(2,1)S(1)}, u32[]{:S(2)}, u32[]{:S(2)}) collective-permute-start(bf16[128,768]{0,1:T(8,128)(2,1)S(1)} %bitcast.121), channel_id=1, source_target_pairs={{1,0},{2,1},{3,2},{4,3},{5,4},{6,5},{7,6},{8,7},{9,8},{10,9},{11,1... | collective-permute-start | bytes 589832 | tf_op jit(solution)/shard_map/ppermute | solution.py:16
  216.5 1.4 fusion.15
  218.9 1.6 fusion.6
  (80 shorter events, 18.3 us)
Async XLA Ops:
  7.2 23.7 %copy-start = (bf16[1,128,1536]{2,1,0:T(8,128)(2,1)S(1)}, bf16[1,128,1536]{2,1,0:T(8,128)(2,1)}, u32[]{:S(2)}) copy-start(bf16[1,128,1536]{2,1,0:T(8,128)(2,1)} %param.11) | copy-start | bytes 1179652
  7.2 47.3 %copy-start.10 = (f32[1536]{0:T(1024)S(1)}, f32[1536]{0:T(1024)}, u32[]{:S(2)}) copy-start(f32[1536]{0:T(1024)} %param.12) | copy-start | bytes 18436
  7.2 47.3 %all-gather.5.cloned.1.call-start = ((), (), s32[]{:S(2)}) async-start(), calls=%async_computation | async-start | bytes 2506752 | tf_op jit(solution)/shard_map/all_gather | solution.py:105
  12.8 85.0 %all-gather.9.cloned.1.call-start = ((), (), s32[]{:S(2)}) async-start(), calls=%async_computation.2 | async-start | bytes 2506752 | tf_op jit(solution)/shard_map/all_gather | solution.py:104
  17.4 123.7 %all-gather.7.cloned.1.call-start = ((), (), s32[]{:S(2)}) async-start(), calls=%async_computation.1 | async-start | bytes 2506752 | tf_op jit(solution)/shard_map/all_gather | solution.py:103
  22.9 161.4 %all-gather.11.cloned.1.call-start = ((), (), s32[]{:S(2)}) async-start(), calls=%async_computation.3 | async-start | bytes 2506752 | tf_op jit(solution)/shard_map/all_gather | solution.py:106
  31.2 66.5 %copy-start.11 = (f32[128]{0:T(128)}, f32[128]{0:T(128)S(1)}, u32[]{:S(2)}) copy-start(f32[128]{0:T(128)S(1)} %fusion.26) | copy-start | bytes 1540
  31.4 109.7 %copy-start.13 = (f32[768]{0:T(1024)S(1)}, f32[768]{0:T(1024)}, u32[]{:S(2)}) copy-start(f32[768]{0:T(1024)} %param.18) | copy-start | bytes 9220
  31.4 109.7 %copy-start.14 = (f32[768]{0:T(1024)S(1)}, f32[768]{0:T(1024)}, u32[]{:S(2)}) copy-start(f32[768]{0:T(1024)} %param.17) | copy-start | bytes 9220
  57.3 133.2 %collective-permute-start = (bf16[128,768]{1,0:T(8,128)(2,1)}, bf16[128,768]{1,0:T(8,128)(2,1)}, u32[]{:S(2)}, u32[]{:S(2)}) collective-permute-start(bf16[128,768]{1,0:T(8,128)(2,1)} %convolution_convert_fusion.11), channel_id=1, source_target_pairs={{0,1},{1,2},{2,3},{3,4},{4,5},{5,6},{6,7},{7,8},{8,9},{9,10},{10,1... | collective-permute-start | bytes 589832 | tf_op jit(solution)/shard_map/ppermute | solution.py:16
  100.6 83.6 %copy-start.7 = (bf16[1,128,1536]{2,1,0:T(8,128)(2,1)S(1)}, bf16[1,128,1536]{2,1,0:T(8,128)(2,1)}, u32[]{:S(2)}) copy-start(bf16[1,128,1536]{2,1,0:T(8,128)(2,1)} %param.21) | copy-start | bytes 1179652
  100.6 91.9 %collective-permute-start.1 = (bf16[128,768]{1,0:T(8,128)(2,1)}, bf16[128,768]{1,0:T(8,128)(2,1)}, u32[]{:S(2)}, u32[]{:S(2)}) collective-permute-start(bf16[128,768]{1,0:T(8,128)(2,1)} %convolution_convert_fusion.10), channel_id=1, source_target_pairs={{0,1},{1,2},{2,3},{3,4},{4,5},{5,6},{6,7},{7,8},{8,9},{9,10},{10,1... | collective-permute-start | bytes 589832 | tf_op jit(solution)/shard_map/ppermute | solution.py:16
  194.3 4.4 %copy-start.6 = (bf16[256,768]{0,1:T(8,128)(2,1)S(1)}, bf16[256,768]{0,1:T(8,128)(2,1)}, u32[]{:S(2)}) copy-start(bf16[256,768]{0,1:T(8,128)(2,1)} %copy.24) | copy-start | bytes 1179652
  205.5 4.2 %copy-start.5 = (bf16[256,6,128]{0,2,1:T(8,128)(2,1)S(1)}, bf16[256,6,128]{0,2,1:T(8,128)(2,1)}, u32[]{:S(2)}) copy-start(bf16[256,6,128]{0,2,1:T(8,128)(2,1)} %fusion.13) | copy-start | bytes 1179652
  205.7 12.2 %copy-start.3 = (bf16[1536,768]{1,0:T(8,128)(2,1)S(1)}, bf16[1536,768]{1,0:T(8,128)(2,1)}, u32[]{:S(2)}) copy-start(bf16[1536,768]{1,0:T(8,128)(2,1)} %all-gather.7.cloned.1.call-done) | copy-start | bytes 7077892
  209.7 10.8 %collective-permute-start.3 = (bf16[128,768]{0,1:T(8,128)(2,1)S(1)}, bf16[128,768]{0,1:T(8,128)(2,1)S(1)}, u32[]{:S(2)}, u32[]{:S(2)}) collective-permute-start(bf16[128,768]{0,1:T(8,128)(2,1)S(1)} %bitcast.122), channel_id=1, source_target_pairs={{1,0},{2,1},{3,2},{4,3},{5,4},{6,5},{7,6},{8,7},{9,8},{10,9},{11,1... | collective-permute-start | bytes 589832 | tf_op jit(solution)/shard_map/ppermute | solution.py:16
  213.0 5.9 %copy-start.1 = (bf16[1536,768]{1,0:T(8,128)(2,1)S(1)}, bf16[1536,768]{1,0:T(8,128)(2,1)}, u32[]{:S(2)}) copy-start(bf16[1536,768]{1,0:T(8,128)(2,1)} %all-gather.11.cloned.1.call-done) | copy-start | bytes 7077892
  213.0 5.9 %copy-start.9 = (bf16[6,128,128]{2,1,0:T(8,128)(2,1)S(1)}, bf16[6,128,128]{2,1,0:T(8,128)(2,1)}, u32[]{:S(2)}) copy-start(bf16[6,128,128]{2,1,0:T(8,128)(2,1)} %convolution_convert_fusion.9) | copy-start | bytes 589828
  213.0 8.5 %collective-permute-start.2 = (bf16[128,768]{0,1:T(8,128)(2,1)S(1)}, bf16[128,768]{0,1:T(8,128)(2,1)S(1)}, u32[]{:S(2)}, u32[]{:S(2)}) collective-permute-start(bf16[128,768]{0,1:T(8,128)(2,1)S(1)} %bitcast.121), channel_id=1, source_target_pairs={{1,0},{2,1},{3,2},{4,3},{5,4},{6,5},{7,6},{8,7},{9,8},{10,9},{11,1... | collective-permute-start | bytes 589832 | tf_op jit(solution)/shard_map/ppermute | solution.py:16
  218.9 1.7 copy-start.2
  220.5 1.7 copy-start.4
  222.2 1.1 copy-start.12
  222.2 1.4 copy-start.8
Sparse Core Ops, SparseCore 0:
  12.9 41.4 all-gather.4
  56.7 40.9 all-gather.8
  100.1 40.9 all-gather.6
  143.2 40.9 all-gather.10
where the time goes:
time: 234 us; the launch traced here: 231 us
  waiting for transfers between devices  136 us (58%)
  matrix products  27.2 us (12%)
  blocking collectives  20.3 us (9%)
  between operations  14.8 us (6%)
  starting transfers between devices  14.5 us (6%)
  local copies, waits for them, and re-layouts  12.8 us (5%)
  other arithmetic  5.48 us (2%)
    all_gather x1, waiting for transfers between devices, shards(): lax.all_gather(partial_weights[3], 'tm', axis=0, tiled=True)  40.8 us
    all_gather x1, waiting for transfers between devices, shards(): lax.all_gather(partial_weights[1], 'tm', axis=0, tiled=True)  36.2 us
    all_gather x1, waiting for transfers between devices, shards(): lax.all_gather(partial_weights[0], 'tm', axis=0, tiled=True)  36.1 us
    all_gather x1, waiting for transfers between devices, shards(): lax.all_gather(partial_weights[2], 'tm', axis=0, tiled=True)  23.1 us
    ppermute x4, starting transfers between devices, from_behind(): return lax.ppermute(block, axis, route)  14.3 us
    dot_general x3, matrix products, attend(): jnp.einsum('hij,jhd->ihd', attention, all_values, preferred_element_type=...  7.7 us
    all_gather x1, blocking collectives, shards(): lax.all_gather(value_weight, 'grp', axis=1, tiled=True)  5.57 us
    all_gather x1, blocking collectives, shards(): lax.all_gather(query_weight, 'grp', axis=1, tiled=True)  5.42 us
  transfers between devices with their start and end apart: 8, of which 4 were waited for; matrix products, arithmetic and copies ran while one was open for 11% of the time, Pallas kernels for 0%

commit v1 on v0

--- a/solution.py
+++ b/solution.py
@@ -1,13 +1,383 @@
 import jax
 import jax.numpy as jnp
 from jax import lax
+from jax.experimental import pallas as pl
+from jax.experimental.pallas import tpu as pltpu
 from jax.sharding import PartitionSpec as P
 
 H = 6
 DH = 128
-
-
 epsilon = 1e-05
+
+F32 = jnp.float32
+BF16 = jnp.bfloat16
+SEG = 128
+D = 1536
+HALF = 384
+HEADS = HALF // DH
+ROWS = 96
+ZS = 4
+BLK = 4 * ROWS
+NT = (((1,), (1,)), ((), ()))
+TN = (((0,), (0,)), ((), ()))
+VMEM_LIMIT = 48 * 1024 * 1024
+
+
+def dot(a, b, dims=(((1,), (0,)), ((), ()))):
+    return lax.dot_general(a, b, dims, preferred_element_type=F32)
+
+
+def place():
+    t = lax.axis_index("tm")
+    return t // 4, (t // 2) % 2, t % 2
+
+
+def plane_columns(z, r):
+    return pl.ds(pl.multiple_of(lax.rem(z - r + ZS, ZS) * BLK, 128), BLK)
+
+
+def normalize_kernel(x_ref, gain_ref, flag_ref, out_ref, held):
+    z, _, _ = place()
+    x = x_ref[...].astype(F32)
+    center = jnp.mean(x, axis=-1, keepdims=True)
+    moved = x - center
+    spread = jnp.mean(jnp.square(moved), axis=-1, keepdims=True)
+    held[...] = (moved * lax.rsqrt(spread + epsilon) * gain_ref[...]).astype(BF16)
+    for r in range(ZS):
+        out_ref[0:SEG, r * BLK : (r + 1) * BLK] = held[:, plane_columns(z, r)]
+    flag = flag_ref[0, 0].astype(F32)
+    out_ref[SEG:, :] = jnp.full((16, D), flag, F32).astype(BF16)
+
+
+def shard_rows(j):
+    _, y, c = place()
+    yy = 1 - y if j % 2 else y
+    cc = 1 - c if j // 2 else c
+    return (2 * yy + cc) * ROWS
+
+
+def fetch_qkv(pieces, weights, sems):
+    copies = []
+    for r in range(ZS):
+        for j in range(4):
+            rows = pl.ds(pl.multiple_of(r * BLK + shard_rows(j), 16), ROWS)
+            for w in range(3):
+                n = (r * 4 + j) * 3 + w
+                copies.append(
+                    pltpu.make_async_copy(
+                        pieces[r * 4 + j].at[w],
+                        weights.at[rows, pl.ds(w * HALF, HALF)],
+                        sems.at[n],
+                    )
+                )
+    for copy in copies:
+        copy.start()
+    return copies
+
+
+def project_kernel(own_ref, oth_ref, cb_ref, pb_ref, *rest):
+    pieces, (kv_ref, cq_ref, pq_ref, flags), (weights, xs, sems) = rest[:16], rest[16:20], rest[20:]
+    flags[0] = own_ref[SEG:, :DH]
+    flags[1] = oth_ref[SEG:, :DH]
+    copies = fetch_qkv(pieces, weights, sems)
+    xs[0:SEG, :] = own_ref[0:SEG, :]
+    xs[SEG:, :] = oth_ref[0:SEG, :]
+    total = None
+    for half in range(2):
+        for copy in copies[half * 24 : half * 24 + 24]:
+            copy.wait()
+        rows = slice(half * 2 * BLK, (half + 1) * 2 * BLK)
+        part = dot(xs[:, rows], weights[rows, :])
+        total = part if total is None else total + part
+    for rec in range(2):
+        rows = slice(rec * SEG, (rec + 1) * SEG)
+        kv_ref[rec] = total[rows, 0 : 2 * HALF].astype(BF16)
+        q = total[rows, 2 * HALF :]
+        cq_ref[rec] = (q + cb_ref[...]).astype(BF16)
+        pq_ref[rec] = (q + pb_ref[...]).astype(BF16)
+
+
+def attend_kernel(flags, cq_ref, pq_ref, kv_ref, mem_ref, pk_ref, p_ref, ctx_ref):
+    row = lax.broadcasted_iota(jnp.int32, (SEG, SEG), 0)
+    col = lax.broadcasted_iota(jnp.int32, (SEG, SEG), 1)
+    scale = DH**-0.5
+    for rec in range(2):
+        flag = flags[rec, 0:1, :].astype(F32)
+        for h in range(HEADS):
+            f = slice(h * DH, (h + 1) * DH)
+            fv = slice(HALF + h * DH, HALF + (h + 1) * DH)
+            cq = cq_ref[rec, :, f]
+            rel = dot(pq_ref[rec, :, f], pk_ref[:, f], NT)
+            rel = pltpu.roll(rel, SEG + 1, 1, stride=1, stride_axis=0)
+            s_mem = (dot(cq, mem_ref[rec, :, f], NT) + rel[:, :SEG]) * scale
+            s_own = (dot(cq, kv_ref[rec, :, f], NT) + rel[:, SEG:]) * scale
+            s_mem = jnp.where(flag == 0, s_mem, -jnp.inf)
+            s_own = jnp.where(col <= row, s_own, -jnp.inf)
+            peak = jnp.maximum(
+                jnp.max(s_mem, axis=-1, keepdims=True), jnp.max(s_own, axis=-1, keepdims=True)
+            )
+            e_mem = jnp.exp(s_mem - peak)
+            e_own = jnp.exp(s_own - peak)
+            norm = 1.0 / (
+                jnp.sum(e_mem, axis=-1, keepdims=True) + jnp.sum(e_own, axis=-1, keepdims=True)
+            )
+            p_mem = (e_mem * norm).astype(BF16)
+            p_own = (e_own * norm).astype(BF16)
+            p_ref[rec, h, :, :SEG] = p_mem
+            p_ref[rec, h, :, SEG:] = p_own
+            ctx = dot(p_mem, mem_ref[rec, :, fv]) + dot(p_own, kv_ref[rec, :, fv])
+            ctx_ref[rec, :, f] = ctx.astype(BF16)
+
+
+def back_kernel(
+    x_ref, cot_own, cot_oth, p_ref, ctx_ref, cq_ref, kv_ref, mem_ref, pk_ref, *rest
+):
+    pieces = rest[:8]
+    lo_own, lo_oth, d_ref, dmem_ref = rest[8:12]
+    wo, cots, cg, sems = rest[12:]
+    z, _, _ = place()
+    copies = []
+    for r in range(ZS):
+        for j in range(4):
+            rows = pl.ds(pl.multiple_of(r * BLK + shard_rows(j), 16), ROWS)
+            src = pieces[r * 2 + j // 2].at[j % 2]
+            copies.append(pltpu.make_async_copy(src, wo.at[rows, :], sems.at[r * 4 + j]))
+    for copy in copies:
+        copy.start()
+    for r in range(ZS):
+        cots[0:SEG, r * BLK : (r + 1) * BLK] = cot_own[:, plane_columns(z, r)]
+        cots[SEG:, r * BLK : (r + 1) * BLK] = cot_oth[:, plane_columns(z, r)]
+    for copy in copies:
+        copy.wait()
+    cg[...] = dot(cots[...], wo[...]).astype(BF16)
+    lo_oth[...] = dot(ctx_ref[1], wo[...], NT).astype(BF16)
+    lo = dot(ctx_ref[0], wo[...], NT)
+    for r in range(ZS):
+        lo_own[:, plane_columns(z, r)] = (
+            x_ref[:, plane_columns(z, r)].astype(F32) + lo[:, r * BLK : (r + 1) * BLK]
+        )
+    row = lax.broadcasted_iota(jnp.int32, (SEG, SEG), 0)
+    col = lax.broadcasted_iota(jnp.int32, (SEG, SEG), 1)
+    flip = jnp.where(row + col == SEG - 1, 1.0, 0.0).astype(BF16)
+    scale = DH**-0.5
+    for rec in range(2):
+        for h in range(HEADS):
+            f = slice(h * DH, (h + 1) * DH)
+            fv = slice(HALF + h * DH, HALF + (h + 1) * DH)
+            fq = slice(2 * HALF + h * DH, 2 * HALF + (h + 1) * DH)
+            g = cg[rec * SEG : (rec + 1) * SEG, f]
+            cq = cq_ref[rec, :, f]
+            k_mem, k_own = mem_ref[rec, :, f], kv_ref[rec, :, f]
+            p_mem, p_own = p_ref[rec, h, :, :SEG], p_ref[rec, h, :, SEG:]
+            dp_mem = dot(g, mem_ref[rec, :, fv], NT)
+            dp_own = dot(g, kv_ref[rec, :, fv], NT)
+            a_mem, a_own = p_mem.astype(F32), p_own.astype(F32)
+            inner = jnp.sum(a_mem * dp_mem + a_own * dp_own, axis=-1, keepdims=True)
+            ds_mem = a_mem * (dp_mem - inner) * scale
+            ds_own = a_own * (dp_own - inner) * scale
+            b_mem, b_own = ds_mem.astype(BF16), ds_own.astype(BF16)
+            rel = dot(flip, jnp.concatenate([b_mem, b_own], axis=1))
+            rel = pltpu.roll(rel, 0, 1, stride=1, stride_axis=0).astype(BF16)
+            rel = dot(flip, rel).astype(BF16)
+            dq = dot(b_mem, k_mem) + dot(b_own, k_own) + dot(rel, pk_ref[:, f])
+            d_ref[rec, :, f] = dot(b_own, cq, TN).astype(BF16)
+            d_ref[rec, :, fv] = dot(p_own, g, TN).astype(BF16)
+            d_ref[rec, :, fq] = dq.astype(BF16)
+            dmem_ref[rec, :, f] = dot(b_mem, cq, TN).astype(BF16)
+            dmem_ref[rec, :, fv] = dot(p_mem, g, TN).astype(BF16)
+
+
+def unproject_kernel(d_ref, ret_ref, *rest):
+    pieces, (np_own, np_oth), (weights, ds, sems) = rest[:16], rest[16:18], rest[18:]
+    copies = fetch_qkv(pieces, weights, sems)
+    for rec in range(2):
+        rows = slice(rec * SEG, (rec + 1) * SEG)
+        kv = d_ref[rec, :, : 2 * HALF].astype(F32) + ret_ref[rec].astype(F32)
+        ds[rows, : 2 * HALF] = kv.astype(BF16)
+        ds[rows, 2 * HALF :] = d_ref[rec, :, 2 * HALF :]
+    for half in range(2):
+        for copy in copies[half * 24 : half * 24 + 24]:
+            copy.wait()
+        rows = slice(half * 2 * BLK, (half + 1) * 2 * BLK)
+        part = dot(ds[...], weights[rows, :], NT)
+        np_own[:, rows] = part[:SEG]
+        np_oth[:, rows] = part[SEG:].astype(BF16)
+
+
+def finish_kernel(
+    x_ref, gain_ref, cot_ref, np_own, np_ret, lo_own, lo_ret, out_ref, grad_ref, total
+):
+    z, _, _ = place()
+    for r in range(ZS):
+        cols = slice(r * BLK, (r + 1) * BLK)
+        there = plane_columns(z, r)
+        total[:, there] = np_own[:, cols] + np_ret[:, cols].astype(F32)
+        out_ref[:, there] = (lo_own[:, there] + lo_ret[:, cols].astype(F32)).astype(BF16)
+    x = x_ref[...].astype(F32)
+    center = jnp.mean(x, axis=-1, keepdims=True)
+    moved = x - center
+    spread = jnp.mean(jnp.square(moved), axis=-1, keepdims=True)
+    rstd = lax.rsqrt(spread + epsilon)
+    hat = moved * rstd
+    g = total[...] * gain_ref[...]
+    mean_g = jnp.mean(g, axis=-1, keepdims=True)
+    mean_gh = jnp.mean(g * hat, axis=-1, keepdims=True)
+    grad = (rstd * (g - mean_g - hat * mean_gh)).astype(BF16)
+    grad_ref[...] = cot_ref[...] + grad
+
+
+def call(kernel, outs, scratch=(), in_specs=None, flops=0, nbytes=0):
+    return pl.pallas_call(
+        kernel,
+        out_shape=outs,
+        in_specs=in_specs,
+        out_specs=jax.tree.map(lambda _: pl.BlockSpec(memory_space=pltpu.VMEM), outs),
+        scratch_shapes=list(scratch),
+        compiler_params=pltpu.CompilerParams(vmem_limit_bytes=VMEM_LIMIT),
+        cost_estimate=pl.CostEstimate(flops=flops, bytes_accessed=nbytes, transcendentals=0),
+    )
+
+
+def shape(*dims, dtype=BF16):
+    return jax.ShapeDtypeStruct(dims, dtype)
+
+
+VM = pl.BlockSpec(memory_space=pltpu.VMEM)
+SM = pl.BlockSpec(memory_space=pltpu.SMEM)
+ANY = pl.BlockSpec(memory_space=pl.ANY)
+
+
+def moved_by(f):
+    route = []
+    for z in range(ZS):
+        for y in range(2):
+            for c in range(2):
+                zz, yy, cc = f(z, y, c)
+                route.append((4 * z + 2 * y + c, 4 * zz + 2 * yy + cc))
+    return lambda block: lax.ppermute(block, "tm", route)
+
+
+up = moved_by(lambda z, y, c: ((z + 1) % ZS, y, c))
+down = moved_by(lambda z, y, c: ((z - 1) % ZS, y, c))
+across = moved_by(lambda z, y, c: (z, 1 - y, c))
+sibling = moved_by(lambda z, y, c: (z, y, 1 - c))
+
+
+def other(block):
+    return lax.ppermute(block, "grp", [(0, 1), (1, 0)])
+
+
+def split_heads(
+    inputs,
+    norm_gain,
+    query_weight,
+    key_weight,
+    value_weight,
+    output_weight,
+    content_bias,
+    position_bias,
+    position_keys,
+    start_flags,
+    cotangent,
+):
+    g = lax.axis_index("grp")
+    x, cot = inputs[0], cotangent[0]
+    gain = norm_gain[None]
+    cb = lax.dynamic_slice_in_dim(content_bias, g * HALF, HALF)[None]
+    pb = lax.dynamic_slice_in_dim(position_bias, g * HALF, HALF)[None]
+    pk = lax.dynamic_slice_in_dim(position_keys, g * HALF, HALF, axis=1)[::-1]
+
+    shard = jnp.stack([key_weight, value_weight, query_weight, output_weight])
+    qkv = shard[:3]
+    normed = call(
+        normalize_kernel,
+        shape(SEG + 16, D),
+        [pltpu.VMEM((SEG, D), BF16)],
+        [VM, VM, SM],
+    )(x, gain, start_flags)
+    normed_oth = other(normed)
+    cot_oth = other(cot)
+
+    shard_y = across(shard)
+    a1, a3 = up(qkv), down(qkv)
+    a2 = up(a1)
+    a1y, a3y, a2y = across(a1), across(a3), across(a2)
+    b0 = jnp.stack([output_weight, shard_y[3]])
+    b1, b3 = up(b0), down(b0)
+    b2 = up(b1)
+    qkv_y = shard_y[:3]
+    here = [qkv, qkv_y, a1, a1y, a2, a2y, a3, a3y]
+    there = [sibling(p) for p in here]
+    pieces = []
+    for r in range(ZS):
+        pieces += here[2 * r : 2 * r + 2] + there[2 * r : 2 * r + 2]
+    out_here = [b0, b1, b2, b3]
+    out_there = [sibling(p) for p in out_here]
+    out_pieces = []
+    for r in range(ZS):
+        out_pieces += [out_here[r], out_there[r]]
+
+    kv, cq, pq, flags = call(
+        project_kernel,
+        (
+            shape(2, SEG, 2 * HALF),
+            shape(2, SEG, HALF),
+            shape(2, SEG, HALF),
+            shape(2, 16, DH),
+        ),
+        [
+            pltpu.VMEM((D, 3 * HALF), BF16),
+            pltpu.VMEM((2 * SEG, D), BF16),
+            pltpu.SemaphoreType.DMA((48,)),
+        ],
+        [VM, VM, VM, VM] + [ANY] * 16,
+    )(normed, normed_oth, cb, pb, *pieces)
+
+    steps = lax.axis_size("tm")
+    mem = lax.ppermute(kv, "tm", [(i, i + 1) for i in range(steps - 1)])
+    p, ctx = call(
+        attend_kernel,
+        (shape(2, HEADS, SEG, 2 * SEG), shape(2, SEG, HALF)),
+        (),
+        [VM] * 6,
+    )(flags, cq, pq, kv, mem, pk)
+
+    lo_own, lo_oth, d, dmem = call(
+        back_kernel,
+        (
+            shape(SEG, D, dtype=F32),
+            shape(SEG, D),
+            shape(2, SEG, 3 * HALF),
+            shape(2, SEG, 2 * HALF),
+        ),
+        [
+            pltpu.VMEM((D, HALF), BF16),
+            pltpu.VMEM((2 * SEG, D), BF16),
+            pltpu.VMEM((2 * SEG, HALF), BF16),
+            pltpu.SemaphoreType.DMA((16,)),
+        ],
+        [VM] * 9 + [ANY] * 8,
+    )(x, cot, cot_oth, p, ctx, cq, kv, mem, pk, *out_pieces)
+    lo_ret = other(lo_oth)
+    ret = lax.ppermute(dmem, "tm", [(i + 1, i) for i in range(steps - 1)])
+    np_own, np_oth = call(
+        unproject_kernel,
+        (shape(SEG, D, dtype=F32), shape(SEG, D)),
+        [
+            pltpu.VMEM((D, 3 * HALF), BF16),
+            pltpu.VMEM((2 * SEG, 3 * HALF), BF16),
+            pltpu.SemaphoreType.DMA((48,)),
+        ],
+        [VM, VM] + [ANY] * 16,
+    )(d, ret, *pieces)
+    np_ret = other(np_oth)
+    layer_out, input_grad = call(
+        finish_kernel,
+        (shape(SEG, D), shape(SEG, D)),
+        [pltpu.VMEM((SEG, D), F32)],
+        [VM] * 7,
+    )(x, gain, cot, np_own, np_ret, lo_own, lo_ret)
+    return (layer_out[None], input_grad[None])
 
 
 def from_behind(block, axis, distance):
@@ -172,4 +542,6 @@
         P("grp", "tm", None),
     )
     out_specs = (P("grp", "tm", None), P("grp", "tm", None))
-    return jax.shard_map(shards, mesh=mesh, in_specs=in_specs, out_specs=out_specs, check_vma=False)
+    split = dict(mesh.shape) == {"grp": 2, "tm": 4 * ZS}
+    body = split_heads if split else shards
+    return jax.shard_map(body, mesh=mesh, in_specs=in_specs, out_specs=out_specs, check_vma=False)

time: 234 us -> 102 us (0.44)
  waiting for transfers between devices: 136 us -> 39.7 us
  matrix products: 27.2 us -> 0 us
  blocking collectives: 20.3 us -> 0 us
  Pallas kernels: 0 us -> 19.3 us
  between operations: 14.8 us -> 1.67 us
  starting transfers between devices: 14.5 us -> 27.5 us
  other arithmetic: 5.48 us -> 1.77 us
    all_gather x4 -> x0, waiting for transfers between devices: 136 us -> none  [the longest x1 40.8 us: shards(): lax.all_gather(partial_weights[3], 'tm', axis=0, tiled=True)]
    ppermute x4 -> x28, waiting for transfers between devices: 0.01 us -> 39.7 us  [the longest x22 23.2 us: moved_by(): return lambda block: lax.ppermute(block, 'tm', route)]
    dot_general x16 -> x0, matrix products: 27.2 us -> none  [the longest x3 7.7 us: attend(): jnp.einsum('hij,jhd->ihd', attention, all_values, preferred_element_type=...]
    all_gather x4 -> x0, blocking collectives: 20.3 us -> none  [the longest x1 5.57 us: shards(): lax.all_gather(value_weight, 'grp', axis=1, tiled=True)]
    pallas_call x0 -> x6, Pallas kernels: none -> 19.3 us  [the longest x1 8.2 us: split_heads(): call(back_kernel, (shape(SEG, D, dtype=F32), shape(SEG, D), shape(2, SEG,...]
    ppermute x4 -> x28, starting transfers between devices: 14.3 us -> 27.5 us  [the longest x22 20.4 us: moved_by(): return lambda block: lax.ppermute(block, 'tm', route)]
    unnamed x32 -> x52, local copies, waits for them, and re-layouts: 2.11 us -> 7.33 us
    reshape x2 -> x0, local copies, waits for them, and re-layouts: 3.7 us -> none  [attend(): padded.reshape(H, length * (2 * length + 1))]
  transfers between devices with their start and end apart: 8 -> 28, of which waited for: 4 -> 10; matrix products, arithmetic and copies ran while one was open for 11% -> 4% of each run, Pallas kernels for 0% -> 6%
where the time goes in v1:
time: 102 us; the launch traced here: 101 us
  waiting for transfers between devices  39.7 us (39%)
  starting transfers between devices  27.5 us (27%)
  Pallas kernels  19.3 us (19%)
  local copies, waits for them, and re-layouts  10.7 us (10%)
  other arithmetic  1.77 us (2%)
  between operations  1.67 us (2%)
    ppermute x22, waiting for transfers between devices, moved_by(): return lambda block: lax.ppermute(block, 'tm', route)  23.2 us
    ppermute x22, starting transfers between devices, moved_by(): return lambda block: lax.ppermute(block, 'tm', route)  20.4 us
    ppermute x4, waiting for transfers between devices, other(): return lax.ppermute(block, 'grp', [(0, 1), (1, 0)])  8.51 us
    pallas_call x1, Pallas kernels, split_heads(): call(back_kernel, (shape(SEG, D, dtype=F32), shape(SEG, D), shape(2, SEG,...  8.2 us
    ppermute x1, waiting for transfers between devices, split_heads(): ret = lax.ppermute(dmem, 'tm', [(i + 1, i) for i in range(steps - 1)])  7.98 us
    unnamed x52, local copies, waits for them, and re-layouts  7.33 us
    pallas_call x1, Pallas kernels, split_heads(): call(unproject_kernel, (shape(SEG, D, dtype=F32), shape(SEG, D)), [pltpu....  3.57 us
    pallas_call x1, Pallas kernels, split_heads(): call(project_kernel, (shape(2, SEG, 2 * HALF), shape(2, SEG, HALF), shape...  3.26 us
  transfers between devices with their start and end apart: 28, of which 10 were waited for; matrix products, arithmetic and copies ran while one was open for 4% of the time, Pallas kernels for 6%

profile of v1, /device:TPU:21, one launch (start us, length us, event | category | flops | bytes accessed | tf_op | source)
XLA Modules:
  0.0 100.6 jit_solution(13225570479629444668)
XLA Ops:
  3.6 1.5 %collective-permute-start.3 = (bf16[3,96,384]{2,1,0:T(8,128)(2,1)S(1)}, bf16[3,96,384]{2,1,0:T(8,128)(2,1)S(1)}, u32[]{:S(2)}, u32[]{:S(2)}) collective-permute-start(bf16[3,96,384]{2,1,0:T(8,128)(2,1)S(1)} %pad_maximum_fusion.1.rest_0_), channel_id=1, source_target_pairs={{0,1},{1,0},{2,3},{3,2},{4,5},{5,4},{6,7},{7,6},{8,9},{9,8},{10,11... | collective-permute-start | bytes 663560 | tf_op jit(solution)/shard_map/ppermute | solution.py:257
  5.8 2.3 %collective-permute-done.13.rest_12_ = bf16[3,96,384]{2,1,0:T(8,128)(2,1)S(1)} collective-permute-done((bf16[3,96,384]{2,1,0:T(8,128)(2,1)S(1)}, bf16[3,96,384]{2,1,0:T(8,128)(2,1)S(1)}, u32[]{:S(2)}, u32[]{:S(2)}) %collective-permute-start.13) | collective-permute-done | bytes 221216 | tf_op jit(solution)/shard_map/ppermute | solution.py:257
  8.1 2.7 %collective-permute-start.15 = (bf16[3,96,384]{2,1,0:T(8,128)(2,1)S(1)}, bf16[3,96,384]{2,1,0:T(8,128)(2,1)S(1)}, u32[]{:S(2)}, u32[]{:S(2)}) collective-permute-start(bf16[3,96,384]{2,1,0:T(8,128)(2,1)S(1)} %collective-permute-done.13.rest_12_), channel_id=1, source_target_pairs={{0,1},{1,0},{2,3},{3,2},{4,5},{5,4},{6,7},{7,6},{8,9},{9,8},{10,11... | collective-permute-start | bytes 663560 | tf_op jit(solution)/shard_map/ppermute | solution.py:257
  12.7 2.9 %collective-permute-start.9 = (bf16[3,96,384]{2,1,0:T(8,128)(2,1)S(1)}, bf16[3,96,384]{2,1,0:T(8,128)(2,1)S(1)}, u32[]{:S(2)}, u32[]{:S(2)}) collective-permute-start(bf16[3,96,384]{2,1,0:T(8,128)(2,1)S(1)} %collective-permute-done.5.rest_4_), channel_id=1, source_target_pairs={{0,4},{1,5},{2,6},{3,7},{4,8},{5,9},{6,10},{7,11},{8,12},{9,13},{1... | collective-permute-start | bytes 663560 | tf_op jit(solution)/shard_map/ppermute | solution.py:257
  17.9 2.2 %collective-permute-done.9.rest_8_ = bf16[3,96,384]{2,1,0:T(8,128)(2,1)S(1)} collective-permute-done((bf16[3,96,384]{2,1,0:T(8,128)(2,1)S(1)}, bf16[3,96,384]{2,1,0:T(8,128)(2,1)S(1)}, u32[]{:S(2)}, u32[]{:S(2)}) %collective-permute-start.9) | collective-permute-done | bytes 221216 | tf_op jit(solution)/shard_map/ppermute | solution.py:257
  20.3 1.7 %collective-permute-done.14.rest_13_ = bf16[3,96,384]{2,1,0:T(8,128)(2,1)} collective-permute-done((bf16[3,96,384]{2,1,0:T(8,128)(2,1)S(1)}, bf16[3,96,384]{2,1,0:T(8,128)(2,1)}, u32[]{:S(2)}, u32[]{:S(2)}) %collective-permute-start.14) | collective-permute-done | bytes 221216 | tf_op jit(solution)/shard_map/ppermute | solution.py:257
  22.1 2.5 %collective-permute-start.4 = (bf16[3,96,384]{2,1,0:T(8,128)(2,1)S(1)}, bf16[3,96,384]{2,1,0:T(8,128)(2,1)}, u32[]{:S(2)}, u32[]{:S(2)}) collective-permute-start(bf16[3,96,384]{2,1,0:T(8,128)(2,1)S(1)} %slice.10.rest_1_), channel_id=1, source_target_pairs={{0,1},{1,0},{2,3},{3,2},{4,5},{5,4},{6,7},{7,6},{8,9},{9,8},{10,11... | collective-permute-start | bytes 663560 | tf_op jit(solution)/shard_map/ppermute | solution.py:257
  25.3 1.5 %collective-permute-done.6.rest_5_ = bf16[3,96,384]{2,1,0:T(8,128)(2,1)} collective-permute-done((bf16[3,96,384]{2,1,0:T(8,128)(2,1)S(1)}, bf16[3,96,384]{2,1,0:T(8,128)(2,1)}, u32[]{:S(2)}, u32[]{:S(2)}) %collective-permute-start.6) | collective-permute-done | bytes 221216 | tf_op jit(solution)/shard_map/ppermute | solution.py:257
  26.8 2.5 %collective-permute-start.16 = (bf16[3,96,384]{2,1,0:T(8,128)(2,1)}, bf16[3,96,384]{2,1,0:T(8,128)(2,1)}, u32[]{:S(2)}, u32[]{:S(2)}) collective-permute-start(bf16[3,96,384]{2,1,0:T(8,128)(2,1)} %collective-permute-done.14.rest_13_), channel_id=1, source_target_pairs={{0,1},{1,0},{2,3},{3,2},{4,5},{5,4},{6,7},{7,6},{8,9},{9,8},{10,11... | collective-permute-start | bytes 663560 | tf_op jit(solution)/shard_map/ppermute | solution.py:257
  30.1 1.5 %collective-permute-done.10.rest_9_ = bf16[3,96,384]{2,1,0:T(8,128)(2,1)} collective-permute-done((bf16[3,96,384]{2,1,0:T(8,128)(2,1)S(1)}, bf16[3,96,384]{2,1,0:T(8,128)(2,1)}, u32[]{:S(2)}, u32[]{:S(2)}) %collective-permute-start.10) | collective-permute-done | bytes 221216 | tf_op jit(solution)/shard_map/ppermute | solution.py:257
  31.5 1.4 %collective-permute-start.12 = (bf16[3,96,384]{2,1,0:T(8,128)(2,1)}, bf16[3,96,384]{2,1,0:T(8,128)(2,1)}, u32[]{:S(2)}, u32[]{:S(2)}) collective-permute-start(bf16[3,96,384]{2,1,0:T(8,128)(2,1)} %collective-permute-done.10.rest_9_), channel_id=1, source_target_pairs={{0,1},{1,0},{2,3},{3,2},{4,5},{5,4},{6,7},{7,6},{8,9},{9,8},{10,11... | collective-permute-start | bytes 663560 | tf_op jit(solution)/shard_map/ppermute | solution.py:257
  37.5 3.3 %shard_map.123 = (bf16[2,128,768]{2,1,0:T(8,128)(2,1)S(1)}, bf16[2,128,384]{2,1,0:T(8,128)(2,1)S(1)}, bf16[2,128,384]{2,1,0:T(8,128)(2,1)S(1)}, bf16[2,16,128]{2,1,0:T(8,128)(2,1)S(1)}) custom-call(bf16[144,1536]{1,0:T(8,128)(2,1)S(1)} %shard_map.122.own_ref, bf16[144,1536]{1,0:T(8,128)(2,1)S(1)} %copy-done.16, f32[1,384]{1,0:T(1,128)S(1)} %broadcast_in_dim.16.cb_ref, ...), custom_call_target="tpu_custom_call" | custom-call | tf_op jit(solution)/shard_map/pallas_call | solution.py:320
  41.4 2.5 %collective-permute-start.17 = (bf16[2,128,768]{2,1,0:T(8,128)(2,1)S(1)}, bf16[2,128,768]{2,1,0:T(8,128)(2,1)S(1)}, u32[]{:S(2)}, u32[]{:S(2)}) collective-permute-start(bf16[2,128,768]{2,1,0:T(8,128)(2,1)S(1)} %get-tuple-element.19.kv_ref), channel_id=1, source_target_pairs={{0,1},{1,2},{2,3},{3,4},{4,5},{5,6},{6,7},{7,8},{8,9},{9,10},{10,1... | collective-permute-start | bytes 1179656 | tf_op jit(solution)/shard_map/ppermute | solution.py:337
  45.8 1.5 %collective-permute-start.23 = (bf16[2,96,384]{2,1,0:T(8,128)(2,1)}, bf16[2,96,384]{2,1,0:T(8,128)(2,1)}, u32[]{:S(2)}, u32[]{:S(2)}) collective-permute-start(bf16[2,96,384]{2,1,0:T(8,128)(2,1)} %pad_maximum_fusion.2.rest_0_), channel_id=1, source_target_pairs={{0,12},{1,13},{2,14},{3,15},{4,0},{5,1},{6,2},{7,3},{8,4},{9,5},{1... | collective-permute-start | bytes 442376 | tf_op jit(solution)/shard_map/ppermute | solution.py:257
  47.3 10.0 %collective-permute-done.19.rest_2_ = bf16[2,96,384]{2,1,0:T(8,128)(2,1)} collective-permute-done((bf16[2,96,384]{2,1,0:T(8,128)(2,1)}, bf16[2,96,384]{2,1,0:T(8,128)(2,1)}, u32[]{:S(2)}, u32[]{:S(2)}) %collective-permute-start.19) | collective-permute-done | bytes 147488 | tf_op jit(solution)/shard_map/ppermute | solution.py:257
  57.8 3.8 %collective-permute-done.21.rest_4_ = bf16[2,96,384]{2,1,0:T(8,128)(2,1)} collective-permute-done((bf16[2,96,384]{2,1,0:T(8,128)(2,1)}, bf16[2,96,384]{2,1,0:T(8,128)(2,1)}, u32[]{:S(2)}, u32[]{:S(2)}) %collective-permute-start.21) | collective-permute-done | bytes 147488 | tf_op jit(solution)/shard_map/ppermute | solution.py:257
  62.8 2.4 %rev.3.pk_ref = bf16[256,384]{1,0:T(8,128)(2,1)S(1)} reverse(bf16[256,384]{1,0:T(8,128)(2,1)} %constant_dynamic-slice_fusion), dimensions={0} | reverse | bytes 393216 | tf_op jit(solution)/shard_map/rev | solution.py:288
  66.2 2.4 %shard_map.124 = (bf16[2,3,128,256]{3,2,1,0:T(8,128)(2,1)S(1)}, bf16[2,128,384]{2,1,0:T(8,128)(2,1)S(1)}) custom-call(bf16[2,16,128]{2,1,0:T(8,128)(2,1)S(1)} %get-tuple-element.16.flags, bf16[2,128,384]{2,1,0:T(8,128)(2,1)S(1)} %copy-done.12, bf16[2,128,384]{2,1,0:T(8,128)(2,1)S(1)} %copy-done.18, bf16[2,128,768]{2,1,0:T(8,128)(2,1)S(1)} %get-tuple-element.19.kv_ref, ...), custom_call_target="tpu_custom_call" | custom-call | tf_op jit(solution)/shard_map/pallas_call | solution.py:338
  68.6 8.2 %shard_map.125 = (f32[128,1536]{1,0:T(8,128)}, bf16[128,1536]{1,0:T(8,128)(2,1)S(1)}, bf16[2,128,1152]{2,1,0:T(8,128)(2,1)S(1)}, bf16[2,128,768]{2,1,0:T(8,128)(2,1)S(1)}) custom-call(bf16[128,1536]{1,0:T(8,128)(2,1)S(1)} %bitcast.9, bf16[128,1536]{1,0:T(8,128)(2,1)S(1)} %bitcast.12, bf16[128,1536]{1,0:T(8,128)(2,1)} %collective-permute-done.cot_oth, ...), custom_call_target="tpu_custom_call" | custom-call | tf_op jit(solution)/shard_map/pallas_call | solution.py:345
  76.8 1.9 %collective-permute-start.25 = (bf16[2,128,768]{2,1,0:T(8,128)(2,1)S(1)}, bf16[2,128,768]{2,1,0:T(8,128)(2,1)S(1)}, u32[]{:S(2)}, u32[]{:S(2)}) collective-permute-start(bf16[2,128,768]{2,1,0:T(8,128)(2,1)S(1)} %get-tuple-element.23), channel_id=1, source_target_pairs={{1,0},{2,1},{3,2},{4,3},{5,4},{6,5},{7,6},{8,7},{9,8},{10,9},{11,1... | collective-permute-start | bytes 1179656 | tf_op jit(solution)/shard_map/ppermute | solution.py:362
  78.9 8.0 %collective-permute-done.25.ret_ref = bf16[2,128,768]{2,1,0:T(8,128)(2,1)S(1)} collective-permute-done((bf16[2,128,768]{2,1,0:T(8,128)(2,1)S(1)}, bf16[2,128,768]{2,1,0:T(8,128)(2,1)S(1)}, u32[]{:S(2)}, u32[]{:S(2)}) %collective-permute-start.25) | collective-permute-done | bytes 393248 | tf_op jit(solution)/shard_map/ppermute | solution.py:362
  86.9 3.6 %shard_map.126 = (f32[128,1536]{1,0:T(8,128)S(1)}, bf16[128,1536]{1,0:T(8,128)(2,1)S(1)}) custom-call(bf16[2,128,1152]{2,1,0:T(8,128)(2,1)S(1)} %get-tuple-element.22.d_ref, bf16[2,128,768]{2,1,0:T(8,128)(2,1)S(1)} %collective-permute-done.25.ret_ref, bf16[3,96,384]{2,1,0:T(8,128)(2,1)S(1)} %pad_maximum_fusion.1.rest_0_, ...), custom_call_target="tpu_custom_call" | custom-call | tf_op jit(solution)/shard_map/pallas_call | solution.py:363
  90.5 8.5 %collective-permute-done.26.np_ret = bf16[128,1536]{1,0:T(8,128)(2,1)S(1)} collective-permute-done((bf16[128,1536]{1,0:T(8,128)(2,1)S(1)}, bf16[128,1536]{1,0:T(8,128)(2,1)S(1)}, u32[]{:S(2)}, u32[]{:S(2)}) %collective-permute-start.26) | collective-permute-done | bytes 393248 | tf_op jit(solution)/shard_map/ppermute | solution.py:267
  99.0 1.5 %shard_map.127 = (bf16[128,1536]{1,0:T(8,128)(2,1)}, bf16[128,1536]{1,0:T(8,128)(2,1)}) custom-call(bf16[128,1536]{1,0:T(8,128)(2,1)S(1)} %bitcast.10, f32[1,1536]{1,0:T(1,128)S(1)} %broadcast_in_dim.15.gain_ref, bf16[128,1536]{1,0:T(8,128)(2,1)S(1)} %bitcast.13, f32[128,1536]{1,0:T(8,128)S(1)} %get-tuple-element.24.np_own, ...), custom_call_target="tpu_custom_call" | custom-call | tf_op jit(solution)/shard_map/pallas_call | solution.py:374
  (102 shorter events, 18.7 us)
Async XLA Ops:
  2.0 10.7 %collective-permute-start.5 = (bf16[3,96,384]{2,1,0:T(8,128)(2,1)S(1)}, bf16[3,96,384]{2,1,0:T(8,128)(2,1)S(1)}, u32[]{:S(2)}, u32[]{:S(2)}) collective-permute-start(bf16[3,96,384]{2,1,0:T(8,128)(2,1)S(1)} %pad_maximum_fusion.1.rest_0_), channel_id=1, source_target_pairs={{0,4},{1,5},{2,6},{3,7},{4,8},{5,9},{6,10},{7,11},{8,12},{9,13},{1... | collective-permute-start | bytes 663560 | tf_op jit(solution)/shard_map/ppermute | solution.py:257
  3.4 12.4 %collective-permute-start.2 = (bf16[4,96,384]{2,1,0:T(8,128)(2,1)S(1)}, bf16[4,96,384]{2,1,0:T(8,128)(2,1)S(1)}, u32[]{:S(2)}, u32[]{:S(2)}) collective-permute-start(bf16[4,96,384]{2,1,0:T(8,128)(2,1)S(1)} %pad_maximum_fusion), channel_id=1, source_target_pairs={{0,2},{1,3},{2,0},{3,1},{4,6},{5,7},{6,4},{7,5},{8,10},{9,11},{10,... | collective-permute-start | bytes 884744 | tf_op jit(solution)/shard_map/ppermute | solution.py:257
  3.6 11.9 %collective-permute-start.3 = (bf16[3,96,384]{2,1,0:T(8,128)(2,1)S(1)}, bf16[3,96,384]{2,1,0:T(8,128)(2,1)S(1)}, u32[]{:S(2)}, u32[]{:S(2)}) collective-permute-start(bf16[3,96,384]{2,1,0:T(8,128)(2,1)S(1)} %pad_maximum_fusion.1.rest_0_), channel_id=1, source_target_pairs={{0,1},{1,0},{2,3},{3,2},{4,5},{5,4},{6,7},{7,6},{8,9},{9,8},{10,11... | collective-permute-start | bytes 663560 | tf_op jit(solution)/shard_map/ppermute | solution.py:257
  8.1 8.6 %collective-permute-start.15 = (bf16[3,96,384]{2,1,0:T(8,128)(2,1)S(1)}, bf16[3,96,384]{2,1,0:T(8,128)(2,1)S(1)}, u32[]{:S(2)}, u32[]{:S(2)}) collective-permute-start(bf16[3,96,384]{2,1,0:T(8,128)(2,1)S(1)} %collective-permute-done.13.rest_12_), channel_id=1, source_target_pairs={{0,1},{1,0},{2,3},{3,2},{4,5},{5,4},{6,7},{7,6},{8,9},{9,8},{10,11... | collective-permute-start | bytes 663560 | tf_op jit(solution)/shard_map/ppermute | solution.py:257
  11.2 18.1 %collective-permute-start.1 = (bf16[144,1536]{1,0:T(8,128)(2,1)S(1)}, bf16[144,1536]{1,0:T(8,128)(2,1)S(1)}, u32[]{:S(2)}, u32[]{:S(2)}) collective-permute-start(bf16[144,1536]{1,0:T(8,128)(2,1)S(1)} %shard_map.122.own_ref), channel_id=1, source_target_pairs={{0,16},{16,0},{1,17},{17,1},{2,18},{18,2},{3,19},{19,3},{4,20},{20... | collective-permute-start | bytes 1327112 | tf_op jit(solution)/shard_map/ppermute | solution.py:267
  12.7 7.4 %collective-permute-start.9 = (bf16[3,96,384]{2,1,0:T(8,128)(2,1)S(1)}, bf16[3,96,384]{2,1,0:T(8,128)(2,1)S(1)}, u32[]{:S(2)}, u32[]{:S(2)}) collective-permute-start(bf16[3,96,384]{2,1,0:T(8,128)(2,1)S(1)} %collective-permute-done.5.rest_4_), channel_id=1, source_target_pairs={{0,4},{1,5},{2,6},{3,7},{4,8},{5,9},{6,10},{7,11},{8,12},{9,13},{1... | collective-permute-start | bytes 663560 | tf_op jit(solution)/shard_map/ppermute | solution.py:257
  15.6 6.5 %collective-permute-start.14 = (bf16[3,96,384]{2,1,0:T(8,128)(2,1)S(1)}, bf16[3,96,384]{2,1,0:T(8,128)(2,1)}, u32[]{:S(2)}, u32[]{:S(2)}) collective-permute-start(bf16[3,96,384]{2,1,0:T(8,128)(2,1)S(1)} %collective-permute-done.13.rest_12_), channel_id=1, source_target_pairs={{0,2},{1,3},{2,0},{3,1},{4,6},{5,7},{6,4},{7,5},{8,10},{9,11},{10,... | collective-permute-start | bytes 663560 | tf_op jit(solution)/shard_map/ppermute | solution.py:257
  15.8 8.8 %collective-permute-start.7 = (bf16[3,96,384]{2,1,0:T(8,128)(2,1)S(1)}, bf16[3,96,384]{2,1,0:T(8,128)(2,1)S(1)}, u32[]{:S(2)}, u32[]{:S(2)}) collective-permute-start(bf16[3,96,384]{2,1,0:T(8,128)(2,1)S(1)} %collective-permute-done.5.rest_4_), channel_id=1, source_target_pairs={{0,1},{1,0},{2,3},{3,2},{4,5},{5,4},{6,7},{7,6},{8,9},{9,8},{10,11... | collective-permute-start | bytes 663560 | tf_op jit(solution)/shard_map/ppermute | solution.py:257
  16.7 10.1 %collective-permute-start.6 = (bf16[3,96,384]{2,1,0:T(8,128)(2,1)S(1)}, bf16[3,96,384]{2,1,0:T(8,128)(2,1)}, u32[]{:S(2)}, u32[]{:S(2)}) collective-permute-start(bf16[3,96,384]{2,1,0:T(8,128)(2,1)S(1)} %collective-permute-done.5.rest_4_), channel_id=1, source_target_pairs={{0,2},{1,3},{2,0},{3,1},{4,6},{5,7},{6,4},{7,5},{8,10},{9,11},{10,... | collective-permute-start | bytes 663560 | tf_op jit(solution)/shard_map/ppermute | solution.py:257
  20.1 11.5 %collective-permute-start.10 = (bf16[3,96,384]{2,1,0:T(8,128)(2,1)S(1)}, bf16[3,96,384]{2,1,0:T(8,128)(2,1)}, u32[]{:S(2)}, u32[]{:S(2)}) collective-permute-start(bf16[3,96,384]{2,1,0:T(8,128)(2,1)S(1)} %collective-permute-done.9.rest_8_), channel_id=1, source_target_pairs={{0,2},{1,3},{2,0},{3,1},{4,6},{5,7},{6,4},{7,5},{8,10},{9,11},{10,... | collective-permute-start | bytes 663560 | tf_op jit(solution)/shard_map/ppermute | solution.py:257
  22.1 12.4 %collective-permute-start.4 = (bf16[3,96,384]{2,1,0:T(8,128)(2,1)S(1)}, bf16[3,96,384]{2,1,0:T(8,128)(2,1)}, u32[]{:S(2)}, u32[]{:S(2)}) collective-permute-start(bf16[3,96,384]{2,1,0:T(8,128)(2,1)S(1)} %slice.10.rest_1_), channel_id=1, source_target_pairs={{0,1},{1,0},{2,3},{3,2},{4,5},{5,4},{6,7},{7,6},{8,9},{9,8},{10,11... | collective-permute-start | bytes 663560 | tf_op jit(solution)/shard_map/ppermute | solution.py:257
  25.2 9.2 %collective-permute-start.11 = (bf16[3,96,384]{2,1,0:T(8,128)(2,1)S(1)}, bf16[3,96,384]{2,1,0:T(8,128)(2,1)}, u32[]{:S(2)}, u32[]{:S(2)}) collective-permute-start(bf16[3,96,384]{2,1,0:T(8,128)(2,1)S(1)} %collective-permute-done.9.rest_8_), channel_id=1, source_target_pairs={{0,1},{1,0},{2,3},{3,2},{4,5},{5,4},{6,7},{7,6},{8,9},{9,8},{10,11... | collective-permute-start | bytes 663560 | tf_op jit(solution)/shard_map/ppermute | solution.py:257
  26.8 7.7 %collective-permute-start.16 = (bf16[3,96,384]{2,1,0:T(8,128)(2,1)}, bf16[3,96,384]{2,1,0:T(8,128)(2,1)}, u32[]{:S(2)}, u32[]{:S(2)}) collective-permute-start(bf16[3,96,384]{2,1,0:T(8,128)(2,1)} %collective-permute-done.14.rest_13_), channel_id=1, source_target_pairs={{0,1},{1,0},{2,3},{3,2},{4,5},{5,4},{6,7},{7,6},{8,9},{9,8},{10,11... | collective-permute-start | bytes 663560 | tf_op jit(solution)/shard_map/ppermute | solution.py:257
  41.4 20.2 %collective-permute-start.17 = (bf16[2,128,768]{2,1,0:T(8,128)(2,1)S(1)}, bf16[2,128,768]{2,1,0:T(8,128)(2,1)S(1)}, u32[]{:S(2)}, u32[]{:S(2)}) collective-permute-start(bf16[2,128,768]{2,1,0:T(8,128)(2,1)S(1)} %get-tuple-element.19.kv_ref), channel_id=1, source_target_pairs={{0,1},{1,2},{2,3},{3,4},{4,5},{5,6},{6,7},{7,8},{8,9},{9,10},{10,1... | collective-permute-start | bytes 1179656 | tf_op jit(solution)/shard_map/ppermute | solution.py:337
  44.6 12.6 %collective-permute-start.19 = (bf16[2,96,384]{2,1,0:T(8,128)(2,1)}, bf16[2,96,384]{2,1,0:T(8,128)(2,1)}, u32[]{:S(2)}, u32[]{:S(2)}) collective-permute-start(bf16[2,96,384]{2,1,0:T(8,128)(2,1)} %pad_maximum_fusion.2.rest_0_), channel_id=1, source_target_pairs={{0,4},{1,5},{2,6},{3,7},{4,8},{5,9},{6,10},{7,11},{8,12},{9,13},{1... | collective-permute-start | bytes 442376 | tf_op jit(solution)/shard_map/ppermute | solution.py:257
  44.6 23.9 %collective-permute-start = (bf16[128,1536]{1,0:T(8,128)(2,1)S(1)}, bf16[128,1536]{1,0:T(8,128)(2,1)}, u32[]{:S(2)}, u32[]{:S(2)}) collective-permute-start(bf16[128,1536]{1,0:T(8,128)(2,1)S(1)} %bitcast.11), channel_id=1, source_target_pairs={{0,16},{16,0},{1,17},{17,1},{2,18},{18,2},{3,19},{19,3},{4,20},{20... | collective-permute-start | bytes 1179656 | tf_op jit(solution)/shard_map/ppermute | solution.py:267
  45.8 11.4 %collective-permute-start.23 = (bf16[2,96,384]{2,1,0:T(8,128)(2,1)}, bf16[2,96,384]{2,1,0:T(8,128)(2,1)}, u32[]{:S(2)}, u32[]{:S(2)}) collective-permute-start(bf16[2,96,384]{2,1,0:T(8,128)(2,1)} %pad_maximum_fusion.2.rest_0_), channel_id=1, source_target_pairs={{0,12},{1,13},{2,14},{3,15},{4,0},{5,1},{6,2},{7,3},{8,4},{9,5},{1... | collective-permute-start | bytes 442376 | tf_op jit(solution)/shard_map/ppermute | solution.py:257
  57.2 11.3 %collective-permute-start.18 = (bf16[2,96,384]{2,1,0:T(8,128)(2,1)}, bf16[2,96,384]{2,1,0:T(8,128)(2,1)}, u32[]{:S(2)}, u32[]{:S(2)}) collective-permute-start(bf16[2,96,384]{2,1,0:T(8,128)(2,1)} %pad_maximum_fusion.2.rest_0_), channel_id=1, source_target_pairs={{0,1},{1,0},{2,3},{3,2},{4,5},{5,4},{6,7},{7,6},{8,9},{9,8},{10,11... | collective-permute-start | bytes 442376 | tf_op jit(solution)/shard_map/ppermute | solution.py:257
  57.3 11.3 %collective-permute-start.20 = (bf16[2,96,384]{2,1,0:T(8,128)(2,1)}, bf16[2,96,384]{2,1,0:T(8,128)(2,1)}, u32[]{:S(2)}, u32[]{:S(2)}) collective-permute-start(bf16[2,96,384]{2,1,0:T(8,128)(2,1)} %collective-permute-done.19.rest_2_), channel_id=1, source_target_pairs={{0,1},{1,0},{2,3},{3,2},{4,5},{5,4},{6,7},{7,6},{8,9},{9,8},{10,11... | collective-permute-start | bytes 442376 | tf_op jit(solution)/shard_map/ppermute | solution.py:257
  61.6 7.0 %collective-permute-start.24 = (bf16[2,96,384]{2,1,0:T(8,128)(2,1)}, bf16[2,96,384]{2,1,0:T(8,128)(2,1)}, u32[]{:S(2)}, u32[]{:S(2)}) collective-permute-start(bf16[2,96,384]{2,1,0:T(8,128)(2,1)} %collective-permute-done.23.rest_6_), channel_id=1, source_target_pairs={{0,1},{1,0},{2,3},{3,2},{4,5},{5,4},{6,7},{7,6},{8,9},{9,8},{10,11... | collective-permute-start | bytes 442376 | tf_op jit(solution)/shard_map/ppermute | solution.py:257
  61.6 7.0 %collective-permute-start.22 = (bf16[2,96,384]{2,1,0:T(8,128)(2,1)}, bf16[2,96,384]{2,1,0:T(8,128)(2,1)}, u32[]{:S(2)}, u32[]{:S(2)}) collective-permute-start(bf16[2,96,384]{2,1,0:T(8,128)(2,1)} %collective-permute-done.21.rest_4_), channel_id=1, source_target_pairs={{0,1},{1,0},{2,3},{3,2},{4,5},{5,4},{6,7},{7,6},{8,9},{9,8},{10,11... | collective-permute-start | bytes 442376 | tf_op jit(solution)/shard_map/ppermute | solution.py:257
  76.8 10.0 %collective-permute-start.25 = (bf16[2,128,768]{2,1,0:T(8,128)(2,1)S(1)}, bf16[2,128,768]{2,1,0:T(8,128)(2,1)S(1)}, u32[]{:S(2)}, u32[]{:S(2)}) collective-permute-start(bf16[2,128,768]{2,1,0:T(8,128)(2,1)S(1)} %get-tuple-element.23), channel_id=1, source_target_pairs={{1,0},{2,1},{3,2},{4,3},{5,4},{6,5},{7,6},{8,7},{9,8},{10,9},{11,1... | collective-permute-start | bytes 1179656 | tf_op jit(solution)/shard_map/ppermute | solution.py:362
  78.8 11.7 %collective-permute-start.27 = (bf16[128,1536]{1,0:T(8,128)(2,1)S(1)}, bf16[128,1536]{1,0:T(8,128)(2,1)S(1)}, u32[]{:S(2)}, u32[]{:S(2)}) collective-permute-start(bf16[128,1536]{1,0:T(8,128)(2,1)S(1)} %get-tuple-element.27), channel_id=1, source_target_pairs={{0,16},{16,0},{1,17},{17,1},{2,18},{18,2},{3,19},{19,3},{4,20},{20... | collective-permute-start | bytes 1179656 | tf_op jit(solution)/shard_map/ppermute | solution.py:267
  90.4 8.6 %collective-permute-start.26 = (bf16[128,1536]{1,0:T(8,128)(2,1)S(1)}, bf16[128,1536]{1,0:T(8,128)(2,1)S(1)}, u32[]{:S(2)}, u32[]{:S(2)}) collective-permute-start(bf16[128,1536]{1,0:T(8,128)(2,1)S(1)} %get-tuple-element.25), channel_id=1, source_target_pairs={{0,16},{16,0},{1,17},{17,1},{2,18},{18,2},{3,19},{19,3},{4,20},{20... | collective-permute-start | bytes 1179656 | tf_op jit(solution)/shard_map/ppermute | solution.py:267
  (30 other events, 233.8 us)

commit v2 on v0

--- a/solution.py
+++ b/solution.py
@@ -1,13 +1,400 @@
 import jax
 import jax.numpy as jnp
 from jax import lax
+from jax.experimental import pallas as pl
+from jax.experimental.pallas import tpu as pltpu
 from jax.sharding import PartitionSpec as P
 
 H = 6
 DH = 128
-
-
 epsilon = 1e-05
+
+F32 = jnp.float32
+BF16 = jnp.bfloat16
+SEG = 128
+D = 1536
+HALF = 384
+HEADS = HALF // DH
+ROWS = 96
+ZS = 4
+BLK = 4 * ROWS
+NT = (((1,), (1,)), ((), ()))
+TN = (((0,), (0,)), ((), ()))
+VMEM_LIMIT = 24 * 1024 * 1024
+
+
+def dot(a, b, dims=(((1,), (0,)), ((), ()))):
+    return lax.dot_general(a, b, dims, preferred_element_type=F32)
+
+
+def place():
+    t = lax.axis_index("tm")
+    return t // 4, (t // 2) % 2, t % 2
+
+
+def plane_columns(z, r):
+    return pl.ds(pl.multiple_of(lax.rem(z - r + ZS, ZS) * BLK, 128), BLK)
+
+
+def pack_kernel(k_ref, v_ref, q_ref, o_ref, out_ref, sems):
+    copies = [
+        pltpu.make_async_copy(ref, out_ref.at[i], sems.at[i])
+        for i, ref in enumerate((k_ref, v_ref, q_ref, o_ref))
+    ]
+    for copy in copies:
+        copy.start()
+    for copy in copies:
+        copy.wait()
+
+
+def normalize_kernel(
+    x_ref, gain_ref, flag_ref, cb_ref, pb_ref, pk_ref, out_ref, biases, pk_out, held
+):
+    z, _, _ = place()
+    x = x_ref[...].astype(F32)
+    center = jnp.mean(x, axis=-1, keepdims=True)
+    moved = x - center
+    spread = jnp.mean(jnp.square(moved), axis=-1, keepdims=True)
+    held[...] = (moved * lax.rsqrt(spread + epsilon) * gain_ref[...]).astype(BF16)
+    for r in range(ZS):
+        out_ref[0:SEG, r * BLK : (r + 1) * BLK] = held[:, plane_columns(z, r)]
+    flag = flag_ref[0, 0].astype(F32)
+    out_ref[SEG:, :] = jnp.full((16, D), flag, F32).astype(BF16)
+    own = pl.ds(pl.multiple_of(lax.axis_index("grp") * HALF, 128), HALF)
+    biases[0:1, :] = cb_ref[:, own]
+    biases[1:2, :] = pb_ref[:, own]
+    row = lax.broadcasted_iota(jnp.int32, (2 * SEG, 2 * SEG), 0)
+    col = lax.broadcasted_iota(jnp.int32, (2 * SEG, 2 * SEG), 1)
+    flip = jnp.where(row + col == 2 * SEG - 1, 1.0, 0.0).astype(BF16)
+    pk_out[...] = dot(flip, pk_ref[:, own]).astype(BF16)
+
+
+def shard_rows(r, j):
+    _, y, c = place()
+    yy = 1 - y if j % 2 else y
+    cc = 1 - c if j // 2 else c
+    return pl.ds(pl.multiple_of(r * BLK + (2 * yy + cc) * ROWS, 16), ROWS)
+
+
+def fetch(pieces, which, weights, sems):
+    copies = []
+    for n in range(4 * ZS):
+        for w in range(2):
+            copies.append(
+                pltpu.make_async_copy(
+                    pieces[n].at[which[n] + w],
+                    weights.at[shard_rows(n // 4, n % 4), pl.ds(w * HALF, HALF)],
+                    sems.at[2 * n + w],
+                )
+            )
+    for copy in copies:
+        copy.start()
+    return copies
+
+
+def accumulate(x, weights, copies, columns):
+    total = None
+    for half in range(2):
+        for copy in copies[half * 16 : half * 16 + 16]:
+            copy.wait()
+        rows = slice(half * 2 * BLK, (half + 1) * 2 * BLK)
+        part = dot(x[:, rows], weights[rows, columns])
+        total = part if total is None else total + part
+    return total
+
+
+def key_value_kernel(own_ref, oth_ref, *rest):
+    pieces, (weights, kv_ref, xs, flags), sems = rest[:16], rest[16:20], rest[20]
+    copies = fetch(pieces, (0,) * 16, weights, sems)
+    flags[0] = own_ref[SEG:, :DH]
+    flags[1] = oth_ref[SEG:, :DH]
+    xs[0:SEG, :] = own_ref[0:SEG, :]
+    xs[SEG:, :] = oth_ref[0:SEG, :]
+    total = accumulate(xs, weights, copies, slice(0, 2 * HALF))
+    kv_ref[0] = total[:SEG].astype(BF16)
+    kv_ref[1] = total[SEG:].astype(BF16)
+
+
+QO_PLACES = (2,) * 9 + (0,) + (2,) + (0,) + (2,) * 4
+
+
+def query_kernel(xs, cot_own, cot_oth, biases, kv_ref, pk_ref, *rest):
+    pieces = rest[:16]
+    weights, cq_ref, cg_ref, rel_ref, own_ref, dp_ref = rest[16:22]
+    cots, sems = rest[22:]
+    z, _, _ = place()
+    copies = fetch(pieces, QO_PLACES, weights, sems)
+    for r in range(ZS):
+        cots[0:SEG, r * BLK : (r + 1) * BLK] = cot_own[:, plane_columns(z, r)]
+        cots[SEG:, r * BLK : (r + 1) * BLK] = cot_oth[:, plane_columns(z, r)]
+    q = accumulate(xs, weights, copies, slice(0, HALF))
+    cq = (q + biases[0:1, :]).astype(BF16)
+    pq = (q + biases[1:2, :]).astype(BF16)
+    cg = dot(cots[...], weights[:, HALF:]).astype(BF16)
+    row = lax.broadcasted_iota(jnp.int32, (SEG, SEG), 0)
+    col = lax.broadcasted_iota(jnp.int32, (SEG, SEG), 1)
+    for rec in range(2):
+        rows = slice(rec * SEG, (rec + 1) * SEG)
+        cq_ref[rec] = cq[rows]
+        cg_ref[rec] = cg[rows]
+        for h in range(HEADS):
+            f, fv = head(h), head(HEADS + h)
+            rel = dot(pq[rows, f], pk_ref[:, f], NT)
+            rel = pltpu.roll(rel, SEG + 1, 1, stride=1, stride_axis=0)
+            rel_ref[rec, h] = rel[:, :SEG]
+            s_own = (dot(cq[rows, f], kv_ref[rec, :, f], NT) + rel[:, SEG:]) * SCALE
+            own_ref[rec, h] = jnp.where(col <= row, s_own, -jnp.inf)
+            dp_ref[rec, h] = dot(cg[rows, f], kv_ref[rec, :, fv], NT)
+
+
+SCALE = DH**-0.5
+
+
+def head(i):
+    return slice(i * DH, (i + 1) * DH)
+
+
+def memory_kernel(
+    flags, cq_ref, cg_ref, rel_ref, own_ref, dp_ref, mem_ref, p_ref, ds_ref, dmem_ref
+):
+    for rec in range(2):
+        flag = flags[rec, 0:1, :].astype(F32)
+        for h in range(HEADS):
+            f, fv = head(h), head(HEADS + h)
+            cq, g = cq_ref[rec, :, f], cg_ref[rec, :, f]
+            s_own = own_ref[rec, h]
+            s_mem = (dot(cq, mem_ref[rec, :, f], NT) + rel_ref[rec, h]) * SCALE
+            s_mem = jnp.where(flag == 0, s_mem, -jnp.inf)
+            dp_mem = dot(g, mem_ref[rec, :, fv], NT)
+            peak = jnp.max(jnp.maximum(s_mem, s_own), axis=-1, keepdims=True)
+            e_mem = jnp.exp(s_mem - peak)
+            e_own = jnp.exp(s_own - peak)
+            norm = 1.0 / jnp.sum(e_mem + e_own, axis=-1, keepdims=True)
+            a_mem, a_own = e_mem * norm, e_own * norm
+            dp_own = dp_ref[rec, h]
+            inner = jnp.sum(a_mem * dp_mem + a_own * dp_own, axis=-1, keepdims=True)
+            p_mem = a_mem.astype(BF16)
+            ds_mem = (a_mem * (dp_mem - inner) * SCALE).astype(BF16)
+            p_ref[rec, h, :, :SEG] = p_mem
+            p_ref[rec, h, :, SEG:] = a_own.astype(BF16)
+            ds_ref[rec, h, :, :SEG] = ds_mem
+            ds_ref[rec, h, :, SEG:] = (a_own * (dp_own - inner) * SCALE).astype(BF16)
+            dmem_ref[rec, :, f] = dot(ds_mem, cq, TN).astype(BF16)
+            dmem_ref[rec, :, fv] = dot(p_mem, g, TN).astype(BF16)
+
+
+def context_kernel(p_ref, kv_ref, mem_ref, wqo, ctx_ref, lo_oth):
+    for rec in range(2):
+        for h in range(HEADS):
+            f, fv = head(h), head(HEADS + h)
+            ctx = dot(p_ref[rec, h, :, :SEG], mem_ref[rec, :, fv])
+            ctx += dot(p_ref[rec, h, :, SEG:], kv_ref[rec, :, fv])
+            ctx_ref[rec, :, f] = ctx.astype(BF16)
+    lo_oth[...] = dot(ctx_ref[1], wqo[:, HALF:], NT).astype(BF16)
+
+
+def own_grad_kernel(
+    x_ref, ctx_ref, p_ref, ds_ref, cq_ref, cg_ref, kv_ref, mem_ref, pk_ref, wkv, wqo,
+    lo_own, np_ref, dq, dkv,
+):
+    z, _, _ = place()
+    row = lax.broadcasted_iota(jnp.int32, (SEG, SEG), 0)
+    col = lax.broadcasted_iota(jnp.int32, (SEG, SEG), 1)
+    flip = jnp.where(row + col == SEG - 1, 1.0, 0.0).astype(BF16)
+    for rec in range(2):
+        rows = slice(rec * SEG, (rec + 1) * SEG)
+        for h in range(HEADS):
+            f, fv = head(h), head(HEADS + h)
+            ds = ds_ref[rec, h]
+            rel = pltpu.roll(dot(flip, ds), 0, 1, stride=1, stride_axis=0).astype(BF16)
+            rel = dot(flip, rel).astype(BF16)
+            total = dot(ds[:, :SEG], mem_ref[rec, :, f]) + dot(ds[:, SEG:], kv_ref[rec, :, f])
+            dq[rows, f] = (total + dot(rel, pk_ref[:, f])).astype(BF16)
+            dkv[rows, f] = dot(ds[:, SEG:], cq_ref[rec, :, f], TN).astype(BF16)
+            dkv[rows, fv] = dot(p_ref[rec, h, :, SEG:], cg_ref[rec, :, f], TN).astype(BF16)
+    np_ref[...] = dot(dq[...], wqo[:, :HALF], NT) + dot(dkv[...], wkv[...], NT)
+    lo = dot(ctx_ref[0], wqo[:, HALF:], NT)
+    for r in range(ZS):
+        there = plane_columns(z, r)
+        lo_own[:, there] = x_ref[:, there].astype(F32) + lo[:, r * BLK : (r + 1) * BLK]
+
+
+def returned_kernel(np_ref, ret_ref, wkv, np_oth):
+    np_oth[...] = (np_ref[SEG:, :] + dot(ret_ref[1], wkv[...], NT)).astype(BF16)
+
+
+def returned_own_kernel(np_ref, ret_ref, wkv, lo_own, lo_ret, np_own, out_ref):
+    z, _, _ = place()
+    np_own[...] = np_ref[:SEG, :] + dot(ret_ref[0], wkv[...], NT)
+    for r in range(ZS):
+        there = plane_columns(z, r)
+        lo = lo_own[:, there] + lo_ret[:, r * BLK : (r + 1) * BLK].astype(F32)
+        out_ref[:, there] = lo.astype(BF16)
+
+
+def finish_kernel(x_ref, gain_ref, cot_ref, np_own, np_ret, grad_ref, total):
+    z, _, _ = place()
+    for r in range(ZS):
+        cols = slice(r * BLK, (r + 1) * BLK)
+        total[:, plane_columns(z, r)] = np_own[:, cols] + np_ret[:, cols].astype(F32)
+    x = x_ref[...].astype(F32)
+    center = jnp.mean(x, axis=-1, keepdims=True)
+    moved = x - center
+    spread = jnp.mean(jnp.square(moved), axis=-1, keepdims=True)
+    rstd = lax.rsqrt(spread + epsilon)
+    hat = moved * rstd
+    g = total[...] * gain_ref[...]
+    mean_g = jnp.mean(g, axis=-1, keepdims=True)
+    mean_gh = jnp.mean(g * hat, axis=-1, keepdims=True)
+    grad = (rstd * (g - mean_g - hat * mean_gh)).astype(BF16)
+    grad_ref[...] = cot_ref[...] + grad
+
+
+def call(kernel, outs, scratch=(), in_specs=None, us=1.0):
+    return pl.pallas_call(
+        kernel,
+        out_shape=outs,
+        in_specs=in_specs,
+        out_specs=jax.tree.map(lambda _: VM, outs),
+        scratch_shapes=list(scratch),
+        compiler_params=pltpu.CompilerParams(vmem_limit_bytes=VMEM_LIMIT),
+        cost_estimate=pl.CostEstimate(
+            flops=0, bytes_accessed=int(us * 3.0e6), transcendentals=0
+        ),
+    )
+
+
+def shape(*dims, dtype=BF16):
+    return jax.ShapeDtypeStruct(dims, dtype)
+
+
+VM = pl.BlockSpec(memory_space=pltpu.VMEM)
+SM = pl.BlockSpec(memory_space=pltpu.SMEM)
+ANY = pl.BlockSpec(memory_space=pl.ANY)
+
+
+def moved_by(f):
+    route = []
+    for z in range(ZS):
+        for y in range(2):
+            for c in range(2):
+                zz, yy, cc = f(z, y, c)
+                route.append((4 * z + 2 * y + c, 4 * zz + 2 * yy + cc))
+    return lambda block: lax.ppermute(block, "tm", route)
+
+
+up = moved_by(lambda z, y, c: ((z + 1) % ZS, y, c))
+down = moved_by(lambda z, y, c: ((z - 1) % ZS, y, c))
+across = moved_by(lambda z, y, c: (z, 1 - y, c))
+sibling = moved_by(lambda z, y, c: (z, y, 1 - c))
+
+
+def other(block):
+    return lax.ppermute(block, "grp", [(0, 1), (1, 0)])
+
+
+def split_heads(
+    inputs,
+    norm_gain,
+    query_weight,
+    key_weight,
+    value_weight,
+    output_weight,
+    content_bias,
+    position_bias,
+    position_keys,
+    start_flags,
+    cotangent,
+):
+    x, cot = inputs[0], cotangent[0]
+    gain = norm_gain[None]
+    w0 = call(
+        pack_kernel, shape(4, ROWS, HALF), [pltpu.SemaphoreType.DMA((4,))], [ANY] * 4, 0.5
+    )(key_weight, value_weight, query_weight, output_weight)
+    normed, biases, pk = call(
+        normalize_kernel,
+        (shape(SEG + 16, D), shape(2, HALF, dtype=F32), shape(2 * SEG, HALF)),
+        [pltpu.VMEM((SEG, D), BF16)],
+        [VM, VM, SM, VM, VM, VM],
+        0.5,
+    )(x, gain, start_flags, content_bias[None], position_bias[None], position_keys)
+    normed_oth = other(normed)
+    cot_oth = other(cot)
+
+    w0y = across(w0)
+    w1, w3 = up(w0), down(w0)
+    w2 = up(w1)
+    w1y, w3y = across(w1), across(w3)
+    w2y_kv = up(w1y[:2])
+    w2y_qo = across(w2[2:])
+    here = [w0, w0y, w1, w1y, w2, w2y_kv, w3, w3y]
+    there = [sibling(p) for p in here]
+    w2y_qo_there = sibling(w2y_qo)
+    kv_pieces, qo_pieces = [], []
+    for r in range(ZS):
+        kv_pieces += here[2 * r : 2 * r + 2] + there[2 * r : 2 * r + 2]
+        if r == 2:
+            qo_pieces += [w2, w2y_qo, there[4], w2y_qo_there]
+        else:
+            qo_pieces += here[2 * r : 2 * r + 2] + there[2 * r : 2 * r + 2]
+
+    wkv, kv, xs, flags = call(
+        key_value_kernel,
+        (
+            shape(D, 2 * HALF),
+            shape(2, SEG, 2 * HALF),
+            shape(2 * SEG, D),
+            shape(2, 16, DH),
+        ),
+        [pltpu.SemaphoreType.DMA((32,))],
+        [VM, VM] + [ANY] * 16,
+        2.0,
+    )(normed, normed_oth, *kv_pieces)
+    steps = lax.axis_size("tm")
+    mem = lax.ppermute(kv, "tm", [(i, i + 1) for i in range(steps - 1)])
+
+    blocks = shape(2, HEADS, SEG, SEG, dtype=F32)
+    wqo, cq, cg, rel, s_own, dp_own = call(
+        query_kernel,
+        (shape(D, 2 * HALF), shape(2, SEG, HALF), shape(2, SEG, HALF), blocks, blocks, blocks),
+        [pltpu.VMEM((2 * SEG, D), BF16), pltpu.SemaphoreType.DMA((32,))],
+        [VM] * 6 + [ANY] * 16,
+        3.0,
+    )(xs, cot, cot_oth, biases, kv, pk, *qo_pieces)
+
+    p, ds, dmem = call(
+        memory_kernel,
+        (
+            shape(2, HEADS, SEG, 2 * SEG),
+            shape(2, HEADS, SEG, 2 * SEG),
+            shape(2, SEG, 2 * HALF),
+        ),
+        (),
+        [VM] * 7,
+        3.0,
+    )(flags, cq, cg, rel, s_own, dp_own, mem)
+    ret = lax.ppermute(dmem, "tm", [(i + 1, i) for i in range(steps - 1)])
+
+    ctx, lo_oth = call(
+        context_kernel, (shape(2, SEG, HALF), shape(SEG, D)), (), [VM] * 4, 1.5
+    )(p, kv, mem, wqo)
+    lo_ret = other(lo_oth)
+    lo_own, partial = call(
+        own_grad_kernel,
+        (shape(SEG, D, dtype=F32), shape(2 * SEG, D, dtype=F32)),
+        [pltpu.VMEM((2 * SEG, HALF), BF16), pltpu.VMEM((2 * SEG, 2 * HALF), BF16)],
+        [VM] * 11,
+        5.0,
+    )(x, ctx, p, ds, cq, cg, kv, mem, pk, wkv, wqo)
+    np_oth = call(returned_kernel, shape(SEG, D), (), [VM] * 3, 1.0)(partial, ret, wkv)
+    np_ret = other(np_oth)
+    np_own, layer_out = call(
+        returned_own_kernel, (shape(SEG, D, dtype=F32), shape(SEG, D)), (), [VM] * 5, 1.0
+    )(partial, ret, wkv, lo_own, lo_ret)
+    input_grad = call(
+        finish_kernel, shape(SEG, D), [pltpu.VMEM((SEG, D), F32)], [VM] * 5, 1.0
+    )(x, gain, cot, np_own, np_ret)
+    return (layer_out[None], input_grad[None])
 
 
 def from_behind(block, axis, distance):
@@ -172,4 +559,6 @@
         P("grp", "tm", None),
     )
     out_specs = (P("grp", "tm", None), P("grp", "tm", None))
-    return jax.shard_map(shards, mesh=mesh, in_specs=in_specs, out_specs=out_specs, check_vma=False)
+    split = dict(mesh.shape) == {"grp": 2, "tm": 4 * ZS}
+    body = split_heads if split else shards
+    return jax.shard_map(body, mesh=mesh, in_specs=in_specs, out_specs=out_specs, check_vma=False)

time: 234 us -> 88.9 us (0.38)
  the two profiles are of different devices: /device:TPU:21 before, /device:TPU:0 now
where the time goes in v2:
time: 88.9 us; the launch traced here: 88.4 us
  waiting for transfers between devices  42.6 us (48%)
  starting transfers between devices  21.7 us (24%)
  Pallas kernels  15.1 us (17%)
  local copies, waits for them, and re-layouts  7.64 us (9%)
  between operations  1.45 us (2%)
    ppermute x17, waiting for transfers between devices, moved_by(): return lambda block: lax.ppermute(block, 'tm', route)  22.4 us
    ppermute x4, waiting for transfers between devices, other(): return lax.ppermute(block, 'grp', [(0, 1), (1, 0)])  20.2 us
    ppermute x17, starting transfers between devices, moved_by(): return lambda block: lax.ppermute(block, 'tm', route)  13 us
    unnamed x16, local copies, waits for them, and re-layouts  5.53 us
    ppermute x4, starting transfers between devices, other(): return lax.ppermute(block, 'grp', [(0, 1), (1, 0)])  5.28 us
    pallas_call x1, Pallas kernels, split_heads(): call(memory_kernel, (shape(2, HEADS, SEG, 2 * SEG), shape(2, HEADS, SEG,...  2.93 us
    pallas_call x1, Pallas kernels, split_heads(): call(own_grad_kernel, (shape(SEG, D, dtype=F32), shape(2 * SEG, D, dtype=...  2.81 us
    pallas_call x1, Pallas kernels, split_heads(): call(query_kernel, (shape(D, 2 * HALF), shape(2, SEG, HALF), shape(2, SEG...  2.22 us
  transfers between devices with their start and end apart: 23, of which 9 were waited for; matrix products, arithmetic and copies ran while one was open for 2% of the time, Pallas kernels for 12%

profile of v2, /device:TPU:0, one launch (start us, length us, event | category | flops | bytes accessed | tf_op | source)
XLA Modules:
  0.0 88.4 jit_solution(14922848913650604931)
XLA Ops:
  4.6 3.1 %collective-permute-start.4 = (bf16[4,96,384]{2,1,0:T(8,128)(2,1)S(1)}, bf16[4,96,384]{2,1,0:T(8,128)(2,1)S(1)}, u32[]{:S(2)}, u32[]{:S(2)}) collective-permute-start(bf16[4,96,384]{2,1,0:T(8,128)(2,1)S(1)} %shard_map.123.rest_0_), channel_id=1, source_target_pairs={{0,4},{1,5},{2,6},{3,7},{4,8},{5,9},{6,10},{7,11},{8,12},{9,13},{1... | collective-permute-start | bytes 884744 | tf_op jit(solution)/shard_map/ppermute | solution.py:283
  7.6 2.1 %collective-permute-start.12 = (bf16[4,96,384]{2,1,0:T(8,128)(2,1)S(1)}, bf16[4,96,384]{2,1,0:T(8,128)(2,1)S(1)}, u32[]{:S(2)}, u32[]{:S(2)}) collective-permute-start(bf16[4,96,384]{2,1,0:T(8,128)(2,1)S(1)} %shard_map.123.rest_0_), channel_id=1, source_target_pairs={{0,12},{1,13},{2,14},{3,15},{4,0},{5,1},{6,2},{7,3},{8,4},{9,5},{1... | collective-permute-start | bytes 884744 | tf_op jit(solution)/shard_map/ppermute | solution.py:283
  9.7 1.7 %collective-permute-start.1 = (bf16[4,96,384]{2,1,0:T(8,128)(2,1)S(1)}, bf16[4,96,384]{2,1,0:T(8,128)(2,1)S(1)}, u32[]{:S(2)}, u32[]{:S(2)}) collective-permute-start(bf16[4,96,384]{2,1,0:T(8,128)(2,1)S(1)} %shard_map.123.rest_0_), channel_id=1, source_target_pairs={{0,2},{1,3},{2,0},{3,1},{4,6},{5,7},{6,4},{7,5},{8,10},{9,11},{10,... | collective-permute-start | bytes 884744 | tf_op jit(solution)/shard_map/ppermute | solution.py:283
  11.4 6.1 %collective-permute-done.4.rest_4_ = bf16[4,96,384]{2,1,0:T(8,128)(2,1)S(1)} collective-permute-done((bf16[4,96,384]{2,1,0:T(8,128)(2,1)S(1)}, bf16[4,96,384]{2,1,0:T(8,128)(2,1)S(1)}, u32[]{:S(2)}, u32[]{:S(2)}) %collective-permute-start.4) | collective-permute-done | bytes 294944 | tf_op jit(solution)/shard_map/ppermute | solution.py:283
  17.5 1.8 %collective-permute-start.5 = (bf16[4,96,384]{2,1,0:T(8,128)(2,1)S(1)}, bf16[4,96,384]{2,1,0:T(8,128)(2,1)S(1)}, u32[]{:S(2)}, u32[]{:S(2)}) collective-permute-start(bf16[4,96,384]{2,1,0:T(8,128)(2,1)S(1)} %collective-permute-done.4.rest_4_), channel_id=1, source_target_pairs={{0,2},{1,3},{2,0},{3,1},{4,6},{5,7},{6,4},{7,5},{8,10},{9,11},{10,... | collective-permute-start | bytes 884744 | tf_op jit(solution)/shard_map/ppermute | solution.py:283
  24.5 1.6 %collective-permute-start = (bf16[144,1536]{1,0:T(8,128)(2,1)S(1)}, bf16[144,1536]{1,0:T(8,128)(2,1)S(1)}, u32[]{:S(2)}, u32[]{:S(2)}) collective-permute-start(bf16[144,1536]{1,0:T(8,128)(2,1)S(1)} %get-tuple-element.24.own_ref), channel_id=1, source_target_pairs={{0,16},{16,0},{1,17},{17,1},{2,18},{18,2},{3,19},{19,3},{4,20},{20... | collective-permute-start | bytes 1327112 | tf_op jit(solution)/shard_map/ppermute | solution.py:293
  26.9 7.4 %collective-permute-done.oth_ref = bf16[144,1536]{1,0:T(8,128)(2,1)S(1)} collective-permute-done((bf16[144,1536]{1,0:T(8,128)(2,1)S(1)}, bf16[144,1536]{1,0:T(8,128)(2,1)S(1)}, u32[]{:S(2)}, u32[]{:S(2)}) %collective-permute-start) | collective-permute-done | bytes 442400 | tf_op jit(solution)/shard_map/ppermute | solution.py:293
  34.3 1.2 %collective-permute-done.13.rest_13_ = bf16[4,96,384]{2,1,0:T(8,128)(2,1)S(1)} collective-permute-done((bf16[4,96,384]{2,1,0:T(8,128)(2,1)S(1)}, bf16[4,96,384]{2,1,0:T(8,128)(2,1)S(1)}, u32[]{:S(2)}, u32[]{:S(2)}) %collective-permute-start.13) | collective-permute-done | bytes 294944 | tf_op jit(solution)/shard_map/ppermute | solution.py:283
  35.5 5.4 %collective-permute-done.8.rest_8_ = bf16[4,96,384]{2,1,0:T(8,128)(2,1)S(1)} collective-permute-done((bf16[4,96,384]{2,1,0:T(8,128)(2,1)S(1)}, bf16[4,96,384]{2,1,0:T(8,128)(2,1)S(1)}, u32[]{:S(2)}, u32[]{:S(2)}) %collective-permute-start.8) | collective-permute-done | bytes 294944 | tf_op jit(solution)/shard_map/ppermute | solution.py:283
  41.4 2.9 %collective-permute-done.9.rest_9_ = bf16[2,96,384]{2,1,0:T(8,128)(2,1)S(1)} collective-permute-done((bf16[2,96,384]{2,1,0:T(8,128)(2,1)S(1)}, bf16[2,96,384]{2,1,0:T(8,128)(2,1)S(1)}, u32[]{:S(2)}, u32[]{:S(2)}) %collective-permute-start.9) | collective-permute-done | bytes 147488 | tf_op jit(solution)/shard_map/ppermute | solution.py:283
  44.3 1.6 %collective-permute-start.16 = (bf16[128,1536]{1,0:T(8,128)(2,1)}, bf16[128,1536]{1,0:T(8,128)(2,1)S(1)}, u32[]{:S(2)}, u32[]{:S(2)}) collective-permute-start(bf16[128,1536]{1,0:T(8,128)(2,1)} %bitcast.7), channel_id=1, source_target_pairs={{0,16},{16,0},{1,17},{17,1},{2,18},{18,2},{3,19},{19,3},{4,20},{20... | collective-permute-start | bytes 1179656 | tf_op jit(solution)/shard_map/ppermute | solution.py:293
  45.9 1.6 %shard_map.124 = (bf16[1536,768]{1,0:T(8,128)(2,1)S(1)}, bf16[2,128,768]{2,1,0:T(8,128)(2,1)S(1)}, bf16[256,1536]{1,0:T(8,128)(2,1)S(1)}, bf16[2,16,128]{2,1,0:T(8,128)(2,1)S(1)}) custom-call(bf16[144,1536]{1,0:T(8,128)(2,1)S(1)} %get-tuple-element.24.own_ref, bf16[144,1536]{1,0:T(8,128)(2,1)S(1)} %collective-permute-done.oth_ref, ...), custom_call_target="tpu_custom_call" | custom-call | bytes 6000000 | tf_op jit(solution)/shard_map/pallas_call | solution.py:341
  47.5 2.1 %collective-permute-start.19 = (bf16[2,128,768]{2,1,0:T(8,128)(2,1)S(1)}, bf16[2,128,768]{2,1,0:T(8,128)(2,1)S(1)}, u32[]{:S(2)}, u32[]{:S(2)}) collective-permute-start(bf16[2,128,768]{2,1,0:T(8,128)(2,1)S(1)} %get-tuple-element.28.kv_ref), channel_id=1, source_target_pairs={{0,1},{1,2},{2,3},{3,4},{4,5},{5,6},{6,7},{7,8},{8,9},{9,10},{10,1... | collective-permute-start | bytes 1179656 | tf_op jit(solution)/shard_map/ppermute | solution.py:354
  50.7 5.7 %collective-permute-done.17.rest_9_ = bf16[2,96,384]{2,1,0:T(8,128)(2,1)S(1)} collective-permute-done((bf16[2,96,384]{2,1,0:T(8,128)(2,1)S(1)}, bf16[2,96,384]{2,1,0:T(8,128)(2,1)S(1)}, u32[]{:S(2)}, u32[]{:S(2)}) %collective-permute-start.17) | collective-permute-done | bytes 147488 | tf_op jit(solution)/shard_map/ppermute | solution.py:283
  56.4 2.0 %collective-permute-start.18 = (bf16[2,96,384]{2,1,0:T(8,128)(2,1)S(1)}, bf16[2,96,384]{2,1,0:T(8,128)(2,1)S(1)}, u32[]{:S(2)}, u32[]{:S(2)}) collective-permute-start(bf16[2,96,384]{2,1,0:T(8,128)(2,1)S(1)} %collective-permute-done.17.rest_9_), channel_id=1, source_target_pairs={{0,1},{1,0},{2,3},{3,2},{4,5},{5,4},{6,7},{7,6},{8,9},{9,8},{10,11... | collective-permute-start | bytes 442376 | tf_op jit(solution)/shard_map/ppermute | solution.py:283
  59.5 2.2 %shard_map.125 = (bf16[1536,768]{1,0:T(8,128)(2,1)S(1)}, bf16[2,128,384]{2,1,0:T(8,128)(2,1)S(1)}, bf16[2,128,384]{2,1,0:T(8,128)(2,1)S(1)}, f32[2,3,128,128]{3,...) custom-call(bf16[256,1536]{1,0:T(8,128)(2,1)S(1)} %get-tuple-element.26.xs, ...), custom_call_target="tpu_custom_call" | custom-call | bytes 9000000 | tf_op jit(solution)/shard_map/pallas_call | solution.py:357
  61.7 2.9 %shard_map.126 = (bf16[2,3,128,256]{3,2,1,0:T(8,128)(2,1)S(1)}, bf16[2,3,128,256]{3,2,1,0:T(8,128)(2,1)S(1)}, bf16[2,128,768]{2,1,0:T(8,128)(2,1)S(1)}) custom-call(bf16[2,16,128]{2,1,0:T(8,128)(2,1)S(1)} %get-tuple-element.25.flags, bf16[2,128,384]{2,1,0:T(8,128)(2,1)S(1)} %get-tuple-element.30.cq_ref, bf16[2,128,384]{2,1,0:T(8,128)(2,1)S(1)} %get-tuple-element.31.cg_ref, ...), custom_call_target="tpu_custom_call" | custom-call | bytes 9000000 | tf_op jit(solution)/shard_map/pallas_call | solution.py:365
  64.6 1.3 %collective-permute-start.20 = (bf16[2,128,768]{2,1,0:T(8,128)(2,1)S(1)}, bf16[2,128,768]{2,1,0:T(8,128)(2,1)S(1)}, u32[]{:S(2)}, u32[]{:S(2)}) collective-permute-start(bf16[2,128,768]{2,1,0:T(8,128)(2,1)S(1)} %get-tuple-element.41), channel_id=1, source_target_pairs={{1,0},{2,1},{3,2},{4,3},{5,4},{6,5},{7,6},{8,7},{9,8},{10,9},{11,1... | collective-permute-start | bytes 1179656 | tf_op jit(solution)/shard_map/ppermute | solution.py:376
  67.5 2.8 %shard_map.128 = (f32[128,1536]{1,0:T(8,128)S(1)}, f32[256,1536]{1,0:T(8,128)S(1)}) custom-call(bf16[128,1536]{1,0:T(8,128)(2,1)S(1)} %bitcast.5, bf16[2,128,384]{2,1,0:T(8,128)(2,1)S(1)} %get-tuple-element.37.ctx_ref, bf16[2,3,128,256]{3,2,1,0:T(8,128)(2,1)S(1)} %get-tuple-element.35.p_ref, bf16[2,3,128,256]{3,2,1,0:T(8,128)(2,1)S(1)} %get-tuple-element.38.ds_ref, ...), custom_call_target="tpu_custom_call" | custom-call | bytes 15000000 | tf_op jit(solution)/shard_map/pallas_call | solution.py:382
  71.2 1.3 %collective-permute-start.22 = (bf16[128,1536]{1,0:T(8,128)(2,1)S(1)}, bf16[128,1536]{1,0:T(8,128)(2,1)S(1)}, u32[]{:S(2)}, u32[]{:S(2)}) collective-permute-start(bf16[128,1536]{1,0:T(8,128)(2,1)S(1)} %shard_map.130), channel_id=1, source_target_pairs={{0,16},{16,0},{1,17},{17,1},{2,18},{18,2},{3,19},{19,3},{4,20},{20... | collective-permute-start | bytes 1179656 | tf_op jit(solution)/shard_map/ppermute | solution.py:293
  72.5 6.0 %collective-permute-done.21.lo_ret = bf16[128,1536]{1,0:T(8,128)(2,1)S(1)} collective-permute-done((bf16[128,1536]{1,0:T(8,128)(2,1)S(1)}, bf16[128,1536]{1,0:T(8,128)(2,1)S(1)}, u32[]{:S(2)}, u32[]{:S(2)}) %collective-permute-start.21) | collective-permute-done | bytes 393248 | tf_op jit(solution)/shard_map/ppermute | solution.py:293
  78.5 1.7 %shard_map.129 = (f32[128,1536]{1,0:T(8,128)S(1)}, bf16[128,1536]{1,0:T(8,128)(2,1)}) custom-call(f32[256,1536]{1,0:T(8,128)S(1)} %get-tuple-element.40.np_ref, bf16[2,128,768]{2,1,0:T(8,128)(2,1)S(1)} %collective-permute-done.20.ret_ref, bf16[1536,768]{1,0:T(8,128)(2,1)S(1)} %get-tuple-element.39.wkv, f32[128,1536]{1,0:T(8,128)S(1)} %get-tuple-element.42.lo_own, ...), custom_call_target="tpu_custom_call" | custom-call | bytes 3000000 | tf_op jit(solution)/shard_map/pallas_call | solution.py:391
  80.2 6.8 %collective-permute-done.22.np_ret = bf16[128,1536]{1,0:T(8,128)(2,1)S(1)} collective-permute-done((bf16[128,1536]{1,0:T(8,128)(2,1)S(1)}, bf16[128,1536]{1,0:T(8,128)(2,1)S(1)}, u32[]{:S(2)}, u32[]{:S(2)}) %collective-permute-start.22) | collective-permute-done | bytes 393248 | tf_op jit(solution)/shard_map/ppermute | solution.py:293
  87.0 1.4 %shard_map.131 = bf16[128,1536]{1,0:T(8,128)(2,1)} custom-call(bf16[128,1536]{1,0:T(8,128)(2,1)S(1)} %bitcast.6, f32[1,1536]{1,0:T(1,128)S(1)} %broadcast_in_dim.15.gain_ref, bf16[128,1536]{1,0:T(8,128)(2,1)S(1)} %bitcast.9, f32[128,1536]{1,0:T(8,128)S(1)} %get-tuple-element.45.np_own, bf16[128,1536]{1,0:T(8,128)(2,1)S(1)} %collective-permute-done.22.np_ret), custom_call_target="tpu_custom_call" | custom-call | bytes 3000000 | tf_op jit(solution)/shard_map/pallas_call | solution.py:394
  (53 shorter events, 14.3 us)
Async XLA Ops:
  4.6 13.0 %collective-permute-start.4 = (bf16[4,96,384]{2,1,0:T(8,128)(2,1)S(1)}, bf16[4,96,384]{2,1,0:T(8,128)(2,1)S(1)}, u32[]{:S(2)}, u32[]{:S(2)}) collective-permute-start(bf16[4,96,384]{2,1,0:T(8,128)(2,1)S(1)} %shard_map.123.rest_0_), channel_id=1, source_target_pairs={{0,4},{1,5},{2,6},{3,7},{4,8},{5,9},{6,10},{7,11},{8,12},{9,13},{1... | collective-permute-start | bytes 884744 | tf_op jit(solution)/shard_map/ppermute | solution.py:283
  7.6 18.4 %collective-permute-start.12 = (bf16[4,96,384]{2,1,0:T(8,128)(2,1)S(1)}, bf16[4,96,384]{2,1,0:T(8,128)(2,1)S(1)}, u32[]{:S(2)}, u32[]{:S(2)}) collective-permute-start(bf16[4,96,384]{2,1,0:T(8,128)(2,1)S(1)} %shard_map.123.rest_0_), channel_id=1, source_target_pairs={{0,12},{1,13},{2,14},{3,15},{4,0},{5,1},{6,2},{7,3},{8,4},{9,5},{1... | collective-permute-start | bytes 884744 | tf_op jit(solution)/shard_map/ppermute | solution.py:283
  9.7 16.3 %collective-permute-start.2 = (bf16[4,96,384]{2,1,0:T(8,128)(2,1)S(1)}, bf16[4,96,384]{2,1,0:T(8,128)(2,1)S(1)}, u32[]{:S(2)}, u32[]{:S(2)}) collective-permute-start(bf16[4,96,384]{2,1,0:T(8,128)(2,1)S(1)} %shard_map.123.rest_0_), channel_id=1, source_target_pairs={{0,1},{1,0},{2,3},{3,2},{4,5},{5,4},{6,7},{7,6},{8,9},{9,8},{10,11... | collective-permute-start | bytes 884744 | tf_op jit(solution)/shard_map/ppermute | solution.py:283
  9.7 16.9 %collective-permute-start.1 = (bf16[4,96,384]{2,1,0:T(8,128)(2,1)S(1)}, bf16[4,96,384]{2,1,0:T(8,128)(2,1)S(1)}, u32[]{:S(2)}, u32[]{:S(2)}) collective-permute-start(bf16[4,96,384]{2,1,0:T(8,128)(2,1)S(1)} %shard_map.123.rest_0_), channel_id=1, source_target_pairs={{0,2},{1,3},{2,0},{3,1},{4,6},{5,7},{6,4},{7,5},{8,10},{9,11},{10,... | collective-permute-start | bytes 884744 | tf_op jit(solution)/shard_map/ppermute | solution.py:283
  17.5 9.1 %collective-permute-start.5 = (bf16[4,96,384]{2,1,0:T(8,128)(2,1)S(1)}, bf16[4,96,384]{2,1,0:T(8,128)(2,1)S(1)}, u32[]{:S(2)}, u32[]{:S(2)}) collective-permute-start(bf16[4,96,384]{2,1,0:T(8,128)(2,1)S(1)} %collective-permute-done.4.rest_4_), channel_id=1, source_target_pairs={{0,2},{1,3},{2,0},{3,1},{4,6},{5,7},{6,4},{7,5},{8,10},{9,11},{10,... | collective-permute-start | bytes 884744 | tf_op jit(solution)/shard_map/ppermute | solution.py:283
  24.5 9.8 %collective-permute-start = (bf16[144,1536]{1,0:T(8,128)(2,1)S(1)}, bf16[144,1536]{1,0:T(8,128)(2,1)S(1)}, u32[]{:S(2)}, u32[]{:S(2)}) collective-permute-start(bf16[144,1536]{1,0:T(8,128)(2,1)S(1)} %get-tuple-element.24.own_ref), channel_id=1, source_target_pairs={{0,16},{16,0},{1,17},{17,1},{2,18},{18,2},{3,19},{19,3},{4,20},{20... | collective-permute-start | bytes 1327112 | tf_op jit(solution)/shard_map/ppermute | solution.py:293
  26.0 8.3 %collective-permute-start.14 = (bf16[4,96,384]{2,1,0:T(8,128)(2,1)S(1)}, bf16[4,96,384]{2,1,0:T(8,128)(2,1)S(1)}, u32[]{:S(2)}, u32[]{:S(2)}) collective-permute-start(bf16[4,96,384]{2,1,0:T(8,128)(2,1)S(1)} %collective-permute-done.12.rest_12_), channel_id=1, source_target_pairs={{0,1},{1,0},{2,3},{3,2},{4,5},{5,4},{6,7},{7,6},{8,9},{9,8},{10,11... | collective-permute-start | bytes 884744 | tf_op jit(solution)/shard_map/ppermute | solution.py:283
  26.0 9.4 %collective-permute-start.13 = (bf16[4,96,384]{2,1,0:T(8,128)(2,1)S(1)}, bf16[4,96,384]{2,1,0:T(8,128)(2,1)S(1)}, u32[]{:S(2)}, u32[]{:S(2)}) collective-permute-start(bf16[4,96,384]{2,1,0:T(8,128)(2,1)S(1)} %collective-permute-done.12.rest_12_), channel_id=1, source_target_pairs={{0,2},{1,3},{2,0},{3,1},{4,6},{5,7},{6,4},{7,5},{8,10},{9,11},{10,... | collective-permute-start | bytes 884744 | tf_op jit(solution)/shard_map/ppermute | solution.py:283
  26.6 14.3 %collective-permute-start.8 = (bf16[4,96,384]{2,1,0:T(8,128)(2,1)S(1)}, bf16[4,96,384]{2,1,0:T(8,128)(2,1)S(1)}, u32[]{:S(2)}, u32[]{:S(2)}) collective-permute-start(bf16[4,96,384]{2,1,0:T(8,128)(2,1)S(1)} %collective-permute-done.4.rest_4_), channel_id=1, source_target_pairs={{0,4},{1,5},{2,6},{3,7},{4,8},{5,9},{6,10},{7,11},{8,12},{9,13},{1... | collective-permute-start | bytes 884744 | tf_op jit(solution)/shard_map/ppermute | solution.py:283
  26.6 14.3 %collective-permute-start.6 = (bf16[4,96,384]{2,1,0:T(8,128)(2,1)S(1)}, bf16[4,96,384]{2,1,0:T(8,128)(2,1)S(1)}, u32[]{:S(2)}, u32[]{:S(2)}) collective-permute-start(bf16[4,96,384]{2,1,0:T(8,128)(2,1)S(1)} %collective-permute-done.4.rest_4_), channel_id=1, source_target_pairs={{0,1},{1,0},{2,3},{3,2},{4,5},{5,4},{6,7},{7,6},{8,9},{9,8},{10,11... | collective-permute-start | bytes 884744 | tf_op jit(solution)/shard_map/ppermute | solution.py:283
  34.3 10.0 %collective-permute-start.3 = (bf16[4,96,384]{2,1,0:T(8,128)(2,1)S(1)}, bf16[4,96,384]{2,1,0:T(8,128)(2,1)S(1)}, u32[]{:S(2)}, u32[]{:S(2)}) collective-permute-start(bf16[4,96,384]{2,1,0:T(8,128)(2,1)S(1)} %collective-permute-done.1.rest_1_), channel_id=1, source_target_pairs={{0,1},{1,0},{2,3},{3,2},{4,5},{5,4},{6,7},{7,6},{8,9},{9,8},{10,11... | collective-permute-start | bytes 884744 | tf_op jit(solution)/shard_map/ppermute | solution.py:283
  34.3 10.0 %collective-permute-start.9 = (bf16[2,96,384]{2,1,0:T(8,128)(2,1)S(1)}, bf16[2,96,384]{2,1,0:T(8,128)(2,1)S(1)}, u32[]{:S(2)}, u32[]{:S(2)}) collective-permute-start(bf16[2,96,384]{2,1,0:T(8,128)(2,1)S(1)} %slice.8), channel_id=1, source_target_pairs={{0,4},{1,5},{2,6},{3,7},{4,8},{5,9},{6,10},{7,11},{8,12},{9,13},{1... | collective-permute-start | bytes 442376 | tf_op jit(solution)/shard_map/ppermute | solution.py:283
  35.5 10.4 %collective-permute-start.15 = (bf16[4,96,384]{2,1,0:T(8,128)(2,1)S(1)}, bf16[4,96,384]{2,1,0:T(8,128)(2,1)S(1)}, u32[]{:S(2)}, u32[]{:S(2)}) collective-permute-start(bf16[4,96,384]{2,1,0:T(8,128)(2,1)S(1)} %collective-permute-done.13.rest_13_), channel_id=1, source_target_pairs={{0,1},{1,0},{2,3},{3,2},{4,5},{5,4},{6,7},{7,6},{8,9},{9,8},{10,11... | collective-permute-start | bytes 884744 | tf_op jit(solution)/shard_map/ppermute | solution.py:283
  40.9 5.0 %collective-permute-start.10 = (bf16[4,96,384]{2,1,0:T(8,128)(2,1)S(1)}, bf16[4,96,384]{2,1,0:T(8,128)(2,1)S(1)}, u32[]{:S(2)}, u32[]{:S(2)}) collective-permute-start(bf16[4,96,384]{2,1,0:T(8,128)(2,1)S(1)} %collective-permute-done.8.rest_8_), channel_id=1, source_target_pairs={{0,1},{1,0},{2,3},{3,2},{4,5},{5,4},{6,7},{7,6},{8,9},{9,8},{10,11... | collective-permute-start | bytes 884744 | tf_op jit(solution)/shard_map/ppermute | solution.py:283
  40.9 5.0 %collective-permute-start.7 = (bf16[4,96,384]{2,1,0:T(8,128)(2,1)S(1)}, bf16[4,96,384]{2,1,0:T(8,128)(2,1)S(1)}, u32[]{:S(2)}, u32[]{:S(2)}) collective-permute-start(bf16[4,96,384]{2,1,0:T(8,128)(2,1)S(1)} %collective-permute-done.5.rest_5_), channel_id=1, source_target_pairs={{0,1},{1,0},{2,3},{3,2},{4,5},{5,4},{6,7},{7,6},{8,9},{9,8},{10,11... | collective-permute-start | bytes 884744 | tf_op jit(solution)/shard_map/ppermute | solution.py:283
  44.3 1.6 %collective-permute-start.11 = (bf16[2,96,384]{2,1,0:T(8,128)(2,1)S(1)}, bf16[2,96,384]{2,1,0:T(8,128)(2,1)S(1)}, u32[]{:S(2)}, u32[]{:S(2)}) collective-permute-start(bf16[2,96,384]{2,1,0:T(8,128)(2,1)S(1)} %collective-permute-done.9.rest_9_), channel_id=1, source_target_pairs={{0,1},{1,0},{2,3},{3,2},{4,5},{5,4},{6,7},{7,6},{8,9},{9,8},{10,11... | collective-permute-start | bytes 442376 | tf_op jit(solution)/shard_map/ppermute | solution.py:283
  44.3 15.2 %copy-start.2 = (bf16[1,128,1536]{2,1,0:T(8,128)(2,1)S(1)}, bf16[1,128,1536]{2,1,0:T(8,128)(2,1)}, u32[]{:S(2)}) copy-start(bf16[1,128,1536]{2,1,0:T(8,128)(2,1)} %param.21) | copy-start | bytes 1179652
  44.3 14.1 %collective-permute-start.16 = (bf16[128,1536]{1,0:T(8,128)(2,1)}, bf16[128,1536]{1,0:T(8,128)(2,1)S(1)}, u32[]{:S(2)}, u32[]{:S(2)}) collective-permute-start(bf16[128,1536]{1,0:T(8,128)(2,1)} %bitcast.7), channel_id=1, source_target_pairs={{0,16},{16,0},{1,17},{17,1},{2,18},{18,2},{3,19},{19,3},{4,20},{20... | collective-permute-start | bytes 1179656 | tf_op jit(solution)/shard_map/ppermute | solution.py:293
  47.5 14.1 %collective-permute-start.19 = (bf16[2,128,768]{2,1,0:T(8,128)(2,1)S(1)}, bf16[2,128,768]{2,1,0:T(8,128)(2,1)S(1)}, u32[]{:S(2)}, u32[]{:S(2)}) collective-permute-start(bf16[2,128,768]{2,1,0:T(8,128)(2,1)S(1)} %get-tuple-element.28.kv_ref), channel_id=1, source_target_pairs={{0,1},{1,2},{2,3},{3,4},{4,5},{5,6},{6,7},{7,8},{8,9},{9,10},{10,1... | collective-permute-start | bytes 1179656 | tf_op jit(solution)/shard_map/ppermute | solution.py:354
  49.7 6.8 %collective-permute-start.17 = (bf16[2,96,384]{2,1,0:T(8,128)(2,1)S(1)}, bf16[2,96,384]{2,1,0:T(8,128)(2,1)S(1)}, u32[]{:S(2)}, u32[]{:S(2)}) collective-permute-start(bf16[2,96,384]{2,1,0:T(8,128)(2,1)S(1)} %slice.9), channel_id=1, source_target_pairs={{0,2},{1,3},{2,0},{3,1},{4,6},{5,7},{6,4},{7,5},{8,10},{9,11},{10,... | collective-permute-start | bytes 442376 | tf_op jit(solution)/shard_map/ppermute | solution.py:283
  56.4 3.0 %collective-permute-start.18 = (bf16[2,96,384]{2,1,0:T(8,128)(2,1)S(1)}, bf16[2,96,384]{2,1,0:T(8,128)(2,1)S(1)}, u32[]{:S(2)}, u32[]{:S(2)}) collective-permute-start(bf16[2,96,384]{2,1,0:T(8,128)(2,1)S(1)} %collective-permute-done.17.rest_9_), channel_id=1, source_target_pairs={{0,1},{1,0},{2,3},{3,2},{4,5},{5,4},{6,7},{7,6},{8,9},{9,8},{10,11... | collective-permute-start | bytes 442376 | tf_op jit(solution)/shard_map/ppermute | solution.py:283
  64.6 5.7 %collective-permute-start.20 = (bf16[2,128,768]{2,1,0:T(8,128)(2,1)S(1)}, bf16[2,128,768]{2,1,0:T(8,128)(2,1)S(1)}, u32[]{:S(2)}, u32[]{:S(2)}) collective-permute-start(bf16[2,128,768]{2,1,0:T(8,128)(2,1)S(1)} %get-tuple-element.41), channel_id=1, source_target_pairs={{1,0},{2,1},{3,2},{4,3},{5,4},{6,5},{7,6},{8,7},{9,8},{10,9},{11,1... | collective-permute-start | bytes 1179656 | tf_op jit(solution)/shard_map/ppermute | solution.py:376
  66.6 11.9 %collective-permute-start.21 = (bf16[128,1536]{1,0:T(8,128)(2,1)S(1)}, bf16[128,1536]{1,0:T(8,128)(2,1)S(1)}, u32[]{:S(2)}, u32[]{:S(2)}) collective-permute-start(bf16[128,1536]{1,0:T(8,128)(2,1)S(1)} %get-tuple-element.43), channel_id=1, source_target_pairs={{0,16},{16,0},{1,17},{17,1},{2,18},{18,2},{3,19},{19,3},{4,20},{20... | collective-permute-start | bytes 1179656 | tf_op jit(solution)/shard_map/ppermute | solution.py:293
  71.2 15.7 %collective-permute-start.22 = (bf16[128,1536]{1,0:T(8,128)(2,1)S(1)}, bf16[128,1536]{1,0:T(8,128)(2,1)S(1)}, u32[]{:S(2)}, u32[]{:S(2)}) collective-permute-start(bf16[128,1536]{1,0:T(8,128)(2,1)S(1)} %shard_map.130), channel_id=1, source_target_pairs={{0,16},{16,0},{1,17},{17,1},{2,18},{18,2},{3,19},{19,3},{4,20},{20... | collective-permute-start | bytes 1179656 | tf_op jit(solution)/shard_map/ppermute | solution.py:293
  (7 other events, 11.3 us)

commit v3 on v2

v3 whole, which is shorter than its diff:
```python
import functools

import jax
import jax.numpy as jnp
from jax import lax
from jax.experimental import pallas as pl
from jax.experimental.pallas import tpu as pltpu
from jax.sharding import PartitionSpec as P

H = 6
DH = 128
epsilon = 1e-05

F32 = jnp.float32
BF16 = jnp.bfloat16
SEG = 128
D = 1536
HALF = 384
HEADS = HALF // DH
ROWS = 96
ZS = 4
BLK = 4 * ROWS
NT = (((1,), (1,)), ((), ()))
TN = (((0,), (0,)), ((), ()))


def dot(a, b, dims=(((1,), (0,)), ((), ()))):
    return lax.dot_general(a, b, dims, preferred_element_type=F32)


def place():
    t = lax.axis_index("tm")
    return t // 4, (t // 2) % 2, t % 2


def plane_columns(z, r):
    return pl.ds(pl.multiple_of(lax.rem(z - r + ZS, ZS) * BLK, 128), BLK)


def lanes(ref):
    return jnp.concatenate([ref[i : i + 1, :] for i in range(ref.shape[0])], axis=1)


def prepare_kernel(
    k_ref, v_ref, q_ref, o_ref, x_ref, gain_ref, pk_ref, flag_ref,
    shard, out_ref, pk_out, held, x_in, gain_in, pk_in, sems,
):
    z, _, _ = place()
    own = pl.ds(pl.multiple_of(lax.axis_index("grp") * HALF, 128), HALF)
    copies = [
        pltpu.make_async_copy(x_ref.at[0], x_in, sems.at[0]),
        pltpu.make_async_copy(gain_ref, gain_in, sems.at[1]),
        pltpu.make_async_copy(pk_ref.at[:, own], pk_in, sems.at[2]),
    ] + [
        pltpu.make_async_copy(ref, shard.at[i], sems.at[3 + i])
        for i, ref in enumerate((k_ref, v_ref, q_ref, o_ref))
    ]
    for copy in copies:
        copy.start()
    for copy in copies:
        copy.wait()
    x = x_in[...].astype(F32)
    center = jnp.mean(x, axis=-1, keepdims=True)
    moved = x - center
    spread = jnp.mean(jnp.square(moved), axis=-1, keepdims=True)
    held[...] = (moved * lax.rsqrt(spread + epsilon) * lanes(gain_in)).astype(BF16)
    for r in range(ZS):
        out_ref[0:SEG, r * BLK : (r + 1) * BLK] = held[:, plane_columns(z, r)]
    flag = flag_ref[0, 0].astype(F32)
    out_ref[SEG:, :] = jnp.full((16, D), flag, F32).astype(BF16)
    row = lax.broadcasted_iota(jnp.int32, (2 * SEG, 2 * SEG), 0)
    col = lax.broadcasted_iota(jnp.int32, (2 * SEG, 2 * SEG), 1)
    flip = jnp.where(row + col == 2 * SEG - 1, 1.0, 0.0).astype(BF16)
    pk_out[...] = dot(flip, pk_in[...]).astype(BF16)


def stage_kernel(shard_ref, normed_ref, shard, normed):
    shard[...] = shard_ref[...]
    normed[...] = normed_ref[...]


def shard_rows(r, j):
    _, y, c = place()
    yy = 1 - y if j % 2 else y
    cc = 1 - c if j // 2 else c
    return pl.ds(pl.multiple_of(r * BLK + (2 * yy + cc) * ROWS, 16), ROWS)


def fetch(pieces, first, weights, sems):
    copies = []
    for n in range(4 * ZS):
        for w in range(2):
            copies.append(
                pltpu.make_async_copy(
                    pieces[n].at[first[n] + w],
                    weights.at[shard_rows(n // 4, n % 4), pl.ds(w * HALF, HALF)],
                    sems.at[2 * n + w],
                )
            )
    for copy in copies:
        copy.start()
    return copies


def accumulate(x, weights, copies, columns):
    total = None
    for half in range(2):
        for copy in copies[half * 16 : half * 16 + 16]:
            copy.wait()
        rows = slice(half * 2 * BLK, (half + 1) * 2 * BLK)
        part = dot(x[:, rows], weights[rows, columns])
        total = part if total is None else total + part
    return total


def key_value_kernel(own_ref, oth_ref, *rest):
    pieces, (weights, kv_own, kv_oth, xs, flags, sems) = rest[:16], rest[16:]
    copies = fetch(pieces, (0,) * 16, weights, sems)
    flags[0] = own_ref[SEG:, :DH]
    flags[1] = oth_ref[SEG:, :DH]
    xs[0:SEG, :] = own_ref[0:SEG, :]
    xs[SEG:, :] = oth_ref[0:SEG, :]
    total = accumulate(xs, weights, copies, slice(0, 2 * HALF))
    kv_own[...] = total[:SEG].astype(BF16)
    kv_oth[...] = total[SEG:].astype(BF16)


SCALE = DH**-0.5
QO_PLACES = (2,) * 9 + (0,) + (2,) + (0,) + (2,) * 4


def head(i):
    return slice(i * DH, (i + 1) * DH)


def own_half(ref):
    g = lax.axis_index("grp")
    parts = [jnp.where(g == 0, ref[h : h + 1], ref[HEADS + h : HEADS + h + 1]) for h in range(HEADS)]
    return jnp.concatenate(parts, axis=1)


def query_kernel(xs, cot_own, cot_oth, cb_ref, pb_ref, kv_own, kv_oth, pk_ref, *rest):
    pieces = rest[:16]
    weights, cq_ref, cg_ref, rel_ref, own_ref, dp_ref = rest[16:22]
    cots, sems = rest[22:]
    z, _, _ = place()
    copies = fetch(pieces, QO_PLACES, weights, sems)
    for r in range(ZS):
        cots[0:SEG, r * BLK : (r + 1) * BLK] = cot_own[:, plane_columns(z, r)]
        cots[SEG:, r * BLK : (r + 1) * BLK] = cot_oth[:, plane_columns(z, r)]
    q = accumulate(xs, weights, copies, slice(0, HALF))
    cq = (q + own_half(cb_ref)).astype(BF16)
    pq = (q + own_half(pb_ref)).astype(BF16)
    cg = dot(cots[...], weights[:, HALF:]).astype(BF16)
    row = lax.broadcasted_iota(jnp.int32, (SEG, SEG), 0)
    col = lax.broadcasted_iota(jnp.int32, (SEG, SEG), 1)
    for rec in range(2):
        rows = slice(rec * SEG, (rec + 1) * SEG)
        kv_ref = (kv_own, kv_oth)[rec]
        cq_ref[rec] = cq[rows]
        cg_ref[rec] = cg[rows]
        for h in range(HEADS):
            f, fv = head(h), head(HEADS + h)
            rel = dot(pq[rows, f], pk_ref[:, f], NT)
            rel = pltpu.roll(rel, SEG + 1, 1, stride=1, stride_axis=0)
            rel_ref[rec, h] = rel[:, :SEG]
            s_own = (dot(cq[rows, f], kv_ref[:, f], NT) + rel[:, SEG:]) * SCALE
            own_ref[rec, h] = jnp.where(col <= row, s_own, -jnp.inf)
            dp_ref[rec, h] = dot(cg[rows, f], kv_ref[:, fv], NT)


def memory_kernel(
    rec, flags, cq_ref, cg_ref, rel_ref, own_ref, dp_ref, kv_ref, mem_ref,
    p_ref, ds_ref, dmem_ref, ctx_ref,
):
    flag = flags[rec, 0:1, :].astype(F32)
    for h in range(HEADS):
        f, fv = head(h), head(HEADS + h)
        cq, g = cq_ref[rec, :, f], cg_ref[rec, :, f]
        s_own = own_ref[rec, h]
        s_mem = (dot(cq, mem_ref[:, f], NT) + rel_ref[rec, h]) * SCALE
        s_mem = jnp.where(flag == 0, s_mem, -jnp.inf)
        dp_mem = dot(g, mem_ref[:, fv], NT)
        peak = jnp.max(jnp.maximum(s_mem, s_own), axis=-1, keepdims=True)
        e_mem = jnp.exp(s_mem - peak)
        e_own = jnp.exp(s_own - peak)
        norm = 1.0 / jnp.sum(e_mem + e_own, axis=-1, keepdims=True)
        a_mem, a_own = e_mem * norm, e_own * norm
        dp_own = dp_ref[rec, h]
        inner = jnp.sum(a_mem * dp_mem + a_own * dp_own, axis=-1, keepdims=True)
        p_mem, p_own = a_mem.astype(BF16), a_own.astype(BF16)
        ctx = dot(p_mem, mem_ref[:, fv]) + dot(p_own, kv_ref[:, fv])
        ctx_ref[:, f] = ctx.astype(BF16)
        ds_mem = (a_mem * (dp_mem - inner) * SCALE).astype(BF16)
        p_ref[h] = p_own
        ds_ref[h, :, :SEG] = ds_mem
        ds_ref[h, :, SEG:] = (a_own * (dp_own - inner) * SCALE).astype(BF16)
        dmem_ref[:, f] = dot(ds_mem, cq, TN).astype(BF16)
        dmem_ref[:, fv] = dot(p_mem, g, TN).astype(BF16)


def grad_kernel(
    rec, p_ref, ds_ref, cq_ref, cg_ref, kv_ref, mem_ref, pk_ref, wkv, wqo, np_ref, dq, dkv
):
    row = lax.broadcasted_iota(jnp.int32, (SEG, SEG), 0)
    col = lax.broadcasted_iota(jnp.int32, (SEG, SEG), 1)
    flip = jnp.where(row + col == SEG - 1, 1.0, 0.0).astype(BF16)
    for h in range(HEADS):
        f, fv = head(h), head(HEADS + h)
        ds = ds_ref[h]
        rel = pltpu.roll(dot(flip, ds), 0, 1, stride=1, stride_axis=0).astype(BF16)
        rel = dot(flip, rel).astype(BF16)
        total = dot(ds[:, :SEG], mem_ref[:, f]) + dot(ds[:, SEG:], kv_ref[:, f])
        dq[:, f] = (total + dot(rel, pk_ref[:, f])).astype(BF16)
        dkv[:, f] = dot(ds[:, SEG:], cq_ref[rec, :, f], TN).astype(BF16)
        dkv[:, fv] = dot(p_ref[h], cg_ref[rec, :, f], TN).astype(BF16)
    np_ref[...] = dot(dq[...], wqo[:, :HALF], NT) + dot(dkv[...], wkv[...], NT)


def returned_kernel(np_ref, ret_ref, wkv, out_ref):
    out_ref[...] = (np_ref[...] + dot(ret_ref[...], wkv[...], NT)).astype(out_ref.dtype)


def partial_output_kernel(ctx_ref, wqo, out_ref):
    out_ref[...] = dot(ctx_ref[...], wqo[:, HALF:], NT).astype(BF16)


def output_kernel(x_ref, ctx_ref, wqo, lo_ret, out_ref, held):
    z, _, _ = place()
    held[...] = dot(ctx_ref[...], wqo[:, HALF:], NT)
    for r in range(ZS):
        cols, there = slice(r * BLK, (r + 1) * BLK), plane_columns(z, r)
        total = held[:, cols] + lo_ret[:, cols].astype(F32)
        out_ref[0, :, there] = (x_ref[0, :, there].astype(F32) + total).astype(BF16)


def finish_kernel(x_ref, gain_ref, cot_ref, np_own, np_ret, grad_ref, total):
    z, _, _ = place()
    for r in range(ZS):
        cols = slice(r * BLK, (r + 1) * BLK)
        total[:, plane_columns(z, r)] = np_own[:, cols] + np_ret[:, cols].astype(F32)
    x = x_ref[0].astype(F32)
    center = jnp.mean(x, axis=-1, keepdims=True)
    moved = x - center
    spread = jnp.mean(jnp.square(moved), axis=-1, keepdims=True)
    rstd = lax.rsqrt(spread + epsilon)
    hat = moved * rstd
    g = total[...] * lanes(gain_ref)
    mean_g = jnp.mean(g, axis=-1, keepdims=True)
    mean_gh = jnp.mean(g * hat, axis=-1, keepdims=True)
    grad = (rstd * (g - mean_g - hat * mean_gh)).astype(BF16)
    grad_ref[0] = cot_ref[...] + grad


def call(kernel, outs, scratch=(), in_specs=None, mib=24):
    return pl.pallas_call(
        kernel,
        out_shape=outs,
        in_specs=in_specs,
        out_specs=jax.tree.map(lambda _: VM, outs),
        scratch_shapes=list(scratch),
        compiler_params=pltpu.CompilerParams(vmem_limit_bytes=mib * 1024 * 1024),
        cost_estimate=pl.CostEstimate(
            flops=0, bytes_accessed=1024, transcendentals=0
        ),
    )


def shape(*dims, dtype=BF16):
    return jax.ShapeDtypeStruct(dims, dtype)


VM = pl.BlockSpec(memory_space=pltpu.VMEM)
SM = pl.BlockSpec(memory_space=pltpu.SMEM)
ANY = pl.BlockSpec(memory_space=pl.ANY)


def moved_by(f):
    route = []
    for z in range(ZS):
        for y in range(2):
            for c in range(2):
                zz, yy, cc = f(z, y, c)
                route.append((4 * z + 2 * y + c, 4 * zz + 2 * yy + cc))
    return lambda block: lax.ppermute(block, "tm", route)


up = moved_by(lambda z, y, c: ((z + 1) % ZS, y, c))
down = moved_by(lambda z, y, c: ((z - 1) % ZS, y, c))
across = moved_by(lambda z, y, c: (z, 1 - y, c))
sibling = moved_by(lambda z, y, c: (z, y, 1 - c))


def after(block, *earlier):
    return lax.optimization_barrier((block, *earlier))[0]


def other(block):
    return lax.ppermute(block, "grp", [(0, 1), (1, 0)])


def split_heads(
    inputs,
    norm_gain,
    query_weight,
    key_weight,
    value_weight,
    output_weight,
    content_bias,
    position_bias,
    position_keys,
    start_flags,
    cotangent,
):
    cot = cotangent[0]
    gain = norm_gain.reshape(D // 128, 128)
    w0, normed, pk = call(
        prepare_kernel,
        (shape(4, ROWS, HALF), shape(SEG + 16, D), shape(2 * SEG, HALF)),
        [
            pltpu.VMEM((SEG, D), BF16),
            pltpu.VMEM((SEG, D), BF16),
            pltpu.VMEM((D // 128, 128), F32),
            pltpu.VMEM((2 * SEG, HALF), BF16),
            pltpu.SemaphoreType.DMA((7,)),
        ],
        [ANY] * 7 + [SM],
        62,
    )(
        key_weight, value_weight, query_weight, output_weight, inputs, gain, position_keys,
        start_flags,
    )
    normed_oth = other(normed)
    w1 = up(w0)
    w0y = across(w0)
    w3 = down(w0)
    w0_near, normed = call(
        stage_kernel, (shape(4, ROWS, HALF), shape(SEG + 16, D)), (), [VM] * 2
    )(w0, normed)
    w1 = after(w1, w0_near)
    cot_oth = other(after(cot, w1))
    w1y = across(w1)
    w2 = up(w1)
    w3y = across(w3)
    w2y_kv = up(after(w1y, w3)[:2])
    w2y_qo = across(after(w2, w3)[2:])
    here = [w0_near, w0y, w1, w1y, w2, w2y_kv, w3, w3y]
    there = [sibling(p) for p in [w0] + here[1:]]
    w2y_qo_there = sibling(w2y_qo)
    kv_pieces = []
    for r in range(ZS):
        kv_pieces += here[2 * r : 2 * r + 2] + there[2 * r : 2 * r + 2]
    qo_pieces = list(kv_pieces)
    qo_pieces[9], qo_pieces[11] = w2y_qo, w2y_qo_there

    half = shape(SEG, 2 * HALF)
    wkv, kv, kv_oth, xs, flags = call(
        key_value_kernel,
        (
            shape(D, 2 * HALF),
            half,
            half,
            shape(2 * SEG, D),
            shape(2, 16, DH),
        ),
        [pltpu.SemaphoreType.DMA((32,))],
        [VM, VM] + [ANY] * 16,
    )(after(normed, w2y_qo, cot_oth), normed_oth, *kv_pieces)
    steps = lax.axis_size("tm")
    onward = [(i, i + 1) for i in range(steps - 1)]
    back = [(i + 1, i) for i in range(steps - 1)]
    mem_oth = lax.ppermute(kv_oth, "tm", onward)
    mem = lax.ppermute(kv, "tm", onward)
    blocks = shape(2, HEADS, SEG, SEG, dtype=F32)
    wqo, cq, cg, rel, s_own, dp_own = call(
        query_kernel,
        (shape(D, 2 * HALF), shape(2, SEG, HALF), shape(2, SEG, HALF), blocks, blocks, blocks),
        [pltpu.VMEM((2 * SEG, D), BF16), pltpu.SemaphoreType.DMA((32,))],
        [VM] * 8 + [ANY] * 16,
    )(
        xs, cot, cot_oth, content_bias.reshape(H, DH), position_bias.reshape(H, DH),
        kv, kv_oth, pk, *qo_pieces,
    )

    def memory(rec, kv_rows, mem_rows):
        return call(
            functools.partial(memory_kernel, rec),
            (shape(HEADS, SEG, SEG), shape(HEADS, SEG, 2 * SEG), half, shape(SEG, HALF)),
            (),
            [VM] * 8,
        )(flags, cq, cg, rel, s_own, dp_own, kv_rows, mem_rows)

    def grads(rec, p, ds, kv_rows, mem_rows):
        return call(
            functools.partial(grad_kernel, rec),
            shape(SEG, D, dtype=F32),
            [pltpu.VMEM((SEG, HALF), BF16), pltpu.VMEM((SEG, 2 * HALF), BF16)],
            [VM] * 9,
        )(p, ds, cq, cg, kv_rows, mem_rows, pk, wkv, wqo)

    p_oth, ds_oth, dmem_oth, ctx_oth = memory(1, kv_oth, mem_oth)
    ret_oth = lax.ppermute(dmem_oth, "tm", back)
    lo_oth = call(partial_output_kernel, shape(SEG, D), (), [VM] * 2)(ctx_oth, wqo)
    lo_ret = other(lo_oth)
    p, ds, dmem, ctx = memory(0, kv, after(mem, lo_oth))
    ret = lax.ppermute(dmem, "tm", back)
    partial_oth = grads(1, after(p_oth, dmem), ds_oth, kv_oth, mem_oth)
    np_oth = call(returned_kernel, shape(SEG, D), (), [VM] * 3)(partial_oth, ret_oth, wkv)
    np_ret = other(np_oth)
    partial = grads(0, after(p, np_oth), ds, kv, mem)
    np_own = call(returned_kernel, shape(SEG, D, dtype=F32), (), [VM] * 3)(partial, ret, wkv)
    layer_out = call(
        output_kernel, shape(1, SEG, D), [pltpu.VMEM((SEG, D), F32)], [VM] * 4
    )(inputs, after(ctx, np_own), wqo, lo_ret)
    input_grad = call(
        finish_kernel, shape(1, SEG, D), [pltpu.VMEM((SEG, D), F32)], [VM] * 5
    )(inputs, gain, cot, after(np_own, layer_out), np_ret)
    return (layer_out, input_grad)


def from_behind(block, axis, distance):
    devices = range(lax.axis_size(axis))
    route = [(i - distance, i) for i in devices if i - distance in devices]
    return lax.ppermute(block, axis, route)


def normalize_project(
    inputs, norm_gain, query_weight, key_weight, value_weight, content_bias, position_bias
):
    widened = inputs.astype(jnp.float32)
    center = jnp.mean(widened, axis=-1, keepdims=True)
    spread = jnp.mean(jnp.square(widened - center), axis=-1, keepdims=True)
    normed = ((widened - center) * lax.rsqrt(spread + epsilon) * norm_gain).astype(jnp.bfloat16)
    projected = jnp.dot(normed, query_weight, preferred_element_type=jnp.float32)
    content_query = (projected + content_bias).astype(jnp.bfloat16)
    position_query = (projected + position_bias).astype(jnp.bfloat16)
    key_rows = jnp.dot(normed, key_weight, preferred_element_type=jnp.float32).astype(jnp.bfloat16)
    value_rows = jnp.dot(normed, value_weight, preferred_element_type=jnp.float32).astype(
        jnp.bfloat16
    )
    return (content_query, position_query, key_rows, value_rows)


def attend(
    content_query,
    position_query,
    key_rows,
    value_rows,
    memory_keys,
    memory_values,
    position_keys,
    keep_memory,
):
    length = content_query.shape[0]
    all_keys = jnp.concatenate([memory_keys, key_rows], axis=0).reshape(2 * length, H, DH)
    all_values = jnp.concatenate([memory_values, value_rows], axis=0).reshape(2 * length, H, DH)
    content = content_query.reshape(length, H, DH)
    located = position_query.reshape(length, H, DH)
    distance_keys = position_keys[::-1].reshape(2 * length, H, DH)
    direct = jnp.einsum("ihd,jhd->hij", content, all_keys, preferred_element_type=jnp.float32)
    relative = jnp.einsum(
        "ihd,jhd->hij", located, distance_keys, preferred_element_type=jnp.float32
    )
    padded = jnp.pad(relative, ((0, 0), (0, 0), (0, 1)))
    skewed = padded.reshape(H, length * (2 * length + 1))[
        :, length - 1 : length - 1 + 2 * length * length
    ]
    skewed = skewed.reshape(H, length, 2 * length)
    scores = (direct + skewed) * DH ** (-0.5)
    key_index = lax.broadcasted_iota(jnp.int32, (length, 2 * length), 1)
    query_index = lax.broadcasted_iota(jnp.int32, (length, 2 * length), 0)
    allowed = (key_index <= query_index + length) & (keep_memory | (key_index >= length))
    scores = jnp.where(allowed[None], scores, -jnp.inf)
    row_peak = lax.stop_gradient(jnp.max(scores, axis=-1, keepdims=True))
    raised = jnp.exp(scores - row_peak)
    attention = (raised / jnp.sum(raised, axis=-1, keepdims=True)).astype(jnp.bfloat16)
    gathered = jnp.einsum("hij,jhd->ihd", attention, all_values, preferred_element_type=jnp.float32)
    return gathered.reshape(length, H * DH).astype(jnp.bfloat16)


def finish(inputs, context, output_weight):
    update = lax.dot_general(
        context,
        output_weight,
        (((context.ndim - 1,), (1,)), ((), ())),
        preferred_element_type=jnp.float32,
    )
    return (inputs.astype(jnp.float32) + update).astype(jnp.bfloat16)


def shards(
    inputs,
    norm_gain,
    query_weight,
    key_weight,
    value_weight,
    output_weight,
    content_bias,
    position_bias,
    position_keys,
    start_flags,
    cotangent,
):
    partial_weights = (
        lax.all_gather(query_weight, "grp", axis=1, tiled=True),
        lax.all_gather(key_weight, "grp", axis=1, tiled=True),
        lax.all_gather(value_weight, "grp", axis=1, tiled=True),
        lax.all_gather(output_weight, "grp", axis=1, tiled=True),
    )
    full_weights = (
        lax.all_gather(partial_weights[0], "tm", axis=0, tiled=True),
        lax.all_gather(partial_weights[1], "tm", axis=0, tiled=True),
        lax.all_gather(partial_weights[2], "tm", axis=0, tiled=True),
        lax.all_gather(partial_weights[3], "tm", axis=0, tiled=True),
    )
    query_full, key_full, value_full, output_full = full_weights
    own_inputs = inputs[0]
    own_cotangent = cotangent[0]
    keep_memory = start_flags[0, 0] == 0

    def project(local_inputs):
        return normalize_project(
            local_inputs, norm_gain, query_full, key_full, value_full, content_bias, position_bias
        )

    projections, project_back = jax.vjp(project, own_inputs)
    content_query, position_query, key_rows, value_rows = projections
    memory_keys, memory_values = from_behind((key_rows, value_rows), "tm", 1)

    def attend_local(
        local_content, local_position, local_keys, local_values, prior_keys, prior_values
    ):
        return attend(
            local_content,
            local_position,
            local_keys,
            local_values,
            prior_keys,
            prior_values,
            position_keys,
            keep_memory,
        )

    context, attend_back = jax.vjp(
        attend_local,
        content_query,
        position_query,
        key_rows,
        value_rows,
        memory_keys,
        memory_values,
    )

    def combine(local_inputs, local_context):
        return finish(local_inputs, local_context, output_full)

    layer_out, finish_back = jax.vjp(combine, own_inputs, context)
    residual_grad, context_grad = finish_back(own_cotangent)
    attend_grads = attend_back(context_grad)
    returned_keys, returned_values = from_behind((attend_grads[4], attend_grads[5]), "tm", -1)
    key_grad = attend_grads[2] + returned_keys
    value_grad = attend_grads[3] + returned_values
    (norm_grad,) = project_back((attend_grads[0], attend_grads[1], key_grad, value_grad))
    input_grad = residual_grad + norm_grad
    return (layer_out[None], input_grad[None])


def solution(mesh):
    in_specs = (
        P("grp", "tm", None),
        P(),
        P("tm", "grp"),
        P("tm", "grp"),
        P("tm", "grp"),
        P("tm", "grp"),
        P(),
        P(),
        P(),
        P("grp", "tm"),
        P("grp", "tm", None),
    )
    out_specs = (P("grp", "tm", None), P("grp", "tm", None))
    split = dict(mesh.shape) == {"grp": 2, "tm": 4 * ZS}
    body = split_heads if split else shards
    return jax.shard_map(body, mesh=mesh, in_specs=in_specs, out_specs=out_specs, check_vma=False)
```

time: 88.9 us -> 73.8 us (0.83)
  the two profiles are of different devices: /device:TPU:0 before, /device:TPU:21 now
where the time goes in v3:
time: 73.8 us; the launch traced here: 72.4 us
  starting transfers between devices  35.5 us (48%)
  Pallas kernels  17.8 us (24%)
  waiting for transfers between devices  15.5 us (21%)
  local copies, waits for them, and re-layouts  2.03 us (3%)
  between operations  1.53 us (2%)
    ppermute x17, starting transfers between devices, moved_by(): return lambda block: lax.ppermute(block, 'tm', route)  19.2 us
    ppermute x17, waiting for transfers between devices, moved_by(): return lambda block: lax.ppermute(block, 'tm', route)  10.1 us
    ppermute x1, starting transfers between devices, split_heads(): mem_oth = lax.ppermute(kv_oth, 'tm', onward)  4.74 us
    ppermute x4, starting transfers between devices, other(): return lax.ppermute(block, 'grp', [(0, 1), (1, 0)])  4.32 us
    ppermute x1, waiting for transfers between devices, split_heads(): ret = lax.ppermute(dmem, 'tm', back)  4.03 us
    pallas_call x2, Pallas kernels, grads(): call(functools.partial(grad_kernel, rec), shape(SEG, D, dtype=F32), [pltp...  3.82 us
    ppermute x1, starting transfers between devices, split_heads(): mem = lax.ppermute(kv, 'tm', onward)  3.43 us
    pallas_call x2, Pallas kernels, memory(): call(functools.partial(memory_kernel, rec), (shape(HEADS, SEG, SEG), shap...  2.64 us
  transfers between devices with their start and end apart: 25, of which 8 were waited for; matrix products, arithmetic and copies ran while one was open for 0% of the time, Pallas kernels for 17%

profile of v3, /device:TPU:21, one launch (start us, length us, event | category | flops | bytes accessed | tf_op | source)
XLA Modules:
  0.0 72.4 jit_solution(7211953732415952021)
XLA Ops:
  1.3 2.4 %shard_map.122 = (bf16[4,96,384]{2,1,0:T(8,128)(2,1)}, bf16[144,1536]{1,0:T(8,128)(2,1)}, bf16[256,384]{1,0:T(8,128)(2,1)}) custom-call(bf16[96,384]{1,0:T(8,128)(2,1)} %k_ref.1, bf16[96,384]{1,0:T(8,128)(2,1)} %v_ref.1, bf16[96,384]{1,0:T(8,128)(2,1)} %q_ref.1, bf16[96,384]{1,0:T(8,128)(2,1)} %o_ref.1, bf16[1,128,1536]{2,1,0:T(8,128)(2,1)} %x_ref.5, ...), custom_call_target="tpu_custom_call" | custom-call | bytes 1024 | tf_op jit(solution)/shard_map/pallas_call | solution.py:317
  3.7 1.4 %collective-permute-start = (bf16[4,96,384]{2,1,0:T(8,128)(2,1)}, bf16[4,96,384]{2,1,0:T(8,128)(2,1)S(1)}, u32[]{:S(2)}, u32[]{:S(2)}) collective-permute-start(bf16[4,96,384]{2,1,0:T(8,128)(2,1)} %get-tuple-element.36.shard_ref), channel_id=1, source_target_pairs={{0,4},{1,5},{2,6},{3,7},{4,8},{5,9},{6,10},{7,11},{8,12},{9,13},{1... | collective-permute-start | bytes 884744 | tf_op jit(solution)/shard_map/ppermute | solution.py:285
  10.0 2.0 %collective-permute-done.rest_4_ = bf16[4,96,384]{2,1,0:T(8,128)(2,1)S(1)} collective-permute-done((bf16[4,96,384]{2,1,0:T(8,128)(2,1)}, bf16[4,96,384]{2,1,0:T(8,128)(2,1)S(1)}, u32[]{:S(2)}, u32[]{:S(2)}) %collective-permute-start) | collective-permute-done | bytes 294944 | tf_op jit(solution)/shard_map/ppermute | solution.py:285
  12.1 1.3 %collective-permute-start.1 = (bf16[4,96,384]{2,1,0:T(8,128)(2,1)S(1)}, bf16[4,96,384]{2,1,0:T(8,128)(2,1)S(1)}, u32[]{:S(2)}, u32[]{:S(2)}) collective-permute-start(bf16[4,96,384]{2,1,0:T(8,128)(2,1)S(1)} %collective-permute-done.rest_4_), channel_id=1, source_target_pairs={{0,4},{1,5},{2,6},{3,7},{4,8},{5,9},{6,10},{7,11},{8,12},{9,13},{1... | collective-permute-start | bytes 884744 | tf_op jit(solution)/shard_map/ppermute | solution.py:285
  13.4 3.0 %collective-permute-done.6.rest_1_ = bf16[4,96,384]{2,1,0:T(8,128)(2,1)S(1)} collective-permute-done((bf16[4,96,384]{2,1,0:T(8,128)(2,1)}, bf16[4,96,384]{2,1,0:T(8,128)(2,1)S(1)}, u32[]{:S(2)}, u32[]{:S(2)}) %collective-permute-start.6) | collective-permute-done | bytes 294944 | tf_op jit(solution)/shard_map/ppermute | solution.py:285
  16.6 2.0 %collective-permute-done.2.rest_12_ = bf16[4,96,384]{2,1,0:T(8,128)(2,1)S(1)} collective-permute-done((bf16[4,96,384]{2,1,0:T(8,128)(2,1)}, bf16[4,96,384]{2,1,0:T(8,128)(2,1)S(1)}, u32[]{:S(2)}, u32[]{:S(2)}) %collective-permute-start.2) | collective-permute-done | bytes 294944 | tf_op jit(solution)/shard_map/ppermute | solution.py:285
  18.7 3.7 %collective-permute-start.8 = (bf16[4,96,384]{2,1,0:T(8,128)(2,1)S(1)}, bf16[4,96,384]{2,1,0:T(8,128)(2,1)S(1)}, u32[]{:S(2)}, u32[]{:S(2)}) collective-permute-start(bf16[4,96,384]{2,1,0:T(8,128)(2,1)S(1)} %collective-permute-done.6.rest_1_), channel_id=1, source_target_pairs={{0,1},{1,0},{2,3},{3,2},{4,5},{5,4},{6,7},{7,6},{8,9},{9,8},{10,11... | collective-permute-start | bytes 884744 | tf_op jit(solution)/shard_map/ppermute | solution.py:285
  23.8 5.4 %collective-permute-start.10 = (bf16[4,96,384]{2,1,0:T(8,128)(2,1)S(1)}, bf16[4,96,384]{2,1,0:T(8,128)(2,1)S(1)}, u32[]{:S(2)}, u32[]{:S(2)}) collective-permute-start(bf16[4,96,384]{2,1,0:T(8,128)(2,1)S(1)} %collective-permute-done.rest_4_), channel_id=1, source_target_pairs={{0,1},{1,0},{2,3},{3,2},{4,5},{5,4},{6,7},{7,6},{8,9},{9,8},{10,11... | collective-permute-start | bytes 884744 | tf_op jit(solution)/shard_map/ppermute | solution.py:285
  30.4 1.6 %collective-permute-start.17 = (bf16[4,96,384]{2,1,0:T(8,128)(2,1)S(1)}, bf16[4,96,384]{2,1,0:T(8,128)(2,1)S(1)}, u32[]{:S(2)}, u32[]{:S(2)}) collective-permute-start(bf16[4,96,384]{2,1,0:T(8,128)(2,1)S(1)} %collective-permute-done.15.rest_13_), channel_id=1, source_target_pairs={{0,1},{1,0},{2,3},{3,2},{4,5},{5,4},{6,7},{7,6},{8,9},{9,8},{10,11... | collective-permute-start | bytes 884744 | tf_op jit(solution)/shard_map/ppermute | solution.py:285
  32.6 2.1 %collective-permute-done.3.rest_9_ = bf16[2,96,384]{2,1,0:T(8,128)(2,1)S(1)} collective-permute-done((bf16[2,96,384]{2,1,0:T(8,128)(2,1)S(1)}, bf16[2,96,384]{2,1,0:T(8,128)(2,1)S(1)}, u32[]{:S(2)}, u32[]{:S(2)}) %collective-permute-start.3) | collective-permute-done | bytes 147488 | tf_op jit(solution)/shard_map/ppermute | solution.py:285
  36.6 1.6 %shard_map.124 = (bf16[1536,768]{1,0:T(8,128)(2,1)S(1)}, bf16[128,768]{1,0:T(8,128)(2,1)S(1)}, bf16[128,768]{1,0:T(8,128)(2,1)S(1)}, bf16[256,1536]{1,0:T(8,128)(2,1)S(1)}, bf16[2,16,128]{2,1,0:T(8,128)(2,1)S(1)}) custom-call(bf16[144,1536]{1,0:T(8,128)(2,1)S(1)} %get-tuple-element.43.own_ref, bf16[144,1536]{1,0:T(8,128)(2,1)S(1)} %collective-permute-done.5.oth_ref, ...), custom_call_target="tpu_custom_call" | custom-call | bytes 1024 | tf_op jit(solution)/shard_map/pallas_call | solution.py:357
  38.2 4.7 %collective-permute-start.20 = (bf16[128,768]{1,0:T(8,128)(2,1)S(1)}, bf16[128,768]{1,0:T(8,128)(2,1)S(1)}, u32[]{:S(2)}, u32[]{:S(2)}) collective-permute-start(bf16[128,768]{1,0:T(8,128)(2,1)S(1)} %get-tuple-element.48.kv_oth.kv_ref), channel_id=1, source_target_pairs={{0,1},{1,2},{2,3},{3,4},{4,5},{5,6},{6,7},{7,8},{8,9},{9,10},{10,1... | collective-permute-start | bytes 589832 | tf_op jit(solution)/shard_map/ppermute | solution.py:372
  43.0 3.4 %collective-permute-start.19 = (bf16[128,768]{1,0:T(8,128)(2,1)S(1)}, bf16[128,768]{1,0:T(8,128)(2,1)S(1)}, u32[]{:S(2)}, u32[]{:S(2)}) collective-permute-start(bf16[128,768]{1,0:T(8,128)(2,1)S(1)} %get-tuple-element.47.kv_own.kv_ref), channel_id=1, source_target_pairs={{0,1},{1,2},{2,3},{3,4},{4,5},{5,6},{6,7},{7,8},{8,9},{9,10},{10,1... | collective-permute-start | bytes 589832 | tf_op jit(solution)/shard_map/ppermute | solution.py:373
  46.5 2.3 %shard_map.125 = (bf16[1536,768]{1,0:T(8,128)(2,1)S(1)}, bf16[2,128,384]{2,1,0:T(8,128)(2,1)S(1)}, bf16[2,128,384]{2,1,0:T(8,128)(2,1)S(1)}, f32[2,3,128,128]{3,...) custom-call(bf16[256,1536]{1,0:T(8,128)(2,1)S(1)} %get-tuple-element.46.xs, ...), custom_call_target="tpu_custom_call" | custom-call | bytes 1024 | tf_op jit(solution)/shard_map/pallas_call | solution.py:375
  48.8 1.3 %shard_map.126 = (bf16[3,128,128]{2,1,0:T(8,128)(2,1)S(1)}, bf16[3,128,256]{2,1,0:T(8,128)(2,1)S(1)}, bf16[128,768]{1,0:T(8,128)(2,1)S(1)}, bf16[128,384]{1,0:T(8,128)(2,1)S(1)}) custom-call(bf16[2,16,128]{2,1,0:T(8,128)(2,1)S(1)} %get-tuple-element.45.flags, bf16[2,128,384]{2,1,0:T(8,128)(2,1)S(1)} %get-tuple-element.50.cq_ref, ...), custom_call_target="tpu_custom_call" | custom-call | bytes 1024 | tf_op jit(solution)/shard_map/pallas_call | solution.py:386
  50.1 1.9 %collective-permute-start.21 = (bf16[128,768]{1,0:T(8,128)(2,1)S(1)}, bf16[128,768]{1,0:T(8,128)(2,1)S(1)}, u32[]{:S(2)}, u32[]{:S(2)}) collective-permute-start(bf16[128,768]{1,0:T(8,128)(2,1)S(1)} %get-tuple-element.65), channel_id=1, source_target_pairs={{1,0},{2,1},{3,2},{4,3},{5,4},{6,5},{7,6},{8,7},{9,8},{10,9},{11,1... | collective-permute-start | bytes 589832 | tf_op jit(solution)/shard_map/ppermute | solution.py:402
  52.6 1.4 %collective-permute-start.23 = (bf16[128,1536]{1,0:T(8,128)(2,1)S(1)}, bf16[128,1536]{1,0:T(8,128)(2,1)S(1)}, u32[]{:S(2)}, u32[]{:S(2)}) collective-permute-start(bf16[128,1536]{1,0:T(8,128)(2,1)S(1)} %shard_map.127), channel_id=1, source_target_pairs={{0,16},{16,0},{1,17},{17,1},{2,18},{18,2},{3,19},{19,3},{4,20},{20... | collective-permute-start | bytes 1179656 | tf_op jit(solution)/shard_map/ppermute | solution.py:299
  54.0 1.3 %shard_map.128 = (bf16[3,128,128]{2,1,0:T(8,128)(2,1)S(1)}, bf16[3,128,256]{2,1,0:T(8,128)(2,1)S(1)}, bf16[128,768]{1,0:T(8,128)(2,1)S(1)}, bf16[128,384]{1,0:T(8,128)(2,1)S(1)}) custom-call(bf16[2,16,128]{2,1,0:T(8,128)(2,1)S(1)} %get-tuple-element.45.flags, bf16[2,128,384]{2,1,0:T(8,128)(2,1)S(1)} %get-tuple-element.50.cq_ref, ...), custom_call_target="tpu_custom_call" | custom-call | bytes 1024 | tf_op jit(solution)/shard_map/pallas_call | solution.py:386
  55.3 1.9 %shard_map.129.np_ref = f32[128,1536]{1,0:T(8,128)S(1)} custom-call(bf16[3,128,128]{2,1,0:T(8,128)(2,1)S(1)} %get-tuple-element.62.p_ref, bf16[3,128,256]{2,1,0:T(8,128)(2,1)S(1)} %get-tuple-element.63.ds_ref, bf16[2,128,384]{2,1,0:T(8,128)(2,1)S(1)} %get-tuple-element.50.cq_ref, bf16[2,128,384]{2,1,0:T(8,128)(2,1)S(1)} %get-tuple-element.51.cg_ref, ...), custom_call_target="tpu_custom_call" | custom-call | bytes 1024 | tf_op jit(solution)/shard_map/pallas_call | solution.py:394
  58.9 1.4 %collective-permute-start.24 = (bf16[128,1536]{1,0:T(8,128)(2,1)S(1)}, bf16[128,1536]{1,0:T(8,128)(2,1)S(1)}, u32[]{:S(2)}, u32[]{:S(2)}) collective-permute-start(bf16[128,1536]{1,0:T(8,128)(2,1)S(1)} %shard_map.130), channel_id=1, source_target_pairs={{0,16},{16,0},{1,17},{17,1},{2,18},{18,2},{3,19},{19,3},{4,20},{20... | collective-permute-start | bytes 1179656 | tf_op jit(solution)/shard_map/ppermute | solution.py:299
  60.3 1.9 %collective-permute-start.22 = (bf16[128,768]{1,0:T(8,128)(2,1)S(1)}, bf16[128,768]{1,0:T(8,128)(2,1)S(1)}, u32[]{:S(2)}, u32[]{:S(2)}) collective-permute-start(bf16[128,768]{1,0:T(8,128)(2,1)S(1)} %get-tuple-element.61), channel_id=1, source_target_pairs={{1,0},{2,1},{3,2},{4,3},{5,4},{6,5},{7,6},{8,7},{9,8},{10,9},{11,1... | collective-permute-start | bytes 589832 | tf_op jit(solution)/shard_map/ppermute | solution.py:406
  62.2 1.9 %shard_map.131.np_ref = f32[128,1536]{1,0:T(8,128)S(1)} custom-call(bf16[3,128,128]{2,1,0:T(8,128)(2,1)S(1)} %get-tuple-element.66.p_ref, bf16[3,128,256]{2,1,0:T(8,128)(2,1)S(1)} %get-tuple-element.67.ds_ref, bf16[2,128,384]{2,1,0:T(8,128)(2,1)S(1)} %get-tuple-element.50.cq_ref, bf16[2,128,384]{2,1,0:T(8,128)(2,1)S(1)} %get-tuple-element.51.cg_ref, ...), custom_call_target="tpu_custom_call" | custom-call | bytes 1024 | tf_op jit(solution)/shard_map/pallas_call | solution.py:394
  64.2 4.0 %collective-permute-done.22.ret_ref = bf16[128,768]{1,0:T(8,128)(2,1)S(1)} collective-permute-done((bf16[128,768]{1,0:T(8,128)(2,1)S(1)}, bf16[128,768]{1,0:T(8,128)(2,1)S(1)}, u32[]{:S(2)}, u32[]{:S(2)}) %collective-permute-start.22) | collective-permute-done | bytes 196640 | tf_op jit(solution)/shard_map/ppermute | solution.py:406
  71.0 1.4 %shard_map.134 = bf16[1,128,1536]{2,1,0:T(8,128)(2,1)} custom-call(bf16[1,128,1536]{2,1,0:T(8,128)(2,1)S(1)} %copy-done, f32[12,128]{1,0:T(8,128)S(1)} %bitcast.8, bf16[128,1536]{1,0:T(8,128)(2,1)S(1)} %bitcast.6, f32[128,1536]{1,0:T(8,128)S(1)} %shard_map.132.np_own, bf16[128,1536]{1,0:T(8,128)(2,1)S(1)} %collective-permute-done.24.np_ret), custom_call_target="tpu_custom_call" | custom-call | bytes 1024 | tf_op jit(solution)/shard_map/pallas_call | solution.py:415
  (57 shorter events, 15.3 us)
Async XLA Ops:
  3.7 8.2 %collective-permute-start = (bf16[4,96,384]{2,1,0:T(8,128)(2,1)}, bf16[4,96,384]{2,1,0:T(8,128)(2,1)S(1)}, u32[]{:S(2)}, u32[]{:S(2)}) collective-permute-start(bf16[4,96,384]{2,1,0:T(8,128)(2,1)} %get-tuple-element.36.shard_ref), channel_id=1, source_target_pairs={{0,4},{1,5},{2,6},{3,7},{4,8},{5,9},{6,10},{7,11},{8,12},{9,13},{1... | collective-permute-start | bytes 884744 | tf_op jit(solution)/shard_map/ppermute | solution.py:285
  5.1 17.3 %collective-permute-start.5 = (bf16[144,1536]{1,0:T(8,128)(2,1)}, bf16[144,1536]{1,0:T(8,128)(2,1)S(1)}, u32[]{:S(2)}, u32[]{:S(2)}) collective-permute-start(bf16[144,1536]{1,0:T(8,128)(2,1)} %get-tuple-element.37.normed_ref), channel_id=1, source_target_pairs={{0,16},{16,0},{1,17},{17,1},{2,18},{18,2},{3,19},{19,3},{4,20},{20... | collective-permute-start | bytes 1327112 | tf_op jit(solution)/shard_map/ppermute | solution.py:299
  6.3 5.8 %collective-permute-start.7 = (bf16[4,96,384]{2,1,0:T(8,128)(2,1)}, bf16[4,96,384]{2,1,0:T(8,128)(2,1)S(1)}, u32[]{:S(2)}, u32[]{:S(2)}) collective-permute-start(bf16[4,96,384]{2,1,0:T(8,128)(2,1)} %get-tuple-element.36.shard_ref), channel_id=1, source_target_pairs={{0,1},{1,0},{2,3},{3,2},{4,5},{5,4},{6,7},{7,6},{8,9},{9,8},{10,11... | collective-permute-start | bytes 884744 | tf_op jit(solution)/shard_map/ppermute | solution.py:285
  7.5 8.8 %collective-permute-start.6 = (bf16[4,96,384]{2,1,0:T(8,128)(2,1)}, bf16[4,96,384]{2,1,0:T(8,128)(2,1)S(1)}, u32[]{:S(2)}, u32[]{:S(2)}) collective-permute-start(bf16[4,96,384]{2,1,0:T(8,128)(2,1)} %get-tuple-element.36.shard_ref), channel_id=1, source_target_pairs={{0,2},{1,3},{2,0},{3,1},{4,6},{5,7},{6,4},{7,5},{8,10},{9,11},{10,... | collective-permute-start | bytes 884744 | tf_op jit(solution)/shard_map/ppermute | solution.py:285
  7.8 10.9 %collective-permute-start.2 = (bf16[4,96,384]{2,1,0:T(8,128)(2,1)}, bf16[4,96,384]{2,1,0:T(8,128)(2,1)S(1)}, u32[]{:S(2)}, u32[]{:S(2)}) collective-permute-start(bf16[4,96,384]{2,1,0:T(8,128)(2,1)} %get-tuple-element.36.shard_ref), channel_id=1, source_target_pairs={{0,12},{1,13},{2,14},{3,15},{4,0},{5,1},{6,2},{7,3},{8,4},{9,5},{1... | collective-permute-start | bytes 884744 | tf_op jit(solution)/shard_map/ppermute | solution.py:285
  12.0 10.5 %collective-permute-start.9 = (bf16[4,96,384]{2,1,0:T(8,128)(2,1)S(1)}, bf16[4,96,384]{2,1,0:T(8,128)(2,1)S(1)}, u32[]{:S(2)}, u32[]{:S(2)}) collective-permute-start(bf16[4,96,384]{2,1,0:T(8,128)(2,1)S(1)} %collective-permute-done.rest_4_), channel_id=1, source_target_pairs={{0,2},{1,3},{2,0},{3,1},{4,6},{5,7},{6,4},{7,5},{8,10},{9,11},{10,... | collective-permute-start | bytes 884744 | tf_op jit(solution)/shard_map/ppermute | solution.py:285
  12.1 11.6 %collective-permute-start.1 = (bf16[4,96,384]{2,1,0:T(8,128)(2,1)S(1)}, bf16[4,96,384]{2,1,0:T(8,128)(2,1)S(1)}, u32[]{:S(2)}, u32[]{:S(2)}) collective-permute-start(bf16[4,96,384]{2,1,0:T(8,128)(2,1)S(1)} %collective-permute-done.rest_4_), channel_id=1, source_target_pairs={{0,4},{1,5},{2,6},{3,7},{4,8},{5,9},{6,10},{7,11},{8,12},{9,13},{1... | collective-permute-start | bytes 884744 | tf_op jit(solution)/shard_map/ppermute | solution.py:285
  16.4 15.7 %collective-permute-start.4 = (bf16[128,1536]{1,0:T(8,128)(2,1)}, bf16[128,1536]{1,0:T(8,128)(2,1)S(1)}, u32[]{:S(2)}, u32[]{:S(2)}) collective-permute-start(bf16[128,1536]{1,0:T(8,128)(2,1)} %bitcast.4), channel_id=1, source_target_pairs={{0,16},{16,0},{1,17},{17,1},{2,18},{18,2},{3,19},{19,3},{4,20},{20... | collective-permute-start | bytes 1179656 | tf_op jit(solution)/shard_map/ppermute | solution.py:299
  18.7 5.2 %collective-permute-start.8 = (bf16[4,96,384]{2,1,0:T(8,128)(2,1)S(1)}, bf16[4,96,384]{2,1,0:T(8,128)(2,1)S(1)}, u32[]{:S(2)}, u32[]{:S(2)}) collective-permute-start(bf16[4,96,384]{2,1,0:T(8,128)(2,1)S(1)} %collective-permute-done.6.rest_1_), channel_id=1, source_target_pairs={{0,1},{1,0},{2,3},{3,2},{4,5},{5,4},{6,7},{7,6},{8,9},{9,8},{10,11... | collective-permute-start | bytes 884744 | tf_op jit(solution)/shard_map/ppermute | solution.py:285
  22.4 6.9 %collective-permute-start.16 = (bf16[4,96,384]{2,1,0:T(8,128)(2,1)S(1)}, bf16[4,96,384]{2,1,0:T(8,128)(2,1)S(1)}, u32[]{:S(2)}, u32[]{:S(2)}) collective-permute-start(bf16[4,96,384]{2,1,0:T(8,128)(2,1)S(1)} %collective-permute-done.2.rest_12_), channel_id=1, source_target_pairs={{0,1},{1,0},{2,3},{3,2},{4,5},{5,4},{6,7},{7,6},{8,9},{9,8},{10,11... | collective-permute-start | bytes 884744 | tf_op jit(solution)/shard_map/ppermute | solution.py:285
  22.5 8.0 %collective-permute-start.15 = (bf16[4,96,384]{2,1,0:T(8,128)(2,1)S(1)}, bf16[4,96,384]{2,1,0:T(8,128)(2,1)S(1)}, u32[]{:S(2)}, u32[]{:S(2)}) collective-permute-start(bf16[4,96,384]{2,1,0:T(8,128)(2,1)S(1)} %collective-permute-done.2.rest_12_), channel_id=1, source_target_pairs={{0,2},{1,3},{2,0},{3,1},{4,6},{5,7},{6,4},{7,5},{8,10},{9,11},{10,... | collective-permute-start | bytes 884744 | tf_op jit(solution)/shard_map/ppermute | solution.py:285
  23.7 8.4 %collective-permute-start.12 = (bf16[2,96,384]{2,1,0:T(8,128)(2,1)S(1)}, bf16[2,96,384]{2,1,0:T(8,128)(2,1)S(1)}, u32[]{:S(2)}, u32[]{:S(2)}) collective-permute-start(bf16[2,96,384]{2,1,0:T(8,128)(2,1)S(1)} %slice.7), channel_id=1, source_target_pairs={{0,4},{1,5},{2,6},{3,7},{4,8},{5,9},{6,10},{7,11},{8,12},{9,13},{1... | collective-permute-start | bytes 442376 | tf_op jit(solution)/shard_map/ppermute | solution.py:285
  23.8 11.7 %collective-permute-start.10 = (bf16[4,96,384]{2,1,0:T(8,128)(2,1)S(1)}, bf16[4,96,384]{2,1,0:T(8,128)(2,1)S(1)}, u32[]{:S(2)}, u32[]{:S(2)}) collective-permute-start(bf16[4,96,384]{2,1,0:T(8,128)(2,1)S(1)} %collective-permute-done.rest_4_), channel_id=1, source_target_pairs={{0,1},{1,0},{2,3},{3,2},{4,5},{5,4},{6,7},{7,6},{8,9},{9,8},{10,11... | collective-permute-start | bytes 884744 | tf_op jit(solution)/shard_map/ppermute | solution.py:285
  29.3 5.4 %collective-permute-start.3 = (bf16[2,96,384]{2,1,0:T(8,128)(2,1)S(1)}, bf16[2,96,384]{2,1,0:T(8,128)(2,1)S(1)}, u32[]{:S(2)}, u32[]{:S(2)}) collective-permute-start(bf16[2,96,384]{2,1,0:T(8,128)(2,1)S(1)} %slice.6), channel_id=1, source_target_pairs={{0,2},{1,3},{2,0},{3,1},{4,6},{5,7},{6,4},{7,5},{8,10},{9,11},{10,... | collective-permute-start | bytes 442376 | tf_op jit(solution)/shard_map/ppermute | solution.py:285
  30.4 5.1 %collective-permute-start.17 = (bf16[4,96,384]{2,1,0:T(8,128)(2,1)S(1)}, bf16[4,96,384]{2,1,0:T(8,128)(2,1)S(1)}, u32[]{:S(2)}, u32[]{:S(2)}) collective-permute-start(bf16[4,96,384]{2,1,0:T(8,128)(2,1)S(1)} %collective-permute-done.15.rest_13_), channel_id=1, source_target_pairs={{0,1},{1,0},{2,3},{3,2},{4,5},{5,4},{6,7},{7,6},{8,9},{9,8},{10,11... | collective-permute-start | bytes 884744 | tf_op jit(solution)/shard_map/ppermute | solution.py:285
  32.1 4.5 %collective-permute-start.11 = (bf16[4,96,384]{2,1,0:T(8,128)(2,1)S(1)}, bf16[4,96,384]{2,1,0:T(8,128)(2,1)S(1)}, u32[]{:S(2)}, u32[]{:S(2)}) collective-permute-start(bf16[4,96,384]{2,1,0:T(8,128)(2,1)S(1)} %collective-permute-done.9.rest_5_), channel_id=1, source_target_pairs={{0,1},{1,0},{2,3},{3,2},{4,5},{5,4},{6,7},{7,6},{8,9},{9,8},{10,11... | collective-permute-start | bytes 884744 | tf_op jit(solution)/shard_map/ppermute | solution.py:285
  32.1 4.5 %collective-permute-start.13 = (bf16[4,96,384]{2,1,0:T(8,128)(2,1)S(1)}, bf16[4,96,384]{2,1,0:T(8,128)(2,1)S(1)}, u32[]{:S(2)}, u32[]{:S(2)}) collective-permute-start(bf16[4,96,384]{2,1,0:T(8,128)(2,1)S(1)} %collective-permute-done.1.rest_8_), channel_id=1, source_target_pairs={{0,1},{1,0},{2,3},{3,2},{4,5},{5,4},{6,7},{7,6},{8,9},{9,8},{10,11... | collective-permute-start | bytes 884744 | tf_op jit(solution)/shard_map/ppermute | solution.py:285
  38.2 10.6 %collective-permute-start.20 = (bf16[128,768]{1,0:T(8,128)(2,1)S(1)}, bf16[128,768]{1,0:T(8,128)(2,1)S(1)}, u32[]{:S(2)}, u32[]{:S(2)}) collective-permute-start(bf16[128,768]{1,0:T(8,128)(2,1)S(1)} %get-tuple-element.48.kv_oth.kv_ref), channel_id=1, source_target_pairs={{0,1},{1,2},{2,3},{3,4},{4,5},{5,6},{6,7},{7,8},{8,9},{9,10},{10,1... | collective-permute-start | bytes 589832 | tf_op jit(solution)/shard_map/ppermute | solution.py:372
  42.9 3.5 %collective-permute-start.18 = (bf16[2,96,384]{2,1,0:T(8,128)(2,1)S(1)}, bf16[2,96,384]{2,1,0:T(8,128)(2,1)S(1)}, u32[]{:S(2)}, u32[]{:S(2)}) collective-permute-start(bf16[2,96,384]{2,1,0:T(8,128)(2,1)S(1)} %collective-permute-done.3.rest_9_), channel_id=1, source_target_pairs={{0,1},{1,0},{2,3},{3,2},{4,5},{5,4},{6,7},{7,6},{8,9},{9,8},{10,11... | collective-permute-start | bytes 442376 | tf_op jit(solution)/shard_map/ppermute | solution.py:285
  43.0 11.0 %collective-permute-start.19 = (bf16[128,768]{1,0:T(8,128)(2,1)S(1)}, bf16[128,768]{1,0:T(8,128)(2,1)S(1)}, u32[]{:S(2)}, u32[]{:S(2)}) collective-permute-start(bf16[128,768]{1,0:T(8,128)(2,1)S(1)} %get-tuple-element.47.kv_own.kv_ref), channel_id=1, source_target_pairs={{0,1},{1,2},{2,3},{3,4},{4,5},{5,6},{6,7},{7,8},{8,9},{9,10},{10,1... | collective-permute-start | bytes 589832 | tf_op jit(solution)/shard_map/ppermute | solution.py:373
  50.1 7.9 %collective-permute-start.21 = (bf16[128,768]{1,0:T(8,128)(2,1)S(1)}, bf16[128,768]{1,0:T(8,128)(2,1)S(1)}, u32[]{:S(2)}, u32[]{:S(2)}) collective-permute-start(bf16[128,768]{1,0:T(8,128)(2,1)S(1)} %get-tuple-element.65), channel_id=1, source_target_pairs={{1,0},{2,1},{3,2},{4,3},{5,4},{6,5},{7,6},{8,7},{9,8},{10,9},{11,1... | collective-permute-start | bytes 589832 | tf_op jit(solution)/shard_map/ppermute | solution.py:402
  52.6 16.6 %collective-permute-start.23 = (bf16[128,1536]{1,0:T(8,128)(2,1)S(1)}, bf16[128,1536]{1,0:T(8,128)(2,1)S(1)}, u32[]{:S(2)}, u32[]{:S(2)}) collective-permute-start(bf16[128,1536]{1,0:T(8,128)(2,1)S(1)} %shard_map.127), channel_id=1, source_target_pairs={{0,16},{16,0},{1,17},{17,1},{2,18},{18,2},{3,19},{19,3},{4,20},{20... | collective-permute-start | bytes 1179656 | tf_op jit(solution)/shard_map/ppermute | solution.py:299
  58.9 12.1 %collective-permute-start.24 = (bf16[128,1536]{1,0:T(8,128)(2,1)S(1)}, bf16[128,1536]{1,0:T(8,128)(2,1)S(1)}, u32[]{:S(2)}, u32[]{:S(2)}) collective-permute-start(bf16[128,1536]{1,0:T(8,128)(2,1)S(1)} %shard_map.130), channel_id=1, source_target_pairs={{0,16},{16,0},{1,17},{17,1},{2,18},{18,2},{3,19},{19,3},{4,20},{20... | collective-permute-start | bytes 1179656 | tf_op jit(solution)/shard_map/ppermute | solution.py:299
  60.3 7.9 %collective-permute-start.22 = (bf16[128,768]{1,0:T(8,128)(2,1)S(1)}, bf16[128,768]{1,0:T(8,128)(2,1)S(1)}, u32[]{:S(2)}, u32[]{:S(2)}) collective-permute-start(bf16[128,768]{1,0:T(8,128)(2,1)S(1)} %get-tuple-element.61), channel_id=1, source_target_pairs={{1,0},{2,1},{3,2},{4,3},{5,4},{6,5},{7,6},{8,7},{9,8},{10,9},{11,1... | collective-permute-start | bytes 589832 | tf_op jit(solution)/shard_map/ppermute | solution.py:406
  (9 other events, 54.4 us)

commit v4 on v3

--- a/solution.py
+++ b/solution.py
@@ -114,15 +114,15 @@
 
 
 def key_value_kernel(own_ref, oth_ref, *rest):
-    pieces, (weights, kv_own, kv_oth, xs, flags, sems) = rest[:16], rest[16:]
+    pieces, (weights, kv_ref, xs, flags, sems) = rest[:16], rest[16:]
     copies = fetch(pieces, (0,) * 16, weights, sems)
     flags[0] = own_ref[SEG:, :DH]
     flags[1] = oth_ref[SEG:, :DH]
     xs[0:SEG, :] = own_ref[0:SEG, :]
     xs[SEG:, :] = oth_ref[0:SEG, :]
     total = accumulate(xs, weights, copies, slice(0, 2 * HALF))
-    kv_own[...] = total[:SEG].astype(BF16)
-    kv_oth[...] = total[SEG:].astype(BF16)
+    kv_ref[0] = total[:SEG].astype(BF16)
+    kv_ref[1] = total[SEG:].astype(BF16)
 
 
 SCALE = DH**-0.5
@@ -139,7 +139,7 @@
     return jnp.concatenate(parts, axis=1)
 
 
-def query_kernel(xs, cot_own, cot_oth, cb_ref, pb_ref, kv_own, kv_oth, pk_ref, *rest):
+def query_kernel(xs, cot_own, cot_oth, cb_ref, pb_ref, kv_ref, pk_ref, *rest):
     pieces = rest[:16]
     weights, cq_ref, cg_ref, rel_ref, own_ref, dp_ref = rest[16:22]
     cots, sems = rest[22:]
@@ -156,7 +156,6 @@
     col = lax.broadcasted_iota(jnp.int32, (SEG, SEG), 1)
     for rec in range(2):
         rows = slice(rec * SEG, (rec + 1) * SEG)
-        kv_ref = (kv_own, kv_oth)[rec]
         cq_ref[rec] = cq[rows]
         cg_ref[rec] = cg[rows]
         for h in range(HEADS):
@@ -164,9 +163,9 @@
             rel = dot(pq[rows, f], pk_ref[:, f], NT)
             rel = pltpu.roll(rel, SEG + 1, 1, stride=1, stride_axis=0)
             rel_ref[rec, h] = rel[:, :SEG]
-            s_own = (dot(cq[rows, f], kv_ref[:, f], NT) + rel[:, SEG:]) * SCALE
+            s_own = (dot(cq[rows, f], kv_ref[rec, :, f], NT) + rel[:, SEG:]) * SCALE
             own_ref[rec, h] = jnp.where(col <= row, s_own, -jnp.inf)
-            dp_ref[rec, h] = dot(cg[rows, f], kv_ref[:, fv], NT)
+            dp_ref[rec, h] = dot(cg[rows, f], kv_ref[rec, :, fv], NT)
 
 
 def memory_kernel(
@@ -178,9 +177,9 @@
         f, fv = head(h), head(HEADS + h)
         cq, g = cq_ref[rec, :, f], cg_ref[rec, :, f]
         s_own = own_ref[rec, h]
-        s_mem = (dot(cq, mem_ref[:, f], NT) + rel_ref[rec, h]) * SCALE
+        s_mem = (dot(cq, mem_ref[rec, :, f], NT) + rel_ref[rec, h]) * SCALE
         s_mem = jnp.where(flag == 0, s_mem, -jnp.inf)
-        dp_mem = dot(g, mem_ref[:, fv], NT)
+        dp_mem = dot(g, mem_ref[rec, :, fv], NT)
         peak = jnp.max(jnp.maximum(s_mem, s_own), axis=-1, keepdims=True)
         e_mem = jnp.exp(s_mem - peak)
         e_own = jnp.exp(s_own - peak)
@@ -189,7 +188,7 @@
         dp_own = dp_ref[rec, h]
         inner = jnp.sum(a_mem * dp_mem + a_own * dp_own, axis=-1, keepdims=True)
         p_mem, p_own = a_mem.astype(BF16), a_own.astype(BF16)
-        ctx = dot(p_mem, mem_ref[:, fv]) + dot(p_own, kv_ref[:, fv])
+        ctx = dot(p_mem, mem_ref[rec, :, fv]) + dot(p_own, kv_ref[rec, :, fv])
         ctx_ref[:, f] = ctx.astype(BF16)
         ds_mem = (a_mem * (dp_mem - inner) * SCALE).astype(BF16)
         p_ref[h] = p_own
@@ -210,7 +209,7 @@
         ds = ds_ref[h]
         rel = pltpu.roll(dot(flip, ds), 0, 1, stride=1, stride_axis=0).astype(BF16)
         rel = dot(flip, rel).astype(BF16)
-        total = dot(ds[:, :SEG], mem_ref[:, f]) + dot(ds[:, SEG:], kv_ref[:, f])
+        total = dot(ds[:, :SEG], mem_ref[rec, :, f]) + dot(ds[:, SEG:], kv_ref[rec, :, f])
         dq[:, f] = (total + dot(rel, pk_ref[:, f])).astype(BF16)
         dkv[:, f] = dot(ds[:, SEG:], cq_ref[rec, :, f], TN).astype(BF16)
         dkv[:, fv] = dot(p_ref[h], cg_ref[rec, :, f], TN).astype(BF16)
@@ -354,12 +353,11 @@
     qo_pieces[9], qo_pieces[11] = w2y_qo, w2y_qo_there
 
     half = shape(SEG, 2 * HALF)
-    wkv, kv, kv_oth, xs, flags = call(
+    wkv, kv, xs, flags = call(
         key_value_kernel,
         (
             shape(D, 2 * HALF),
-            half,
-            half,
+            shape(2, SEG, 2 * HALF),
             shape(2 * SEG, D),
             shape(2, 16, DH),
         ),
@@ -369,17 +367,16 @@
     steps = lax.axis_size("tm")
     onward = [(i, i + 1) for i in range(steps - 1)]
     back = [(i + 1, i) for i in range(steps - 1)]
-    mem_oth = lax.ppermute(kv_oth, "tm", onward)
     mem = lax.ppermute(kv, "tm", onward)
     blocks = shape(2, HEADS, SEG, SEG, dtype=F32)
     wqo, cq, cg, rel, s_own, dp_own = call(
         query_kernel,
         (shape(D, 2 * HALF), shape(2, SEG, HALF), shape(2, SEG, HALF), blocks, blocks, blocks),
         [pltpu.VMEM((2 * SEG, D), BF16), pltpu.SemaphoreType.DMA((32,))],
-        [VM] * 8 + [ANY] * 16,
+        [VM] * 7 + [ANY] * 16,
     )(
         xs, cot, cot_oth, content_bias.reshape(H, DH), position_bias.reshape(H, DH),
-        kv, kv_oth, pk, *qo_pieces,
+        kv, pk, *qo_pieces,
     )
 
     def memory(rec, kv_rows, mem_rows):
@@ -398,13 +395,13 @@
             [VM] * 9,
         )(p, ds, cq, cg, kv_rows, mem_rows, pk, wkv, wqo)
 
-    p_oth, ds_oth, dmem_oth, ctx_oth = memory(1, kv_oth, mem_oth)
-    ret_oth = lax.ppermute(dmem_oth, "tm", back)
+    p_oth, ds_oth, dmem_oth, ctx_oth = memory(1, kv, mem)
     lo_oth = call(partial_output_kernel, shape(SEG, D), (), [VM] * 2)(ctx_oth, wqo)
     lo_ret = other(lo_oth)
+    ret_oth = lax.ppermute(dmem_oth, "tm", back)
     p, ds, dmem, ctx = memory(0, kv, after(mem, lo_oth))
-    ret = lax.ppermute(dmem, "tm", back)
-    partial_oth = grads(1, after(p_oth, dmem), ds_oth, kv_oth, mem_oth)
+    ret = lax.ppermute(after(dmem, lo_ret), "tm", back)
+    partial_oth = grads(1, after(p_oth, dmem), ds_oth, kv, mem)
     np_oth = call(returned_kernel, shape(SEG, D), (), [VM] * 3)(partial_oth, ret_oth, wkv)
     np_ret = other(np_oth)
     partial = grads(0, after(p, np_oth), ds, kv, mem)

time: 73.8 us -> 72.6 us (0.984); the launches traced: 72.4 us -> 72.3 us
  waiting for transfers between devices: 15.5 us -> 19.8 us
  starting transfers between devices: 35.5 us -> 31.3 us
    ppermute x2 -> x1, starting transfers between devices: 6.65 us -> 2.1 us  [split_heads(): ret = lax.ppermute(after(dmem, lo_ret), 'tm', back)]
    ppermute x1, waiting for transfers between devices: 0.78 us -> 3.46 us  [split_heads(): ret_oth = lax.ppermute(dmem_oth, 'tm', back)]
    ppermute x17, waiting for transfers between devices: 10.1 us -> 11.5 us  [moved_by(): return lambda block: lax.ppermute(block, 'tm', route)]
    ppermute x1, starting transfers between devices: 3.43 us -> 4.74 us  [split_heads(): mem = lax.ppermute(kv, 'tm', onward)]
    ppermute x4, starting transfers between devices: 4.32 us -> 3.06 us  [other(): return lax.ppermute(block, 'grp', [(0, 1), (1, 0)])]
    ppermute x1, waiting for transfers between devices: 0.01 us -> 0.97 us  [split_heads(): mem = lax.ppermute(kv, 'tm', onward)]
    ppermute x2 -> x1, waiting for transfers between devices: 4.04 us -> 3.85 us  [split_heads(): ret = lax.ppermute(after(dmem, lo_ret), 'tm', back)]
  transfers between devices with their start and end apart: 25 -> 24, of which waited for: 8 -> 9; matrix products, arithmetic and copies ran while one was open for 0% -> 0% of each run, Pallas kernels for 17% -> 15%
where the time goes in v4:
time: 72.6 us; the launch traced here: 72.3 us
  starting transfers between devices  31.3 us (43%)
  waiting for transfers between devices  19.8 us (27%)
  Pallas kernels  17.8 us (25%)
  local copies, waits for them, and re-layouts  2.03 us (3%)
  between operations  1.48 us (2%)
    ppermute x17, starting transfers between devices, moved_by(): return lambda block: lax.ppermute(block, 'tm', route)  19.2 us
    ppermute x17, waiting for transfers between devices, moved_by(): return lambda block: lax.ppermute(block, 'tm', route)  11.5 us
    ppermute x1, starting transfers between devices, split_heads(): mem = lax.ppermute(kv, 'tm', onward)  4.74 us
    ppermute x1, waiting for transfers between devices, split_heads(): ret = lax.ppermute(after(dmem, lo_ret), 'tm', back)  3.85 us
    pallas_call x2, Pallas kernels, grads(): call(functools.partial(grad_kernel, rec), shape(SEG, D, dtype=F32), [pltp...  3.81 us
    ppermute x1, waiting for transfers between devices, split_heads(): ret_oth = lax.ppermute(dmem_oth, 'tm', back)  3.46 us
    ppermute x4, starting transfers between devices, other(): return lax.ppermute(block, 'grp', [(0, 1), (1, 0)])  3.06 us
    pallas_call x2, Pallas kernels, memory(): call(functools.partial(memory_kernel, rec), (shape(HEADS, SEG, SEG), shap...  2.64 us
  transfers between devices with their start and end apart: 24, of which 9 were waited for; matrix products, arithmetic and copies ran while one was open for 0% of the time, Pallas kernels for 15%

profile of v4, /device:TPU:21, one launch (start us, length us, event | category | flops | bytes accessed | tf_op | source)
XLA Modules:
  0.0 72.3 jit_solution(17071512841758135379)
XLA Ops:
  1.3 2.4 %shard_map.122 = (bf16[4,96,384]{2,1,0:T(8,128)(2,1)}, bf16[144,1536]{1,0:T(8,128)(2,1)}, bf16[256,384]{1,0:T(8,128)(2,1)}) custom-call(bf16[96,384]{1,0:T(8,128)(2,1)} %k_ref.1, bf16[96,384]{1,0:T(8,128)(2,1)} %v_ref.1, bf16[96,384]{1,0:T(8,128)(2,1)} %q_ref.1, bf16[96,384]{1,0:T(8,128)(2,1)} %o_ref.1, bf16[1,128,1536]{2,1,0:T(8,128)(2,1)} %x_ref.5, ...), custom_call_target="tpu_custom_call" | custom-call | bytes 1024 | tf_op jit(solution)/shard_map/pallas_call | solution.py:316
  3.7 1.4 %collective-permute-start = (bf16[4,96,384]{2,1,0:T(8,128)(2,1)}, bf16[4,96,384]{2,1,0:T(8,128)(2,1)S(1)}, u32[]{:S(2)}, u32[]{:S(2)}) collective-permute-start(bf16[4,96,384]{2,1,0:T(8,128)(2,1)} %get-tuple-element.36.shard_ref), channel_id=1, source_target_pairs={{0,4},{1,5},{2,6},{3,7},{4,8},{5,9},{6,10},{7,11},{8,12},{9,13},{1... | collective-permute-start | bytes 884744 | tf_op jit(solution)/shard_map/ppermute | solution.py:284
  10.0 2.0 %collective-permute-done.rest_4_ = bf16[4,96,384]{2,1,0:T(8,128)(2,1)S(1)} collective-permute-done((bf16[4,96,384]{2,1,0:T(8,128)(2,1)}, bf16[4,96,384]{2,1,0:T(8,128)(2,1)S(1)}, u32[]{:S(2)}, u32[]{:S(2)}) %collective-permute-start) | collective-permute-done | bytes 294944 | tf_op jit(solution)/shard_map/ppermute | solution.py:284
  12.1 1.3 %collective-permute-start.1 = (bf16[4,96,384]{2,1,0:T(8,128)(2,1)S(1)}, bf16[4,96,384]{2,1,0:T(8,128)(2,1)S(1)}, u32[]{:S(2)}, u32[]{:S(2)}) collective-permute-start(bf16[4,96,384]{2,1,0:T(8,128)(2,1)S(1)} %collective-permute-done.rest_4_), channel_id=1, source_target_pairs={{0,4},{1,5},{2,6},{3,7},{4,8},{5,9},{6,10},{7,11},{8,12},{9,13},{1... | collective-permute-start | bytes 884744 | tf_op jit(solution)/shard_map/ppermute | solution.py:284
  13.4 3.0 %collective-permute-done.6.rest_1_ = bf16[4,96,384]{2,1,0:T(8,128)(2,1)S(1)} collective-permute-done((bf16[4,96,384]{2,1,0:T(8,128)(2,1)}, bf16[4,96,384]{2,1,0:T(8,128)(2,1)S(1)}, u32[]{:S(2)}, u32[]{:S(2)}) %collective-permute-start.6) | collective-permute-done | bytes 294944 | tf_op jit(solution)/shard_map/ppermute | solution.py:284
  16.6 2.0 %collective-permute-done.2.rest_12_ = bf16[4,96,384]{2,1,0:T(8,128)(2,1)S(1)} collective-permute-done((bf16[4,96,384]{2,1,0:T(8,128)(2,1)}, bf16[4,96,384]{2,1,0:T(8,128)(2,1)S(1)}, u32[]{:S(2)}, u32[]{:S(2)}) %collective-permute-start.2) | collective-permute-done | bytes 294944 | tf_op jit(solution)/shard_map/ppermute | solution.py:284
  18.7 3.7 %collective-permute-start.8 = (bf16[4,96,384]{2,1,0:T(8,128)(2,1)S(1)}, bf16[4,96,384]{2,1,0:T(8,128)(2,1)S(1)}, u32[]{:S(2)}, u32[]{:S(2)}) collective-permute-start(bf16[4,96,384]{2,1,0:T(8,128)(2,1)S(1)} %collective-permute-done.6.rest_1_), channel_id=1, source_target_pairs={{0,1},{1,0},{2,3},{3,2},{4,5},{5,4},{6,7},{7,6},{8,9},{9,8},{10,11... | collective-permute-start | bytes 884744 | tf_op jit(solution)/shard_map/ppermute | solution.py:284
  23.8 5.4 %collective-permute-start.10 = (bf16[4,96,384]{2,1,0:T(8,128)(2,1)S(1)}, bf16[4,96,384]{2,1,0:T(8,128)(2,1)S(1)}, u32[]{:S(2)}, u32[]{:S(2)}) collective-permute-start(bf16[4,96,384]{2,1,0:T(8,128)(2,1)S(1)} %collective-permute-done.rest_4_), channel_id=1, source_target_pairs={{0,1},{1,0},{2,3},{3,2},{4,5},{5,4},{6,7},{7,6},{8,9},{9,8},{10,11... | collective-permute-start | bytes 884744 | tf_op jit(solution)/shard_map/ppermute | solution.py:284
  30.4 1.6 %collective-permute-start.17 = (bf16[4,96,384]{2,1,0:T(8,128)(2,1)S(1)}, bf16[4,96,384]{2,1,0:T(8,128)(2,1)S(1)}, u32[]{:S(2)}, u32[]{:S(2)}) collective-permute-start(bf16[4,96,384]{2,1,0:T(8,128)(2,1)S(1)} %collective-permute-done.15.rest_13_), channel_id=1, source_target_pairs={{0,1},{1,0},{2,3},{3,2},{4,5},{5,4},{6,7},{7,6},{8,9},{9,8},{10,11... | collective-permute-start | bytes 884744 | tf_op jit(solution)/shard_map/ppermute | solution.py:284
  32.6 2.1 %collective-permute-done.3.rest_9_ = bf16[2,96,384]{2,1,0:T(8,128)(2,1)S(1)} collective-permute-done((bf16[2,96,384]{2,1,0:T(8,128)(2,1)S(1)}, bf16[2,96,384]{2,1,0:T(8,128)(2,1)S(1)}, u32[]{:S(2)}, u32[]{:S(2)}) %collective-permute-start.3) | collective-permute-done | bytes 147488 | tf_op jit(solution)/shard_map/ppermute | solution.py:284
  36.6 1.6 %shard_map.124 = (bf16[1536,768]{1,0:T(8,128)(2,1)S(1)}, bf16[2,128,768]{2,1,0:T(8,128)(2,1)S(1)}, bf16[256,1536]{1,0:T(8,128)(2,1)S(1)}, bf16[2,16,128]{2,1,0:T(8,128)(2,1)S(1)}) custom-call(bf16[144,1536]{1,0:T(8,128)(2,1)S(1)} %get-tuple-element.43.own_ref, bf16[144,1536]{1,0:T(8,128)(2,1)S(1)} %collective-permute-done.5.oth_ref, ...), custom_call_target="tpu_custom_call" | custom-call | bytes 1024 | tf_op jit(solution)/shard_map/pallas_call | solution.py:356
  38.2 4.7 %collective-permute-start.19 = (bf16[2,128,768]{2,1,0:T(8,128)(2,1)S(1)}, bf16[2,128,768]{2,1,0:T(8,128)(2,1)S(1)}, u32[]{:S(2)}, u32[]{:S(2)}) collective-permute-start(bf16[2,128,768]{2,1,0:T(8,128)(2,1)S(1)} %get-tuple-element.47.kv_ref), channel_id=1, source_target_pairs={{0,1},{1,2},{2,3},{3,4},{4,5},{5,6},{6,7},{7,8},{8,9},{9,10},{10,1... | collective-permute-start | bytes 1179656 | tf_op jit(solution)/shard_map/ppermute | solution.py:370
  43.0 1.4 %collective-permute-done.18.rest_11_ = bf16[2,96,384]{2,1,0:T(8,128)(2,1)S(1)} collective-permute-done((bf16[2,96,384]{2,1,0:T(8,128)(2,1)S(1)}, bf16[2,96,384]{2,1,0:T(8,128)(2,1)S(1)}, u32[]{:S(2)}, u32[]{:S(2)}) %collective-permute-start.18) | collective-permute-done | bytes 147488 | tf_op jit(solution)/shard_map/ppermute | solution.py:284
  44.4 2.3 %shard_map.125 = (bf16[1536,768]{1,0:T(8,128)(2,1)S(1)}, bf16[2,128,384]{2,1,0:T(8,128)(2,1)S(1)}, bf16[2,128,384]{2,1,0:T(8,128)(2,1)S(1)}, f32[2,3,128,128]{3,...) custom-call(bf16[256,1536]{1,0:T(8,128)(2,1)S(1)} %get-tuple-element.46.xs, ...), custom_call_target="tpu_custom_call" | custom-call | bytes 1024 | tf_op jit(solution)/shard_map/pallas_call | solution.py:372
  47.6 1.3 %shard_map.126 = (bf16[3,128,128]{2,1,0:T(8,128)(2,1)S(1)}, bf16[3,128,256]{2,1,0:T(8,128)(2,1)S(1)}, bf16[128,768]{1,0:T(8,128)(2,1)S(1)}, bf16[128,384]{1,0:T(8,128)(2,1)S(1)}) custom-call(bf16[2,16,128]{2,1,0:T(8,128)(2,1)S(1)} %get-tuple-element.45.flags, bf16[2,128,384]{2,1,0:T(8,128)(2,1)S(1)} %get-tuple-element.49.cq_ref, ...), custom_call_target="tpu_custom_call" | custom-call | bytes 1024 | tf_op jit(solution)/shard_map/pallas_call | solution.py:383
  50.6 2.2 %collective-permute-start.20 = (bf16[128,768]{1,0:T(8,128)(2,1)S(1)}, bf16[128,768]{1,0:T(8,128)(2,1)S(1)}, u32[]{:S(2)}, u32[]{:S(2)}) collective-permute-start(bf16[128,768]{1,0:T(8,128)(2,1)S(1)} %get-tuple-element.64), channel_id=1, source_target_pairs={{1,0},{2,1},{3,2},{4,3},{5,4},{6,5},{7,6},{8,7},{9,8},{10,9},{11,1... | collective-permute-start | bytes 589832 | tf_op jit(solution)/shard_map/ppermute | solution.py:401
  52.8 1.3 %shard_map.128 = (bf16[3,128,128]{2,1,0:T(8,128)(2,1)S(1)}, bf16[3,128,256]{2,1,0:T(8,128)(2,1)S(1)}, bf16[128,768]{1,0:T(8,128)(2,1)S(1)}, bf16[128,384]{1,0:T(8,128)(2,1)S(1)}) custom-call(bf16[2,16,128]{2,1,0:T(8,128)(2,1)S(1)} %get-tuple-element.45.flags, bf16[2,128,384]{2,1,0:T(8,128)(2,1)S(1)} %get-tuple-element.49.cq_ref, ...), custom_call_target="tpu_custom_call" | custom-call | bytes 1024 | tf_op jit(solution)/shard_map/pallas_call | solution.py:383
  54.1 1.9 %shard_map.129.np_ref = f32[128,1536]{1,0:T(8,128)S(1)} custom-call(bf16[3,128,128]{2,1,0:T(8,128)(2,1)S(1)} %get-tuple-element.61.p_ref, bf16[3,128,256]{2,1,0:T(8,128)(2,1)S(1)} %get-tuple-element.62.ds_ref, bf16[2,128,384]{2,1,0:T(8,128)(2,1)S(1)} %get-tuple-element.49.cq_ref, bf16[2,128,384]{2,1,0:T(8,128)(2,1)S(1)} %get-tuple-element.50.cg_ref, ...), custom_call_target="tpu_custom_call" | custom-call | bytes 1024 | tf_op jit(solution)/shard_map/pallas_call | solution.py:391
  56.0 3.5 %collective-permute-done.20.ret_ref = bf16[128,768]{1,0:T(8,128)(2,1)S(1)} collective-permute-done((bf16[128,768]{1,0:T(8,128)(2,1)S(1)}, bf16[128,768]{1,0:T(8,128)(2,1)S(1)}, u32[]{:S(2)}, u32[]{:S(2)}) %collective-permute-start.20) | collective-permute-done | bytes 196640 | tf_op jit(solution)/shard_map/ppermute | solution.py:401
  60.9 2.1 %collective-permute-start.22 = (bf16[128,768]{1,0:T(8,128)(2,1)S(1)}, bf16[128,768]{1,0:T(8,128)(2,1)S(1)}, u32[]{:S(2)}, u32[]{:S(2)}) collective-permute-start(bf16[128,768]{1,0:T(8,128)(2,1)S(1)} %get-tuple-element.67), channel_id=1, source_target_pairs={{1,0},{2,1},{3,2},{4,3},{5,4},{6,5},{7,6},{8,7},{9,8},{10,9},{11,1... | collective-permute-start | bytes 589832 | tf_op jit(solution)/shard_map/ppermute | solution.py:403
  63.0 1.9 %shard_map.131.np_ref = f32[128,1536]{1,0:T(8,128)S(1)} custom-call(bf16[3,128,128]{2,1,0:T(8,128)(2,1)S(1)} %get-tuple-element.65.p_ref, bf16[3,128,256]{2,1,0:T(8,128)(2,1)S(1)} %get-tuple-element.66.ds_ref, bf16[2,128,384]{2,1,0:T(8,128)(2,1)S(1)} %get-tuple-element.49.cq_ref, bf16[2,128,384]{2,1,0:T(8,128)(2,1)S(1)} %get-tuple-element.50.cg_ref, ...), custom_call_target="tpu_custom_call" | custom-call | bytes 1024 | tf_op jit(solution)/shard_map/pallas_call | solution.py:391
  64.9 3.9 %collective-permute-done.22.ret_ref = bf16[128,768]{1,0:T(8,128)(2,1)S(1)} collective-permute-done((bf16[128,768]{1,0:T(8,128)(2,1)S(1)}, bf16[128,768]{1,0:T(8,128)(2,1)S(1)}, u32[]{:S(2)}, u32[]{:S(2)}) %collective-permute-start.22) | collective-permute-done | bytes 196640 | tf_op jit(solution)/shard_map/ppermute | solution.py:403
  69.7 1.3 %shard_map.133 = bf16[1,128,1536]{2,1,0:T(8,128)(2,1)} custom-call(bf16[1,128,1536]{2,1,0:T(8,128)(2,1)S(1)} %copy-done, bf16[128,384]{1,0:T(8,128)(2,1)S(1)} %get-tuple-element.68.ctx_ref, bf16[1536,768]{1,0:T(8,128)(2,1)S(1)} %get-tuple-element.55.wqo, bf16[128,1536]{1,0:T(8,128)(2,1)S(1)} %collective-permute-done.21.lo_ret), custom_call_target="tpu_custom_call" | custom-call | bytes 1024 | tf_op jit(solution)/shard_map/pallas_call | solution.py:409
  70.9 1.4 %shard_map.134 = bf16[1,128,1536]{2,1,0:T(8,128)(2,1)} custom-call(bf16[1,128,1536]{2,1,0:T(8,128)(2,1)S(1)} %copy-done, f32[12,128]{1,0:T(8,128)S(1)} %bitcast.8, bf16[128,1536]{1,0:T(8,128)(2,1)S(1)} %bitcast.6, f32[128,1536]{1,0:T(8,128)S(1)} %shard_map.132.np_own, bf16[128,1536]{1,0:T(8,128)(2,1)S(1)} %collective-permute-done.23.np_ret), custom_call_target="tpu_custom_call" | custom-call | bytes 1024 | tf_op jit(solution)/shard_map/pallas_call | solution.py:412
  (55 shorter events, 15.2 us)
Async XLA Ops:
  3.7 8.2 %collective-permute-start = (bf16[4,96,384]{2,1,0:T(8,128)(2,1)}, bf16[4,96,384]{2,1,0:T(8,128)(2,1)S(1)}, u32[]{:S(2)}, u32[]{:S(2)}) collective-permute-start(bf16[4,96,384]{2,1,0:T(8,128)(2,1)} %get-tuple-element.36.shard_ref), channel_id=1, source_target_pairs={{0,4},{1,5},{2,6},{3,7},{4,8},{5,9},{6,10},{7,11},{8,12},{9,13},{1... | collective-permute-start | bytes 884744 | tf_op jit(solution)/shard_map/ppermute | solution.py:284
  5.1 17.3 %collective-permute-start.5 = (bf16[144,1536]{1,0:T(8,128)(2,1)}, bf16[144,1536]{1,0:T(8,128)(2,1)S(1)}, u32[]{:S(2)}, u32[]{:S(2)}) collective-permute-start(bf16[144,1536]{1,0:T(8,128)(2,1)} %get-tuple-element.37.normed_ref), channel_id=1, source_target_pairs={{0,16},{16,0},{1,17},{17,1},{2,18},{18,2},{3,19},{19,3},{4,20},{20... | collective-permute-start | bytes 1327112 | tf_op jit(solution)/shard_map/ppermute | solution.py:298
  6.3 5.8 %collective-permute-start.7 = (bf16[4,96,384]{2,1,0:T(8,128)(2,1)}, bf16[4,96,384]{2,1,0:T(8,128)(2,1)S(1)}, u32[]{:S(2)}, u32[]{:S(2)}) collective-permute-start(bf16[4,96,384]{2,1,0:T(8,128)(2,1)} %get-tuple-element.36.shard_ref), channel_id=1, source_target_pairs={{0,1},{1,0},{2,3},{3,2},{4,5},{5,4},{6,7},{7,6},{8,9},{9,8},{10,11... | collective-permute-start | bytes 884744 | tf_op jit(solution)/shard_map/ppermute | solution.py:284
  7.5 8.8 %collective-permute-start.6 = (bf16[4,96,384]{2,1,0:T(8,128)(2,1)}, bf16[4,96,384]{2,1,0:T(8,128)(2,1)S(1)}, u32[]{:S(2)}, u32[]{:S(2)}) collective-permute-start(bf16[4,96,384]{2,1,0:T(8,128)(2,1)} %get-tuple-element.36.shard_ref), channel_id=1, source_target_pairs={{0,2},{1,3},{2,0},{3,1},{4,6},{5,7},{6,4},{7,5},{8,10},{9,11},{10,... | collective-permute-start | bytes 884744 | tf_op jit(solution)/shard_map/ppermute | solution.py:284
  7.8 10.9 %collective-permute-start.2 = (bf16[4,96,384]{2,1,0:T(8,128)(2,1)}, bf16[4,96,384]{2,1,0:T(8,128)(2,1)S(1)}, u32[]{:S(2)}, u32[]{:S(2)}) collective-permute-start(bf16[4,96,384]{2,1,0:T(8,128)(2,1)} %get-tuple-element.36.shard_ref), channel_id=1, source_target_pairs={{0,12},{1,13},{2,14},{3,15},{4,0},{5,1},{6,2},{7,3},{8,4},{9,5},{1... | collective-permute-start | bytes 884744 | tf_op jit(solution)/shard_map/ppermute | solution.py:284
  12.0 10.5 %collective-permute-start.9 = (bf16[4,96,384]{2,1,0:T(8,128)(2,1)S(1)}, bf16[4,96,384]{2,1,0:T(8,128)(2,1)S(1)}, u32[]{:S(2)}, u32[]{:S(2)}) collective-permute-start(bf16[4,96,384]{2,1,0:T(8,128)(2,1)S(1)} %collective-permute-done.rest_4_), channel_id=1, source_target_pairs={{0,2},{1,3},{2,0},{3,1},{4,6},{5,7},{6,4},{7,5},{8,10},{9,11},{10,... | collective-permute-start | bytes 884744 | tf_op jit(solution)/shard_map/ppermute | solution.py:284
  12.1 11.6 %collective-permute-start.1 = (bf16[4,96,384]{2,1,0:T(8,128)(2,1)S(1)}, bf16[4,96,384]{2,1,0:T(8,128)(2,1)S(1)}, u32[]{:S(2)}, u32[]{:S(2)}) collective-permute-start(bf16[4,96,384]{2,1,0:T(8,128)(2,1)S(1)} %collective-permute-done.rest_4_), channel_id=1, source_target_pairs={{0,4},{1,5},{2,6},{3,7},{4,8},{5,9},{6,10},{7,11},{8,12},{9,13},{1... | collective-permute-start | bytes 884744 | tf_op jit(solution)/shard_map/ppermute | solution.py:284
  16.4 15.7 %collective-permute-start.4 = (bf16[128,1536]{1,0:T(8,128)(2,1)}, bf16[128,1536]{1,0:T(8,128)(2,1)S(1)}, u32[]{:S(2)}, u32[]{:S(2)}) collective-permute-start(bf16[128,1536]{1,0:T(8,128)(2,1)} %bitcast.4), channel_id=1, source_target_pairs={{0,16},{16,0},{1,17},{17,1},{2,18},{18,2},{3,19},{19,3},{4,20},{20... | collective-permute-start | bytes 1179656 | tf_op jit(solution)/shard_map/ppermute | solution.py:298
  18.7 5.2 %collective-permute-start.8 = (bf16[4,96,384]{2,1,0:T(8,128)(2,1)S(1)}, bf16[4,96,384]{2,1,0:T(8,128)(2,1)S(1)}, u32[]{:S(2)}, u32[]{:S(2)}) collective-permute-start(bf16[4,96,384]{2,1,0:T(8,128)(2,1)S(1)} %collective-permute-done.6.rest_1_), channel_id=1, source_target_pairs={{0,1},{1,0},{2,3},{3,2},{4,5},{5,4},{6,7},{7,6},{8,9},{9,8},{10,11... | collective-permute-start | bytes 884744 | tf_op jit(solution)/shard_map/ppermute | solution.py:284
  22.4 6.9 %collective-permute-start.16 = (bf16[4,96,384]{2,1,0:T(8,128)(2,1)S(1)}, bf16[4,96,384]{2,1,0:T(8,128)(2,1)S(1)}, u32[]{:S(2)}, u32[]{:S(2)}) collective-permute-start(bf16[4,96,384]{2,1,0:T(8,128)(2,1)S(1)} %collective-permute-done.2.rest_12_), channel_id=1, source_target_pairs={{0,1},{1,0},{2,3},{3,2},{4,5},{5,4},{6,7},{7,6},{8,9},{9,8},{10,11... | collective-permute-start | bytes 884744 | tf_op jit(solution)/shard_map/ppermute | solution.py:284
  22.5 8.0 %collective-permute-start.15 = (bf16[4,96,384]{2,1,0:T(8,128)(2,1)S(1)}, bf16[4,96,384]{2,1,0:T(8,128)(2,1)S(1)}, u32[]{:S(2)}, u32[]{:S(2)}) collective-permute-start(bf16[4,96,384]{2,1,0:T(8,128)(2,1)S(1)} %collective-permute-done.2.rest_12_), channel_id=1, source_target_pairs={{0,2},{1,3},{2,0},{3,1},{4,6},{5,7},{6,4},{7,5},{8,10},{9,11},{10,... | collective-permute-start | bytes 884744 | tf_op jit(solution)/shard_map/ppermute | solution.py:284
  23.7 8.4 %collective-permute-start.12 = (bf16[2,96,384]{2,1,0:T(8,128)(2,1)S(1)}, bf16[2,96,384]{2,1,0:T(8,128)(2,1)S(1)}, u32[]{:S(2)}, u32[]{:S(2)}) collective-permute-start(bf16[2,96,384]{2,1,0:T(8,128)(2,1)S(1)} %slice.7), channel_id=1, source_target_pairs={{0,4},{1,5},{2,6},{3,7},{4,8},{5,9},{6,10},{7,11},{8,12},{9,13},{1... | collective-permute-start | bytes 442376 | tf_op jit(solution)/shard_map/ppermute | solution.py:284
  23.8 11.7 %collective-permute-start.10 = (bf16[4,96,384]{2,1,0:T(8,128)(2,1)S(1)}, bf16[4,96,384]{2,1,0:T(8,128)(2,1)S(1)}, u32[]{:S(2)}, u32[]{:S(2)}) collective-permute-start(bf16[4,96,384]{2,1,0:T(8,128)(2,1)S(1)} %collective-permute-done.rest_4_), channel_id=1, source_target_pairs={{0,1},{1,0},{2,3},{3,2},{4,5},{5,4},{6,7},{7,6},{8,9},{9,8},{10,11... | collective-permute-start | bytes 884744 | tf_op jit(solution)/shard_map/ppermute | solution.py:284
  29.3 5.4 %collective-permute-start.3 = (bf16[2,96,384]{2,1,0:T(8,128)(2,1)S(1)}, bf16[2,96,384]{2,1,0:T(8,128)(2,1)S(1)}, u32[]{:S(2)}, u32[]{:S(2)}) collective-permute-start(bf16[2,96,384]{2,1,0:T(8,128)(2,1)S(1)} %slice.6), channel_id=1, source_target_pairs={{0,2},{1,3},{2,0},{3,1},{4,6},{5,7},{6,4},{7,5},{8,10},{9,11},{10,... | collective-permute-start | bytes 442376 | tf_op jit(solution)/shard_map/ppermute | solution.py:284
  30.4 5.1 %collective-permute-start.17 = (bf16[4,96,384]{2,1,0:T(8,128)(2,1)S(1)}, bf16[4,96,384]{2,1,0:T(8,128)(2,1)S(1)}, u32[]{:S(2)}, u32[]{:S(2)}) collective-permute-start(bf16[4,96,384]{2,1,0:T(8,128)(2,1)S(1)} %collective-permute-done.15.rest_13_), channel_id=1, source_target_pairs={{0,1},{1,0},{2,3},{3,2},{4,5},{5,4},{6,7},{7,6},{8,9},{9,8},{10,11... | collective-permute-start | bytes 884744 | tf_op jit(solution)/shard_map/ppermute | solution.py:284
  32.1 4.5 %collective-permute-start.11 = (bf16[4,96,384]{2,1,0:T(8,128)(2,1)S(1)}, bf16[4,96,384]{2,1,0:T(8,128)(2,1)S(1)}, u32[]{:S(2)}, u32[]{:S(2)}) collective-permute-start(bf16[4,96,384]{2,1,0:T(8,128)(2,1)S(1)} %collective-permute-done.9.rest_5_), channel_id=1, source_target_pairs={{0,1},{1,0},{2,3},{3,2},{4,5},{5,4},{6,7},{7,6},{8,9},{9,8},{10,11... | collective-permute-start | bytes 884744 | tf_op jit(solution)/shard_map/ppermute | solution.py:284
  32.1 4.5 %collective-permute-start.13 = (bf16[4,96,384]{2,1,0:T(8,128)(2,1)S(1)}, bf16[4,96,384]{2,1,0:T(8,128)(2,1)S(1)}, u32[]{:S(2)}, u32[]{:S(2)}) collective-permute-start(bf16[4,96,384]{2,1,0:T(8,128)(2,1)S(1)} %collective-permute-done.1.rest_8_), channel_id=1, source_target_pairs={{0,1},{1,0},{2,3},{3,2},{4,5},{5,4},{6,7},{7,6},{8,9},{9,8},{10,11... | collective-permute-start | bytes 884744 | tf_op jit(solution)/shard_map/ppermute | solution.py:284
  34.7 1.9 %collective-permute-start.14 = (bf16[2,96,384]{2,1,0:T(8,128)(2,1)S(1)}, bf16[2,96,384]{2,1,0:T(8,128)(2,1)S(1)}, u32[]{:S(2)}, u32[]{:S(2)}) collective-permute-start(bf16[2,96,384]{2,1,0:T(8,128)(2,1)S(1)} %collective-permute-done.12.rest_9_), channel_id=1, source_target_pairs={{0,1},{1,0},{2,3},{3,2},{4,5},{5,4},{6,7},{7,6},{8,9},{9,8},{10,11... | collective-permute-start | bytes 442376 | tf_op jit(solution)/shard_map/ppermute | solution.py:284
  38.2 9.4 %collective-permute-start.19 = (bf16[2,128,768]{2,1,0:T(8,128)(2,1)S(1)}, bf16[2,128,768]{2,1,0:T(8,128)(2,1)S(1)}, u32[]{:S(2)}, u32[]{:S(2)}) collective-permute-start(bf16[2,128,768]{2,1,0:T(8,128)(2,1)S(1)} %get-tuple-element.47.kv_ref), channel_id=1, source_target_pairs={{0,1},{1,2},{2,3},{3,4},{4,5},{5,6},{6,7},{7,8},{8,9},{9,10},{10,1... | collective-permute-start | bytes 1179656 | tf_op jit(solution)/shard_map/ppermute | solution.py:370
  42.9 1.4 %collective-permute-start.18 = (bf16[2,96,384]{2,1,0:T(8,128)(2,1)S(1)}, bf16[2,96,384]{2,1,0:T(8,128)(2,1)S(1)}, u32[]{:S(2)}, u32[]{:S(2)}) collective-permute-start(bf16[2,96,384]{2,1,0:T(8,128)(2,1)S(1)} %collective-permute-done.3.rest_9_), channel_id=1, source_target_pairs={{0,1},{1,0},{2,3},{3,2},{4,5},{5,4},{6,7},{7,6},{8,9},{9,8},{10,11... | collective-permute-start | bytes 442376 | tf_op jit(solution)/shard_map/ppermute | solution.py:284
  49.5 11.4 %collective-permute-start.21 = (bf16[128,1536]{1,0:T(8,128)(2,1)S(1)}, bf16[128,1536]{1,0:T(8,128)(2,1)S(1)}, u32[]{:S(2)}, u32[]{:S(2)}) collective-permute-start(bf16[128,1536]{1,0:T(8,128)(2,1)S(1)} %shard_map.127), channel_id=1, source_target_pairs={{0,16},{16,0},{1,17},{17,1},{2,18},{18,2},{3,19},{19,3},{4,20},{20... | collective-permute-start | bytes 1179656 | tf_op jit(solution)/shard_map/ppermute | solution.py:298
  50.6 8.9 %collective-permute-start.20 = (bf16[128,768]{1,0:T(8,128)(2,1)S(1)}, bf16[128,768]{1,0:T(8,128)(2,1)S(1)}, u32[]{:S(2)}, u32[]{:S(2)}) collective-permute-start(bf16[128,768]{1,0:T(8,128)(2,1)S(1)} %get-tuple-element.64), channel_id=1, source_target_pairs={{1,0},{2,1},{3,2},{4,3},{5,4},{6,5},{7,6},{8,7},{9,8},{10,9},{11,1... | collective-permute-start | bytes 589832 | tf_op jit(solution)/shard_map/ppermute | solution.py:401
  60.4 10.6 %collective-permute-start.23 = (bf16[128,1536]{1,0:T(8,128)(2,1)S(1)}, bf16[128,1536]{1,0:T(8,128)(2,1)S(1)}, u32[]{:S(2)}, u32[]{:S(2)}) collective-permute-start(bf16[128,1536]{1,0:T(8,128)(2,1)S(1)} %shard_map.130), channel_id=1, source_target_pairs={{0,16},{16,0},{1,17},{17,1},{2,18},{18,2},{3,19},{19,3},{4,20},{20... | collective-permute-start | bytes 1179656 | tf_op jit(solution)/shard_map/ppermute | solution.py:298
  60.9 7.9 %collective-permute-start.22 = (bf16[128,768]{1,0:T(8,128)(2,1)S(1)}, bf16[128,768]{1,0:T(8,128)(2,1)S(1)}, u32[]{:S(2)}, u32[]{:S(2)}) collective-permute-start(bf16[128,768]{1,0:T(8,128)(2,1)S(1)} %get-tuple-element.67), channel_id=1, source_target_pairs={{1,0},{2,1},{3,2},{4,3},{5,4},{6,5},{7,6},{8,7},{9,8},{10,9},{11,1... | collective-permute-start | bytes 589832 | tf_op jit(solution)/shard_map/ppermute | solution.py:403
  (8 other events, 43.3 us)

commit v5 on v4

--- a/solution.py
+++ b/solution.py
@@ -233,22 +233,36 @@
         out_ref[0, :, there] = (x_ref[0, :, there].astype(F32) + total).astype(BF16)
 
 
-def finish_kernel(x_ref, gain_ref, cot_ref, np_own, np_ret, grad_ref, total):
+def hat_kernel(x_ref, gain_ref, cot_ref, hat_ref, rstd_ref, gain_out, cot_out, held):
     z, _, _ = place()
-    for r in range(ZS):
-        cols = slice(r * BLK, (r + 1) * BLK)
-        total[:, plane_columns(z, r)] = np_own[:, cols] + np_ret[:, cols].astype(F32)
     x = x_ref[0].astype(F32)
     center = jnp.mean(x, axis=-1, keepdims=True)
     moved = x - center
     spread = jnp.mean(jnp.square(moved), axis=-1, keepdims=True)
     rstd = lax.rsqrt(spread + epsilon)
-    hat = moved * rstd
-    g = total[...] * lanes(gain_ref)
-    mean_g = jnp.mean(g, axis=-1, keepdims=True)
-    mean_gh = jnp.mean(g * hat, axis=-1, keepdims=True)
-    grad = (rstd * (g - mean_g - hat * mean_gh)).astype(BF16)
-    grad_ref[0] = cot_ref[...] + grad
+    held[0:SEG, :] = moved * rstd
+    held[SEG:, :] = jnp.broadcast_to(lanes(gain_ref), (8, D))
+    rstd_ref[...] = jnp.broadcast_to(rstd, (SEG, 128))
+    for r in range(ZS):
+        cols, there = slice(r * BLK, (r + 1) * BLK), plane_columns(z, r)
+        hat_ref[:, cols] = held[0:SEG, there]
+        gain_out[:, cols] = held[SEG:, there]
+        cot_out[:, cols] = cot_ref[:, there]
+
+
+def finish_kernel(hat_ref, rstd_ref, gain_ref, cot_ref, np_own, np_ret, grad_ref):
+    z, _, _ = place()
+    step = 32
+    for i in range(0, SEG, step):
+        rows = slice(i, i + step)
+        hat, rstd = hat_ref[rows, :], rstd_ref[rows, 0:1]
+        g = (np_own[rows, :] + np_ret[rows, :].astype(F32)) * gain_ref[0:1, :]
+        mean_g = jnp.mean(g, axis=-1, keepdims=True)
+        mean_gh = jnp.mean(g * hat, axis=-1, keepdims=True)
+        grad = (rstd * (g - mean_g - hat * mean_gh)).astype(BF16)
+        total = cot_ref[rows, :] + grad
+        for r in range(ZS):
+            grad_ref[0, rows, plane_columns(z, r)] = total[:, r * BLK : (r + 1) * BLK]
 
 
 def call(kernel, outs, scratch=(), in_specs=None, mib=24):
@@ -405,13 +419,26 @@
     np_oth = call(returned_kernel, shape(SEG, D), (), [VM] * 3)(partial_oth, ret_oth, wkv)
     np_ret = other(np_oth)
     partial = grads(0, after(p, np_oth), ds, kv, mem)
-    np_own = call(returned_kernel, shape(SEG, D, dtype=F32), (), [VM] * 3)(partial, ret, wkv)
     layer_out = call(
         output_kernel, shape(1, SEG, D), [pltpu.VMEM((SEG, D), F32)], [VM] * 4
-    )(inputs, after(ctx, np_own), wqo, lo_ret)
-    input_grad = call(
-        finish_kernel, shape(1, SEG, D), [pltpu.VMEM((SEG, D), F32)], [VM] * 5
-    )(inputs, gain, cot, after(np_own, layer_out), np_ret)
+    )(inputs, after(ctx, partial), wqo, lo_ret)
+    np_own = call(returned_kernel, shape(SEG, D, dtype=F32), (), [VM] * 3)(
+        after(partial, layer_out), ret, wkv
+    )
+    hat = call(
+        hat_kernel,
+        (
+            shape(SEG, D, dtype=F32),
+            shape(SEG, 128, dtype=F32),
+            shape(8, D, dtype=F32),
+            shape(SEG, D),
+        ),
+        [pltpu.VMEM((SEG + 8, D), F32)],
+        [VM] * 3,
+    )(inputs, gain, after(cot, partial))
+    input_grad = call(finish_kernel, shape(1, SEG, D), (), [VM] * 6)(
+        *hat, after(np_own, hat[0]), np_ret
+    )
     return (layer_out, input_grad)
 
 

time: 72.6 us -> 72 us (level); the launches traced: 72.3 us -> 70.8 us
  waiting for transfers between devices: 19.8 us -> 18.1 us
    ppermute x1, waiting for transfers between devices: 3.85 us -> 2.17 us  [split_heads(): ret = lax.ppermute(after(dmem, lo_ret), 'tm', back)]
    pallas_call x1 -> x2, Pallas kernels: 1.42 us -> 1.52 us  [the longest x1 1.14 us: split_heads(): call(finish_kernel, shape(1, SEG, D), (), [VM] * 6)]
where the time goes in v5:
time: 72 us; the launch traced here: 70.8 us
  starting transfers between devices  31.3 us (43%)
  waiting for transfers between devices  18.1 us (25%)
  Pallas kernels  17.9 us (25%)
  local copies, waits for them, and re-layouts  2.03 us (3%)
  between operations  1.5 us (2%)
    ppermute x17, starting transfers between devices, moved_by(): return lambda block: lax.ppermute(block, 'tm', route)  19.2 us
    ppermute x17, waiting for transfers between devices, moved_by(): return lambda block: lax.ppermute(block, 'tm', route)  11.5 us
    ppermute x1, starting transfers between devices, split_heads(): mem = lax.ppermute(kv, 'tm', onward)  4.74 us
    pallas_call x2, Pallas kernels, grads(): call(functools.partial(grad_kernel, rec), shape(SEG, D, dtype=F32), [pltp...  3.82 us
    ppermute x1, waiting for transfers between devices, split_heads(): ret_oth = lax.ppermute(dmem_oth, 'tm', back)  3.46 us
    ppermute x4, starting transfers between devices, other(): return lax.ppermute(block, 'grp', [(0, 1), (1, 0)])  3.06 us
    pallas_call x2, Pallas kernels, memory(): call(functools.partial(memory_kernel, rec), (shape(HEADS, SEG, SEG), shap...  2.64 us
    pallas_call x1, Pallas kernels, split_heads(): call(prepare_kernel, (shape(4, ROWS, HALF), shape(SEG + 16, D), shape(2 *...  2.45 us
  transfers between devices with their start and end apart: 24, of which 9 were waited for; matrix products, arithmetic and copies ran while one was open for 0% of the time, Pallas kernels for 15%

profile of v5, /device:TPU:21, one launch (start us, length us, event | category | flops | bytes accessed | tf_op | source)
XLA Modules:
  0.0 70.8 jit_solution(819383728212896625)
XLA Ops:
  1.3 2.4 %shard_map.122 = (bf16[4,96,384]{2,1,0:T(8,128)(2,1)}, bf16[144,1536]{1,0:T(8,128)(2,1)}, bf16[256,384]{1,0:T(8,128)(2,1)}) custom-call(bf16[96,384]{1,0:T(8,128)(2,1)} %k_ref.1, bf16[96,384]{1,0:T(8,128)(2,1)} %v_ref.1, bf16[96,384]{1,0:T(8,128)(2,1)} %q_ref.1, bf16[96,384]{1,0:T(8,128)(2,1)} %o_ref.1, bf16[1,128,1536]{2,1,0:T(8,128)(2,1)} %x_ref.5, ...), custom_call_target="tpu_custom_call" | custom-call | bytes 1024 | tf_op jit(solution)/shard_map/pallas_call | solution.py:330
  3.7 1.4 %collective-permute-start = (bf16[4,96,384]{2,1,0:T(8,128)(2,1)}, bf16[4,96,384]{2,1,0:T(8,128)(2,1)S(1)}, u32[]{:S(2)}, u32[]{:S(2)}) collective-permute-start(bf16[4,96,384]{2,1,0:T(8,128)(2,1)} %get-tuple-element.42.shard_ref), channel_id=1, source_target_pairs={{0,4},{1,5},{2,6},{3,7},{4,8},{5,9},{6,10},{7,11},{8,12},{9,13},{1... | collective-permute-start | bytes 884744 | tf_op jit(solution)/shard_map/ppermute | solution.py:298
  10.0 2.0 %collective-permute-done.rest_4_ = bf16[4,96,384]{2,1,0:T(8,128)(2,1)S(1)} collective-permute-done((bf16[4,96,384]{2,1,0:T(8,128)(2,1)}, bf16[4,96,384]{2,1,0:T(8,128)(2,1)S(1)}, u32[]{:S(2)}, u32[]{:S(2)}) %collective-permute-start) | collective-permute-done | bytes 294944 | tf_op jit(solution)/shard_map/ppermute | solution.py:298
  12.1 1.3 %collective-permute-start.1 = (bf16[4,96,384]{2,1,0:T(8,128)(2,1)S(1)}, bf16[4,96,384]{2,1,0:T(8,128)(2,1)S(1)}, u32[]{:S(2)}, u32[]{:S(2)}) collective-permute-start(bf16[4,96,384]{2,1,0:T(8,128)(2,1)S(1)} %collective-permute-done.rest_4_), channel_id=1, source_target_pairs={{0,4},{1,5},{2,6},{3,7},{4,8},{5,9},{6,10},{7,11},{8,12},{9,13},{1... | collective-permute-start | bytes 884744 | tf_op jit(solution)/shard_map/ppermute | solution.py:298
  13.4 3.0 %collective-permute-done.6.rest_1_ = bf16[4,96,384]{2,1,0:T(8,128)(2,1)S(1)} collective-permute-done((bf16[4,96,384]{2,1,0:T(8,128)(2,1)}, bf16[4,96,384]{2,1,0:T(8,128)(2,1)S(1)}, u32[]{:S(2)}, u32[]{:S(2)}) %collective-permute-start.6) | collective-permute-done | bytes 294944 | tf_op jit(solution)/shard_map/ppermute | solution.py:298
  16.6 2.0 %collective-permute-done.2.rest_12_ = bf16[4,96,384]{2,1,0:T(8,128)(2,1)S(1)} collective-permute-done((bf16[4,96,384]{2,1,0:T(8,128)(2,1)}, bf16[4,96,384]{2,1,0:T(8,128)(2,1)S(1)}, u32[]{:S(2)}, u32[]{:S(2)}) %collective-permute-start.2) | collective-permute-done | bytes 294944 | tf_op jit(solution)/shard_map/ppermute | solution.py:298
  18.7 3.7 %collective-permute-start.8 = (bf16[4,96,384]{2,1,0:T(8,128)(2,1)S(1)}, bf16[4,96,384]{2,1,0:T(8,128)(2,1)S(1)}, u32[]{:S(2)}, u32[]{:S(2)}) collective-permute-start(bf16[4,96,384]{2,1,0:T(8,128)(2,1)S(1)} %collective-permute-done.6.rest_1_), channel_id=1, source_target_pairs={{0,1},{1,0},{2,3},{3,2},{4,5},{5,4},{6,7},{7,6},{8,9},{9,8},{10,11... | collective-permute-start | bytes 884744 | tf_op jit(solution)/shard_map/ppermute | solution.py:298
  22.5 1.2 %collective-permute-start.15 = (bf16[4,96,384]{2,1,0:T(8,128)(2,1)S(1)}, bf16[4,96,384]{2,1,0:T(8,128)(2,1)S(1)}, u32[]{:S(2)}, u32[]{:S(2)}) collective-permute-start(bf16[4,96,384]{2,1,0:T(8,128)(2,1)S(1)} %collective-permute-done.2.rest_12_), channel_id=1, source_target_pairs={{0,2},{1,3},{2,0},{3,1},{4,6},{5,7},{6,4},{7,5},{8,10},{9,11},{10,... | collective-permute-start | bytes 884744 | tf_op jit(solution)/shard_map/ppermute | solution.py:298
  23.8 5.4 %collective-permute-start.10 = (bf16[4,96,384]{2,1,0:T(8,128)(2,1)S(1)}, bf16[4,96,384]{2,1,0:T(8,128)(2,1)S(1)}, u32[]{:S(2)}, u32[]{:S(2)}) collective-permute-start(bf16[4,96,384]{2,1,0:T(8,128)(2,1)S(1)} %collective-permute-done.rest_4_), channel_id=1, source_target_pairs={{0,1},{1,0},{2,3},{3,2},{4,5},{5,4},{6,7},{7,6},{8,9},{9,8},{10,11... | collective-permute-start | bytes 884744 | tf_op jit(solution)/shard_map/ppermute | solution.py:298
  30.4 1.6 %collective-permute-start.17 = (bf16[4,96,384]{2,1,0:T(8,128)(2,1)S(1)}, bf16[4,96,384]{2,1,0:T(8,128)(2,1)S(1)}, u32[]{:S(2)}, u32[]{:S(2)}) collective-permute-start(bf16[4,96,384]{2,1,0:T(8,128)(2,1)S(1)} %collective-permute-done.15.rest_13_), channel_id=1, source_target_pairs={{0,1},{1,0},{2,3},{3,2},{4,5},{5,4},{6,7},{7,6},{8,9},{9,8},{10,11... | collective-permute-start | bytes 884744 | tf_op jit(solution)/shard_map/ppermute | solution.py:298
  32.6 2.1 %collective-permute-done.3.rest_9_ = bf16[2,96,384]{2,1,0:T(8,128)(2,1)S(1)} collective-permute-done((bf16[2,96,384]{2,1,0:T(8,128)(2,1)S(1)}, bf16[2,96,384]{2,1,0:T(8,128)(2,1)S(1)}, u32[]{:S(2)}, u32[]{:S(2)}) %collective-permute-start.3) | collective-permute-done | bytes 147488 | tf_op jit(solution)/shard_map/ppermute | solution.py:298
  36.6 1.6 %shard_map.124 = (bf16[1536,768]{1,0:T(8,128)(2,1)S(1)}, bf16[2,128,768]{2,1,0:T(8,128)(2,1)S(1)}, bf16[256,1536]{1,0:T(8,128)(2,1)S(1)}, bf16[2,16,128]{2,1,0:T(8,128)(2,1)S(1)}) custom-call(bf16[144,1536]{1,0:T(8,128)(2,1)S(1)} %get-tuple-element.49.own_ref, bf16[144,1536]{1,0:T(8,128)(2,1)S(1)} %collective-permute-done.5.oth_ref, ...), custom_call_target="tpu_custom_call" | custom-call | bytes 1024 | tf_op jit(solution)/shard_map/pallas_call | solution.py:370
  38.2 4.7 %collective-permute-start.19 = (bf16[2,128,768]{2,1,0:T(8,128)(2,1)S(1)}, bf16[2,128,768]{2,1,0:T(8,128)(2,1)S(1)}, u32[]{:S(2)}, u32[]{:S(2)}) collective-permute-start(bf16[2,128,768]{2,1,0:T(8,128)(2,1)S(1)} %get-tuple-element.53.kv_ref), channel_id=1, source_target_pairs={{0,1},{1,2},{2,3},{3,4},{4,5},{5,6},{6,7},{7,8},{8,9},{9,10},{10,1... | collective-permute-start | bytes 1179656 | tf_op jit(solution)/shard_map/ppermute | solution.py:384
  43.0 1.4 %collective-permute-done.18.rest_11_ = bf16[2,96,384]{2,1,0:T(8,128)(2,1)S(1)} collective-permute-done((bf16[2,96,384]{2,1,0:T(8,128)(2,1)S(1)}, bf16[2,96,384]{2,1,0:T(8,128)(2,1)S(1)}, u32[]{:S(2)}, u32[]{:S(2)}) %collective-permute-start.18) | collective-permute-done | bytes 147488 | tf_op jit(solution)/shard_map/ppermute | solution.py:298
  44.4 2.3 %shard_map.125 = (bf16[1536,768]{1,0:T(8,128)(2,1)S(1)}, bf16[2,128,384]{2,1,0:T(8,128)(2,1)S(1)}, bf16[2,128,384]{2,1,0:T(8,128)(2,1)S(1)}, f32[2,3,128,128]{3,...) custom-call(bf16[256,1536]{1,0:T(8,128)(2,1)S(1)} %get-tuple-element.52.xs, ...), custom_call_target="tpu_custom_call" | custom-call | bytes 1024 | tf_op jit(solution)/shard_map/pallas_call | solution.py:386
  47.6 1.3 %shard_map.126 = (bf16[3,128,128]{2,1,0:T(8,128)(2,1)S(1)}, bf16[3,128,256]{2,1,0:T(8,128)(2,1)S(1)}, bf16[128,768]{1,0:T(8,128)(2,1)S(1)}, bf16[128,384]{1,0:T(8,128)(2,1)S(1)}) custom-call(bf16[2,16,128]{2,1,0:T(8,128)(2,1)S(1)} %get-tuple-element.51.flags, bf16[2,128,384]{2,1,0:T(8,128)(2,1)S(1)} %get-tuple-element.55.cq_ref, ...), custom_call_target="tpu_custom_call" | custom-call | bytes 1024 | tf_op jit(solution)/shard_map/pallas_call | solution.py:397
  50.6 2.2 %collective-permute-start.20 = (bf16[128,768]{1,0:T(8,128)(2,1)S(1)}, bf16[128,768]{1,0:T(8,128)(2,1)S(1)}, u32[]{:S(2)}, u32[]{:S(2)}) collective-permute-start(bf16[128,768]{1,0:T(8,128)(2,1)S(1)} %get-tuple-element.70), channel_id=1, source_target_pairs={{1,0},{2,1},{3,2},{4,3},{5,4},{6,5},{7,6},{8,7},{9,8},{10,9},{11,1... | collective-permute-start | bytes 589832 | tf_op jit(solution)/shard_map/ppermute | solution.py:415
  52.8 1.3 %shard_map.128 = (bf16[3,128,128]{2,1,0:T(8,128)(2,1)S(1)}, bf16[3,128,256]{2,1,0:T(8,128)(2,1)S(1)}, bf16[128,768]{1,0:T(8,128)(2,1)S(1)}, bf16[128,384]{1,0:T(8,128)(2,1)S(1)}) custom-call(bf16[2,16,128]{2,1,0:T(8,128)(2,1)S(1)} %get-tuple-element.51.flags, bf16[2,128,384]{2,1,0:T(8,128)(2,1)S(1)} %get-tuple-element.55.cq_ref, ...), custom_call_target="tpu_custom_call" | custom-call | bytes 1024 | tf_op jit(solution)/shard_map/pallas_call | solution.py:397
  54.1 1.9 %shard_map.129.np_ref = f32[128,1536]{1,0:T(8,128)S(1)} custom-call(bf16[3,128,128]{2,1,0:T(8,128)(2,1)S(1)} %get-tuple-element.67.p_ref, bf16[3,128,256]{2,1,0:T(8,128)(2,1)S(1)} %get-tuple-element.68.ds_ref, bf16[2,128,384]{2,1,0:T(8,128)(2,1)S(1)} %get-tuple-element.55.cq_ref, bf16[2,128,384]{2,1,0:T(8,128)(2,1)S(1)} %get-tuple-element.56.cg_ref, ...), custom_call_target="tpu_custom_call" | custom-call | bytes 1024 | tf_op jit(solution)/shard_map/pallas_call | solution.py:405
  56.0 3.5 %collective-permute-done.20.ret_ref = bf16[128,768]{1,0:T(8,128)(2,1)S(1)} collective-permute-done((bf16[128,768]{1,0:T(8,128)(2,1)S(1)}, bf16[128,768]{1,0:T(8,128)(2,1)S(1)}, u32[]{:S(2)}, u32[]{:S(2)}) %collective-permute-start.20) | collective-permute-done | bytes 196640 | tf_op jit(solution)/shard_map/ppermute | solution.py:415
  60.9 2.1 %collective-permute-start.22 = (bf16[128,768]{1,0:T(8,128)(2,1)S(1)}, bf16[128,768]{1,0:T(8,128)(2,1)S(1)}, u32[]{:S(2)}, u32[]{:S(2)}) collective-permute-start(bf16[128,768]{1,0:T(8,128)(2,1)S(1)} %get-tuple-element.80), channel_id=1, source_target_pairs={{1,0},{2,1},{3,2},{4,3},{5,4},{6,5},{7,6},{8,7},{9,8},{10,9},{11,1... | collective-permute-start | bytes 589832 | tf_op jit(solution)/shard_map/ppermute | solution.py:417
  63.0 1.9 %shard_map.131.np_ref = f32[128,1536]{1,0:T(8,128)S(1)} custom-call(bf16[3,128,128]{2,1,0:T(8,128)(2,1)S(1)} %get-tuple-element.71.p_ref, bf16[3,128,256]{2,1,0:T(8,128)(2,1)S(1)} %get-tuple-element.72.ds_ref, bf16[2,128,384]{2,1,0:T(8,128)(2,1)S(1)} %get-tuple-element.55.cq_ref, bf16[2,128,384]{2,1,0:T(8,128)(2,1)S(1)} %get-tuple-element.56.cg_ref, ...), custom_call_target="tpu_custom_call" | custom-call | bytes 1024 | tf_op jit(solution)/shard_map/pallas_call | solution.py:405
  65.3 1.3 %shard_map.132 = bf16[1,128,1536]{2,1,0:T(8,128)(2,1)} custom-call(bf16[1,128,1536]{2,1,0:T(8,128)(2,1)S(1)} %copy-done, bf16[128,384]{1,0:T(8,128)(2,1)S(1)} %get-tuple-element.73.ctx_ref, bf16[1536,768]{1,0:T(8,128)(2,1)S(1)} %get-tuple-element.61.wqo, bf16[128,1536]{1,0:T(8,128)(2,1)S(1)} %collective-permute-done.21.lo_ret), custom_call_target="tpu_custom_call" | custom-call | bytes 1024 | tf_op jit(solution)/shard_map/pallas_call | solution.py:422
  66.6 2.2 %collective-permute-done.22.ret_ref = bf16[128,768]{1,0:T(8,128)(2,1)S(1)} collective-permute-done((bf16[128,768]{1,0:T(8,128)(2,1)S(1)}, bf16[128,768]{1,0:T(8,128)(2,1)S(1)}, u32[]{:S(2)}, u32[]{:S(2)}) %collective-permute-start.22) | collective-permute-done | bytes 196640 | tf_op jit(solution)/shard_map/ppermute | solution.py:417
  (56 shorter events, 15.5 us)
Async XLA Ops:
  3.7 8.2 %collective-permute-start = (bf16[4,96,384]{2,1,0:T(8,128)(2,1)}, bf16[4,96,384]{2,1,0:T(8,128)(2,1)S(1)}, u32[]{:S(2)}, u32[]{:S(2)}) collective-permute-start(bf16[4,96,384]{2,1,0:T(8,128)(2,1)} %get-tuple-element.42.shard_ref), channel_id=1, source_target_pairs={{0,4},{1,5},{2,6},{3,7},{4,8},{5,9},{6,10},{7,11},{8,12},{9,13},{1... | collective-permute-start | bytes 884744 | tf_op jit(solution)/shard_map/ppermute | solution.py:298
  5.1 17.3 %collective-permute-start.5 = (bf16[144,1536]{1,0:T(8,128)(2,1)}, bf16[144,1536]{1,0:T(8,128)(2,1)S(1)}, u32[]{:S(2)}, u32[]{:S(2)}) collective-permute-start(bf16[144,1536]{1,0:T(8,128)(2,1)} %get-tuple-element.43.normed_ref), channel_id=1, source_target_pairs={{0,16},{16,0},{1,17},{17,1},{2,18},{18,2},{3,19},{19,3},{4,20},{20... | collective-permute-start | bytes 1327112 | tf_op jit(solution)/shard_map/ppermute | solution.py:312
  6.3 5.8 %collective-permute-start.7 = (bf16[4,96,384]{2,1,0:T(8,128)(2,1)}, bf16[4,96,384]{2,1,0:T(8,128)(2,1)S(1)}, u32[]{:S(2)}, u32[]{:S(2)}) collective-permute-start(bf16[4,96,384]{2,1,0:T(8,128)(2,1)} %get-tuple-element.42.shard_ref), channel_id=1, source_target_pairs={{0,1},{1,0},{2,3},{3,2},{4,5},{5,4},{6,7},{7,6},{8,9},{9,8},{10,11... | collective-permute-start | bytes 884744 | tf_op jit(solution)/shard_map/ppermute | solution.py:298
  7.5 8.8 %collective-permute-start.6 = (bf16[4,96,384]{2,1,0:T(8,128)(2,1)}, bf16[4,96,384]{2,1,0:T(8,128)(2,1)S(1)}, u32[]{:S(2)}, u32[]{:S(2)}) collective-permute-start(bf16[4,96,384]{2,1,0:T(8,128)(2,1)} %get-tuple-element.42.shard_ref), channel_id=1, source_target_pairs={{0,2},{1,3},{2,0},{3,1},{4,6},{5,7},{6,4},{7,5},{8,10},{9,11},{10,... | collective-permute-start | bytes 884744 | tf_op jit(solution)/shard_map/ppermute | solution.py:298
  7.8 10.9 %collective-permute-start.2 = (bf16[4,96,384]{2,1,0:T(8,128)(2,1)}, bf16[4,96,384]{2,1,0:T(8,128)(2,1)S(1)}, u32[]{:S(2)}, u32[]{:S(2)}) collective-permute-start(bf16[4,96,384]{2,1,0:T(8,128)(2,1)} %get-tuple-element.42.shard_ref), channel_id=1, source_target_pairs={{0,12},{1,13},{2,14},{3,15},{4,0},{5,1},{6,2},{7,3},{8,4},{9,5},{1... | collective-permute-start | bytes 884744 | tf_op jit(solution)/shard_map/ppermute | solution.py:298
  12.0 10.5 %collective-permute-start.9 = (bf16[4,96,384]{2,1,0:T(8,128)(2,1)S(1)}, bf16[4,96,384]{2,1,0:T(8,128)(2,1)S(1)}, u32[]{:S(2)}, u32[]{:S(2)}) collective-permute-start(bf16[4,96,384]{2,1,0:T(8,128)(2,1)S(1)} %collective-permute-done.rest_4_), channel_id=1, source_target_pairs={{0,2},{1,3},{2,0},{3,1},{4,6},{5,7},{6,4},{7,5},{8,10},{9,11},{10,... | collective-permute-start | bytes 884744 | tf_op jit(solution)/shard_map/ppermute | solution.py:298
  12.1 11.6 %collective-permute-start.1 = (bf16[4,96,384]{2,1,0:T(8,128)(2,1)S(1)}, bf16[4,96,384]{2,1,0:T(8,128)(2,1)S(1)}, u32[]{:S(2)}, u32[]{:S(2)}) collective-permute-start(bf16[4,96,384]{2,1,0:T(8,128)(2,1)S(1)} %collective-permute-done.rest_4_), channel_id=1, source_target_pairs={{0,4},{1,5},{2,6},{3,7},{4,8},{5,9},{6,10},{7,11},{8,12},{9,13},{1... | collective-permute-start | bytes 884744 | tf_op jit(solution)/shard_map/ppermute | solution.py:298
  16.4 15.7 %collective-permute-start.4 = (bf16[128,1536]{1,0:T(8,128)(2,1)}, bf16[128,1536]{1,0:T(8,128)(2,1)S(1)}, u32[]{:S(2)}, u32[]{:S(2)}) collective-permute-start(bf16[128,1536]{1,0:T(8,128)(2,1)} %bitcast.4), channel_id=1, source_target_pairs={{0,16},{16,0},{1,17},{17,1},{2,18},{18,2},{3,19},{19,3},{4,20},{20... | collective-permute-start | bytes 1179656 | tf_op jit(solution)/shard_map/ppermute | solution.py:312
  18.7 5.2 %collective-permute-start.8 = (bf16[4,96,384]{2,1,0:T(8,128)(2,1)S(1)}, bf16[4,96,384]{2,1,0:T(8,128)(2,1)S(1)}, u32[]{:S(2)}, u32[]{:S(2)}) collective-permute-start(bf16[4,96,384]{2,1,0:T(8,128)(2,1)S(1)} %collective-permute-done.6.rest_1_), channel_id=1, source_target_pairs={{0,1},{1,0},{2,3},{3,2},{4,5},{5,4},{6,7},{7,6},{8,9},{9,8},{10,11... | collective-permute-start | bytes 884744 | tf_op jit(solution)/shard_map/ppermute | solution.py:298
  22.4 6.9 %collective-permute-start.16 = (bf16[4,96,384]{2,1,0:T(8,128)(2,1)S(1)}, bf16[4,96,384]{2,1,0:T(8,128)(2,1)S(1)}, u32[]{:S(2)}, u32[]{:S(2)}) collective-permute-start(bf16[4,96,384]{2,1,0:T(8,128)(2,1)S(1)} %collective-permute-done.2.rest_12_), channel_id=1, source_target_pairs={{0,1},{1,0},{2,3},{3,2},{4,5},{5,4},{6,7},{7,6},{8,9},{9,8},{10,11... | collective-permute-start | bytes 884744 | tf_op jit(solution)/shard_map/ppermute | solution.py:298
  22.5 8.0 %collective-permute-start.15 = (bf16[4,96,384]{2,1,0:T(8,128)(2,1)S(1)}, bf16[4,96,384]{2,1,0:T(8,128)(2,1)S(1)}, u32[]{:S(2)}, u32[]{:S(2)}) collective-permute-start(bf16[4,96,384]{2,1,0:T(8,128)(2,1)S(1)} %collective-permute-done.2.rest_12_), channel_id=1, source_target_pairs={{0,2},{1,3},{2,0},{3,1},{4,6},{5,7},{6,4},{7,5},{8,10},{9,11},{10,... | collective-permute-start | bytes 884744 | tf_op jit(solution)/shard_map/ppermute | solution.py:298
  23.7 8.4 %collective-permute-start.12 = (bf16[2,96,384]{2,1,0:T(8,128)(2,1)S(1)}, bf16[2,96,384]{2,1,0:T(8,128)(2,1)S(1)}, u32[]{:S(2)}, u32[]{:S(2)}) collective-permute-start(bf16[2,96,384]{2,1,0:T(8,128)(2,1)S(1)} %slice.7), channel_id=1, source_target_pairs={{0,4},{1,5},{2,6},{3,7},{4,8},{5,9},{6,10},{7,11},{8,12},{9,13},{1... | collective-permute-start | bytes 442376 | tf_op jit(solution)/shard_map/ppermute | solution.py:298
  23.8 11.7 %collective-permute-start.10 = (bf16[4,96,384]{2,1,0:T(8,128)(2,1)S(1)}, bf16[4,96,384]{2,1,0:T(8,128)(2,1)S(1)}, u32[]{:S(2)}, u32[]{:S(2)}) collective-permute-start(bf16[4,96,384]{2,1,0:T(8,128)(2,1)S(1)} %collective-permute-done.rest_4_), channel_id=1, source_target_pairs={{0,1},{1,0},{2,3},{3,2},{4,5},{5,4},{6,7},{7,6},{8,9},{9,8},{10,11... | collective-permute-start | bytes 884744 | tf_op jit(solution)/shard_map/ppermute | solution.py:298
  29.3 5.4 %collective-permute-start.3 = (bf16[2,96,384]{2,1,0:T(8,128)(2,1)S(1)}, bf16[2,96,384]{2,1,0:T(8,128)(2,1)S(1)}, u32[]{:S(2)}, u32[]{:S(2)}) collective-permute-start(bf16[2,96,384]{2,1,0:T(8,128)(2,1)S(1)} %slice.6), channel_id=1, source_target_pairs={{0,2},{1,3},{2,0},{3,1},{4,6},{5,7},{6,4},{7,5},{8,10},{9,11},{10,... | collective-permute-start | bytes 442376 | tf_op jit(solution)/shard_map/ppermute | solution.py:298
  30.4 5.1 %collective-permute-start.17 = (bf16[4,96,384]{2,1,0:T(8,128)(2,1)S(1)}, bf16[4,96,384]{2,1,0:T(8,128)(2,1)S(1)}, u32[]{:S(2)}, u32[]{:S(2)}) collective-permute-start(bf16[4,96,384]{2,1,0:T(8,128)(2,1)S(1)} %collective-permute-done.15.rest_13_), channel_id=1, source_target_pairs={{0,1},{1,0},{2,3},{3,2},{4,5},{5,4},{6,7},{7,6},{8,9},{9,8},{10,11... | collective-permute-start | bytes 884744 | tf_op jit(solution)/shard_map/ppermute | solution.py:298
  32.1 4.5 %collective-permute-start.11 = (bf16[4,96,384]{2,1,0:T(8,128)(2,1)S(1)}, bf16[4,96,384]{2,1,0:T(8,128)(2,1)S(1)}, u32[]{:S(2)}, u32[]{:S(2)}) collective-permute-start(bf16[4,96,384]{2,1,0:T(8,128)(2,1)S(1)} %collective-permute-done.9.rest_5_), channel_id=1, source_target_pairs={{0,1},{1,0},{2,3},{3,2},{4,5},{5,4},{6,7},{7,6},{8,9},{9,8},{10,11... | collective-permute-start | bytes 884744 | tf_op jit(solution)/shard_map/ppermute | solution.py:298
  32.1 4.5 %collective-permute-start.13 = (bf16[4,96,384]{2,1,0:T(8,128)(2,1)S(1)}, bf16[4,96,384]{2,1,0:T(8,128)(2,1)S(1)}, u32[]{:S(2)}, u32[]{:S(2)}) collective-permute-start(bf16[4,96,384]{2,1,0:T(8,128)(2,1)S(1)} %collective-permute-done.1.rest_8_), channel_id=1, source_target_pairs={{0,1},{1,0},{2,3},{3,2},{4,5},{5,4},{6,7},{7,6},{8,9},{9,8},{10,11... | collective-permute-start | bytes 884744 | tf_op jit(solution)/shard_map/ppermute | solution.py:298
  34.7 1.9 %collective-permute-start.14 = (bf16[2,96,384]{2,1,0:T(8,128)(2,1)S(1)}, bf16[2,96,384]{2,1,0:T(8,128)(2,1)S(1)}, u32[]{:S(2)}, u32[]{:S(2)}) collective-permute-start(bf16[2,96,384]{2,1,0:T(8,128)(2,1)S(1)} %collective-permute-done.12.rest_9_), channel_id=1, source_target_pairs={{0,1},{1,0},{2,3},{3,2},{4,5},{5,4},{6,7},{7,6},{8,9},{9,8},{10,11... | collective-permute-start | bytes 442376 | tf_op jit(solution)/shard_map/ppermute | solution.py:298
  38.2 9.4 %collective-permute-start.19 = (bf16[2,128,768]{2,1,0:T(8,128)(2,1)S(1)}, bf16[2,128,768]{2,1,0:T(8,128)(2,1)S(1)}, u32[]{:S(2)}, u32[]{:S(2)}) collective-permute-start(bf16[2,128,768]{2,1,0:T(8,128)(2,1)S(1)} %get-tuple-element.53.kv_ref), channel_id=1, source_target_pairs={{0,1},{1,2},{2,3},{3,4},{4,5},{5,6},{6,7},{7,8},{8,9},{9,10},{10,1... | collective-permute-start | bytes 1179656 | tf_op jit(solution)/shard_map/ppermute | solution.py:384
  42.9 1.4 %collective-permute-start.18 = (bf16[2,96,384]{2,1,0:T(8,128)(2,1)S(1)}, bf16[2,96,384]{2,1,0:T(8,128)(2,1)S(1)}, u32[]{:S(2)}, u32[]{:S(2)}) collective-permute-start(bf16[2,96,384]{2,1,0:T(8,128)(2,1)S(1)} %collective-permute-done.3.rest_9_), channel_id=1, source_target_pairs={{0,1},{1,0},{2,3},{3,2},{4,5},{5,4},{6,7},{7,6},{8,9},{9,8},{10,11... | collective-permute-start | bytes 442376 | tf_op jit(solution)/shard_map/ppermute | solution.py:298
  49.5 11.4 %collective-permute-start.21 = (bf16[128,1536]{1,0:T(8,128)(2,1)S(1)}, bf16[128,1536]{1,0:T(8,128)(2,1)S(1)}, u32[]{:S(2)}, u32[]{:S(2)}) collective-permute-start(bf16[128,1536]{1,0:T(8,128)(2,1)S(1)} %shard_map.127), channel_id=1, source_target_pairs={{0,16},{16,0},{1,17},{17,1},{2,18},{18,2},{3,19},{19,3},{4,20},{20... | collective-permute-start | bytes 1179656 | tf_op jit(solution)/shard_map/ppermute | solution.py:312
  50.6 8.9 %collective-permute-start.20 = (bf16[128,768]{1,0:T(8,128)(2,1)S(1)}, bf16[128,768]{1,0:T(8,128)(2,1)S(1)}, u32[]{:S(2)}, u32[]{:S(2)}) collective-permute-start(bf16[128,768]{1,0:T(8,128)(2,1)S(1)} %get-tuple-element.70), channel_id=1, source_target_pairs={{1,0},{2,1},{3,2},{4,3},{5,4},{6,5},{7,6},{8,7},{9,8},{10,9},{11,1... | collective-permute-start | bytes 589832 | tf_op jit(solution)/shard_map/ppermute | solution.py:415
  60.4 9.3 %collective-permute-start.23 = (bf16[128,1536]{1,0:T(8,128)(2,1)S(1)}, bf16[128,1536]{1,0:T(8,128)(2,1)S(1)}, u32[]{:S(2)}, u32[]{:S(2)}) collective-permute-start(bf16[128,1536]{1,0:T(8,128)(2,1)S(1)} %shard_map.130), channel_id=1, source_target_pairs={{0,16},{16,0},{1,17},{17,1},{2,18},{18,2},{3,19},{19,3},{4,20},{20... | collective-permute-start | bytes 1179656 | tf_op jit(solution)/shard_map/ppermute | solution.py:312
  60.9 7.9 %collective-permute-start.22 = (bf16[128,768]{1,0:T(8,128)(2,1)S(1)}, bf16[128,768]{1,0:T(8,128)(2,1)S(1)}, u32[]{:S(2)}, u32[]{:S(2)}) collective-permute-start(bf16[128,768]{1,0:T(8,128)(2,1)S(1)} %get-tuple-element.80), channel_id=1, source_target_pairs={{1,0},{2,1},{3,2},{4,3},{5,4},{6,5},{7,6},{8,7},{9,8},{10,9},{11,1... | collective-permute-start | bytes 589832 | tf_op jit(solution)/shard_map/ppermute | solution.py:417
  (8 other events, 41.1 us)

commit v6 on v5

--- a/solution.py
+++ b/solution.py
@@ -114,15 +114,15 @@
 
 
 def key_value_kernel(own_ref, oth_ref, *rest):
-    pieces, (weights, kv_ref, xs, flags, sems) = rest[:16], rest[16:]
+    pieces, (weights, kv_own, kv_oth, xs, flags, sems) = rest[:16], rest[16:]
     copies = fetch(pieces, (0,) * 16, weights, sems)
     flags[0] = own_ref[SEG:, :DH]
     flags[1] = oth_ref[SEG:, :DH]
     xs[0:SEG, :] = own_ref[0:SEG, :]
     xs[SEG:, :] = oth_ref[0:SEG, :]
     total = accumulate(xs, weights, copies, slice(0, 2 * HALF))
-    kv_ref[0] = total[:SEG].astype(BF16)
-    kv_ref[1] = total[SEG:].astype(BF16)
+    kv_own[...] = total[:SEG].astype(BF16)
+    kv_oth[...] = total[SEG:].astype(BF16)
 
 
 SCALE = DH**-0.5
@@ -139,7 +139,7 @@
     return jnp.concatenate(parts, axis=1)
 
 
-def query_kernel(xs, cot_own, cot_oth, cb_ref, pb_ref, kv_ref, pk_ref, *rest):
+def query_kernel(xs, cot_own, cot_oth, cb_ref, pb_ref, kv_own, kv_oth, pk_ref, *rest):
     pieces = rest[:16]
     weights, cq_ref, cg_ref, rel_ref, own_ref, dp_ref = rest[16:22]
     cots, sems = rest[22:]
@@ -154,18 +154,21 @@
     cg = dot(cots[...], weights[:, HALF:]).astype(BF16)
     row = lax.broadcasted_iota(jnp.int32, (SEG, SEG), 0)
     col = lax.broadcasted_iota(jnp.int32, (SEG, SEG), 1)
+    every = [(rec, h) for rec in range(2) for h in range(HEADS)]
+    rows = [slice(rec * SEG, (rec + 1) * SEG) for rec in range(2)]
+    kv = (kv_own, kv_oth)
+    rel = [dot(pq[rows[rec], head(h)], pk_ref[:, head(h)], NT) for rec, h in every]
+    own = [dot(cq[rows[rec], head(h)], kv[rec][:, head(h)], NT) for rec, h in every]
+    for rec, h in every:
+        dp_ref[rec, h] = dot(cg[rows[rec], head(h)], kv[rec][:, head(HEADS + h)], NT)
+    for n, (rec, h) in enumerate(every):
+        turned = pltpu.roll(rel[n], SEG + 1, 1, stride=1, stride_axis=0)
+        rel_ref[rec, h] = turned[:, :SEG]
+        s_own = (own[n] + turned[:, SEG:]) * SCALE
+        own_ref[rec, h] = jnp.where(col <= row, s_own, -jnp.inf)
     for rec in range(2):
-        rows = slice(rec * SEG, (rec + 1) * SEG)
-        cq_ref[rec] = cq[rows]
-        cg_ref[rec] = cg[rows]
-        for h in range(HEADS):
-            f, fv = head(h), head(HEADS + h)
-            rel = dot(pq[rows, f], pk_ref[:, f], NT)
-            rel = pltpu.roll(rel, SEG + 1, 1, stride=1, stride_axis=0)
-            rel_ref[rec, h] = rel[:, :SEG]
-            s_own = (dot(cq[rows, f], kv_ref[rec, :, f], NT) + rel[:, SEG:]) * SCALE
-            own_ref[rec, h] = jnp.where(col <= row, s_own, -jnp.inf)
-            dp_ref[rec, h] = dot(cg[rows, f], kv_ref[rec, :, fv], NT)
+        cq_ref[rec] = cq[rows[rec]]
+        cg_ref[rec] = cg[rows[rec]]
 
 
 def memory_kernel(
@@ -173,64 +176,70 @@
     p_ref, ds_ref, dmem_ref, ctx_ref,
 ):
     flag = flags[rec, 0:1, :].astype(F32)
-    for h in range(HEADS):
+    heads = range(HEADS)
+    s_mem = [dot(cq_ref[rec, :, head(h)], mem_ref[:, head(h)], NT) for h in heads]
+    dp_mem = [dot(cg_ref[rec, :, head(h)], mem_ref[:, head(HEADS + h)], NT) for h in heads]
+    parts = []
+    for h in heads:
+        s = jnp.where(flag == 0, (s_mem[h] + rel_ref[rec, h]) * SCALE, -jnp.inf)
+        s_own, dp_own = own_ref[rec, h], dp_ref[rec, h]
+        peak = jnp.max(jnp.maximum(s, s_own), axis=-1, keepdims=True)
+        e_mem, e_own = jnp.exp(s - peak), jnp.exp(s_own - peak)
+        norm = 1.0 / jnp.sum(e_mem + e_own, axis=-1, keepdims=True)
+        inner = jnp.sum(e_mem * dp_mem[h] + e_own * dp_own, axis=-1, keepdims=True) * norm
+        a_mem, a_own = e_mem * norm, e_own * norm
+        p_mem, p_own = a_mem.astype(BF16), a_own.astype(BF16)
+        ds_mem = (a_mem * (dp_mem[h] - inner) * SCALE).astype(BF16)
+        ds_own = (a_own * (dp_own - inner) * SCALE).astype(BF16)
+        p_ref[h] = p_own
+        ds_ref[:, 2 * SEG * h : 2 * SEG * h + SEG] = ds_mem
+        ds_ref[:, 2 * SEG * h + SEG : 2 * SEG * (h + 1)] = ds_own
+        parts.append((p_mem, p_own, ds_mem))
+    for h in heads:
         f, fv = head(h), head(HEADS + h)
-        cq, g = cq_ref[rec, :, f], cg_ref[rec, :, f]
-        s_own = own_ref[rec, h]
-        s_mem = (dot(cq, mem_ref[rec, :, f], NT) + rel_ref[rec, h]) * SCALE
-        s_mem = jnp.where(flag == 0, s_mem, -jnp.inf)
-        dp_mem = dot(g, mem_ref[rec, :, fv], NT)
-        peak = jnp.max(jnp.maximum(s_mem, s_own), axis=-1, keepdims=True)
-        e_mem = jnp.exp(s_mem - peak)
-        e_own = jnp.exp(s_own - peak)
-        norm = 1.0 / jnp.sum(e_mem + e_own, axis=-1, keepdims=True)
-        a_mem, a_own = e_mem * norm, e_own * norm
-        dp_own = dp_ref[rec, h]
-        inner = jnp.sum(a_mem * dp_mem + a_own * dp_own, axis=-1, keepdims=True)
-        p_mem, p_own = a_mem.astype(BF16), a_own.astype(BF16)
-        ctx = dot(p_mem, mem_ref[rec, :, fv]) + dot(p_own, kv_ref[rec, :, fv])
+        p_mem, p_own, ds_mem = parts[h]
+        dmem_ref[:, f] = dot(ds_mem, cq_ref[rec, :, f], TN).astype(BF16)
+        dmem_ref[:, fv] = dot(p_mem, cg_ref[rec, :, f], TN).astype(BF16)
+        ctx = dot(p_mem, mem_ref[:, fv]) + dot(p_own, kv_ref[:, fv])
         ctx_ref[:, f] = ctx.astype(BF16)
-        ds_mem = (a_mem * (dp_mem - inner) * SCALE).astype(BF16)
-        p_ref[h] = p_own
-        ds_ref[h, :, :SEG] = ds_mem
-        ds_ref[h, :, SEG:] = (a_own * (dp_own - inner) * SCALE).astype(BF16)
-        dmem_ref[:, f] = dot(ds_mem, cq, TN).astype(BF16)
-        dmem_ref[:, fv] = dot(p_mem, g, TN).astype(BF16)
 
 
 def grad_kernel(
-    rec, p_ref, ds_ref, cq_ref, cg_ref, kv_ref, mem_ref, pk_ref, wkv, wqo, np_ref, dq, dkv
+    rec, p_ref, ds_ref, cq_ref, cg_ref, kv_ref, mem_ref, pk_ref, wqo, np_ref, dkv, dq
 ):
     row = lax.broadcasted_iota(jnp.int32, (SEG, SEG), 0)
     col = lax.broadcasted_iota(jnp.int32, (SEG, SEG), 1)
     flip = jnp.where(row + col == SEG - 1, 1.0, 0.0).astype(BF16)
-    for h in range(HEADS):
+    both = [slice(2 * SEG * h, 2 * SEG * (h + 1)) for h in range(HEADS)]
+    rel = dot(flip, ds_ref[...])
+    rel = [pltpu.roll(rel[:, w], 0, 1, stride=1, stride_axis=0).astype(BF16) for w in both]
+    rel = dot(flip, jnp.concatenate(rel, axis=1)).astype(BF16)
+    for h, w in enumerate(both):
         f, fv = head(h), head(HEADS + h)
-        ds = ds_ref[h]
-        rel = pltpu.roll(dot(flip, ds), 0, 1, stride=1, stride_axis=0).astype(BF16)
-        rel = dot(flip, rel).astype(BF16)
-        total = dot(ds[:, :SEG], mem_ref[rec, :, f]) + dot(ds[:, SEG:], kv_ref[rec, :, f])
-        dq[:, f] = (total + dot(rel, pk_ref[:, f])).astype(BF16)
-        dkv[:, f] = dot(ds[:, SEG:], cq_ref[rec, :, f], TN).astype(BF16)
+        ds_mem, ds_own = ds_ref[:, w][:, :SEG], ds_ref[:, w][:, SEG:]
+        dkv[:, f] = dot(ds_own, cq_ref[rec, :, f], TN).astype(BF16)
         dkv[:, fv] = dot(p_ref[h], cg_ref[rec, :, f], TN).astype(BF16)
-    np_ref[...] = dot(dq[...], wqo[:, :HALF], NT) + dot(dkv[...], wkv[...], NT)
-
-
-def returned_kernel(np_ref, ret_ref, wkv, out_ref):
-    out_ref[...] = (np_ref[...] + dot(ret_ref[...], wkv[...], NT)).astype(out_ref.dtype)
+        total = dot(ds_mem, mem_ref[:, f]) + dot(ds_own, kv_ref[:, f])
+        dq[:, f] = (total + dot(rel[:, w], pk_ref[:, f])).astype(BF16)
+    np_ref[...] = dot(dq[...], wqo[:, :HALF], NT)
+
+
+def returned_kernel(np_ref, dkv_ref, ret_ref, wkv, out_ref):
+    dkv = (dkv_ref[...].astype(F32) + ret_ref[...].astype(F32)).astype(BF16)
+    out_ref[...] = (np_ref[...] + dot(dkv, wkv[...], NT)).astype(out_ref.dtype)
 
 
 def partial_output_kernel(ctx_ref, wqo, out_ref):
     out_ref[...] = dot(ctx_ref[...], wqo[:, HALF:], NT).astype(BF16)
 
 
-def output_kernel(x_ref, ctx_ref, wqo, lo_ret, out_ref, held):
+def output_kernel(x_ref, ctx_ref, wqo, lo_ret, out_ref):
     z, _, _ = place()
-    held[...] = dot(ctx_ref[...], wqo[:, HALF:], NT)
+    total = dot(ctx_ref[...], wqo[:, HALF:], NT)
     for r in range(ZS):
         cols, there = slice(r * BLK, (r + 1) * BLK), plane_columns(z, r)
-        total = held[:, cols] + lo_ret[:, cols].astype(F32)
-        out_ref[0, :, there] = (x_ref[0, :, there].astype(F32) + total).astype(BF16)
+        part = total[:, cols] + lo_ret[:, cols].astype(F32)
+        out_ref[0, :, there] = (x_ref[0, :, there].astype(F32) + part).astype(BF16)
 
 
 def hat_kernel(x_ref, gain_ref, cot_ref, hat_ref, rstd_ref, gain_out, cot_out, held):
@@ -367,11 +376,12 @@
     qo_pieces[9], qo_pieces[11] = w2y_qo, w2y_qo_there
 
     half = shape(SEG, 2 * HALF)
-    wkv, kv, xs, flags = call(
+    wkv, kv, kv_oth, xs, flags = call(
         key_value_kernel,
         (
             shape(D, 2 * HALF),
-            shape(2, SEG, 2 * HALF),
+            half,
+            half,
             shape(2 * SEG, D),
             shape(2, 16, DH),
         ),
@@ -381,22 +391,23 @@
     steps = lax.axis_size("tm")
     onward = [(i, i + 1) for i in range(steps - 1)]
     back = [(i + 1, i) for i in range(steps - 1)]
+    mem_oth = lax.ppermute(kv_oth, "tm", onward)
     mem = lax.ppermute(kv, "tm", onward)
     blocks = shape(2, HEADS, SEG, SEG, dtype=F32)
     wqo, cq, cg, rel, s_own, dp_own = call(
         query_kernel,
         (shape(D, 2 * HALF), shape(2, SEG, HALF), shape(2, SEG, HALF), blocks, blocks, blocks),
         [pltpu.VMEM((2 * SEG, D), BF16), pltpu.SemaphoreType.DMA((32,))],
-        [VM] * 7 + [ANY] * 16,
+        [VM] * 8 + [ANY] * 16,
     )(
         xs, cot, cot_oth, content_bias.reshape(H, DH), position_bias.reshape(H, DH),
-        kv, pk, *qo_pieces,
+        kv, kv_oth, pk, *qo_pieces,
     )
 
     def memory(rec, kv_rows, mem_rows):
         return call(
             functools.partial(memory_kernel, rec),
-            (shape(HEADS, SEG, SEG), shape(HEADS, SEG, 2 * SEG), half, shape(SEG, HALF)),
+            (shape(HEADS, SEG, SEG), shape(SEG, HEADS * 2 * SEG), half, shape(SEG, HALF)),
             (),
             [VM] * 8,
         )(flags, cq, cg, rel, s_own, dp_own, kv_rows, mem_rows)
@@ -404,26 +415,28 @@
     def grads(rec, p, ds, kv_rows, mem_rows):
         return call(
             functools.partial(grad_kernel, rec),
-            shape(SEG, D, dtype=F32),
-            [pltpu.VMEM((SEG, HALF), BF16), pltpu.VMEM((SEG, 2 * HALF), BF16)],
-            [VM] * 9,
-        )(p, ds, cq, cg, kv_rows, mem_rows, pk, wkv, wqo)
-
-    p_oth, ds_oth, dmem_oth, ctx_oth = memory(1, kv, mem)
+            (shape(SEG, D, dtype=F32), half),
+            [pltpu.VMEM((SEG, HALF), BF16)],
+            [VM] * 8,
+        )(p, ds, cq, cg, kv_rows, mem_rows, pk, wqo)
+
+    p_oth, ds_oth, dmem_oth, ctx_oth = memory(1, kv_oth, mem_oth)
     lo_oth = call(partial_output_kernel, shape(SEG, D), (), [VM] * 2)(ctx_oth, wqo)
     lo_ret = other(lo_oth)
     ret_oth = lax.ppermute(dmem_oth, "tm", back)
-    p, ds, dmem, ctx = memory(0, kv, after(mem, lo_oth))
+    partial_oth, dkv_oth = grads(1, after(p_oth, lo_oth), ds_oth, kv_oth, mem_oth)
+    np_oth = call(returned_kernel, shape(SEG, D), (), [VM] * 4)(
+        partial_oth, dkv_oth, ret_oth, wkv
+    )
+    np_ret = other(np_oth)
+    p, ds, dmem, ctx = memory(0, kv, after(mem, np_oth))
     ret = lax.ppermute(after(dmem, lo_ret), "tm", back)
-    partial_oth = grads(1, after(p_oth, dmem), ds_oth, kv, mem)
-    np_oth = call(returned_kernel, shape(SEG, D), (), [VM] * 3)(partial_oth, ret_oth, wkv)
-    np_ret = other(np_oth)
-    partial = grads(0, after(p, np_oth), ds, kv, mem)
+    partial, dkv = grads(0, after(p, dmem), ds, kv, mem)
     layer_out = call(
-        output_kernel, shape(1, SEG, D), [pltpu.VMEM((SEG, D), F32)], [VM] * 4
+        output_kernel, shape(1, SEG, D), (), [VM] * 4
     )(inputs, after(ctx, partial), wqo, lo_ret)
-    np_own = call(returned_kernel, shape(SEG, D, dtype=F32), (), [VM] * 3)(
-        after(partial, layer_out), ret, wkv
+    np_own = call(returned_kernel, shape(SEG, D, dtype=F32), (), [VM] * 4)(
+        after(partial, layer_out), dkv, ret, wkv
     )
     hat = call(
         hat_kernel,

time: 72 us -> 69.8 us (0.969); the launches traced: 70.8 us -> 69.5 us
  starting transfers between devices: 31.3 us -> 36.6 us
  waiting for transfers between devices: 18.1 us -> 14.3 us
  Pallas kernels: 17.9 us -> 14.9 us
    ppermute x0 -> x1, starting transfers between devices: none -> 4.74 us  [split_heads(): mem_oth = lax.ppermute(kv_oth, 'tm', onward)]
    ppermute x1, waiting for transfers between devices: 3.46 us -> 0.47 us  [split_heads(): ret_oth = lax.ppermute(dmem_oth, 'tm', back)]
    pallas_call x6, Pallas kernels: 8.46 us -> 6.75 us  [the longest x2 2.08 us: grads(): call(functools.partial(grad_kernel, rec), (shape(SEG, D, dtype=F32), half...]
    pallas_call x2, Pallas kernels: 2.64 us -> 1.46 us  [memory(): call(functools.partial(memory_kernel, rec), (shape(HEADS, SEG, SEG), shap...]
    ppermute x1, starting transfers between devices: 2.1 us -> 3.18 us  [split_heads(): ret = lax.ppermute(after(dmem, lo_ret), 'tm', back)]
    ppermute x1, waiting for transfers between devices: 0.97 us -> 0.01 us  [split_heads(): mem = lax.ppermute(kv, 'tm', onward)]
  transfers between devices with their start and end apart: 24 -> 25, of which waited for: 9 -> 8; matrix products, arithmetic and copies ran while one was open for 0% -> 0% of each run, Pallas kernels for 15% -> 12%
where the time goes in v6:
time: 69.8 us; the launch traced here: 69.5 us
  starting transfers between devices  36.6 us (52%)
  Pallas kernels  14.9 us (21%)
  waiting for transfers between devices  14.3 us (20%)
  local copies, waits for them, and re-layouts  2.03 us (3%)
  between operations  1.53 us (2%)
    ppermute x17, starting transfers between devices, moved_by(): return lambda block: lax.ppermute(block, 'tm', route)  19.2 us
    ppermute x17, waiting for transfers between devices, moved_by(): return lambda block: lax.ppermute(block, 'tm', route)  11.5 us
    ppermute x1, starting transfers between devices, split_heads(): mem_oth = lax.ppermute(kv_oth, 'tm', onward)  4.74 us
    ppermute x1, starting transfers between devices, split_heads(): mem = lax.ppermute(kv, 'tm', onward)  4.12 us
    ppermute x1, starting transfers between devices, split_heads(): ret = lax.ppermute(after(dmem, lo_ret), 'tm', back)  3.18 us
    ppermute x4, starting transfers between devices, other(): return lax.ppermute(block, 'grp', [(0, 1), (1, 0)])  3.06 us
    pallas_call x1, Pallas kernels, split_heads(): call(prepare_kernel, (shape(4, ROWS, HALF), shape(SEG + 16, D), shape(2 *...  2.45 us
    ppermute x1, waiting for transfers between devices, split_heads(): ret = lax.ppermute(after(dmem, lo_ret), 'tm', back)  2.39 us
  transfers between devices with their start and end apart: 25, of which 8 were waited for; matrix products, arithmetic and copies ran while one was open for 0% of the time, Pallas kernels for 12%

profile of v6, /device:TPU:21, one launch (start us, length us, event | category | flops | bytes accessed | tf_op | source)
XLA Modules:
  0.0 69.5 jit_solution(7583043718227448469)
XLA Ops:
  1.3 2.4 %shard_map.122 = (bf16[4,96,384]{2,1,0:T(8,128)(2,1)}, bf16[144,1536]{1,0:T(8,128)(2,1)}, bf16[256,384]{1,0:T(8,128)(2,1)}) custom-call(bf16[96,384]{1,0:T(8,128)(2,1)} %k_ref.1, bf16[96,384]{1,0:T(8,128)(2,1)} %v_ref.1, bf16[96,384]{1,0:T(8,128)(2,1)} %q_ref.1, bf16[96,384]{1,0:T(8,128)(2,1)} %o_ref.1, bf16[1,128,1536]{2,1,0:T(8,128)(2,1)} %x_ref.5, ...), custom_call_target="tpu_custom_call" | custom-call | bytes 1024 | tf_op jit(solution)/shard_map/pallas_call | solution.py:339
  3.7 1.4 %collective-permute-start = (bf16[4,96,384]{2,1,0:T(8,128)(2,1)}, bf16[4,96,384]{2,1,0:T(8,128)(2,1)S(1)}, u32[]{:S(2)}, u32[]{:S(2)}) collective-permute-start(bf16[4,96,384]{2,1,0:T(8,128)(2,1)} %get-tuple-element.47.shard_ref), channel_id=1, source_target_pairs={{0,4},{1,5},{2,6},{3,7},{4,8},{5,9},{6,10},{7,11},{8,12},{9,13},{1... | collective-permute-start | bytes 884744 | tf_op jit(solution)/shard_map/ppermute | solution.py:307
  5.1 1.2 %collective-permute-start.5 = (bf16[144,1536]{1,0:T(8,128)(2,1)}, bf16[144,1536]{1,0:T(8,128)(2,1)S(1)}, u32[]{:S(2)}, u32[]{:S(2)}) collective-permute-start(bf16[144,1536]{1,0:T(8,128)(2,1)} %get-tuple-element.48.normed_ref), channel_id=1, source_target_pairs={{0,16},{16,0},{1,17},{17,1},{2,18},{18,2},{3,19},{19,3},{4,20},{20... | collective-permute-start | bytes 1327112 | tf_op jit(solution)/shard_map/ppermute | solution.py:321
  6.3 1.2 %collective-permute-start.7 = (bf16[4,96,384]{2,1,0:T(8,128)(2,1)}, bf16[4,96,384]{2,1,0:T(8,128)(2,1)S(1)}, u32[]{:S(2)}, u32[]{:S(2)}) collective-permute-start(bf16[4,96,384]{2,1,0:T(8,128)(2,1)} %get-tuple-element.47.shard_ref), channel_id=1, source_target_pairs={{0,1},{1,0},{2,3},{3,2},{4,5},{5,4},{6,7},{7,6},{8,9},{9,8},{10,11... | collective-permute-start | bytes 884744 | tf_op jit(solution)/shard_map/ppermute | solution.py:307
  10.0 2.0 %collective-permute-done.rest_4_ = bf16[4,96,384]{2,1,0:T(8,128)(2,1)S(1)} collective-permute-done((bf16[4,96,384]{2,1,0:T(8,128)(2,1)}, bf16[4,96,384]{2,1,0:T(8,128)(2,1)S(1)}, u32[]{:S(2)}, u32[]{:S(2)}) %collective-permute-start) | collective-permute-done | bytes 294944 | tf_op jit(solution)/shard_map/ppermute | solution.py:307
  12.1 1.3 %collective-permute-start.1 = (bf16[4,96,384]{2,1,0:T(8,128)(2,1)S(1)}, bf16[4,96,384]{2,1,0:T(8,128)(2,1)S(1)}, u32[]{:S(2)}, u32[]{:S(2)}) collective-permute-start(bf16[4,96,384]{2,1,0:T(8,128)(2,1)S(1)} %collective-permute-done.rest_4_), channel_id=1, source_target_pairs={{0,4},{1,5},{2,6},{3,7},{4,8},{5,9},{6,10},{7,11},{8,12},{9,13},{1... | collective-permute-start | bytes 884744 | tf_op jit(solution)/shard_map/ppermute | solution.py:307
  13.4 3.0 %collective-permute-done.6.rest_1_ = bf16[4,96,384]{2,1,0:T(8,128)(2,1)S(1)} collective-permute-done((bf16[4,96,384]{2,1,0:T(8,128)(2,1)}, bf16[4,96,384]{2,1,0:T(8,128)(2,1)S(1)}, u32[]{:S(2)}, u32[]{:S(2)}) %collective-permute-start.6) | collective-permute-done | bytes 294944 | tf_op jit(solution)/shard_map/ppermute | solution.py:307
  16.6 2.0 %collective-permute-done.2.rest_12_ = bf16[4,96,384]{2,1,0:T(8,128)(2,1)S(1)} collective-permute-done((bf16[4,96,384]{2,1,0:T(8,128)(2,1)}, bf16[4,96,384]{2,1,0:T(8,128)(2,1)S(1)}, u32[]{:S(2)}, u32[]{:S(2)}) %collective-permute-start.2) | collective-permute-done | bytes 294944 | tf_op jit(solution)/shard_map/ppermute | solution.py:307
  18.7 3.7 %collective-permute-start.8 = (bf16[4,96,384]{2,1,0:T(8,128)(2,1)S(1)}, bf16[4,96,384]{2,1,0:T(8,128)(2,1)S(1)}, u32[]{:S(2)}, u32[]{:S(2)}) collective-permute-start(bf16[4,96,384]{2,1,0:T(8,128)(2,1)S(1)} %collective-permute-done.6.rest_1_), channel_id=1, source_target_pairs={{0,1},{1,0},{2,3},{3,2},{4,5},{5,4},{6,7},{7,6},{8,9},{9,8},{10,11... | collective-permute-start | bytes 884744 | tf_op jit(solution)/shard_map/ppermute | solution.py:307
  22.5 1.2 %collective-permute-start.15 = (bf16[4,96,384]{2,1,0:T(8,128)(2,1)S(1)}, bf16[4,96,384]{2,1,0:T(8,128)(2,1)S(1)}, u32[]{:S(2)}, u32[]{:S(2)}) collective-permute-start(bf16[4,96,384]{2,1,0:T(8,128)(2,1)S(1)} %collective-permute-done.2.rest_12_), channel_id=1, source_target_pairs={{0,2},{1,3},{2,0},{3,1},{4,6},{5,7},{6,4},{7,5},{8,10},{9,11},{10,... | collective-permute-start | bytes 884744 | tf_op jit(solution)/shard_map/ppermute | solution.py:307
  23.8 5.4 %collective-permute-start.10 = (bf16[4,96,384]{2,1,0:T(8,128)(2,1)S(1)}, bf16[4,96,384]{2,1,0:T(8,128)(2,1)S(1)}, u32[]{:S(2)}, u32[]{:S(2)}) collective-permute-start(bf16[4,96,384]{2,1,0:T(8,128)(2,1)S(1)} %collective-permute-done.rest_4_), channel_id=1, source_target_pairs={{0,1},{1,0},{2,3},{3,2},{4,5},{5,4},{6,7},{7,6},{8,9},{9,8},{10,11... | collective-permute-start | bytes 884744 | tf_op jit(solution)/shard_map/ppermute | solution.py:307
  29.3 1.2 %collective-permute-start.3 = (bf16[2,96,384]{2,1,0:T(8,128)(2,1)S(1)}, bf16[2,96,384]{2,1,0:T(8,128)(2,1)S(1)}, u32[]{:S(2)}, u32[]{:S(2)}) collective-permute-start(bf16[2,96,384]{2,1,0:T(8,128)(2,1)S(1)} %slice.6), channel_id=1, source_target_pairs={{0,2},{1,3},{2,0},{3,1},{4,6},{5,7},{6,4},{7,5},{8,10},{9,11},{10,... | collective-permute-start | bytes 442376 | tf_op jit(solution)/shard_map/ppermute | solution.py:307
  30.4 1.6 %collective-permute-start.17 = (bf16[4,96,384]{2,1,0:T(8,128)(2,1)S(1)}, bf16[4,96,384]{2,1,0:T(8,128)(2,1)S(1)}, u32[]{:S(2)}, u32[]{:S(2)}) collective-permute-start(bf16[4,96,384]{2,1,0:T(8,128)(2,1)S(1)} %collective-permute-done.15.rest_13_), channel_id=1, source_target_pairs={{0,1},{1,0},{2,3},{3,2},{4,5},{5,4},{6,7},{7,6},{8,9},{9,8},{10,11... | collective-permute-start | bytes 884744 | tf_op jit(solution)/shard_map/ppermute | solution.py:307
  32.6 2.1 %collective-permute-done.3.rest_9_ = bf16[2,96,384]{2,1,0:T(8,128)(2,1)S(1)} collective-permute-done((bf16[2,96,384]{2,1,0:T(8,128)(2,1)S(1)}, bf16[2,96,384]{2,1,0:T(8,128)(2,1)S(1)}, u32[]{:S(2)}, u32[]{:S(2)}) %collective-permute-start.3) | collective-permute-done | bytes 147488 | tf_op jit(solution)/shard_map/ppermute | solution.py:307
  36.6 1.6 %shard_map.124 = (bf16[1536,768]{1,0:T(8,128)(2,1)S(1)}, bf16[128,768]{1,0:T(8,128)(2,1)S(1)}, bf16[128,768]{1,0:T(8,128)(2,1)S(1)}, bf16[256,1536]{1,0:T(8,128)(2,1)S(1)}, bf16[2,16,128]{2,1,0:T(8,128)(2,1)S(1)}) custom-call(bf16[144,1536]{1,0:T(8,128)(2,1)S(1)} %get-tuple-element.54.own_ref, bf16[144,1536]{1,0:T(8,128)(2,1)S(1)} %collective-permute-done.5.oth_ref, ...), custom_call_target="tpu_custom_call" | custom-call | bytes 1024 | tf_op jit(solution)/shard_map/pallas_call | solution.py:379
  38.2 4.7 %collective-permute-start.20 = (bf16[128,768]{1,0:T(8,128)(2,1)S(1)}, bf16[128,768]{1,0:T(8,128)(2,1)S(1)}, u32[]{:S(2)}, u32[]{:S(2)}) collective-permute-start(bf16[128,768]{1,0:T(8,128)(2,1)S(1)} %get-tuple-element.59.kv_oth.kv_ref), channel_id=1, source_target_pairs={{0,1},{1,2},{2,3},{3,4},{4,5},{5,6},{6,7},{7,8},{8,9},{9,10},{10,1... | collective-permute-start | bytes 589832 | tf_op jit(solution)/shard_map/ppermute | solution.py:394
  43.0 1.4 %collective-permute-done.18.rest_11_ = bf16[2,96,384]{2,1,0:T(8,128)(2,1)S(1)} collective-permute-done((bf16[2,96,384]{2,1,0:T(8,128)(2,1)S(1)}, bf16[2,96,384]{2,1,0:T(8,128)(2,1)S(1)}, u32[]{:S(2)}, u32[]{:S(2)}) %collective-permute-start.18) | collective-permute-done | bytes 147488 | tf_op jit(solution)/shard_map/ppermute | solution.py:307
  44.4 2.2 %shard_map.125 = (bf16[1536,768]{1,0:T(8,128)(2,1)S(1)}, bf16[2,128,384]{2,1,0:T(8,128)(2,1)S(1)}, bf16[2,128,384]{2,1,0:T(8,128)(2,1)S(1)}, f32[2,3,128,128]{3,...) custom-call(bf16[256,1536]{1,0:T(8,128)(2,1)S(1)} %get-tuple-element.57.xs, ...), custom_call_target="tpu_custom_call" | custom-call | bytes 1024 | tf_op jit(solution)/shard_map/pallas_call | solution.py:397
  49.0 2.3 %collective-permute-start.21 = (bf16[128,768]{1,0:T(8,128)(2,1)S(1)}, bf16[128,768]{1,0:T(8,128)(2,1)S(1)}, u32[]{:S(2)}, u32[]{:S(2)}) collective-permute-start(bf16[128,768]{1,0:T(8,128)(2,1)S(1)} %get-tuple-element.73), channel_id=1, source_target_pairs={{1,0},{2,1},{3,2},{4,3},{5,4},{6,5},{7,6},{8,7},{9,8},{10,9},{11,1... | collective-permute-start | bytes 589832 | tf_op jit(solution)/shard_map/ppermute | solution.py:426
  51.3 4.1 %collective-permute-start.19 = (bf16[128,768]{1,0:T(8,128)(2,1)S(1)}, bf16[128,768]{1,0:T(8,128)(2,1)S(1)}, u32[]{:S(2)}, u32[]{:S(2)}) collective-permute-start(bf16[128,768]{1,0:T(8,128)(2,1)S(1)} %get-tuple-element.58.kv_own.kv_ref), channel_id=1, source_target_pairs={{0,1},{1,2},{2,3},{3,4},{4,5},{5,6},{6,7},{7,8},{8,9},{9,10},{10,1... | collective-permute-start | bytes 589832 | tf_op jit(solution)/shard_map/ppermute | solution.py:395
  59.1 3.2 %collective-permute-start.23 = (bf16[128,768]{1,0:T(8,128)(2,1)S(1)}, bf16[128,768]{1,0:T(8,128)(2,1)S(1)}, u32[]{:S(2)}, u32[]{:S(2)}) collective-permute-start(bf16[128,768]{1,0:T(8,128)(2,1)S(1)} %get-tuple-element.90), channel_id=1, source_target_pairs={{1,0},{2,1},{3,2},{4,3},{5,4},{6,5},{7,6},{8,7},{9,8},{10,9},{11,1... | collective-permute-start | bytes 589832 | tf_op jit(solution)/shard_map/ppermute | solution.py:433
  63.7 1.3 %shard_map.132 = bf16[1,128,1536]{2,1,0:T(8,128)(2,1)} custom-call(bf16[1,128,1536]{2,1,0:T(8,128)(2,1)S(1)} %copy-done, bf16[128,384]{1,0:T(8,128)(2,1)S(1)} %get-tuple-element.82.ctx_ref, bf16[1536,768]{1,0:T(8,128)(2,1)S(1)} %get-tuple-element.68.wqo, bf16[128,1536]{1,0:T(8,128)(2,1)S(1)} %collective-permute-done.22.lo_ret), custom_call_target="tpu_custom_call" | custom-call | bytes 1024 | tf_op jit(solution)/shard_map/pallas_call | solution.py:435
  65.0 2.4 %collective-permute-done.23.ret_ref = bf16[128,768]{1,0:T(8,128)(2,1)S(1)} collective-permute-done((bf16[128,768]{1,0:T(8,128)(2,1)S(1)}, bf16[128,768]{1,0:T(8,128)(2,1)S(1)}, u32[]{:S(2)}, u32[]{:S(2)}) %collective-permute-start.23) | collective-permute-done | bytes 196640 | tf_op jit(solution)/shard_map/ppermute | solution.py:433
  68.3 1.2 %shard_map.135 = bf16[1,128,1536]{2,1,0:T(8,128)(2,1)} custom-call(f32[128,1536]{1,0:T(8,128)S(1)} %get-tuple-element.84.hat_ref, f32[128,128]{1,0:T(8,128)S(1)} %get-tuple-element.85.rstd_ref, f32[8,1536]{1,0:T(8,128)S(1)} %get-tuple-element.86.gain_ref, bf16[128,1536]{1,0:T(8,128)(2,1)S(1)} %get-tuple-element.87.cot_ref, ...), custom_call_target="tpu_custom_call" | custom-call | bytes 1024 | tf_op jit(solution)/shard_map/pallas_call | solution.py:452
  (58 shorter events, 13.8 us)
Async XLA Ops:
  3.7 8.2 %collective-permute-start = (bf16[4,96,384]{2,1,0:T(8,128)(2,1)}, bf16[4,96,384]{2,1,0:T(8,128)(2,1)S(1)}, u32[]{:S(2)}, u32[]{:S(2)}) collective-permute-start(bf16[4,96,384]{2,1,0:T(8,128)(2,1)} %get-tuple-element.47.shard_ref), channel_id=1, source_target_pairs={{0,4},{1,5},{2,6},{3,7},{4,8},{5,9},{6,10},{7,11},{8,12},{9,13},{1... | collective-permute-start | bytes 884744 | tf_op jit(solution)/shard_map/ppermute | solution.py:307
  5.1 17.3 %collective-permute-start.5 = (bf16[144,1536]{1,0:T(8,128)(2,1)}, bf16[144,1536]{1,0:T(8,128)(2,1)S(1)}, u32[]{:S(2)}, u32[]{:S(2)}) collective-permute-start(bf16[144,1536]{1,0:T(8,128)(2,1)} %get-tuple-element.48.normed_ref), channel_id=1, source_target_pairs={{0,16},{16,0},{1,17},{17,1},{2,18},{18,2},{3,19},{19,3},{4,20},{20... | collective-permute-start | bytes 1327112 | tf_op jit(solution)/shard_map/ppermute | solution.py:321
  6.3 5.8 %collective-permute-start.7 = (bf16[4,96,384]{2,1,0:T(8,128)(2,1)}, bf16[4,96,384]{2,1,0:T(8,128)(2,1)S(1)}, u32[]{:S(2)}, u32[]{:S(2)}) collective-permute-start(bf16[4,96,384]{2,1,0:T(8,128)(2,1)} %get-tuple-element.47.shard_ref), channel_id=1, source_target_pairs={{0,1},{1,0},{2,3},{3,2},{4,5},{5,4},{6,7},{7,6},{8,9},{9,8},{10,11... | collective-permute-start | bytes 884744 | tf_op jit(solution)/shard_map/ppermute | solution.py:307
  7.5 8.8 %collective-permute-start.6 = (bf16[4,96,384]{2,1,0:T(8,128)(2,1)}, bf16[4,96,384]{2,1,0:T(8,128)(2,1)S(1)}, u32[]{:S(2)}, u32[]{:S(2)}) collective-permute-start(bf16[4,96,384]{2,1,0:T(8,128)(2,1)} %get-tuple-element.47.shard_ref), channel_id=1, source_target_pairs={{0,2},{1,3},{2,0},{3,1},{4,6},{5,7},{6,4},{7,5},{8,10},{9,11},{10,... | collective-permute-start | bytes 884744 | tf_op jit(solution)/shard_map/ppermute | solution.py:307
  7.8 10.9 %collective-permute-start.2 = (bf16[4,96,384]{2,1,0:T(8,128)(2,1)}, bf16[4,96,384]{2,1,0:T(8,128)(2,1)S(1)}, u32[]{:S(2)}, u32[]{:S(2)}) collective-permute-start(bf16[4,96,384]{2,1,0:T(8,128)(2,1)} %get-tuple-element.47.shard_ref), channel_id=1, source_target_pairs={{0,12},{1,13},{2,14},{3,15},{4,0},{5,1},{6,2},{7,3},{8,4},{9,5},{1... | collective-permute-start | bytes 884744 | tf_op jit(solution)/shard_map/ppermute | solution.py:307
  12.0 10.5 %collective-permute-start.9 = (bf16[4,96,384]{2,1,0:T(8,128)(2,1)S(1)}, bf16[4,96,384]{2,1,0:T(8,128)(2,1)S(1)}, u32[]{:S(2)}, u32[]{:S(2)}) collective-permute-start(bf16[4,96,384]{2,1,0:T(8,128)(2,1)S(1)} %collective-permute-done.rest_4_), channel_id=1, source_target_pairs={{0,2},{1,3},{2,0},{3,1},{4,6},{5,7},{6,4},{7,5},{8,10},{9,11},{10,... | collective-permute-start | bytes 884744 | tf_op jit(solution)/shard_map/ppermute | solution.py:307
  12.1 11.6 %collective-permute-start.1 = (bf16[4,96,384]{2,1,0:T(8,128)(2,1)S(1)}, bf16[4,96,384]{2,1,0:T(8,128)(2,1)S(1)}, u32[]{:S(2)}, u32[]{:S(2)}) collective-permute-start(bf16[4,96,384]{2,1,0:T(8,128)(2,1)S(1)} %collective-permute-done.rest_4_), channel_id=1, source_target_pairs={{0,4},{1,5},{2,6},{3,7},{4,8},{5,9},{6,10},{7,11},{8,12},{9,13},{1... | collective-permute-start | bytes 884744 | tf_op jit(solution)/shard_map/ppermute | solution.py:307
  16.4 15.7 %collective-permute-start.4 = (bf16[128,1536]{1,0:T(8,128)(2,1)}, bf16[128,1536]{1,0:T(8,128)(2,1)S(1)}, u32[]{:S(2)}, u32[]{:S(2)}) collective-permute-start(bf16[128,1536]{1,0:T(8,128)(2,1)} %bitcast.4), channel_id=1, source_target_pairs={{0,16},{16,0},{1,17},{17,1},{2,18},{18,2},{3,19},{19,3},{4,20},{20... | collective-permute-start | bytes 1179656 | tf_op jit(solution)/shard_map/ppermute | solution.py:321
  18.7 5.2 %collective-permute-start.8 = (bf16[4,96,384]{2,1,0:T(8,128)(2,1)S(1)}, bf16[4,96,384]{2,1,0:T(8,128)(2,1)S(1)}, u32[]{:S(2)}, u32[]{:S(2)}) collective-permute-start(bf16[4,96,384]{2,1,0:T(8,128)(2,1)S(1)} %collective-permute-done.6.rest_1_), channel_id=1, source_target_pairs={{0,1},{1,0},{2,3},{3,2},{4,5},{5,4},{6,7},{7,6},{8,9},{9,8},{10,11... | collective-permute-start | bytes 884744 | tf_op jit(solution)/shard_map/ppermute | solution.py:307
  22.4 6.9 %collective-permute-start.16 = (bf16[4,96,384]{2,1,0:T(8,128)(2,1)S(1)}, bf16[4,96,384]{2,1,0:T(8,128)(2,1)S(1)}, u32[]{:S(2)}, u32[]{:S(2)}) collective-permute-start(bf16[4,96,384]{2,1,0:T(8,128)(2,1)S(1)} %collective-permute-done.2.rest_12_), channel_id=1, source_target_pairs={{0,1},{1,0},{2,3},{3,2},{4,5},{5,4},{6,7},{7,6},{8,9},{9,8},{10,11... | collective-permute-start | bytes 884744 | tf_op jit(solution)/shard_map/ppermute | solution.py:307
  22.5 8.0 %collective-permute-start.15 = (bf16[4,96,384]{2,1,0:T(8,128)(2,1)S(1)}, bf16[4,96,384]{2,1,0:T(8,128)(2,1)S(1)}, u32[]{:S(2)}, u32[]{:S(2)}) collective-permute-start(bf16[4,96,384]{2,1,0:T(8,128)(2,1)S(1)} %collective-permute-done.2.rest_12_), channel_id=1, source_target_pairs={{0,2},{1,3},{2,0},{3,1},{4,6},{5,7},{6,4},{7,5},{8,10},{9,11},{10,... | collective-permute-start | bytes 884744 | tf_op jit(solution)/shard_map/ppermute | solution.py:307
  23.7 8.4 %collective-permute-start.12 = (bf16[2,96,384]{2,1,0:T(8,128)(2,1)S(1)}, bf16[2,96,384]{2,1,0:T(8,128)(2,1)S(1)}, u32[]{:S(2)}, u32[]{:S(2)}) collective-permute-start(bf16[2,96,384]{2,1,0:T(8,128)(2,1)S(1)} %slice.7), channel_id=1, source_target_pairs={{0,4},{1,5},{2,6},{3,7},{4,8},{5,9},{6,10},{7,11},{8,12},{9,13},{1... | collective-permute-start | bytes 442376 | tf_op jit(solution)/shard_map/ppermute | solution.py:307
  23.8 11.7 %collective-permute-start.10 = (bf16[4,96,384]{2,1,0:T(8,128)(2,1)S(1)}, bf16[4,96,384]{2,1,0:T(8,128)(2,1)S(1)}, u32[]{:S(2)}, u32[]{:S(2)}) collective-permute-start(bf16[4,96,384]{2,1,0:T(8,128)(2,1)S(1)} %collective-permute-done.rest_4_), channel_id=1, source_target_pairs={{0,1},{1,0},{2,3},{3,2},{4,5},{5,4},{6,7},{7,6},{8,9},{9,8},{10,11... | collective-permute-start | bytes 884744 | tf_op jit(solution)/shard_map/ppermute | solution.py:307
  29.3 5.4 %collective-permute-start.3 = (bf16[2,96,384]{2,1,0:T(8,128)(2,1)S(1)}, bf16[2,96,384]{2,1,0:T(8,128)(2,1)S(1)}, u32[]{:S(2)}, u32[]{:S(2)}) collective-permute-start(bf16[2,96,384]{2,1,0:T(8,128)(2,1)S(1)} %slice.6), channel_id=1, source_target_pairs={{0,2},{1,3},{2,0},{3,1},{4,6},{5,7},{6,4},{7,5},{8,10},{9,11},{10,... | collective-permute-start | bytes 442376 | tf_op jit(solution)/shard_map/ppermute | solution.py:307
  30.4 5.1 %collective-permute-start.17 = (bf16[4,96,384]{2,1,0:T(8,128)(2,1)S(1)}, bf16[4,96,384]{2,1,0:T(8,128)(2,1)S(1)}, u32[]{:S(2)}, u32[]{:S(2)}) collective-permute-start(bf16[4,96,384]{2,1,0:T(8,128)(2,1)S(1)} %collective-permute-done.15.rest_13_), channel_id=1, source_target_pairs={{0,1},{1,0},{2,3},{3,2},{4,5},{5,4},{6,7},{7,6},{8,9},{9,8},{10,11... | collective-permute-start | bytes 884744 | tf_op jit(solution)/shard_map/ppermute | solution.py:307
  32.1 4.5 %collective-permute-start.11 = (bf16[4,96,384]{2,1,0:T(8,128)(2,1)S(1)}, bf16[4,96,384]{2,1,0:T(8,128)(2,1)S(1)}, u32[]{:S(2)}, u32[]{:S(2)}) collective-permute-start(bf16[4,96,384]{2,1,0:T(8,128)(2,1)S(1)} %collective-permute-done.9.rest_5_), channel_id=1, source_target_pairs={{0,1},{1,0},{2,3},{3,2},{4,5},{5,4},{6,7},{7,6},{8,9},{9,8},{10,11... | collective-permute-start | bytes 884744 | tf_op jit(solution)/shard_map/ppermute | solution.py:307
  32.1 4.5 %collective-permute-start.13 = (bf16[4,96,384]{2,1,0:T(8,128)(2,1)S(1)}, bf16[4,96,384]{2,1,0:T(8,128)(2,1)S(1)}, u32[]{:S(2)}, u32[]{:S(2)}) collective-permute-start(bf16[4,96,384]{2,1,0:T(8,128)(2,1)S(1)} %collective-permute-done.1.rest_8_), channel_id=1, source_target_pairs={{0,1},{1,0},{2,3},{3,2},{4,5},{5,4},{6,7},{7,6},{8,9},{9,8},{10,11... | collective-permute-start | bytes 884744 | tf_op jit(solution)/shard_map/ppermute | solution.py:307
  34.7 1.9 %collective-permute-start.14 = (bf16[2,96,384]{2,1,0:T(8,128)(2,1)S(1)}, bf16[2,96,384]{2,1,0:T(8,128)(2,1)S(1)}, u32[]{:S(2)}, u32[]{:S(2)}) collective-permute-start(bf16[2,96,384]{2,1,0:T(8,128)(2,1)S(1)} %collective-permute-done.12.rest_9_), channel_id=1, source_target_pairs={{0,1},{1,0},{2,3},{3,2},{4,5},{5,4},{6,7},{7,6},{8,9},{9,8},{10,11... | collective-permute-start | bytes 442376 | tf_op jit(solution)/shard_map/ppermute | solution.py:307
  38.2 8.4 %collective-permute-start.20 = (bf16[128,768]{1,0:T(8,128)(2,1)S(1)}, bf16[128,768]{1,0:T(8,128)(2,1)S(1)}, u32[]{:S(2)}, u32[]{:S(2)}) collective-permute-start(bf16[128,768]{1,0:T(8,128)(2,1)S(1)} %get-tuple-element.59.kv_oth.kv_ref), channel_id=1, source_target_pairs={{0,1},{1,2},{2,3},{3,4},{4,5},{5,6},{6,7},{7,8},{8,9},{9,10},{10,1... | collective-permute-start | bytes 589832 | tf_op jit(solution)/shard_map/ppermute | solution.py:394
  47.8 11.3 %collective-permute-start.22 = (bf16[128,1536]{1,0:T(8,128)(2,1)S(1)}, bf16[128,1536]{1,0:T(8,128)(2,1)S(1)}, u32[]{:S(2)}, u32[]{:S(2)}) collective-permute-start(bf16[128,1536]{1,0:T(8,128)(2,1)S(1)} %shard_map.127), channel_id=1, source_target_pairs={{0,16},{16,0},{1,17},{17,1},{2,18},{18,2},{3,19},{19,3},{4,20},{20... | collective-permute-start | bytes 1179656 | tf_op jit(solution)/shard_map/ppermute | solution.py:321
  49.0 8.0 %collective-permute-start.21 = (bf16[128,768]{1,0:T(8,128)(2,1)S(1)}, bf16[128,768]{1,0:T(8,128)(2,1)S(1)}, u32[]{:S(2)}, u32[]{:S(2)}) collective-permute-start(bf16[128,768]{1,0:T(8,128)(2,1)S(1)} %get-tuple-element.73), channel_id=1, source_target_pairs={{1,0},{2,1},{3,2},{4,3},{5,4},{6,5},{7,6},{8,7},{9,8},{10,9},{11,1... | collective-permute-start | bytes 589832 | tf_op jit(solution)/shard_map/ppermute | solution.py:426
  51.3 7.1 %collective-permute-start.19 = (bf16[128,768]{1,0:T(8,128)(2,1)S(1)}, bf16[128,768]{1,0:T(8,128)(2,1)S(1)}, u32[]{:S(2)}, u32[]{:S(2)}) collective-permute-start(bf16[128,768]{1,0:T(8,128)(2,1)S(1)} %get-tuple-element.58.kv_own.kv_ref), channel_id=1, source_target_pairs={{0,1},{1,2},{2,3},{3,4},{4,5},{5,6},{6,7},{7,8},{8,9},{9,10},{10,1... | collective-permute-start | bytes 589832 | tf_op jit(solution)/shard_map/ppermute | solution.py:395
  57.9 10.4 %collective-permute-start.24 = (bf16[128,1536]{1,0:T(8,128)(2,1)S(1)}, bf16[128,1536]{1,0:T(8,128)(2,1)S(1)}, u32[]{:S(2)}, u32[]{:S(2)}) collective-permute-start(bf16[128,1536]{1,0:T(8,128)(2,1)S(1)} %shard_map.129), channel_id=1, source_target_pairs={{0,16},{16,0},{1,17},{17,1},{2,18},{18,2},{3,19},{19,3},{4,20},{20... | collective-permute-start | bytes 1179656 | tf_op jit(solution)/shard_map/ppermute | solution.py:321
  59.1 8.3 %collective-permute-start.23 = (bf16[128,768]{1,0:T(8,128)(2,1)S(1)}, bf16[128,768]{1,0:T(8,128)(2,1)S(1)}, u32[]{:S(2)}, u32[]{:S(2)}) collective-permute-start(bf16[128,768]{1,0:T(8,128)(2,1)S(1)} %get-tuple-element.90), channel_id=1, source_target_pairs={{1,0},{2,1},{3,2},{4,3},{5,4},{6,5},{7,6},{8,7},{9,8},{10,9},{11,1... | collective-permute-start | bytes 589832 | tf_op jit(solution)/shard_map/ppermute | solution.py:433
  (9 other events, 49.7 us)

commit v7 on v6

--- a/solution.py
+++ b/solution.py
@@ -103,14 +103,9 @@
 
 
 def accumulate(x, weights, copies, columns):
-    total = None
-    for half in range(2):
-        for copy in copies[half * 16 : half * 16 + 16]:
-            copy.wait()
-        rows = slice(half * 2 * BLK, (half + 1) * 2 * BLK)
-        part = dot(x[:, rows], weights[rows, columns])
-        total = part if total is None else total + part
-    return total
+    for copy in copies:
+        copy.wait()
+    return dot(x[...], weights[:, columns])
 
 
 def key_value_kernel(own_ref, oth_ref, *rest):
@@ -429,15 +424,6 @@
         partial_oth, dkv_oth, ret_oth, wkv
     )
     np_ret = other(np_oth)
-    p, ds, dmem, ctx = memory(0, kv, after(mem, np_oth))
-    ret = lax.ppermute(after(dmem, lo_ret), "tm", back)
-    partial, dkv = grads(0, after(p, dmem), ds, kv, mem)
-    layer_out = call(
-        output_kernel, shape(1, SEG, D), (), [VM] * 4
-    )(inputs, after(ctx, partial), wqo, lo_ret)
-    np_own = call(returned_kernel, shape(SEG, D, dtype=F32), (), [VM] * 4)(
-        after(partial, layer_out), dkv, ret, wkv
-    )
     hat = call(
         hat_kernel,
         (
@@ -448,7 +434,16 @@
         ),
         [pltpu.VMEM((SEG + 8, D), F32)],
         [VM] * 3,
-    )(inputs, gain, after(cot, partial))
+    )(inputs, gain, after(cot, np_oth))
+    p, ds, dmem, ctx = memory(0, kv, after(mem, np_oth, hat[0]))
+    ret = lax.ppermute(after(dmem, lo_ret), "tm", back)
+    partial, dkv = grads(0, after(p, dmem), ds, kv, mem)
+    layer_out = call(
+        output_kernel, shape(1, SEG, D), (), [VM] * 4
+    )(inputs, after(ctx, partial), wqo, lo_ret)
+    np_own = call(returned_kernel, shape(SEG, D, dtype=F32), (), [VM] * 4)(
+        after(partial, layer_out), dkv, ret, wkv
+    )
     input_grad = call(finish_kernel, shape(1, SEG, D), (), [VM] * 6)(
         *hat, after(np_own, hat[0]), np_ret
     )

time: 69.8 us -> 69.6 us (level)
  no operation moved by 1% of the time
where the time goes in v7:
time: 69.6 us; the launch traced here: 69.3 us
  starting transfers between devices  36.3 us (52%)
  Pallas kernels  14.8 us (21%)
  waiting for transfers between devices  14.7 us (21%)
  local copies, waits for them, and re-layouts  2.03 us (3%)
  between operations  1.53 us (2%)
    ppermute x17, starting transfers between devices, moved_by(): return lambda block: lax.ppermute(block, 'tm', route)  19.2 us
    ppermute x17, waiting for transfers between devices, moved_by(): return lambda block: lax.ppermute(block, 'tm', route)  11.5 us
    ppermute x1, starting transfers between devices, split_heads(): mem_oth = lax.ppermute(kv_oth, 'tm', onward)  4.74 us
    ppermute x1, starting transfers between devices, split_heads(): mem = lax.ppermute(kv, 'tm', onward)  4.15 us
    ppermute x4, starting transfers between devices, other(): return lax.ppermute(block, 'grp', [(0, 1), (1, 0)])  3.05 us
    ppermute x1, starting transfers between devices, split_heads(): ret = lax.ppermute(after(dmem, lo_ret), 'tm', back)  2.82 us
    ppermute x1, waiting for transfers between devices, split_heads(): ret = lax.ppermute(after(dmem, lo_ret), 'tm', back)  2.78 us
    pallas_call x1, Pallas kernels, split_heads(): call(prepare_kernel, (shape(4, ROWS, HALF), shape(SEG + 16, D), shape(2 *...  2.45 us
  transfers between devices with their start and end apart: 25, of which 8 were waited for; matrix products, arithmetic and copies ran while one was open for 0% of the time, Pallas kernels for 12%

profile of v7, /device:TPU:21, one launch (start us, length us, event | category | flops | bytes accessed | tf_op | source)
XLA Modules:
  0.0 69.3 jit_solution(3147594148209098404)
XLA Ops:
  1.3 2.4 %shard_map.122 = (bf16[4,96,384]{2,1,0:T(8,128)(2,1)}, bf16[144,1536]{1,0:T(8,128)(2,1)}, bf16[256,384]{1,0:T(8,128)(2,1)}) custom-call(bf16[96,384]{1,0:T(8,128)(2,1)} %k_ref.1, bf16[96,384]{1,0:T(8,128)(2,1)} %v_ref.1, bf16[96,384]{1,0:T(8,128)(2,1)} %q_ref.1, bf16[96,384]{1,0:T(8,128)(2,1)} %o_ref.1, bf16[1,128,1536]{2,1,0:T(8,128)(2,1)} %x_ref.5, ...), custom_call_target="tpu_custom_call" | custom-call | bytes 1024 | tf_op jit(solution)/shard_map/pallas_call | solution.py:334
  3.7 1.4 %collective-permute-start = (bf16[4,96,384]{2,1,0:T(8,128)(2,1)}, bf16[4,96,384]{2,1,0:T(8,128)(2,1)S(1)}, u32[]{:S(2)}, u32[]{:S(2)}) collective-permute-start(bf16[4,96,384]{2,1,0:T(8,128)(2,1)} %get-tuple-element.47.shard_ref), channel_id=1, source_target_pairs={{0,4},{1,5},{2,6},{3,7},{4,8},{5,9},{6,10},{7,11},{8,12},{9,13},{1... | collective-permute-start | bytes 884744 | tf_op jit(solution)/shard_map/ppermute | solution.py:302
  5.1 1.2 %collective-permute-start.5 = (bf16[144,1536]{1,0:T(8,128)(2,1)}, bf16[144,1536]{1,0:T(8,128)(2,1)S(1)}, u32[]{:S(2)}, u32[]{:S(2)}) collective-permute-start(bf16[144,1536]{1,0:T(8,128)(2,1)} %get-tuple-element.48.normed_ref), channel_id=1, source_target_pairs={{0,16},{16,0},{1,17},{17,1},{2,18},{18,2},{3,19},{19,3},{4,20},{20... | collective-permute-start | bytes 1327112 | tf_op jit(solution)/shard_map/ppermute | solution.py:316
  6.3 1.2 %collective-permute-start.7 = (bf16[4,96,384]{2,1,0:T(8,128)(2,1)}, bf16[4,96,384]{2,1,0:T(8,128)(2,1)S(1)}, u32[]{:S(2)}, u32[]{:S(2)}) collective-permute-start(bf16[4,96,384]{2,1,0:T(8,128)(2,1)} %get-tuple-element.47.shard_ref), channel_id=1, source_target_pairs={{0,1},{1,0},{2,3},{3,2},{4,5},{5,4},{6,7},{7,6},{8,9},{9,8},{10,11... | collective-permute-start | bytes 884744 | tf_op jit(solution)/shard_map/ppermute | solution.py:302
  10.0 2.0 %collective-permute-done.rest_4_ = bf16[4,96,384]{2,1,0:T(8,128)(2,1)S(1)} collective-permute-done((bf16[4,96,384]{2,1,0:T(8,128)(2,1)}, bf16[4,96,384]{2,1,0:T(8,128)(2,1)S(1)}, u32[]{:S(2)}, u32[]{:S(2)}) %collective-permute-start) | collective-permute-done | bytes 294944 | tf_op jit(solution)/shard_map/ppermute | solution.py:302
  12.1 1.3 %collective-permute-start.1 = (bf16[4,96,384]{2,1,0:T(8,128)(2,1)S(1)}, bf16[4,96,384]{2,1,0:T(8,128)(2,1)S(1)}, u32[]{:S(2)}, u32[]{:S(2)}) collective-permute-start(bf16[4,96,384]{2,1,0:T(8,128)(2,1)S(1)} %collective-permute-done.rest_4_), channel_id=1, source_target_pairs={{0,4},{1,5},{2,6},{3,7},{4,8},{5,9},{6,10},{7,11},{8,12},{9,13},{1... | collective-permute-start | bytes 884744 | tf_op jit(solution)/shard_map/ppermute | solution.py:302
  13.4 3.0 %collective-permute-done.6.rest_1_ = bf16[4,96,384]{2,1,0:T(8,128)(2,1)S(1)} collective-permute-done((bf16[4,96,384]{2,1,0:T(8,128)(2,1)}, bf16[4,96,384]{2,1,0:T(8,128)(2,1)S(1)}, u32[]{:S(2)}, u32[]{:S(2)}) %collective-permute-start.6) | collective-permute-done | bytes 294944 | tf_op jit(solution)/shard_map/ppermute | solution.py:302
  16.6 2.0 %collective-permute-done.2.rest_12_ = bf16[4,96,384]{2,1,0:T(8,128)(2,1)S(1)} collective-permute-done((bf16[4,96,384]{2,1,0:T(8,128)(2,1)}, bf16[4,96,384]{2,1,0:T(8,128)(2,1)S(1)}, u32[]{:S(2)}, u32[]{:S(2)}) %collective-permute-start.2) | collective-permute-done | bytes 294944 | tf_op jit(solution)/shard_map/ppermute | solution.py:302
  18.7 3.7 %collective-permute-start.8 = (bf16[4,96,384]{2,1,0:T(8,128)(2,1)S(1)}, bf16[4,96,384]{2,1,0:T(8,128)(2,1)S(1)}, u32[]{:S(2)}, u32[]{:S(2)}) collective-permute-start(bf16[4,96,384]{2,1,0:T(8,128)(2,1)S(1)} %collective-permute-done.6.rest_1_), channel_id=1, source_target_pairs={{0,1},{1,0},{2,3},{3,2},{4,5},{5,4},{6,7},{7,6},{8,9},{9,8},{10,11... | collective-permute-start | bytes 884744 | tf_op jit(solution)/shard_map/ppermute | solution.py:302
  22.5 1.2 %collective-permute-start.15 = (bf16[4,96,384]{2,1,0:T(8,128)(2,1)S(1)}, bf16[4,96,384]{2,1,0:T(8,128)(2,1)S(1)}, u32[]{:S(2)}, u32[]{:S(2)}) collective-permute-start(bf16[4,96,384]{2,1,0:T(8,128)(2,1)S(1)} %collective-permute-done.2.rest_12_), channel_id=1, source_target_pairs={{0,2},{1,3},{2,0},{3,1},{4,6},{5,7},{6,4},{7,5},{8,10},{9,11},{10,... | collective-permute-start | bytes 884744 | tf_op jit(solution)/shard_map/ppermute | solution.py:302
  23.8 5.4 %collective-permute-start.10 = (bf16[4,96,384]{2,1,0:T(8,128)(2,1)S(1)}, bf16[4,96,384]{2,1,0:T(8,128)(2,1)S(1)}, u32[]{:S(2)}, u32[]{:S(2)}) collective-permute-start(bf16[4,96,384]{2,1,0:T(8,128)(2,1)S(1)} %collective-permute-done.rest_4_), channel_id=1, source_target_pairs={{0,1},{1,0},{2,3},{3,2},{4,5},{5,4},{6,7},{7,6},{8,9},{9,8},{10,11... | collective-permute-start | bytes 884744 | tf_op jit(solution)/shard_map/ppermute | solution.py:302
  29.3 1.2 %collective-permute-start.3 = (bf16[2,96,384]{2,1,0:T(8,128)(2,1)S(1)}, bf16[2,96,384]{2,1,0:T(8,128)(2,1)S(1)}, u32[]{:S(2)}, u32[]{:S(2)}) collective-permute-start(bf16[2,96,384]{2,1,0:T(8,128)(2,1)S(1)} %slice.6), channel_id=1, source_target_pairs={{0,2},{1,3},{2,0},{3,1},{4,6},{5,7},{6,4},{7,5},{8,10},{9,11},{10,... | collective-permute-start | bytes 442376 | tf_op jit(solution)/shard_map/ppermute | solution.py:302
  30.4 1.6 %collective-permute-start.17 = (bf16[4,96,384]{2,1,0:T(8,128)(2,1)S(1)}, bf16[4,96,384]{2,1,0:T(8,128)(2,1)S(1)}, u32[]{:S(2)}, u32[]{:S(2)}) collective-permute-start(bf16[4,96,384]{2,1,0:T(8,128)(2,1)S(1)} %collective-permute-done.15.rest_13_), channel_id=1, source_target_pairs={{0,1},{1,0},{2,3},{3,2},{4,5},{5,4},{6,7},{7,6},{8,9},{9,8},{10,11... | collective-permute-start | bytes 884744 | tf_op jit(solution)/shard_map/ppermute | solution.py:302
  32.6 2.1 %collective-permute-done.3.rest_9_ = bf16[2,96,384]{2,1,0:T(8,128)(2,1)S(1)} collective-permute-done((bf16[2,96,384]{2,1,0:T(8,128)(2,1)S(1)}, bf16[2,96,384]{2,1,0:T(8,128)(2,1)S(1)}, u32[]{:S(2)}, u32[]{:S(2)}) %collective-permute-start.3) | collective-permute-done | bytes 147488 | tf_op jit(solution)/shard_map/ppermute | solution.py:302
  36.6 1.5 %shard_map.124 = (bf16[1536,768]{1,0:T(8,128)(2,1)S(1)}, bf16[128,768]{1,0:T(8,128)(2,1)S(1)}, bf16[128,768]{1,0:T(8,128)(2,1)S(1)}, bf16[256,1536]{1,0:T(8,128)(2,1)S(1)}, bf16[2,16,128]{2,1,0:T(8,128)(2,1)S(1)}) custom-call(bf16[144,1536]{1,0:T(8,128)(2,1)S(1)} %get-tuple-element.54.own_ref, bf16[144,1536]{1,0:T(8,128)(2,1)S(1)} %collective-permute-done.5.oth_ref, ...), custom_call_target="tpu_custom_call" | custom-call | bytes 1024 | tf_op jit(solution)/shard_map/pallas_call | solution.py:374
  38.1 4.7 %collective-permute-start.20 = (bf16[128,768]{1,0:T(8,128)(2,1)S(1)}, bf16[128,768]{1,0:T(8,128)(2,1)S(1)}, u32[]{:S(2)}, u32[]{:S(2)}) collective-permute-start(bf16[128,768]{1,0:T(8,128)(2,1)S(1)} %get-tuple-element.59.kv_oth.kv_ref), channel_id=1, source_target_pairs={{0,1},{1,2},{2,3},{3,4},{4,5},{5,6},{6,7},{7,8},{8,9},{9,10},{10,1... | collective-permute-start | bytes 589832 | tf_op jit(solution)/shard_map/ppermute | solution.py:389
  42.9 1.4 %collective-permute-done.18.rest_11_ = bf16[2,96,384]{2,1,0:T(8,128)(2,1)S(1)} collective-permute-done((bf16[2,96,384]{2,1,0:T(8,128)(2,1)S(1)}, bf16[2,96,384]{2,1,0:T(8,128)(2,1)S(1)}, u32[]{:S(2)}, u32[]{:S(2)}) %collective-permute-start.18) | collective-permute-done | bytes 147488 | tf_op jit(solution)/shard_map/ppermute | solution.py:302
  44.3 2.1 %shard_map.125 = (bf16[1536,768]{1,0:T(8,128)(2,1)S(1)}, bf16[2,128,384]{2,1,0:T(8,128)(2,1)S(1)}, bf16[2,128,384]{2,1,0:T(8,128)(2,1)S(1)}, f32[2,3,128,128]{3,...) custom-call(bf16[256,1536]{1,0:T(8,128)(2,1)S(1)} %get-tuple-element.57.xs, ...), custom_call_target="tpu_custom_call" | custom-call | bytes 1024 | tf_op jit(solution)/shard_map/pallas_call | solution.py:392
  48.8 2.3 %collective-permute-start.21 = (bf16[128,768]{1,0:T(8,128)(2,1)S(1)}, bf16[128,768]{1,0:T(8,128)(2,1)S(1)}, u32[]{:S(2)}, u32[]{:S(2)}) collective-permute-start(bf16[128,768]{1,0:T(8,128)(2,1)S(1)} %get-tuple-element.73), channel_id=1, source_target_pairs={{1,0},{2,1},{3,2},{4,3},{5,4},{6,5},{7,6},{8,7},{9,8},{10,9},{11,1... | collective-permute-start | bytes 589832 | tf_op jit(solution)/shard_map/ppermute | solution.py:421
  51.1 4.2 %collective-permute-start.19 = (bf16[128,768]{1,0:T(8,128)(2,1)S(1)}, bf16[128,768]{1,0:T(8,128)(2,1)S(1)}, u32[]{:S(2)}, u32[]{:S(2)}) collective-permute-start(bf16[128,768]{1,0:T(8,128)(2,1)S(1)} %get-tuple-element.58.kv_own.kv_ref), channel_id=1, source_target_pairs={{0,1},{1,2},{2,3},{3,4},{4,5},{5,6},{6,7},{7,8},{8,9},{9,10},{10,1... | collective-permute-start | bytes 589832 | tf_op jit(solution)/shard_map/ppermute | solution.py:390
  59.3 2.8 %collective-permute-start.23 = (bf16[128,768]{1,0:T(8,128)(2,1)S(1)}, bf16[128,768]{1,0:T(8,128)(2,1)S(1)}, u32[]{:S(2)}, u32[]{:S(2)}) collective-permute-start(bf16[128,768]{1,0:T(8,128)(2,1)S(1)} %get-tuple-element.90), channel_id=1, source_target_pairs={{1,0},{2,1},{3,2},{4,3},{5,4},{6,5},{7,6},{8,7},{9,8},{10,9},{11,1... | collective-permute-start | bytes 589832 | tf_op jit(solution)/shard_map/ppermute | solution.py:439
  63.2 1.3 %shard_map.133 = bf16[1,128,1536]{2,1,0:T(8,128)(2,1)} custom-call(bf16[1,128,1536]{2,1,0:T(8,128)(2,1)S(1)} %copy-done, bf16[128,384]{1,0:T(8,128)(2,1)S(1)} %get-tuple-element.84.ctx_ref, bf16[1536,768]{1,0:T(8,128)(2,1)S(1)} %get-tuple-element.68.wqo, bf16[128,1536]{1,0:T(8,128)(2,1)S(1)} %collective-permute-done.22.lo_ret), custom_call_target="tpu_custom_call" | custom-call | bytes 1024 | tf_op jit(solution)/shard_map/pallas_call | solution.py:441
  64.5 2.8 %collective-permute-done.23.ret_ref = bf16[128,768]{1,0:T(8,128)(2,1)S(1)} collective-permute-done((bf16[128,768]{1,0:T(8,128)(2,1)S(1)}, bf16[128,768]{1,0:T(8,128)(2,1)S(1)}, u32[]{:S(2)}, u32[]{:S(2)}) %collective-permute-start.23) | collective-permute-done | bytes 196640 | tf_op jit(solution)/shard_map/ppermute | solution.py:439
  68.2 1.2 %shard_map.135 = bf16[1,128,1536]{2,1,0:T(8,128)(2,1)} custom-call(f32[128,1536]{1,0:T(8,128)S(1)} %get-tuple-element.76.hat_ref, f32[128,128]{1,0:T(8,128)S(1)} %get-tuple-element.85.rstd_ref, f32[8,1536]{1,0:T(8,128)S(1)} %get-tuple-element.86.gain_ref, bf16[128,1536]{1,0:T(8,128)(2,1)S(1)} %get-tuple-element.87.cot_ref, ...), custom_call_target="tpu_custom_call" | custom-call | bytes 1024 | tf_op jit(solution)/shard_map/pallas_call | solution.py:447
  (58 shorter events, 13.7 us)
Async XLA Ops:
  3.7 8.2 %collective-permute-start = (bf16[4,96,384]{2,1,0:T(8,128)(2,1)}, bf16[4,96,384]{2,1,0:T(8,128)(2,1)S(1)}, u32[]{:S(2)}, u32[]{:S(2)}) collective-permute-start(bf16[4,96,384]{2,1,0:T(8,128)(2,1)} %get-tuple-element.47.shard_ref), channel_id=1, source_target_pairs={{0,4},{1,5},{2,6},{3,7},{4,8},{5,9},{6,10},{7,11},{8,12},{9,13},{1... | collective-permute-start | bytes 884744 | tf_op jit(solution)/shard_map/ppermute | solution.py:302
  5.1 17.3 %collective-permute-start.5 = (bf16[144,1536]{1,0:T(8,128)(2,1)}, bf16[144,1536]{1,0:T(8,128)(2,1)S(1)}, u32[]{:S(2)}, u32[]{:S(2)}) collective-permute-start(bf16[144,1536]{1,0:T(8,128)(2,1)} %get-tuple-element.48.normed_ref), channel_id=1, source_target_pairs={{0,16},{16,0},{1,17},{17,1},{2,18},{18,2},{3,19},{19,3},{4,20},{20... | collective-permute-start | bytes 1327112 | tf_op jit(solution)/shard_map/ppermute | solution.py:316
  6.3 5.8 %collective-permute-start.7 = (bf16[4,96,384]{2,1,0:T(8,128)(2,1)}, bf16[4,96,384]{2,1,0:T(8,128)(2,1)S(1)}, u32[]{:S(2)}, u32[]{:S(2)}) collective-permute-start(bf16[4,96,384]{2,1,0:T(8,128)(2,1)} %get-tuple-element.47.shard_ref), channel_id=1, source_target_pairs={{0,1},{1,0},{2,3},{3,2},{4,5},{5,4},{6,7},{7,6},{8,9},{9,8},{10,11... | collective-permute-start | bytes 884744 | tf_op jit(solution)/shard_map/ppermute | solution.py:302
  7.5 8.8 %collective-permute-start.6 = (bf16[4,96,384]{2,1,0:T(8,128)(2,1)}, bf16[4,96,384]{2,1,0:T(8,128)(2,1)S(1)}, u32[]{:S(2)}, u32[]{:S(2)}) collective-permute-start(bf16[4,96,384]{2,1,0:T(8,128)(2,1)} %get-tuple-element.47.shard_ref), channel_id=1, source_target_pairs={{0,2},{1,3},{2,0},{3,1},{4,6},{5,7},{6,4},{7,5},{8,10},{9,11},{10,... | collective-permute-start | bytes 884744 | tf_op jit(solution)/shard_map/ppermute | solution.py:302
  7.8 10.9 %collective-permute-start.2 = (bf16[4,96,384]{2,1,0:T(8,128)(2,1)}, bf16[4,96,384]{2,1,0:T(8,128)(2,1)S(1)}, u32[]{:S(2)}, u32[]{:S(2)}) collective-permute-start(bf16[4,96,384]{2,1,0:T(8,128)(2,1)} %get-tuple-element.47.shard_ref), channel_id=1, source_target_pairs={{0,12},{1,13},{2,14},{3,15},{4,0},{5,1},{6,2},{7,3},{8,4},{9,5},{1... | collective-permute-start | bytes 884744 | tf_op jit(solution)/shard_map/ppermute | solution.py:302
  12.0 10.5 %collective-permute-start.9 = (bf16[4,96,384]{2,1,0:T(8,128)(2,1)S(1)}, bf16[4,96,384]{2,1,0:T(8,128)(2,1)S(1)}, u32[]{:S(2)}, u32[]{:S(2)}) collective-permute-start(bf16[4,96,384]{2,1,0:T(8,128)(2,1)S(1)} %collective-permute-done.rest_4_), channel_id=1, source_target_pairs={{0,2},{1,3},{2,0},{3,1},{4,6},{5,7},{6,4},{7,5},{8,10},{9,11},{10,... | collective-permute-start | bytes 884744 | tf_op jit(solution)/shard_map/ppermute | solution.py:302
  12.1 11.6 %collective-permute-start.1 = (bf16[4,96,384]{2,1,0:T(8,128)(2,1)S(1)}, bf16[4,96,384]{2,1,0:T(8,128)(2,1)S(1)}, u32[]{:S(2)}, u32[]{:S(2)}) collective-permute-start(bf16[4,96,384]{2,1,0:T(8,128)(2,1)S(1)} %collective-permute-done.rest_4_), channel_id=1, source_target_pairs={{0,4},{1,5},{2,6},{3,7},{4,8},{5,9},{6,10},{7,11},{8,12},{9,13},{1... | collective-permute-start | bytes 884744 | tf_op jit(solution)/shard_map/ppermute | solution.py:302
  16.4 15.7 %collective-permute-start.4 = (bf16[128,1536]{1,0:T(8,128)(2,1)}, bf16[128,1536]{1,0:T(8,128)(2,1)S(1)}, u32[]{:S(2)}, u32[]{:S(2)}) collective-permute-start(bf16[128,1536]{1,0:T(8,128)(2,1)} %bitcast.4), channel_id=1, source_target_pairs={{0,16},{16,0},{1,17},{17,1},{2,18},{18,2},{3,19},{19,3},{4,20},{20... | collective-permute-start | bytes 1179656 | tf_op jit(solution)/shard_map/ppermute | solution.py:316
  18.7 5.2 %collective-permute-start.8 = (bf16[4,96,384]{2,1,0:T(8,128)(2,1)S(1)}, bf16[4,96,384]{2,1,0:T(8,128)(2,1)S(1)}, u32[]{:S(2)}, u32[]{:S(2)}) collective-permute-start(bf16[4,96,384]{2,1,0:T(8,128)(2,1)S(1)} %collective-permute-done.6.rest_1_), channel_id=1, source_target_pairs={{0,1},{1,0},{2,3},{3,2},{4,5},{5,4},{6,7},{7,6},{8,9},{9,8},{10,11... | collective-permute-start | bytes 884744 | tf_op jit(solution)/shard_map/ppermute | solution.py:302
  22.4 6.9 %collective-permute-start.16 = (bf16[4,96,384]{2,1,0:T(8,128)(2,1)S(1)}, bf16[4,96,384]{2,1,0:T(8,128)(2,1)S(1)}, u32[]{:S(2)}, u32[]{:S(2)}) collective-permute-start(bf16[4,96,384]{2,1,0:T(8,128)(2,1)S(1)} %collective-permute-done.2.rest_12_), channel_id=1, source_target_pairs={{0,1},{1,0},{2,3},{3,2},{4,5},{5,4},{6,7},{7,6},{8,9},{9,8},{10,11... | collective-permute-start | bytes 884744 | tf_op jit(solution)/shard_map/ppermute | solution.py:302
  22.5 8.0 %collective-permute-start.15 = (bf16[4,96,384]{2,1,0:T(8,128)(2,1)S(1)}, bf16[4,96,384]{2,1,0:T(8,128)(2,1)S(1)}, u32[]{:S(2)}, u32[]{:S(2)}) collective-permute-start(bf16[4,96,384]{2,1,0:T(8,128)(2,1)S(1)} %collective-permute-done.2.rest_12_), channel_id=1, source_target_pairs={{0,2},{1,3},{2,0},{3,1},{4,6},{5,7},{6,4},{7,5},{8,10},{9,11},{10,... | collective-permute-start | bytes 884744 | tf_op jit(solution)/shard_map/ppermute | solution.py:302
  23.7 8.4 %collective-permute-start.12 = (bf16[2,96,384]{2,1,0:T(8,128)(2,1)S(1)}, bf16[2,96,384]{2,1,0:T(8,128)(2,1)S(1)}, u32[]{:S(2)}, u32[]{:S(2)}) collective-permute-start(bf16[2,96,384]{2,1,0:T(8,128)(2,1)S(1)} %slice.7), channel_id=1, source_target_pairs={{0,4},{1,5},{2,6},{3,7},{4,8},{5,9},{6,10},{7,11},{8,12},{9,13},{1... | collective-permute-start | bytes 442376 | tf_op jit(solution)/shard_map/ppermute | solution.py:302
  23.8 11.7 %collective-permute-start.10 = (bf16[4,96,384]{2,1,0:T(8,128)(2,1)S(1)}, bf16[4,96,384]{2,1,0:T(8,128)(2,1)S(1)}, u32[]{:S(2)}, u32[]{:S(2)}) collective-permute-start(bf16[4,96,384]{2,1,0:T(8,128)(2,1)S(1)} %collective-permute-done.rest_4_), channel_id=1, source_target_pairs={{0,1},{1,0},{2,3},{3,2},{4,5},{5,4},{6,7},{7,6},{8,9},{9,8},{10,11... | collective-permute-start | bytes 884744 | tf_op jit(solution)/shard_map/ppermute | solution.py:302
  29.3 5.4 %collective-permute-start.3 = (bf16[2,96,384]{2,1,0:T(8,128)(2,1)S(1)}, bf16[2,96,384]{2,1,0:T(8,128)(2,1)S(1)}, u32[]{:S(2)}, u32[]{:S(2)}) collective-permute-start(bf16[2,96,384]{2,1,0:T(8,128)(2,1)S(1)} %slice.6), channel_id=1, source_target_pairs={{0,2},{1,3},{2,0},{3,1},{4,6},{5,7},{6,4},{7,5},{8,10},{9,11},{10,... | collective-permute-start | bytes 442376 | tf_op jit(solution)/shard_map/ppermute | solution.py:302
  30.4 5.1 %collective-permute-start.17 = (bf16[4,96,384]{2,1,0:T(8,128)(2,1)S(1)}, bf16[4,96,384]{2,1,0:T(8,128)(2,1)S(1)}, u32[]{:S(2)}, u32[]{:S(2)}) collective-permute-start(bf16[4,96,384]{2,1,0:T(8,128)(2,1)S(1)} %collective-permute-done.15.rest_13_), channel_id=1, source_target_pairs={{0,1},{1,0},{2,3},{3,2},{4,5},{5,4},{6,7},{7,6},{8,9},{9,8},{10,11... | collective-permute-start | bytes 884744 | tf_op jit(solution)/shard_map/ppermute | solution.py:302
  32.1 4.5 %collective-permute-start.11 = (bf16[4,96,384]{2,1,0:T(8,128)(2,1)S(1)}, bf16[4,96,384]{2,1,0:T(8,128)(2,1)S(1)}, u32[]{:S(2)}, u32[]{:S(2)}) collective-permute-start(bf16[4,96,384]{2,1,0:T(8,128)(2,1)S(1)} %collective-permute-done.9.rest_5_), channel_id=1, source_target_pairs={{0,1},{1,0},{2,3},{3,2},{4,5},{5,4},{6,7},{7,6},{8,9},{9,8},{10,11... | collective-permute-start | bytes 884744 | tf_op jit(solution)/shard_map/ppermute | solution.py:302
  32.1 4.5 %collective-permute-start.13 = (bf16[4,96,384]{2,1,0:T(8,128)(2,1)S(1)}, bf16[4,96,384]{2,1,0:T(8,128)(2,1)S(1)}, u32[]{:S(2)}, u32[]{:S(2)}) collective-permute-start(bf16[4,96,384]{2,1,0:T(8,128)(2,1)S(1)} %collective-permute-done.1.rest_8_), channel_id=1, source_target_pairs={{0,1},{1,0},{2,3},{3,2},{4,5},{5,4},{6,7},{7,6},{8,9},{9,8},{10,11... | collective-permute-start | bytes 884744 | tf_op jit(solution)/shard_map/ppermute | solution.py:302
  34.7 1.9 %collective-permute-start.14 = (bf16[2,96,384]{2,1,0:T(8,128)(2,1)S(1)}, bf16[2,96,384]{2,1,0:T(8,128)(2,1)S(1)}, u32[]{:S(2)}, u32[]{:S(2)}) collective-permute-start(bf16[2,96,384]{2,1,0:T(8,128)(2,1)S(1)} %collective-permute-done.12.rest_9_), channel_id=1, source_target_pairs={{0,1},{1,0},{2,3},{3,2},{4,5},{5,4},{6,7},{7,6},{8,9},{9,8},{10,11... | collective-permute-start | bytes 442376 | tf_op jit(solution)/shard_map/ppermute | solution.py:302
  38.1 8.3 %collective-permute-start.20 = (bf16[128,768]{1,0:T(8,128)(2,1)S(1)}, bf16[128,768]{1,0:T(8,128)(2,1)S(1)}, u32[]{:S(2)}, u32[]{:S(2)}) collective-permute-start(bf16[128,768]{1,0:T(8,128)(2,1)S(1)} %get-tuple-element.59.kv_oth.kv_ref), channel_id=1, source_target_pairs={{0,1},{1,2},{2,3},{3,4},{4,5},{5,6},{6,7},{7,8},{8,9},{9,10},{10,1... | collective-permute-start | bytes 589832 | tf_op jit(solution)/shard_map/ppermute | solution.py:389
  47.7 11.6 %collective-permute-start.22 = (bf16[128,1536]{1,0:T(8,128)(2,1)S(1)}, bf16[128,1536]{1,0:T(8,128)(2,1)S(1)}, u32[]{:S(2)}, u32[]{:S(2)}) collective-permute-start(bf16[128,1536]{1,0:T(8,128)(2,1)S(1)} %shard_map.127), channel_id=1, source_target_pairs={{0,16},{16,0},{1,17},{17,1},{2,18},{18,2},{3,19},{19,3},{4,20},{20... | collective-permute-start | bytes 1179656 | tf_op jit(solution)/shard_map/ppermute | solution.py:316
  48.8 8.0 %collective-permute-start.21 = (bf16[128,768]{1,0:T(8,128)(2,1)S(1)}, bf16[128,768]{1,0:T(8,128)(2,1)S(1)}, u32[]{:S(2)}, u32[]{:S(2)}) collective-permute-start(bf16[128,768]{1,0:T(8,128)(2,1)S(1)} %get-tuple-element.73), channel_id=1, source_target_pairs={{1,0},{2,1},{3,2},{4,3},{5,4},{6,5},{7,6},{8,7},{9,8},{10,9},{11,1... | collective-permute-start | bytes 589832 | tf_op jit(solution)/shard_map/ppermute | solution.py:421
  51.1 7.4 %collective-permute-start.19 = (bf16[128,768]{1,0:T(8,128)(2,1)S(1)}, bf16[128,768]{1,0:T(8,128)(2,1)S(1)}, u32[]{:S(2)}, u32[]{:S(2)}) collective-permute-start(bf16[128,768]{1,0:T(8,128)(2,1)S(1)} %get-tuple-element.58.kv_own.kv_ref), channel_id=1, source_target_pairs={{0,1},{1,2},{2,3},{3,4},{4,5},{5,6},{6,7},{7,8},{8,9},{9,10},{10,1... | collective-permute-start | bytes 589832 | tf_op jit(solution)/shard_map/ppermute | solution.py:390
  57.7 10.5 %collective-permute-start.24 = (bf16[128,1536]{1,0:T(8,128)(2,1)S(1)}, bf16[128,1536]{1,0:T(8,128)(2,1)S(1)}, u32[]{:S(2)}, u32[]{:S(2)}) collective-permute-start(bf16[128,1536]{1,0:T(8,128)(2,1)S(1)} %shard_map.129), channel_id=1, source_target_pairs={{0,16},{16,0},{1,17},{17,1},{2,18},{18,2},{3,19},{19,3},{4,20},{20... | collective-permute-start | bytes 1179656 | tf_op jit(solution)/shard_map/ppermute | solution.py:316
  59.3 7.9 %collective-permute-start.23 = (bf16[128,768]{1,0:T(8,128)(2,1)S(1)}, bf16[128,768]{1,0:T(8,128)(2,1)S(1)}, u32[]{:S(2)}, u32[]{:S(2)}) collective-permute-start(bf16[128,768]{1,0:T(8,128)(2,1)S(1)} %get-tuple-element.90), channel_id=1, source_target_pairs={{1,0},{2,1},{3,2},{4,3},{5,4},{6,5},{7,6},{8,7},{9,8},{10,9},{11,1... | collective-permute-start | bytes 589832 | tf_op jit(solution)/shard_map/ppermute | solution.py:439
  (9 other events, 42.0 us)

commit v8 on v7

--- a/solution.py
+++ b/solution.py
@@ -167,9 +167,12 @@
 
 
 def memory_kernel(
-    rec, flags, cq_ref, cg_ref, rel_ref, own_ref, dp_ref, kv_ref, mem_ref,
-    p_ref, ds_ref, dmem_ref, ctx_ref,
-):
+    rec, flags, cq_ref, cg_ref, rel_ref, own_ref, dp_ref, kv_ref, mem_ref, *rest
+):
+    if rec == 0:
+        p_ref, ds_ref, dmem_ref, ctx_ref = rest
+    else:
+        wqo, p_ref, ds_ref, dmem_ref, lo_ref, ctx_ref = rest
     flag = flags[rec, 0:1, :].astype(F32)
     heads = range(HEADS)
     s_mem = [dot(cq_ref[rec, :, head(h)], mem_ref[:, head(h)], NT) for h in heads]
@@ -197,6 +200,8 @@
         dmem_ref[:, fv] = dot(p_mem, cg_ref[rec, :, f], TN).astype(BF16)
         ctx = dot(p_mem, mem_ref[:, fv]) + dot(p_own, kv_ref[:, fv])
         ctx_ref[:, f] = ctx.astype(BF16)
+    if rec == 1:
+        lo_ref[...] = dot(ctx_ref[...], wqo[:, HALF:], NT).astype(BF16)
 
 
 def grad_kernel(
@@ -224,12 +229,12 @@
     out_ref[...] = (np_ref[...] + dot(dkv, wkv[...], NT)).astype(out_ref.dtype)
 
 
-def partial_output_kernel(ctx_ref, wqo, out_ref):
-    out_ref[...] = dot(ctx_ref[...], wqo[:, HALF:], NT).astype(BF16)
-
-
-def output_kernel(x_ref, ctx_ref, wqo, lo_ret, out_ref):
+def own_kernel(
+    x_ref, ctx_ref, lo_ret, p_ref, ds_ref, cq_ref, cg_ref, kv_ref, mem_ref, pk_ref, wqo,
+    np_ref, dkv, out_ref, dq,
+):
     z, _, _ = place()
+    grad_kernel(0, p_ref, ds_ref, cq_ref, cg_ref, kv_ref, mem_ref, pk_ref, wqo, np_ref, dkv, dq)
     total = dot(ctx_ref[...], wqo[:, HALF:], NT)
     for r in range(ZS):
         cols, there = slice(r * BLK, (r + 1) * BLK), plane_columns(z, r)
@@ -399,13 +404,14 @@
         kv, kv_oth, pk, *qo_pieces,
     )
 
-    def memory(rec, kv_rows, mem_rows):
+    def memory(rec, *rows):
+        last = shape(SEG, D) if rec else shape(SEG, HALF)
         return call(
             functools.partial(memory_kernel, rec),
-            (shape(HEADS, SEG, SEG), shape(SEG, HEADS * 2 * SEG), half, shape(SEG, HALF)),
-            (),
-            [VM] * 8,
-        )(flags, cq, cg, rel, s_own, dp_own, kv_rows, mem_rows)
+            (shape(HEADS, SEG, SEG), shape(SEG, HEADS * 2 * SEG), half, last),
+            [pltpu.VMEM((SEG, HALF), BF16)] if rec else (),
+            [VM] * (6 + len(rows)),
+        )(flags, cq, cg, rel, s_own, dp_own, *rows)
 
     def grads(rec, p, ds, kv_rows, mem_rows):
         return call(
@@ -415,8 +421,7 @@
             [VM] * 8,
         )(p, ds, cq, cg, kv_rows, mem_rows, pk, wqo)
 
-    p_oth, ds_oth, dmem_oth, ctx_oth = memory(1, kv_oth, mem_oth)
-    lo_oth = call(partial_output_kernel, shape(SEG, D), (), [VM] * 2)(ctx_oth, wqo)
+    p_oth, ds_oth, dmem_oth, lo_oth = memory(1, kv_oth, mem_oth, wqo)
     lo_ret = other(lo_oth)
     ret_oth = lax.ppermute(dmem_oth, "tm", back)
     partial_oth, dkv_oth = grads(1, after(p_oth, lo_oth), ds_oth, kv_oth, mem_oth)
@@ -437,12 +442,14 @@
     )(inputs, gain, after(cot, np_oth))
     p, ds, dmem, ctx = memory(0, kv, after(mem, np_oth, hat[0]))
     ret = lax.ppermute(after(dmem, lo_ret), "tm", back)
-    partial, dkv = grads(0, after(p, dmem), ds, kv, mem)
-    layer_out = call(
-        output_kernel, shape(1, SEG, D), (), [VM] * 4
-    )(inputs, after(ctx, partial), wqo, lo_ret)
+    partial, dkv, layer_out = call(
+        own_kernel,
+        (shape(SEG, D, dtype=F32), half, shape(1, SEG, D)),
+        [pltpu.VMEM((SEG, HALF), BF16)],
+        [VM] * 11,
+    )(inputs, ctx, lo_ret, after(p, dmem), ds, cq, cg, kv, mem, pk, wqo)
     np_own = call(returned_kernel, shape(SEG, D, dtype=F32), (), [VM] * 4)(
-        after(partial, layer_out), dkv, ret, wkv
+        partial, dkv, ret, wkv
     )
     input_grad = call(finish_kernel, shape(1, SEG, D), (), [VM] * 6)(
         *hat, after(np_own, hat[0]), np_ret

time: 69.6 us -> 69.5 us (level)
    pallas_call x2 -> x1, Pallas kernels: 2.08 us -> 1.05 us  [grads(): call(functools.partial(grad_kernel, rec), (shape(SEG, D, dtype=F32), half...]
    pallas_call x2 -> x1, Pallas kernels: 1.79 us -> 2.17 us  [split_heads(): call(own_kernel, (shape(SEG, D, dtype=F32), half, shape(1, SEG, D)), [plt...]
where the time goes in v8:
time: 69.5 us; the launch traced here: 69.2 us
  starting transfers between devices  36.3 us (52%)
  waiting for transfers between devices  14.8 us (21%)
  Pallas kernels  14.5 us (21%)
  local copies, waits for them, and re-layouts  2.03 us (3%)
  between operations  1.51 us (2%)
    ppermute x17, starting transfers between devices, moved_by(): return lambda block: lax.ppermute(block, 'tm', route)  19.2 us
    ppermute x17, waiting for transfers between devices, moved_by(): return lambda block: lax.ppermute(block, 'tm', route)  11.5 us
    ppermute x1, starting transfers between devices, split_heads(): mem_oth = lax.ppermute(kv_oth, 'tm', onward)  4.74 us
    ppermute x1, starting transfers between devices, split_heads(): mem = lax.ppermute(kv, 'tm', onward)  4.15 us
    ppermute x4, starting transfers between devices, other(): return lax.ppermute(block, 'grp', [(0, 1), (1, 0)])  3.06 us
    ppermute x1, waiting for transfers between devices, split_heads(): ret = lax.ppermute(after(dmem, lo_ret), 'tm', back)  2.93 us
    ppermute x1, starting transfers between devices, split_heads(): ret = lax.ppermute(after(dmem, lo_ret), 'tm', back)  2.82 us
    pallas_call x1, Pallas kernels, split_heads(): call(prepare_kernel, (shape(4, ROWS, HALF), shape(SEG + 16, D), shape(2 *...  2.45 us
  transfers between devices with their start and end apart: 25, of which 8 were waited for; matrix products, arithmetic and copies ran while one was open for 0% of the time, Pallas kernels for 12%

profile of v8, /device:TPU:21, one launch (start us, length us, event | category | flops | bytes accessed | tf_op | source)
XLA Modules:
  0.0 69.2 jit_solution(2278533674470675726)
XLA Ops:
  1.3 2.4 %shard_map.122 = (bf16[4,96,384]{2,1,0:T(8,128)(2,1)}, bf16[144,1536]{1,0:T(8,128)(2,1)}, bf16[256,384]{1,0:T(8,128)(2,1)}) custom-call(bf16[96,384]{1,0:T(8,128)(2,1)} %k_ref.1, bf16[96,384]{1,0:T(8,128)(2,1)} %v_ref.1, bf16[96,384]{1,0:T(8,128)(2,1)} %q_ref.1, bf16[96,384]{1,0:T(8,128)(2,1)} %o_ref.1, bf16[1,128,1536]{2,1,0:T(8,128)(2,1)} %x_ref.5, ...), custom_call_target="tpu_custom_call" | custom-call | bytes 1024 | tf_op jit(solution)/shard_map/pallas_call | solution.py:339
  3.7 1.4 %collective-permute-start = (bf16[4,96,384]{2,1,0:T(8,128)(2,1)}, bf16[4,96,384]{2,1,0:T(8,128)(2,1)S(1)}, u32[]{:S(2)}, u32[]{:S(2)}) collective-permute-start(bf16[4,96,384]{2,1,0:T(8,128)(2,1)} %get-tuple-element.46.shard_ref), channel_id=1, source_target_pairs={{0,4},{1,5},{2,6},{3,7},{4,8},{5,9},{6,10},{7,11},{8,12},{9,13},{1... | collective-permute-start | bytes 884744 | tf_op jit(solution)/shard_map/ppermute | solution.py:307
  5.1 1.2 %collective-permute-start.5 = (bf16[144,1536]{1,0:T(8,128)(2,1)}, bf16[144,1536]{1,0:T(8,128)(2,1)S(1)}, u32[]{:S(2)}, u32[]{:S(2)}) collective-permute-start(bf16[144,1536]{1,0:T(8,128)(2,1)} %get-tuple-element.47.normed_ref), channel_id=1, source_target_pairs={{0,16},{16,0},{1,17},{17,1},{2,18},{18,2},{3,19},{19,3},{4,20},{20... | collective-permute-start | bytes 1327112 | tf_op jit(solution)/shard_map/ppermute | solution.py:321
  6.3 1.2 %collective-permute-start.7 = (bf16[4,96,384]{2,1,0:T(8,128)(2,1)}, bf16[4,96,384]{2,1,0:T(8,128)(2,1)S(1)}, u32[]{:S(2)}, u32[]{:S(2)}) collective-permute-start(bf16[4,96,384]{2,1,0:T(8,128)(2,1)} %get-tuple-element.46.shard_ref), channel_id=1, source_target_pairs={{0,1},{1,0},{2,3},{3,2},{4,5},{5,4},{6,7},{7,6},{8,9},{9,8},{10,11... | collective-permute-start | bytes 884744 | tf_op jit(solution)/shard_map/ppermute | solution.py:307
  10.0 2.0 %collective-permute-done.rest_4_ = bf16[4,96,384]{2,1,0:T(8,128)(2,1)S(1)} collective-permute-done((bf16[4,96,384]{2,1,0:T(8,128)(2,1)}, bf16[4,96,384]{2,1,0:T(8,128)(2,1)S(1)}, u32[]{:S(2)}, u32[]{:S(2)}) %collective-permute-start) | collective-permute-done | bytes 294944 | tf_op jit(solution)/shard_map/ppermute | solution.py:307
  12.1 1.3 %collective-permute-start.1 = (bf16[4,96,384]{2,1,0:T(8,128)(2,1)S(1)}, bf16[4,96,384]{2,1,0:T(8,128)(2,1)S(1)}, u32[]{:S(2)}, u32[]{:S(2)}) collective-permute-start(bf16[4,96,384]{2,1,0:T(8,128)(2,1)S(1)} %collective-permute-done.rest_4_), channel_id=1, source_target_pairs={{0,4},{1,5},{2,6},{3,7},{4,8},{5,9},{6,10},{7,11},{8,12},{9,13},{1... | collective-permute-start | bytes 884744 | tf_op jit(solution)/shard_map/ppermute | solution.py:307
  13.4 3.0 %collective-permute-done.6.rest_1_ = bf16[4,96,384]{2,1,0:T(8,128)(2,1)S(1)} collective-permute-done((bf16[4,96,384]{2,1,0:T(8,128)(2,1)}, bf16[4,96,384]{2,1,0:T(8,128)(2,1)S(1)}, u32[]{:S(2)}, u32[]{:S(2)}) %collective-permute-start.6) | collective-permute-done | bytes 294944 | tf_op jit(solution)/shard_map/ppermute | solution.py:307
  16.6 2.0 %collective-permute-done.2.rest_12_ = bf16[4,96,384]{2,1,0:T(8,128)(2,1)S(1)} collective-permute-done((bf16[4,96,384]{2,1,0:T(8,128)(2,1)}, bf16[4,96,384]{2,1,0:T(8,128)(2,1)S(1)}, u32[]{:S(2)}, u32[]{:S(2)}) %collective-permute-start.2) | collective-permute-done | bytes 294944 | tf_op jit(solution)/shard_map/ppermute | solution.py:307
  18.7 3.7 %collective-permute-start.8 = (bf16[4,96,384]{2,1,0:T(8,128)(2,1)S(1)}, bf16[4,96,384]{2,1,0:T(8,128)(2,1)S(1)}, u32[]{:S(2)}, u32[]{:S(2)}) collective-permute-start(bf16[4,96,384]{2,1,0:T(8,128)(2,1)S(1)} %collective-permute-done.6.rest_1_), channel_id=1, source_target_pairs={{0,1},{1,0},{2,3},{3,2},{4,5},{5,4},{6,7},{7,6},{8,9},{9,8},{10,11... | collective-permute-start | bytes 884744 | tf_op jit(solution)/shard_map/ppermute | solution.py:307
  22.5 1.2 %collective-permute-start.15 = (bf16[4,96,384]{2,1,0:T(8,128)(2,1)S(1)}, bf16[4,96,384]{2,1,0:T(8,128)(2,1)S(1)}, u32[]{:S(2)}, u32[]{:S(2)}) collective-permute-start(bf16[4,96,384]{2,1,0:T(8,128)(2,1)S(1)} %collective-permute-done.2.rest_12_), channel_id=1, source_target_pairs={{0,2},{1,3},{2,0},{3,1},{4,6},{5,7},{6,4},{7,5},{8,10},{9,11},{10,... | collective-permute-start | bytes 884744 | tf_op jit(solution)/shard_map/ppermute | solution.py:307
  23.8 5.4 %collective-permute-start.10 = (bf16[4,96,384]{2,1,0:T(8,128)(2,1)S(1)}, bf16[4,96,384]{2,1,0:T(8,128)(2,1)S(1)}, u32[]{:S(2)}, u32[]{:S(2)}) collective-permute-start(bf16[4,96,384]{2,1,0:T(8,128)(2,1)S(1)} %collective-permute-done.rest_4_), channel_id=1, source_target_pairs={{0,1},{1,0},{2,3},{3,2},{4,5},{5,4},{6,7},{7,6},{8,9},{9,8},{10,11... | collective-permute-start | bytes 884744 | tf_op jit(solution)/shard_map/ppermute | solution.py:307
  29.3 1.2 %collective-permute-start.3 = (bf16[2,96,384]{2,1,0:T(8,128)(2,1)S(1)}, bf16[2,96,384]{2,1,0:T(8,128)(2,1)S(1)}, u32[]{:S(2)}, u32[]{:S(2)}) collective-permute-start(bf16[2,96,384]{2,1,0:T(8,128)(2,1)S(1)} %slice.6), channel_id=1, source_target_pairs={{0,2},{1,3},{2,0},{3,1},{4,6},{5,7},{6,4},{7,5},{8,10},{9,11},{10,... | collective-permute-start | bytes 442376 | tf_op jit(solution)/shard_map/ppermute | solution.py:307
  30.4 1.6 %collective-permute-start.17 = (bf16[4,96,384]{2,1,0:T(8,128)(2,1)S(1)}, bf16[4,96,384]{2,1,0:T(8,128)(2,1)S(1)}, u32[]{:S(2)}, u32[]{:S(2)}) collective-permute-start(bf16[4,96,384]{2,1,0:T(8,128)(2,1)S(1)} %collective-permute-done.15.rest_13_), channel_id=1, source_target_pairs={{0,1},{1,0},{2,3},{3,2},{4,5},{5,4},{6,7},{7,6},{8,9},{9,8},{10,11... | collective-permute-start | bytes 884744 | tf_op jit(solution)/shard_map/ppermute | solution.py:307
  32.6 2.1 %collective-permute-done.3.rest_9_ = bf16[2,96,384]{2,1,0:T(8,128)(2,1)S(1)} collective-permute-done((bf16[2,96,384]{2,1,0:T(8,128)(2,1)S(1)}, bf16[2,96,384]{2,1,0:T(8,128)(2,1)S(1)}, u32[]{:S(2)}, u32[]{:S(2)}) %collective-permute-start.3) | collective-permute-done | bytes 147488 | tf_op jit(solution)/shard_map/ppermute | solution.py:307
  36.6 1.5 %shard_map.124 = (bf16[1536,768]{1,0:T(8,128)(2,1)S(1)}, bf16[128,768]{1,0:T(8,128)(2,1)S(1)}, bf16[128,768]{1,0:T(8,128)(2,1)S(1)}, bf16[256,1536]{1,0:T(8,128)(2,1)S(1)}, bf16[2,16,128]{2,1,0:T(8,128)(2,1)S(1)}) custom-call(bf16[144,1536]{1,0:T(8,128)(2,1)S(1)} %get-tuple-element.53.own_ref, bf16[144,1536]{1,0:T(8,128)(2,1)S(1)} %collective-permute-done.5.oth_ref, ...), custom_call_target="tpu_custom_call" | custom-call | bytes 1024 | tf_op jit(solution)/shard_map/pallas_call | solution.py:379
  38.1 4.7 %collective-permute-start.20 = (bf16[128,768]{1,0:T(8,128)(2,1)S(1)}, bf16[128,768]{1,0:T(8,128)(2,1)S(1)}, u32[]{:S(2)}, u32[]{:S(2)}) collective-permute-start(bf16[128,768]{1,0:T(8,128)(2,1)S(1)} %get-tuple-element.58.kv_oth.kv_ref), channel_id=1, source_target_pairs={{0,1},{1,2},{2,3},{3,4},{4,5},{5,6},{6,7},{7,8},{8,9},{9,10},{10,1... | collective-permute-start | bytes 589832 | tf_op jit(solution)/shard_map/ppermute | solution.py:394
  42.9 1.4 %collective-permute-done.18.rest_11_ = bf16[2,96,384]{2,1,0:T(8,128)(2,1)S(1)} collective-permute-done((bf16[2,96,384]{2,1,0:T(8,128)(2,1)S(1)}, bf16[2,96,384]{2,1,0:T(8,128)(2,1)S(1)}, u32[]{:S(2)}, u32[]{:S(2)}) %collective-permute-start.18) | collective-permute-done | bytes 147488 | tf_op jit(solution)/shard_map/ppermute | solution.py:307
  44.3 2.1 %shard_map.125 = (bf16[1536,768]{1,0:T(8,128)(2,1)S(1)}, bf16[2,128,384]{2,1,0:T(8,128)(2,1)S(1)}, bf16[2,128,384]{2,1,0:T(8,128)(2,1)S(1)}, f32[2,3,128,128]{3,...) custom-call(bf16[256,1536]{1,0:T(8,128)(2,1)S(1)} %get-tuple-element.56.xs, ...), custom_call_target="tpu_custom_call" | custom-call | bytes 1024 | tf_op jit(solution)/shard_map/pallas_call | solution.py:397
  48.6 2.3 %collective-permute-start.21 = (bf16[128,768]{1,0:T(8,128)(2,1)S(1)}, bf16[128,768]{1,0:T(8,128)(2,1)S(1)}, u32[]{:S(2)}, u32[]{:S(2)}) collective-permute-start(bf16[128,768]{1,0:T(8,128)(2,1)S(1)} %get-tuple-element.72), channel_id=1, source_target_pairs={{1,0},{2,1},{3,2},{4,3},{5,4},{6,5},{7,6},{8,7},{9,8},{10,9},{11,1... | collective-permute-start | bytes 589832 | tf_op jit(solution)/shard_map/ppermute | solution.py:426
  51.0 4.2 %collective-permute-start.19 = (bf16[128,768]{1,0:T(8,128)(2,1)S(1)}, bf16[128,768]{1,0:T(8,128)(2,1)S(1)}, u32[]{:S(2)}, u32[]{:S(2)}) collective-permute-start(bf16[128,768]{1,0:T(8,128)(2,1)S(1)} %get-tuple-element.57.kv_own.kv_ref), channel_id=1, source_target_pairs={{0,1},{1,2},{2,3},{3,4},{4,5},{5,6},{6,7},{7,8},{8,9},{9,10},{10,1... | collective-permute-start | bytes 589832 | tf_op jit(solution)/shard_map/ppermute | solution.py:395
  59.2 2.8 %collective-permute-start.23 = (bf16[128,768]{1,0:T(8,128)(2,1)S(1)}, bf16[128,768]{1,0:T(8,128)(2,1)S(1)}, u32[]{:S(2)}, u32[]{:S(2)}) collective-permute-start(bf16[128,768]{1,0:T(8,128)(2,1)S(1)} %get-tuple-element.88), channel_id=1, source_target_pairs={{1,0},{2,1},{3,2},{4,3},{5,4},{6,5},{7,6},{8,7},{9,8},{10,9},{11,1... | collective-permute-start | bytes 589832 | tf_op jit(solution)/shard_map/ppermute | solution.py:444
  62.0 2.2 %shard_map.131 = (f32[128,1536]{1,0:T(8,128)S(1)}, bf16[128,768]{1,0:T(8,128)(2,1)S(1)}, bf16[1,128,1536]{2,1,0:T(8,128)(2,1)}) custom-call(bf16[1,128,1536]{2,1,0:T(8,128)(2,1)S(1)} %copy-done, bf16[128,384]{1,0:T(8,128)(2,1)S(1)} %get-tuple-element.77.ctx_ref, bf16[128,1536]{1,0:T(8,128)(2,1)S(1)} %collective-permute-done.22.lo_ret, ...), custom_call_target="tpu_custom_call" | custom-call | bytes 1024 | tf_op jit(solution)/shard_map/pallas_call | solution.py:445
  64.2 2.9 %collective-permute-done.23.ret_ref = bf16[128,768]{1,0:T(8,128)(2,1)S(1)} collective-permute-done((bf16[128,768]{1,0:T(8,128)(2,1)S(1)}, bf16[128,768]{1,0:T(8,128)(2,1)S(1)}, u32[]{:S(2)}, u32[]{:S(2)}) %collective-permute-start.23) | collective-permute-done | bytes 196640 | tf_op jit(solution)/shard_map/ppermute | solution.py:444
  68.0 1.2 %shard_map.133 = bf16[1,128,1536]{2,1,0:T(8,128)(2,1)} custom-call(f32[128,1536]{1,0:T(8,128)S(1)} %get-tuple-element.75.hat_ref, f32[128,128]{1,0:T(8,128)S(1)} %get-tuple-element.83.rstd_ref, f32[8,1536]{1,0:T(8,128)S(1)} %get-tuple-element.84.gain_ref, bf16[128,1536]{1,0:T(8,128)(2,1)S(1)} %get-tuple-element.85.cot_ref, ...), custom_call_target="tpu_custom_call" | custom-call | bytes 1024 | tf_op jit(solution)/shard_map/pallas_call | solution.py:454
  (56 shorter events, 12.5 us)
Async XLA Ops:
  3.7 8.2 %collective-permute-start = (bf16[4,96,384]{2,1,0:T(8,128)(2,1)}, bf16[4,96,384]{2,1,0:T(8,128)(2,1)S(1)}, u32[]{:S(2)}, u32[]{:S(2)}) collective-permute-start(bf16[4,96,384]{2,1,0:T(8,128)(2,1)} %get-tuple-element.46.shard_ref), channel_id=1, source_target_pairs={{0,4},{1,5},{2,6},{3,7},{4,8},{5,9},{6,10},{7,11},{8,12},{9,13},{1... | collective-permute-start | bytes 884744 | tf_op jit(solution)/shard_map/ppermute | solution.py:307
  5.1 17.3 %collective-permute-start.5 = (bf16[144,1536]{1,0:T(8,128)(2,1)}, bf16[144,1536]{1,0:T(8,128)(2,1)S(1)}, u32[]{:S(2)}, u32[]{:S(2)}) collective-permute-start(bf16[144,1536]{1,0:T(8,128)(2,1)} %get-tuple-element.47.normed_ref), channel_id=1, source_target_pairs={{0,16},{16,0},{1,17},{17,1},{2,18},{18,2},{3,19},{19,3},{4,20},{20... | collective-permute-start | bytes 1327112 | tf_op jit(solution)/shard_map/ppermute | solution.py:321
  6.3 5.8 %collective-permute-start.7 = (bf16[4,96,384]{2,1,0:T(8,128)(2,1)}, bf16[4,96,384]{2,1,0:T(8,128)(2,1)S(1)}, u32[]{:S(2)}, u32[]{:S(2)}) collective-permute-start(bf16[4,96,384]{2,1,0:T(8,128)(2,1)} %get-tuple-element.46.shard_ref), channel_id=1, source_target_pairs={{0,1},{1,0},{2,3},{3,2},{4,5},{5,4},{6,7},{7,6},{8,9},{9,8},{10,11... | collective-permute-start | bytes 884744 | tf_op jit(solution)/shard_map/ppermute | solution.py:307
  7.5 8.8 %collective-permute-start.6 = (bf16[4,96,384]{2,1,0:T(8,128)(2,1)}, bf16[4,96,384]{2,1,0:T(8,128)(2,1)S(1)}, u32[]{:S(2)}, u32[]{:S(2)}) collective-permute-start(bf16[4,96,384]{2,1,0:T(8,128)(2,1)} %get-tuple-element.46.shard_ref), channel_id=1, source_target_pairs={{0,2},{1,3},{2,0},{3,1},{4,6},{5,7},{6,4},{7,5},{8,10},{9,11},{10,... | collective-permute-start | bytes 884744 | tf_op jit(solution)/shard_map/ppermute | solution.py:307
  7.8 10.9 %collective-permute-start.2 = (bf16[4,96,384]{2,1,0:T(8,128)(2,1)}, bf16[4,96,384]{2,1,0:T(8,128)(2,1)S(1)}, u32[]{:S(2)}, u32[]{:S(2)}) collective-permute-start(bf16[4,96,384]{2,1,0:T(8,128)(2,1)} %get-tuple-element.46.shard_ref), channel_id=1, source_target_pairs={{0,12},{1,13},{2,14},{3,15},{4,0},{5,1},{6,2},{7,3},{8,4},{9,5},{1... | collective-permute-start | bytes 884744 | tf_op jit(solution)/shard_map/ppermute | solution.py:307
  12.0 10.5 %collective-permute-start.9 = (bf16[4,96,384]{2,1,0:T(8,128)(2,1)S(1)}, bf16[4,96,384]{2,1,0:T(8,128)(2,1)S(1)}, u32[]{:S(2)}, u32[]{:S(2)}) collective-permute-start(bf16[4,96,384]{2,1,0:T(8,128)(2,1)S(1)} %collective-permute-done.rest_4_), channel_id=1, source_target_pairs={{0,2},{1,3},{2,0},{3,1},{4,6},{5,7},{6,4},{7,5},{8,10},{9,11},{10,... | collective-permute-start | bytes 884744 | tf_op jit(solution)/shard_map/ppermute | solution.py:307
  12.1 11.6 %collective-permute-start.1 = (bf16[4,96,384]{2,1,0:T(8,128)(2,1)S(1)}, bf16[4,96,384]{2,1,0:T(8,128)(2,1)S(1)}, u32[]{:S(2)}, u32[]{:S(2)}) collective-permute-start(bf16[4,96,384]{2,1,0:T(8,128)(2,1)S(1)} %collective-permute-done.rest_4_), channel_id=1, source_target_pairs={{0,4},{1,5},{2,6},{3,7},{4,8},{5,9},{6,10},{7,11},{8,12},{9,13},{1... | collective-permute-start | bytes 884744 | tf_op jit(solution)/shard_map/ppermute | solution.py:307
  16.4 15.7 %collective-permute-start.4 = (bf16[128,1536]{1,0:T(8,128)(2,1)}, bf16[128,1536]{1,0:T(8,128)(2,1)S(1)}, u32[]{:S(2)}, u32[]{:S(2)}) collective-permute-start(bf16[128,1536]{1,0:T(8,128)(2,1)} %bitcast.4), channel_id=1, source_target_pairs={{0,16},{16,0},{1,17},{17,1},{2,18},{18,2},{3,19},{19,3},{4,20},{20... | collective-permute-start | bytes 1179656 | tf_op jit(solution)/shard_map/ppermute | solution.py:321
  18.7 5.2 %collective-permute-start.8 = (bf16[4,96,384]{2,1,0:T(8,128)(2,1)S(1)}, bf16[4,96,384]{2,1,0:T(8,128)(2,1)S(1)}, u32[]{:S(2)}, u32[]{:S(2)}) collective-permute-start(bf16[4,96,384]{2,1,0:T(8,128)(2,1)S(1)} %collective-permute-done.6.rest_1_), channel_id=1, source_target_pairs={{0,1},{1,0},{2,3},{3,2},{4,5},{5,4},{6,7},{7,6},{8,9},{9,8},{10,11... | collective-permute-start | bytes 884744 | tf_op jit(solution)/shard_map/ppermute | solution.py:307
  22.4 6.9 %collective-permute-start.16 = (bf16[4,96,384]{2,1,0:T(8,128)(2,1)S(1)}, bf16[4,96,384]{2,1,0:T(8,128)(2,1)S(1)}, u32[]{:S(2)}, u32[]{:S(2)}) collective-permute-start(bf16[4,96,384]{2,1,0:T(8,128)(2,1)S(1)} %collective-permute-done.2.rest_12_), channel_id=1, source_target_pairs={{0,1},{1,0},{2,3},{3,2},{4,5},{5,4},{6,7},{7,6},{8,9},{9,8},{10,11... | collective-permute-start | bytes 884744 | tf_op jit(solution)/shard_map/ppermute | solution.py:307
  22.5 8.0 %collective-permute-start.15 = (bf16[4,96,384]{2,1,0:T(8,128)(2,1)S(1)}, bf16[4,96,384]{2,1,0:T(8,128)(2,1)S(1)}, u32[]{:S(2)}, u32[]{:S(2)}) collective-permute-start(bf16[4,96,384]{2,1,0:T(8,128)(2,1)S(1)} %collective-permute-done.2.rest_12_), channel_id=1, source_target_pairs={{0,2},{1,3},{2,0},{3,1},{4,6},{5,7},{6,4},{7,5},{8,10},{9,11},{10,... | collective-permute-start | bytes 884744 | tf_op jit(solution)/shard_map/ppermute | solution.py:307
  23.7 8.4 %collective-permute-start.12 = (bf16[2,96,384]{2,1,0:T(8,128)(2,1)S(1)}, bf16[2,96,384]{2,1,0:T(8,128)(2,1)S(1)}, u32[]{:S(2)}, u32[]{:S(2)}) collective-permute-start(bf16[2,96,384]{2,1,0:T(8,128)(2,1)S(1)} %slice.7), channel_id=1, source_target_pairs={{0,4},{1,5},{2,6},{3,7},{4,8},{5,9},{6,10},{7,11},{8,12},{9,13},{1... | collective-permute-start | bytes 442376 | tf_op jit(solution)/shard_map/ppermute | solution.py:307
  23.8 11.7 %collective-permute-start.10 = (bf16[4,96,384]{2,1,0:T(8,128)(2,1)S(1)}, bf16[4,96,384]{2,1,0:T(8,128)(2,1)S(1)}, u32[]{:S(2)}, u32[]{:S(2)}) collective-permute-start(bf16[4,96,384]{2,1,0:T(8,128)(2,1)S(1)} %collective-permute-done.rest_4_), channel_id=1, source_target_pairs={{0,1},{1,0},{2,3},{3,2},{4,5},{5,4},{6,7},{7,6},{8,9},{9,8},{10,11... | collective-permute-start | bytes 884744 | tf_op jit(solution)/shard_map/ppermute | solution.py:307
  29.3 5.4 %collective-permute-start.3 = (bf16[2,96,384]{2,1,0:T(8,128)(2,1)S(1)}, bf16[2,96,384]{2,1,0:T(8,128)(2,1)S(1)}, u32[]{:S(2)}, u32[]{:S(2)}) collective-permute-start(bf16[2,96,384]{2,1,0:T(8,128)(2,1)S(1)} %slice.6), channel_id=1, source_target_pairs={{0,2},{1,3},{2,0},{3,1},{4,6},{5,7},{6,4},{7,5},{8,10},{9,11},{10,... | collective-permute-start | bytes 442376 | tf_op jit(solution)/shard_map/ppermute | solution.py:307
  30.4 5.1 %collective-permute-start.17 = (bf16[4,96,384]{2,1,0:T(8,128)(2,1)S(1)}, bf16[4,96,384]{2,1,0:T(8,128)(2,1)S(1)}, u32[]{:S(2)}, u32[]{:S(2)}) collective-permute-start(bf16[4,96,384]{2,1,0:T(8,128)(2,1)S(1)} %collective-permute-done.15.rest_13_), channel_id=1, source_target_pairs={{0,1},{1,0},{2,3},{3,2},{4,5},{5,4},{6,7},{7,6},{8,9},{9,8},{10,11... | collective-permute-start | bytes 884744 | tf_op jit(solution)/shard_map/ppermute | solution.py:307
  32.1 4.5 %collective-permute-start.11 = (bf16[4,96,384]{2,1,0:T(8,128)(2,1)S(1)}, bf16[4,96,384]{2,1,0:T(8,128)(2,1)S(1)}, u32[]{:S(2)}, u32[]{:S(2)}) collective-permute-start(bf16[4,96,384]{2,1,0:T(8,128)(2,1)S(1)} %collective-permute-done.9.rest_5_), channel_id=1, source_target_pairs={{0,1},{1,0},{2,3},{3,2},{4,5},{5,4},{6,7},{7,6},{8,9},{9,8},{10,11... | collective-permute-start | bytes 884744 | tf_op jit(solution)/shard_map/ppermute | solution.py:307
  32.1 4.5 %collective-permute-start.13 = (bf16[4,96,384]{2,1,0:T(8,128)(2,1)S(1)}, bf16[4,96,384]{2,1,0:T(8,128)(2,1)S(1)}, u32[]{:S(2)}, u32[]{:S(2)}) collective-permute-start(bf16[4,96,384]{2,1,0:T(8,128)(2,1)S(1)} %collective-permute-done.1.rest_8_), channel_id=1, source_target_pairs={{0,1},{1,0},{2,3},{3,2},{4,5},{5,4},{6,7},{7,6},{8,9},{9,8},{10,11... | collective-permute-start | bytes 884744 | tf_op jit(solution)/shard_map/ppermute | solution.py:307
  34.7 1.9 %collective-permute-start.14 = (bf16[2,96,384]{2,1,0:T(8,128)(2,1)S(1)}, bf16[2,96,384]{2,1,0:T(8,128)(2,1)S(1)}, u32[]{:S(2)}, u32[]{:S(2)}) collective-permute-start(bf16[2,96,384]{2,1,0:T(8,128)(2,1)S(1)} %collective-permute-done.12.rest_9_), channel_id=1, source_target_pairs={{0,1},{1,0},{2,3},{3,2},{4,5},{5,4},{6,7},{7,6},{8,9},{9,8},{10,11... | collective-permute-start | bytes 442376 | tf_op jit(solution)/shard_map/ppermute | solution.py:307
  38.1 8.3 %collective-permute-start.20 = (bf16[128,768]{1,0:T(8,128)(2,1)S(1)}, bf16[128,768]{1,0:T(8,128)(2,1)S(1)}, u32[]{:S(2)}, u32[]{:S(2)}) collective-permute-start(bf16[128,768]{1,0:T(8,128)(2,1)S(1)} %get-tuple-element.58.kv_oth.kv_ref), channel_id=1, source_target_pairs={{0,1},{1,2},{2,3},{3,4},{4,5},{5,6},{6,7},{7,8},{8,9},{9,10},{10,1... | collective-permute-start | bytes 589832 | tf_op jit(solution)/shard_map/ppermute | solution.py:394
  47.5 11.6 %collective-permute-start.22 = (bf16[128,1536]{1,0:T(8,128)(2,1)S(1)}, bf16[128,1536]{1,0:T(8,128)(2,1)S(1)}, u32[]{:S(2)}, u32[]{:S(2)}) collective-permute-start(bf16[128,1536]{1,0:T(8,128)(2,1)S(1)} %get-tuple-element.67), channel_id=1, source_target_pairs={{0,16},{16,0},{1,17},{17,1},{2,18},{18,2},{3,19},{19,3},{4,20},{20... | collective-permute-start | bytes 1179656 | tf_op jit(solution)/shard_map/ppermute | solution.py:321
  48.6 8.0 %collective-permute-start.21 = (bf16[128,768]{1,0:T(8,128)(2,1)S(1)}, bf16[128,768]{1,0:T(8,128)(2,1)S(1)}, u32[]{:S(2)}, u32[]{:S(2)}) collective-permute-start(bf16[128,768]{1,0:T(8,128)(2,1)S(1)} %get-tuple-element.72), channel_id=1, source_target_pairs={{1,0},{2,1},{3,2},{4,3},{5,4},{6,5},{7,6},{8,7},{9,8},{10,9},{11,1... | collective-permute-start | bytes 589832 | tf_op jit(solution)/shard_map/ppermute | solution.py:426
  51.0 7.4 %collective-permute-start.19 = (bf16[128,768]{1,0:T(8,128)(2,1)S(1)}, bf16[128,768]{1,0:T(8,128)(2,1)S(1)}, u32[]{:S(2)}, u32[]{:S(2)}) collective-permute-start(bf16[128,768]{1,0:T(8,128)(2,1)S(1)} %get-tuple-element.57.kv_own.kv_ref), channel_id=1, source_target_pairs={{0,1},{1,2},{2,3},{3,4},{4,5},{5,6},{6,7},{7,8},{8,9},{9,10},{10,1... | collective-permute-start | bytes 589832 | tf_op jit(solution)/shard_map/ppermute | solution.py:395
  57.5 10.5 %collective-permute-start.24 = (bf16[128,1536]{1,0:T(8,128)(2,1)S(1)}, bf16[128,1536]{1,0:T(8,128)(2,1)S(1)}, u32[]{:S(2)}, u32[]{:S(2)}) collective-permute-start(bf16[128,1536]{1,0:T(8,128)(2,1)S(1)} %shard_map.128), channel_id=1, source_target_pairs={{0,16},{16,0},{1,17},{17,1},{2,18},{18,2},{3,19},{19,3},{4,20},{20... | collective-permute-start | bytes 1179656 | tf_op jit(solution)/shard_map/ppermute | solution.py:321
  59.2 7.9 %collective-permute-start.23 = (bf16[128,768]{1,0:T(8,128)(2,1)S(1)}, bf16[128,768]{1,0:T(8,128)(2,1)S(1)}, u32[]{:S(2)}, u32[]{:S(2)}) collective-permute-start(bf16[128,768]{1,0:T(8,128)(2,1)S(1)} %get-tuple-element.88), channel_id=1, source_target_pairs={{1,0},{2,1},{3,2},{4,3},{5,4},{6,5},{7,6},{8,7},{9,8},{10,9},{11,1... | collective-permute-start | bytes 589832 | tf_op jit(solution)/shard_map/ppermute | solution.py:444
  (9 other events, 42.0 us)

commit v9 on v8

--- a/solution.py
+++ b/solution.py
@@ -261,7 +261,7 @@
 
 def finish_kernel(hat_ref, rstd_ref, gain_ref, cot_ref, np_own, np_ret, grad_ref):
     z, _, _ = place()
-    step = 32
+    step = 16
     for i in range(0, SEG, step):
         rows = slice(i, i + step)
         hat, rstd = hat_ref[rows, :], rstd_ref[rows, 0:1]

time: 69.5 us -> 69.5 us (level)
  no operation moved by 1% of the time
where the time goes in v9:
time: 69.5 us; the launch traced here: 69.2 us
  starting transfers between devices  36.3 us (52%)
  waiting for transfers between devices  14.8 us (21%)
  Pallas kernels  14.5 us (21%)
  local copies, waits for them, and re-layouts  2.03 us (3%)
  between operations  1.51 us (2%)
    ppermute x17, starting transfers between devices, moved_by(): return lambda block: lax.ppermute(block, 'tm', route)  19.2 us
    ppermute x17, waiting for transfers between devices, moved_by(): return lambda block: lax.ppermute(block, 'tm', route)  11.5 us
    ppermute x1, starting transfers between devices, split_heads(): mem_oth = lax.ppermute(kv_oth, 'tm', onward)  4.74 us
    ppermute x1, starting transfers between devices, split_heads(): mem = lax.ppermute(kv, 'tm', onward)  4.15 us
    ppermute x4, starting transfers between devices, other(): return lax.ppermute(block, 'grp', [(0, 1), (1, 0)])  3.06 us
    ppermute x1, waiting for transfers between devices, split_heads(): ret = lax.ppermute(after(dmem, lo_ret), 'tm', back)  2.93 us
    ppermute x1, starting transfers between devices, split_heads(): ret = lax.ppermute(after(dmem, lo_ret), 'tm', back)  2.82 us
    pallas_call x1, Pallas kernels, split_heads(): call(prepare_kernel, (shape(4, ROWS, HALF), shape(SEG + 16, D), shape(2 *...  2.45 us
  transfers between devices with their start and end apart: 25, of which 8 were waited for; matrix products, arithmetic and copies ran while one was open for 0% of the time, Pallas kernels for 12%

profile of v9, /device:TPU:21, one launch (start us, length us, event | category | flops | bytes accessed | tf_op | source)
XLA Modules:
  0.0 69.2 jit_solution(14881681846262388403)
XLA Ops:
  1.3 2.4 %shard_map.122 = (bf16[4,96,384]{2,1,0:T(8,128)(2,1)}, bf16[144,1536]{1,0:T(8,128)(2,1)}, bf16[256,384]{1,0:T(8,128)(2,1)}) custom-call(bf16[96,384]{1,0:T(8,128)(2,1)} %k_ref.1, bf16[96,384]{1,0:T(8,128)(2,1)} %v_ref.1, bf16[96,384]{1,0:T(8,128)(2,1)} %q_ref.1, bf16[96,384]{1,0:T(8,128)(2,1)} %o_ref.1, bf16[1,128,1536]{2,1,0:T(8,128)(2,1)} %x_ref.5, ...), custom_call_target="tpu_custom_call" | custom-call | bytes 1024 | tf_op jit(solution)/shard_map/pallas_call | solution.py:339
  3.7 1.4 %collective-permute-start = (bf16[4,96,384]{2,1,0:T(8,128)(2,1)}, bf16[4,96,384]{2,1,0:T(8,128)(2,1)S(1)}, u32[]{:S(2)}, u32[]{:S(2)}) collective-permute-start(bf16[4,96,384]{2,1,0:T(8,128)(2,1)} %get-tuple-element.46.shard_ref), channel_id=1, source_target_pairs={{0,4},{1,5},{2,6},{3,7},{4,8},{5,9},{6,10},{7,11},{8,12},{9,13},{1... | collective-permute-start | bytes 884744 | tf_op jit(solution)/shard_map/ppermute | solution.py:307
  5.1 1.2 %collective-permute-start.5 = (bf16[144,1536]{1,0:T(8,128)(2,1)}, bf16[144,1536]{1,0:T(8,128)(2,1)S(1)}, u32[]{:S(2)}, u32[]{:S(2)}) collective-permute-start(bf16[144,1536]{1,0:T(8,128)(2,1)} %get-tuple-element.47.normed_ref), channel_id=1, source_target_pairs={{0,16},{16,0},{1,17},{17,1},{2,18},{18,2},{3,19},{19,3},{4,20},{20... | collective-permute-start | bytes 1327112 | tf_op jit(solution)/shard_map/ppermute | solution.py:321
  6.3 1.2 %collective-permute-start.7 = (bf16[4,96,384]{2,1,0:T(8,128)(2,1)}, bf16[4,96,384]{2,1,0:T(8,128)(2,1)S(1)}, u32[]{:S(2)}, u32[]{:S(2)}) collective-permute-start(bf16[4,96,384]{2,1,0:T(8,128)(2,1)} %get-tuple-element.46.shard_ref), channel_id=1, source_target_pairs={{0,1},{1,0},{2,3},{3,2},{4,5},{5,4},{6,7},{7,6},{8,9},{9,8},{10,11... | collective-permute-start | bytes 884744 | tf_op jit(solution)/shard_map/ppermute | solution.py:307
  10.0 2.0 %collective-permute-done.rest_4_ = bf16[4,96,384]{2,1,0:T(8,128)(2,1)S(1)} collective-permute-done((bf16[4,96,384]{2,1,0:T(8,128)(2,1)}, bf16[4,96,384]{2,1,0:T(8,128)(2,1)S(1)}, u32[]{:S(2)}, u32[]{:S(2)}) %collective-permute-start) | collective-permute-done | bytes 294944 | tf_op jit(solution)/shard_map/ppermute | solution.py:307
  12.1 1.3 %collective-permute-start.1 = (bf16[4,96,384]{2,1,0:T(8,128)(2,1)S(1)}, bf16[4,96,384]{2,1,0:T(8,128)(2,1)S(1)}, u32[]{:S(2)}, u32[]{:S(2)}) collective-permute-start(bf16[4,96,384]{2,1,0:T(8,128)(2,1)S(1)} %collective-permute-done.rest_4_), channel_id=1, source_target_pairs={{0,4},{1,5},{2,6},{3,7},{4,8},{5,9},{6,10},{7,11},{8,12},{9,13},{1... | collective-permute-start | bytes 884744 | tf_op jit(solution)/shard_map/ppermute | solution.py:307
  13.4 3.0 %collective-permute-done.6.rest_1_ = bf16[4,96,384]{2,1,0:T(8,128)(2,1)S(1)} collective-permute-done((bf16[4,96,384]{2,1,0:T(8,128)(2,1)}, bf16[4,96,384]{2,1,0:T(8,128)(2,1)S(1)}, u32[]{:S(2)}, u32[]{:S(2)}) %collective-permute-start.6) | collective-permute-done | bytes 294944 | tf_op jit(solution)/shard_map/ppermute | solution.py:307
  16.6 2.0 %collective-permute-done.2.rest_12_ = bf16[4,96,384]{2,1,0:T(8,128)(2,1)S(1)} collective-permute-done((bf16[4,96,384]{2,1,0:T(8,128)(2,1)}, bf16[4,96,384]{2,1,0:T(8,128)(2,1)S(1)}, u32[]{:S(2)}, u32[]{:S(2)}) %collective-permute-start.2) | collective-permute-done | bytes 294944 | tf_op jit(solution)/shard_map/ppermute | solution.py:307
  18.7 3.7 %collective-permute-start.8 = (bf16[4,96,384]{2,1,0:T(8,128)(2,1)S(1)}, bf16[4,96,384]{2,1,0:T(8,128)(2,1)S(1)}, u32[]{:S(2)}, u32[]{:S(2)}) collective-permute-start(bf16[4,96,384]{2,1,0:T(8,128)(2,1)S(1)} %collective-permute-done.6.rest_1_), channel_id=1, source_target_pairs={{0,1},{1,0},{2,3},{3,2},{4,5},{5,4},{6,7},{7,6},{8,9},{9,8},{10,11... | collective-permute-start | bytes 884744 | tf_op jit(solution)/shard_map/ppermute | solution.py:307
  22.5 1.2 %collective-permute-start.15 = (bf16[4,96,384]{2,1,0:T(8,128)(2,1)S(1)}, bf16[4,96,384]{2,1,0:T(8,128)(2,1)S(1)}, u32[]{:S(2)}, u32[]{:S(2)}) collective-permute-start(bf16[4,96,384]{2,1,0:T(8,128)(2,1)S(1)} %collective-permute-done.2.rest_12_), channel_id=1, source_target_pairs={{0,2},{1,3},{2,0},{3,1},{4,6},{5,7},{6,4},{7,5},{8,10},{9,11},{10,... | collective-permute-start | bytes 884744 | tf_op jit(solution)/shard_map/ppermute | solution.py:307
  23.8 5.4 %collective-permute-start.10 = (bf16[4,96,384]{2,1,0:T(8,128)(2,1)S(1)}, bf16[4,96,384]{2,1,0:T(8,128)(2,1)S(1)}, u32[]{:S(2)}, u32[]{:S(2)}) collective-permute-start(bf16[4,96,384]{2,1,0:T(8,128)(2,1)S(1)} %collective-permute-done.rest_4_), channel_id=1, source_target_pairs={{0,1},{1,0},{2,3},{3,2},{4,5},{5,4},{6,7},{7,6},{8,9},{9,8},{10,11... | collective-permute-start | bytes 884744 | tf_op jit(solution)/shard_map/ppermute | solution.py:307
  29.3 1.2 %collective-permute-start.3 = (bf16[2,96,384]{2,1,0:T(8,128)(2,1)S(1)}, bf16[2,96,384]{2,1,0:T(8,128)(2,1)S(1)}, u32[]{:S(2)}, u32[]{:S(2)}) collective-permute-start(bf16[2,96,384]{2,1,0:T(8,128)(2,1)S(1)} %slice.6), channel_id=1, source_target_pairs={{0,2},{1,3},{2,0},{3,1},{4,6},{5,7},{6,4},{7,5},{8,10},{9,11},{10,... | collective-permute-start | bytes 442376 | tf_op jit(solution)/shard_map/ppermute | solution.py:307
  30.4 1.6 %collective-permute-start.17 = (bf16[4,96,384]{2,1,0:T(8,128)(2,1)S(1)}, bf16[4,96,384]{2,1,0:T(8,128)(2,1)S(1)}, u32[]{:S(2)}, u32[]{:S(2)}) collective-permute-start(bf16[4,96,384]{2,1,0:T(8,128)(2,1)S(1)} %collective-permute-done.15.rest_13_), channel_id=1, source_target_pairs={{0,1},{1,0},{2,3},{3,2},{4,5},{5,4},{6,7},{7,6},{8,9},{9,8},{10,11... | collective-permute-start | bytes 884744 | tf_op jit(solution)/shard_map/ppermute | solution.py:307
  32.6 2.1 %collective-permute-done.3.rest_9_ = bf16[2,96,384]{2,1,0:T(8,128)(2,1)S(1)} collective-permute-done((bf16[2,96,384]{2,1,0:T(8,128)(2,1)S(1)}, bf16[2,96,384]{2,1,0:T(8,128)(2,1)S(1)}, u32[]{:S(2)}, u32[]{:S(2)}) %collective-permute-start.3) | collective-permute-done | bytes 147488 | tf_op jit(solution)/shard_map/ppermute | solution.py:307
  36.6 1.5 %shard_map.124 = (bf16[1536,768]{1,0:T(8,128)(2,1)S(1)}, bf16[128,768]{1,0:T(8,128)(2,1)S(1)}, bf16[128,768]{1,0:T(8,128)(2,1)S(1)}, bf16[256,1536]{1,0:T(8,128)(2,1)S(1)}, bf16[2,16,128]{2,1,0:T(8,128)(2,1)S(1)}) custom-call(bf16[144,1536]{1,0:T(8,128)(2,1)S(1)} %get-tuple-element.53.own_ref, bf16[144,1536]{1,0:T(8,128)(2,1)S(1)} %collective-permute-done.5.oth_ref, ...), custom_call_target="tpu_custom_call" | custom-call | bytes 1024 | tf_op jit(solution)/shard_map/pallas_call | solution.py:379
  38.1 4.7 %collective-permute-start.20 = (bf16[128,768]{1,0:T(8,128)(2,1)S(1)}, bf16[128,768]{1,0:T(8,128)(2,1)S(1)}, u32[]{:S(2)}, u32[]{:S(2)}) collective-permute-start(bf16[128,768]{1,0:T(8,128)(2,1)S(1)} %get-tuple-element.58.kv_oth.kv_ref), channel_id=1, source_target_pairs={{0,1},{1,2},{2,3},{3,4},{4,5},{5,6},{6,7},{7,8},{8,9},{9,10},{10,1... | collective-permute-start | bytes 589832 | tf_op jit(solution)/shard_map/ppermute | solution.py:394
  42.9 1.4 %collective-permute-done.18.rest_11_ = bf16[2,96,384]{2,1,0:T(8,128)(2,1)S(1)} collective-permute-done((bf16[2,96,384]{2,1,0:T(8,128)(2,1)S(1)}, bf16[2,96,384]{2,1,0:T(8,128)(2,1)S(1)}, u32[]{:S(2)}, u32[]{:S(2)}) %collective-permute-start.18) | collective-permute-done | bytes 147488 | tf_op jit(solution)/shard_map/ppermute | solution.py:307
  44.3 2.1 %shard_map.125 = (bf16[1536,768]{1,0:T(8,128)(2,1)S(1)}, bf16[2,128,384]{2,1,0:T(8,128)(2,1)S(1)}, bf16[2,128,384]{2,1,0:T(8,128)(2,1)S(1)}, f32[2,3,128,128]{3,...) custom-call(bf16[256,1536]{1,0:T(8,128)(2,1)S(1)} %get-tuple-element.56.xs, ...), custom_call_target="tpu_custom_call" | custom-call | bytes 1024 | tf_op jit(solution)/shard_map/pallas_call | solution.py:397
  48.6 2.3 %collective-permute-start.21 = (bf16[128,768]{1,0:T(8,128)(2,1)S(1)}, bf16[128,768]{1,0:T(8,128)(2,1)S(1)}, u32[]{:S(2)}, u32[]{:S(2)}) collective-permute-start(bf16[128,768]{1,0:T(8,128)(2,1)S(1)} %get-tuple-element.72), channel_id=1, source_target_pairs={{1,0},{2,1},{3,2},{4,3},{5,4},{6,5},{7,6},{8,7},{9,8},{10,9},{11,1... | collective-permute-start | bytes 589832 | tf_op jit(solution)/shard_map/ppermute | solution.py:426
  51.0 4.2 %collective-permute-start.19 = (bf16[128,768]{1,0:T(8,128)(2,1)S(1)}, bf16[128,768]{1,0:T(8,128)(2,1)S(1)}, u32[]{:S(2)}, u32[]{:S(2)}) collective-permute-start(bf16[128,768]{1,0:T(8,128)(2,1)S(1)} %get-tuple-element.57.kv_own.kv_ref), channel_id=1, source_target_pairs={{0,1},{1,2},{2,3},{3,4},{4,5},{5,6},{6,7},{7,8},{8,9},{9,10},{10,1... | collective-permute-start | bytes 589832 | tf_op jit(solution)/shard_map/ppermute | solution.py:395
  59.2 2.8 %collective-permute-start.23 = (bf16[128,768]{1,0:T(8,128)(2,1)S(1)}, bf16[128,768]{1,0:T(8,128)(2,1)S(1)}, u32[]{:S(2)}, u32[]{:S(2)}) collective-permute-start(bf16[128,768]{1,0:T(8,128)(2,1)S(1)} %get-tuple-element.88), channel_id=1, source_target_pairs={{1,0},{2,1},{3,2},{4,3},{5,4},{6,5},{7,6},{8,7},{9,8},{10,9},{11,1... | collective-permute-start | bytes 589832 | tf_op jit(solution)/shard_map/ppermute | solution.py:444
  62.0 2.2 %shard_map.131 = (f32[128,1536]{1,0:T(8,128)S(1)}, bf16[128,768]{1,0:T(8,128)(2,1)S(1)}, bf16[1,128,1536]{2,1,0:T(8,128)(2,1)}) custom-call(bf16[1,128,1536]{2,1,0:T(8,128)(2,1)S(1)} %copy-done, bf16[128,384]{1,0:T(8,128)(2,1)S(1)} %get-tuple-element.77.ctx_ref, bf16[128,1536]{1,0:T(8,128)(2,1)S(1)} %collective-permute-done.22.lo_ret, ...), custom_call_target="tpu_custom_call" | custom-call | bytes 1024 | tf_op jit(solution)/shard_map/pallas_call | solution.py:445
  64.2 2.9 %collective-permute-done.23.ret_ref = bf16[128,768]{1,0:T(8,128)(2,1)S(1)} collective-permute-done((bf16[128,768]{1,0:T(8,128)(2,1)S(1)}, bf16[128,768]{1,0:T(8,128)(2,1)S(1)}, u32[]{:S(2)}, u32[]{:S(2)}) %collective-permute-start.23) | collective-permute-done | bytes 196640 | tf_op jit(solution)/shard_map/ppermute | solution.py:444
  68.0 1.2 %shard_map.133 = bf16[1,128,1536]{2,1,0:T(8,128)(2,1)} custom-call(f32[128,1536]{1,0:T(8,128)S(1)} %get-tuple-element.75.hat_ref, f32[128,128]{1,0:T(8,128)S(1)} %get-tuple-element.83.rstd_ref, f32[8,1536]{1,0:T(8,128)S(1)} %get-tuple-element.84.gain_ref, bf16[128,1536]{1,0:T(8,128)(2,1)S(1)} %get-tuple-element.85.cot_ref, ...), custom_call_target="tpu_custom_call" | custom-call | bytes 1024 | tf_op jit(solution)/shard_map/pallas_call | solution.py:454
  (56 shorter events, 12.5 us)
Async XLA Ops:
  3.7 8.2 %collective-permute-start = (bf16[4,96,384]{2,1,0:T(8,128)(2,1)}, bf16[4,96,384]{2,1,0:T(8,128)(2,1)S(1)}, u32[]{:S(2)}, u32[]{:S(2)}) collective-permute-start(bf16[4,96,384]{2,1,0:T(8,128)(2,1)} %get-tuple-element.46.shard_ref), channel_id=1, source_target_pairs={{0,4},{1,5},{2,6},{3,7},{4,8},{5,9},{6,10},{7,11},{8,12},{9,13},{1... | collective-permute-start | bytes 884744 | tf_op jit(solution)/shard_map/ppermute | solution.py:307
  5.1 17.3 %collective-permute-start.5 = (bf16[144,1536]{1,0:T(8,128)(2,1)}, bf16[144,1536]{1,0:T(8,128)(2,1)S(1)}, u32[]{:S(2)}, u32[]{:S(2)}) collective-permute-start(bf16[144,1536]{1,0:T(8,128)(2,1)} %get-tuple-element.47.normed_ref), channel_id=1, source_target_pairs={{0,16},{16,0},{1,17},{17,1},{2,18},{18,2},{3,19},{19,3},{4,20},{20... | collective-permute-start | bytes 1327112 | tf_op jit(solution)/shard_map/ppermute | solution.py:321
  6.3 5.8 %collective-permute-start.7 = (bf16[4,96,384]{2,1,0:T(8,128)(2,1)}, bf16[4,96,384]{2,1,0:T(8,128)(2,1)S(1)}, u32[]{:S(2)}, u32[]{:S(2)}) collective-permute-start(bf16[4,96,384]{2,1,0:T(8,128)(2,1)} %get-tuple-element.46.shard_ref), channel_id=1, source_target_pairs={{0,1},{1,0},{2,3},{3,2},{4,5},{5,4},{6,7},{7,6},{8,9},{9,8},{10,11... | collective-permute-start | bytes 884744 | tf_op jit(solution)/shard_map/ppermute | solution.py:307
  7.5 8.8 %collective-permute-start.6 = (bf16[4,96,384]{2,1,0:T(8,128)(2,1)}, bf16[4,96,384]{2,1,0:T(8,128)(2,1)S(1)}, u32[]{:S(2)}, u32[]{:S(2)}) collective-permute-start(bf16[4,96,384]{2,1,0:T(8,128)(2,1)} %get-tuple-element.46.shard_ref), channel_id=1, source_target_pairs={{0,2},{1,3},{2,0},{3,1},{4,6},{5,7},{6,4},{7,5},{8,10},{9,11},{10,... | collective-permute-start | bytes 884744 | tf_op jit(solution)/shard_map/ppermute | solution.py:307
  7.8 10.9 %collective-permute-start.2 = (bf16[4,96,384]{2,1,0:T(8,128)(2,1)}, bf16[4,96,384]{2,1,0:T(8,128)(2,1)S(1)}, u32[]{:S(2)}, u32[]{:S(2)}) collective-permute-start(bf16[4,96,384]{2,1,0:T(8,128)(2,1)} %get-tuple-element.46.shard_ref), channel_id=1, source_target_pairs={{0,12},{1,13},{2,14},{3,15},{4,0},{5,1},{6,2},{7,3},{8,4},{9,5},{1... | collective-permute-start | bytes 884744 | tf_op jit(solution)/shard_map/ppermute | solution.py:307
  12.0 10.5 %collective-permute-start.9 = (bf16[4,96,384]{2,1,0:T(8,128)(2,1)S(1)}, bf16[4,96,384]{2,1,0:T(8,128)(2,1)S(1)}, u32[]{:S(2)}, u32[]{:S(2)}) collective-permute-start(bf16[4,96,384]{2,1,0:T(8,128)(2,1)S(1)} %collective-permute-done.rest_4_), channel_id=1, source_target_pairs={{0,2},{1,3},{2,0},{3,1},{4,6},{5,7},{6,4},{7,5},{8,10},{9,11},{10,... | collective-permute-start | bytes 884744 | tf_op jit(solution)/shard_map/ppermute | solution.py:307
  12.1 11.6 %collective-permute-start.1 = (bf16[4,96,384]{2,1,0:T(8,128)(2,1)S(1)}, bf16[4,96,384]{2,1,0:T(8,128)(2,1)S(1)}, u32[]{:S(2)}, u32[]{:S(2)}) collective-permute-start(bf16[4,96,384]{2,1,0:T(8,128)(2,1)S(1)} %collective-permute-done.rest_4_), channel_id=1, source_target_pairs={{0,4},{1,5},{2,6},{3,7},{4,8},{5,9},{6,10},{7,11},{8,12},{9,13},{1... | collective-permute-start | bytes 884744 | tf_op jit(solution)/shard_map/ppermute | solution.py:307
  16.4 15.7 %collective-permute-start.4 = (bf16[128,1536]{1,0:T(8,128)(2,1)}, bf16[128,1536]{1,0:T(8,128)(2,1)S(1)}, u32[]{:S(2)}, u32[]{:S(2)}) collective-permute-start(bf16[128,1536]{1,0:T(8,128)(2,1)} %bitcast.4), channel_id=1, source_target_pairs={{0,16},{16,0},{1,17},{17,1},{2,18},{18,2},{3,19},{19,3},{4,20},{20... | collective-permute-start | bytes 1179656 | tf_op jit(solution)/shard_map/ppermute | solution.py:321
  18.7 5.2 %collective-permute-start.8 = (bf16[4,96,384]{2,1,0:T(8,128)(2,1)S(1)}, bf16[4,96,384]{2,1,0:T(8,128)(2,1)S(1)}, u32[]{:S(2)}, u32[]{:S(2)}) collective-permute-start(bf16[4,96,384]{2,1,0:T(8,128)(2,1)S(1)} %collective-permute-done.6.rest_1_), channel_id=1, source_target_pairs={{0,1},{1,0},{2,3},{3,2},{4,5},{5,4},{6,7},{7,6},{8,9},{9,8},{10,11... | collective-permute-start | bytes 884744 | tf_op jit(solution)/shard_map/ppermute | solution.py:307
  22.4 6.9 %collective-permute-start.16 = (bf16[4,96,384]{2,1,0:T(8,128)(2,1)S(1)}, bf16[4,96,384]{2,1,0:T(8,128)(2,1)S(1)}, u32[]{:S(2)}, u32[]{:S(2)}) collective-permute-start(bf16[4,96,384]{2,1,0:T(8,128)(2,1)S(1)} %collective-permute-done.2.rest_12_), channel_id=1, source_target_pairs={{0,1},{1,0},{2,3},{3,2},{4,5},{5,4},{6,7},{7,6},{8,9},{9,8},{10,11... | collective-permute-start | bytes 884744 | tf_op jit(solution)/shard_map/ppermute | solution.py:307
  22.5 8.0 %collective-permute-start.15 = (bf16[4,96,384]{2,1,0:T(8,128)(2,1)S(1)}, bf16[4,96,384]{2,1,0:T(8,128)(2,1)S(1)}, u32[]{:S(2)}, u32[]{:S(2)}) collective-permute-start(bf16[4,96,384]{2,1,0:T(8,128)(2,1)S(1)} %collective-permute-done.2.rest_12_), channel_id=1, source_target_pairs={{0,2},{1,3},{2,0},{3,1},{4,6},{5,7},{6,4},{7,5},{8,10},{9,11},{10,... | collective-permute-start | bytes 884744 | tf_op jit(solution)/shard_map/ppermute | solution.py:307
  23.7 8.4 %collective-permute-start.12 = (bf16[2,96,384]{2,1,0:T(8,128)(2,1)S(1)}, bf16[2,96,384]{2,1,0:T(8,128)(2,1)S(1)}, u32[]{:S(2)}, u32[]{:S(2)}) collective-permute-start(bf16[2,96,384]{2,1,0:T(8,128)(2,1)S(1)} %slice.7), channel_id=1, source_target_pairs={{0,4},{1,5},{2,6},{3,7},{4,8},{5,9},{6,10},{7,11},{8,12},{9,13},{1... | collective-permute-start | bytes 442376 | tf_op jit(solution)/shard_map/ppermute | solution.py:307
  23.8 11.7 %collective-permute-start.10 = (bf16[4,96,384]{2,1,0:T(8,128)(2,1)S(1)}, bf16[4,96,384]{2,1,0:T(8,128)(2,1)S(1)}, u32[]{:S(2)}, u32[]{:S(2)}) collective-permute-start(bf16[4,96,384]{2,1,0:T(8,128)(2,1)S(1)} %collective-permute-done.rest_4_), channel_id=1, source_target_pairs={{0,1},{1,0},{2,3},{3,2},{4,5},{5,4},{6,7},{7,6},{8,9},{9,8},{10,11... | collective-permute-start | bytes 884744 | tf_op jit(solution)/shard_map/ppermute | solution.py:307
  29.3 5.4 %collective-permute-start.3 = (bf16[2,96,384]{2,1,0:T(8,128)(2,1)S(1)}, bf16[2,96,384]{2,1,0:T(8,128)(2,1)S(1)}, u32[]{:S(2)}, u32[]{:S(2)}) collective-permute-start(bf16[2,96,384]{2,1,0:T(8,128)(2,1)S(1)} %slice.6), channel_id=1, source_target_pairs={{0,2},{1,3},{2,0},{3,1},{4,6},{5,7},{6,4},{7,5},{8,10},{9,11},{10,... | collective-permute-start | bytes 442376 | tf_op jit(solution)/shard_map/ppermute | solution.py:307
  30.4 5.1 %collective-permute-start.17 = (bf16[4,96,384]{2,1,0:T(8,128)(2,1)S(1)}, bf16[4,96,384]{2,1,0:T(8,128)(2,1)S(1)}, u32[]{:S(2)}, u32[]{:S(2)}) collective-permute-start(bf16[4,96,384]{2,1,0:T(8,128)(2,1)S(1)} %collective-permute-done.15.rest_13_), channel_id=1, source_target_pairs={{0,1},{1,0},{2,3},{3,2},{4,5},{5,4},{6,7},{7,6},{8,9},{9,8},{10,11... | collective-permute-start | bytes 884744 | tf_op jit(solution)/shard_map/ppermute | solution.py:307
  32.1 4.5 %collective-permute-start.11 = (bf16[4,96,384]{2,1,0:T(8,128)(2,1)S(1)}, bf16[4,96,384]{2,1,0:T(8,128)(2,1)S(1)}, u32[]{:S(2)}, u32[]{:S(2)}) collective-permute-start(bf16[4,96,384]{2,1,0:T(8,128)(2,1)S(1)} %collective-permute-done.9.rest_5_), channel_id=1, source_target_pairs={{0,1},{1,0},{2,3},{3,2},{4,5},{5,4},{6,7},{7,6},{8,9},{9,8},{10,11... | collective-permute-start | bytes 884744 | tf_op jit(solution)/shard_map/ppermute | solution.py:307
  32.1 4.5 %collective-permute-start.13 = (bf16[4,96,384]{2,1,0:T(8,128)(2,1)S(1)}, bf16[4,96,384]{2,1,0:T(8,128)(2,1)S(1)}, u32[]{:S(2)}, u32[]{:S(2)}) collective-permute-start(bf16[4,96,384]{2,1,0:T(8,128)(2,1)S(1)} %collective-permute-done.1.rest_8_), channel_id=1, source_target_pairs={{0,1},{1,0},{2,3},{3,2},{4,5},{5,4},{6,7},{7,6},{8,9},{9,8},{10,11... | collective-permute-start | bytes 884744 | tf_op jit(solution)/shard_map/ppermute | solution.py:307
  34.7 1.9 %collective-permute-start.14 = (bf16[2,96,384]{2,1,0:T(8,128)(2,1)S(1)}, bf16[2,96,384]{2,1,0:T(8,128)(2,1)S(1)}, u32[]{:S(2)}, u32[]{:S(2)}) collective-permute-start(bf16[2,96,384]{2,1,0:T(8,128)(2,1)S(1)} %collective-permute-done.12.rest_9_), channel_id=1, source_target_pairs={{0,1},{1,0},{2,3},{3,2},{4,5},{5,4},{6,7},{7,6},{8,9},{9,8},{10,11... | collective-permute-start | bytes 442376 | tf_op jit(solution)/shard_map/ppermute | solution.py:307
  38.1 8.3 %collective-permute-start.20 = (bf16[128,768]{1,0:T(8,128)(2,1)S(1)}, bf16[128,768]{1,0:T(8,128)(2,1)S(1)}, u32[]{:S(2)}, u32[]{:S(2)}) collective-permute-start(bf16[128,768]{1,0:T(8,128)(2,1)S(1)} %get-tuple-element.58.kv_oth.kv_ref), channel_id=1, source_target_pairs={{0,1},{1,2},{2,3},{3,4},{4,5},{5,6},{6,7},{7,8},{8,9},{9,10},{10,1... | collective-permute-start | bytes 589832 | tf_op jit(solution)/shard_map/ppermute | solution.py:394
  47.5 11.6 %collective-permute-start.22 = (bf16[128,1536]{1,0:T(8,128)(2,1)S(1)}, bf16[128,1536]{1,0:T(8,128)(2,1)S(1)}, u32[]{:S(2)}, u32[]{:S(2)}) collective-permute-start(bf16[128,1536]{1,0:T(8,128)(2,1)S(1)} %get-tuple-element.67), channel_id=1, source_target_pairs={{0,16},{16,0},{1,17},{17,1},{2,18},{18,2},{3,19},{19,3},{4,20},{20... | collective-permute-start | bytes 1179656 | tf_op jit(solution)/shard_map/ppermute | solution.py:321
  48.6 8.0 %collective-permute-start.21 = (bf16[128,768]{1,0:T(8,128)(2,1)S(1)}, bf16[128,768]{1,0:T(8,128)(2,1)S(1)}, u32[]{:S(2)}, u32[]{:S(2)}) collective-permute-start(bf16[128,768]{1,0:T(8,128)(2,1)S(1)} %get-tuple-element.72), channel_id=1, source_target_pairs={{1,0},{2,1},{3,2},{4,3},{5,4},{6,5},{7,6},{8,7},{9,8},{10,9},{11,1... | collective-permute-start | bytes 589832 | tf_op jit(solution)/shard_map/ppermute | solution.py:426
  51.0 7.4 %collective-permute-start.19 = (bf16[128,768]{1,0:T(8,128)(2,1)S(1)}, bf16[128,768]{1,0:T(8,128)(2,1)S(1)}, u32[]{:S(2)}, u32[]{:S(2)}) collective-permute-start(bf16[128,768]{1,0:T(8,128)(2,1)S(1)} %get-tuple-element.57.kv_own.kv_ref), channel_id=1, source_target_pairs={{0,1},{1,2},{2,3},{3,4},{4,5},{5,6},{6,7},{7,8},{8,9},{9,10},{10,1... | collective-permute-start | bytes 589832 | tf_op jit(solution)/shard_map/ppermute | solution.py:395
  57.5 10.5 %collective-permute-start.24 = (bf16[128,1536]{1,0:T(8,128)(2,1)S(1)}, bf16[128,1536]{1,0:T(8,128)(2,1)S(1)}, u32[]{:S(2)}, u32[]{:S(2)}) collective-permute-start(bf16[128,1536]{1,0:T(8,128)(2,1)S(1)} %shard_map.128), channel_id=1, source_target_pairs={{0,16},{16,0},{1,17},{17,1},{2,18},{18,2},{3,19},{19,3},{4,20},{20... | collective-permute-start | bytes 1179656 | tf_op jit(solution)/shard_map/ppermute | solution.py:321
  59.2 7.9 %collective-permute-start.23 = (bf16[128,768]{1,0:T(8,128)(2,1)S(1)}, bf16[128,768]{1,0:T(8,128)(2,1)S(1)}, u32[]{:S(2)}, u32[]{:S(2)}) collective-permute-start(bf16[128,768]{1,0:T(8,128)(2,1)S(1)} %get-tuple-element.88), channel_id=1, source_target_pairs={{1,0},{2,1},{3,2},{4,3},{5,4},{6,5},{7,6},{8,7},{9,8},{10,9},{11,1... | collective-permute-start | bytes 589832 | tf_op jit(solution)/shard_map/ppermute | solution.py:444
  (9 other events, 42.0 us)
